TPU v7x, 128 devices: a whole 4x4x4 slice. The times are simulated.
128 devices in a mesh: gx: 8 (over z_lo, y), gy: 8 (over x, core), gz: 2 (over z_hi).
Axes of the slice: x: 4, y: 4, z: 4 (z_hi: 2, z_lo: 2; z = z_hi * 2 + z_lo), core: 2. Of those that a mesh axis runs over, the one named last changes fastest.
Arguments:
- orbitals: float32 [32, 64, 64, 256], P(None, 'gx', 'gy', 'gz'), may hold values from -6 to 6
- potential: float32 [64, 64, 256], P('gx', 'gy', 'gz'), may hold values from 0 to 2
- projector: float32 [4, 1048576], P(None, ('gx', 'gy', 'gz')), may hold values from -0.1875 to 0.1875
- point_cell: int32 [1048576], P(('gx', 'gy', 'gz')), may hold values from 0 to 8191
- target: int32 [1048576], P(('gx', 'gy', 'gz')), may hold values from 0 to 53
- point_count: int32 [8, 8, 2], P('gx', 'gy', 'gz'), may hold values from 2730 to 8192, as said below
- coupling: float32 [256, 4], P(('gx', 'gy', 'gz')), may hold values from 1 to 3
Outputs:
- subspace: float32 [32, 64, 64, 256], P(None, 'gx', 'gy', 'gz')
Inputs may be any that keep to these rules, and one draw needn't show every extreme that they name: Some domain has exactly 8192 live point slots; slots from point_count on are ignored.
All inputs are finite; a program needn't handle non-finite values.
Results may differ from a plain program's by a relative error of at most 0.0003.
Values sent between devices are 32-bit elements; how exact they have to be, the bound alone decides.
No kernel may reach another device: no remote copies, remote signals or barrier semaphores. Data moves between devices by JAX's collectives and lax.ppermute only.
A program may use at most 128 MiB of HBM per device.

v0:
```python
import jax
import jax.numpy as jnp
from jax import lax
from jax.sharding import PartitionSpec as P

DEGREE = 4


STENCIL = (
    -5369.0 / 1800.0,
    12.0 / 7.0,
    -15.0 / 56.0,
    10.0 / 189.0,
    -1.0 / 112.0,
    2.0 / 1925.0,
    -1.0 / 16632.0,
)
FILTER_CENTRE = 9.5
FILTER_HALF = 5.5


def extended(cells, sides, width):
    for axis, dim in sides:
        count = lax.axis_size(axis)
        head = lax.slice_in_dim(cells, 0, width, axis=dim)
        tail = lax.slice_in_dim(cells, cells.shape[dim] - width, cells.shape[dim], axis=dim)
        cells = jnp.concatenate(
            [
                lax.ppermute(tail, axis, [(i, (i + 1) % count) for i in range(count)]),
                cells,
                lax.ppermute(head, axis, [((i + 1) % count, i) for i in range(count)]),
            ],
            axis=dim,
        )
    return cells


def local(orbitals, potential, projector, point_cell, target, point_count, coupling):
    bands, size_x, size_y, size_z = orbitals.shape
    cells = size_x * size_y * size_z
    channels, slots = projector.shape
    atoms_here = coupling.shape[0]
    targets = 27 * atoms_here
    width = channels * bands
    alive_mask = (lax.iota(jnp.int32, slots) < point_count.reshape(())).astype(jnp.float32)
    weight = projector * alive_mask[None, :]
    onehot = (target[None, :] == lax.iota(jnp.int32, targets)[:, None]).astype(jnp.float32)

    def laplace(field):
        summed = 3.0 * STENCIL[0] * field
        padded = extended(field, (("gx", 1), ("gy", 2), ("gz", 3)), 6)
        along_x = padded[:, :, 6 : 6 + size_y, 6 : 6 + size_z]
        along_y = padded[:, 6 : 6 + size_x, :, 6 : 6 + size_z]
        along_z = padded[:, 6 : 6 + size_x, 6 : 6 + size_y, :]
        for offset in range(1, 7):
            paired = (
                along_x[:, 6 + offset : 6 + offset + size_x]
                + along_x[:, 6 - offset : 6 - offset + size_x]
            )
            paired = (
                paired
                + along_y[:, :, 6 + offset : 6 + offset + size_y]
                + along_y[:, :, 6 - offset : 6 - offset + size_y]
            )
            paired = (
                paired
                + along_z[:, :, :, 6 + offset : 6 + offset + size_z]
                + along_z[:, :, :, 6 - offset : 6 - offset + size_z]
            )
            summed = summed + STENCIL[offset] * paired
        return summed

    def nonlocal_term(field):
        flattened = field.reshape(bands, cells)
        at_points = jnp.take(flattened, point_cell, axis=1)
        weighted = (weight[:, None, :] * at_points[None, :, :]).reshape(width, slots)
        partial_sums = lax.dot_general(
            onehot, weighted, (((1,), (1,)), ((), ())), precision=lax.Precision.HIGHEST
        )
        blocks = partial_sums.reshape(3, 3, 3, atoms_here * width)
        padded = extended(blocks, (("gx", 0), ("gy", 1), ("gz", 2)), 1)
        owned_sums = jnp.sum(padded[0::2, 0::2, 0::2], axis=(0, 1, 2))
        scaled = (owned_sums.reshape(atoms_here, channels, bands) * coupling[:, :, None]).reshape(
            1, 1, 1, atoms_here * width
        )
        nearby = extended(scaled, (("gx", 0), ("gy", 1), ("gz", 2)), 1).reshape(targets, width)
        back = lax.dot_general(
            nearby, onehot, (((0,), (0,)), ((), ())), precision=lax.Precision.HIGHEST
        )
        values = jnp.sum(back.reshape(channels, bands, slots) * weight[:, None, :], axis=0)
        added = jnp.zeros((bands, cells), jnp.float32).at[:, point_cell].add(values)
        return added.reshape(field.shape)

    def hamiltonian(field):
        return -0.5 * laplace(field) + potential[None] * field + nonlocal_term(field)

    previous = orbitals
    current = (hamiltonian(orbitals) - FILTER_CENTRE * orbitals) / FILTER_HALF
    for degree_step in range(DEGREE - 1):
        following = 2.0 * (hamiltonian(current) - FILTER_CENTRE * current) / FILTER_HALF - previous
        previous, current = (current, following)
    flattened = current.reshape(bands, cells)
    local_gram = jnp.dot(flattened, flattened.T, precision=lax.Precision.HIGHEST)
    total_cells = cells * lax.axis_size("gx") * lax.axis_size("gy") * lax.axis_size("gz")
    gram_matrix = lax.psum(local_gram, ("gx", "gy", "gz")) / float(total_cells)
    lower_factor = jnp.linalg.cholesky(gram_matrix)
    inverse = jax.scipy.linalg.solve_triangular(
        lower_factor, jnp.eye(bands, dtype=jnp.float32), lower=True
    )
    return jnp.dot(inverse, flattened, precision=lax.Precision.HIGHEST).reshape(orbitals.shape)


def solution(mesh):
    in_specs = (
        P(None, "gx", "gy", "gz"),
        P("gx", "gy", "gz"),
        P(None, ("gx", "gy", "gz")),
        P(("gx", "gy", "gz")),
        P(("gx", "gy", "gz")),
        P("gx", "gy", "gz"),
        P(("gx", "gy", "gz"), None),
    )
    out_specs = P(None, "gx", "gy", "gz")
    return jax.shard_map(local, mesh=mesh, in_specs=in_specs, out_specs=out_specs, check_vma=False)
```

profile of v0, /device:TPU:1, one launch (start us, length us, event | category | flops | bytes accessed | tf_op | source)
XLA Modules:
  0.0 1222.4 jit_solution(3604539444504780047)
XLA Ops:
  11.4 30.1 %gather_fusion = f32[8192,32]{1,0:T(8,128)} fusion(f32[32,8192]{0,1:T(8,128)} %bitcast.91, s32[8192]{0:T(1024)S(1)} %get-tuple-element.61), kind=kCustom, calls=%fused_computation.clone | custom fusion | bytes 2129920 | tf_op jit(solution)/shard_map/jit(_take)/gather | solution.py:75
  41.5 7.6 select_bitcast_fusion.3
  73.5 13.3 %collective-permute-done.9 = f32[5,1,3,256]{3,2,1,0:T(4,128)S(1)} collective-permute-done((f32[5,1,3,256]{3,2,1,0:T(4,128)S(1)}, f32[5,1,3,256]{3,2,1,0:T(4,128)S(1)}, u32[]{:S(2)}, u32[]{:S(2)}) %collective-permute-start.9) | collective-permute-done | bytes 15392 | tf_op jit(solution)/shard_map/ppermute | solution.py:31
  112.7 11.5 fusion.265
  143.0 54.2 %collective-permute-done.17 = f32[3,3,1,256]{3,2,1,0:T(1,128)S(1)} collective-permute-done((f32[3,3,1,256]{3,2,1,0:T(1,128)S(1)}, f32[3,3,1,256]{3,2,1,0:T(1,128)S(1)}, u32[]{:S(2)}, u32[]{:S(2)}) %collective-permute-start.17) | collective-permute-done | bytes 9248 | tf_op jit(solution)/shard_map/ppermute | solution.py:31
  202.3 46.9 %scatter_custom_fusion = f32[32,8192]{0,1:T(8,128)} fusion(s32[8192]{0:T(1024)S(1)} %get-tuple-element.62, f32[8192,32]{1,0:T(8,128)} %copy.110, f32[]{:T(128)} %constant.83.clone.1), kind=kCustom, calls=%fused_computation.119 | custom fusion | flops 262144 | bytes 1049088 | tf_op jit(solution)/shard_map/scatter-add | solution.py:91
  263.2 23.4 %broadcast_multiply_fusion.4 = (f32[32,8,8,128]{3,0,2,1:T(8,128)S(1)}, f32[32,8,8,128]{3,0,2,1:T(8,128)}) fusion(f32[32,8,8,128]{3,0,2,1:T(8,128)S(1)} %copy.111, f32[8,8,128]{2,1,0:T(8,128)S(1)} %copy-done.15, f32[32,20,6,128]{3,0,2,1:T(8,128)} %collective-permute-done.2, f32[32,20,8,128]{3,0,2,1:T(8,128)} %copy-done, ...), kind=kLoop, calls=%fused_computation.418 | loop fusion | flops 25690112 | bytes 23977984 | tf_op jit(solution)/shard_map/div | solution.py:98
  290.8 30.1 %gather_fusion.1 = f32[8192,32]{1,0:T(8,128)} fusion(f32[32,8192]{0,1:T(8,128)} %bitcast.93, s32[8192]{0:T(1024)S(1)} %get-tuple-element.61), kind=kCustom, calls=%fused_computation.1.clone | custom fusion | bytes 2129920 | tf_op jit(solution)/shard_map/jit(_take)/gather | solution.py:75
  320.9 7.4 select_bitcast_fusion.2
  337.1 14.9 %collective-permute-done.19 = f32[32,6,8,128]{3,0,2,1:T(8,128)S(1)} collective-permute-done((f32[32,6,8,128]{3,0,2,1:T(8,128)}, f32[32,6,8,128]{3,0,2,1:T(8,128)S(1)}, u32[]{:S(2)}, u32[]{:S(2)}) %collective-permute-start.19) | collective-permute-done | bytes 786464 | tf_op jit(solution)/shard_map/ppermute | solution.py:29
  366.2 13.9 %collective-permute-done.27 = f32[5,1,3,256]{3,2,1,0:T(4,128)S(1)} collective-permute-done((f32[5,1,3,256]{3,2,1,0:T(4,128)S(1)}, f32[5,1,3,256]{3,2,1,0:T(4,128)S(1)}, u32[]{:S(2)}, u32[]{:S(2)}) %collective-permute-start.27) | collective-permute-done | bytes 15392 | tf_op jit(solution)/shard_map/ppermute | solution.py:31
  418.4 46.5 %scatter_custom_fusion.1 = f32[32,8192]{0,1:T(8,128)} fusion(s32[8192]{0:T(1024)S(1)} %get-tuple-element.62, f32[8192,32]{1,0:T(8,128)} %copy.120, f32[]{:T(128)} %constant.83.clone.1), kind=kCustom, calls=%fused_computation.117 | custom fusion | flops 262144 | bytes 1049088 | tf_op jit(solution)/shard_map/scatter-add | solution.py:91
  473.2 11.3 fusion.264
  506.5 15.7 %collective-permute-done.23 = f32[32,20,20,6]{0,2,3,1:T(8,128)} collective-permute-done((f32[32,20,20,6]{0,2,3,1:T(8,128)}, f32[32,20,20,6]{0,2,3,1:T(8,128)}, u32[]{:S(2)}, u32[]{:S(2)}) %collective-permute-start.23) | collective-permute-done | bytes 307232 | tf_op jit(solution)/shard_map/ppermute | solution.py:29
  527.7 26.1 %collective-permute-done.22 = f32[32,20,20,6]{0,2,3,1:T(8,128)} collective-permute-done((f32[32,20,20,6]{0,2,3,1:T(8,128)}, f32[32,20,20,6]{0,2,3,1:T(8,128)}, u32[]{:S(2)}, u32[]{:S(2)}) %collective-permute-start.22) | collective-permute-done | bytes 307232 | tf_op jit(solution)/shard_map/ppermute | solution.py:31
  559.4 16.7 %fusion.147 = f32[32,8,8,128]{3,0,2,1:T(8,128)S(1)} fusion(f32[32,8,8,128]{3,0,2,1:T(8,128)} %copy.121, f32[32,8,8,128]{3,0,2,1:T(8,128)S(1)} %get-tuple-element.6, f32[32,6,8,128]{3,0,2,1:T(8,128)} %copy-done.9, f32[32,6,8,128]{3,0,2,1:T(8,128)} %copy-done.10, f32[32,20,20,6]{3,0,2,1:T(8,128)} %copy.116, f32[32,20,6,128]{3,0,2,1:T(8,128)} %collective-permute-done.20, ...), kind=kLoop, calls=%fused_computation.251 | loop fusion | flops 32243712 | bytes 23977984 | tf_op jit(solution)/shard_map/sub | solution.py:100
  580.3 30.1 %gather_fusion.2 = f32[8192,32]{1,0:T(8,128)} fusion(f32[32,8192]{0,1:T(8,128)} %bitcast.94, s32[8192]{0:T(1024)S(1)} %get-tuple-element.61), kind=kCustom, calls=%fused_computation.2.clone | custom fusion | bytes 2129920 | tf_op jit(solution)/shard_map/jit(_take)/gather | solution.py:75
  650.9 8.0 collective-permute-done.45
  676.8 10.5 collective-permute-start.51
  703.0 46.5 %scatter_custom_fusion.2 = f32[32,8192]{0,1:T(8,128)} fusion(s32[8192]{0:T(1024)S(1)} %get-tuple-element.62, f32[8192,32]{1,0:T(8,128)} %copy.130, f32[]{:T(128)} %constant.83.clone.1), kind=kCustom, calls=%fused_computation.115 | custom fusion | flops 262144 | bytes 1049088 | tf_op jit(solution)/shard_map/scatter-add | solution.py:91
  758.4 11.3 fusion.263
  791.7 15.6 %collective-permute-done.41 = f32[32,20,20,6]{0,2,3,1:T(8,128)} collective-permute-done((f32[32,20,20,6]{0,2,3,1:T(8,128)}, f32[32,20,20,6]{0,2,3,1:T(8,128)}, u32[]{:S(2)}, u32[]{:S(2)}) %collective-permute-start.41) | collective-permute-done | bytes 307232 | tf_op jit(solution)/shard_map/ppermute | solution.py:29
  812.9 26.1 %collective-permute-done.40 = f32[32,20,20,6]{0,2,3,1:T(8,128)} collective-permute-done((f32[32,20,20,6]{0,2,3,1:T(8,128)}, f32[32,20,20,6]{0,2,3,1:T(8,128)}, u32[]{:S(2)}, u32[]{:S(2)}) %collective-permute-start.40) | collective-permute-done | bytes 307232 | tf_op jit(solution)/shard_map/ppermute | solution.py:31
  844.6 16.0 %fusion.95 = f32[32,8,8,128]{3,0,2,1:T(8,128)S(1)} fusion(f32[32,8,8,128]{3,0,2,1:T(8,128)} %copy.131, f32[32,8,8,128]{3,0,2,1:T(8,128)S(1)} %fusion.147, f32[32,6,8,128]{3,0,2,1:T(8,128)S(1)} %copy-done.7, f32[32,6,8,128]{3,0,2,1:T(8,128)} %copy-done.8, f32[32,20,20,6]{3,0,2,1:T(8,128)} %copy.126, f32[32,20,6,128]{3,0,2,1:T(8,128)} %copy-done.5, ...), kind=kLoop, calls=%fused_computation.199 | loop fusion | flops 32505856 | bytes 22929408 | tf_op jit(solution)/shard_map/sub | solution.py:100
  864.7 30.1 %gather_fusion.3 = f32[8192,32]{1,0:T(8,128)} fusion(f32[32,8192]{0,1:T(8,128)} %bitcast.92, s32[8192]{0:T(1024)S(1)} %get-tuple-element.61), kind=kCustom, calls=%fused_computation.3.clone | custom fusion | bytes 2129920 | tf_op jit(solution)/shard_map/jit(_take)/gather | solution.py:75
  960.7 10.5 collective-permute-start.69
  986.1 46.5 %scatter_custom_fusion.3 = f32[32,8192]{0,1:T(8,128)} fusion(s32[8192]{0:T(1024)S(1)} %get-tuple-element.62, f32[8192,32]{1,0:T(8,128)} %copy.139, f32[]{:T(128)} %constant.83.clone.1), kind=kCustom, calls=%fused_computation.113 | custom fusion | flops 262144 | bytes 1049088 | tf_op jit(solution)/shard_map/scatter-add | solution.py:91
  1040.9 11.5 fusion.262
  1074.3 15.6 %collective-permute-done.59 = f32[32,20,20,6]{0,2,3,1:T(8,128)} collective-permute-done((f32[32,20,20,6]{0,2,3,1:T(8,128)}, f32[32,20,20,6]{0,2,3,1:T(8,128)}, u32[]{:S(2)}, u32[]{:S(2)}) %collective-permute-start.59) | collective-permute-done | bytes 307232 | tf_op jit(solution)/shard_map/ppermute | solution.py:29
  1095.4 26.1 %collective-permute-done.58 = f32[32,20,20,6]{0,2,3,1:T(8,128)} collective-permute-done((f32[32,20,20,6]{0,2,3,1:T(8,128)}, f32[32,20,20,6]{0,2,3,1:T(8,128)}, u32[]{:S(2)}, u32[]{:S(2)}) %collective-permute-start.58) | collective-permute-done | bytes 307232 | tf_op jit(solution)/shard_map/ppermute | solution.py:31
  1127.1 15.3 %fusion.43 = f32[32,8,8,128]{3,0,2,1:T(8,128)S(1)} fusion(f32[32,8,8,128]{3,0,2,1:T(8,128)S(1)} %fusion.147, f32[32,8,8,128]{3,0,2,1:T(8,128)} %copy.140, f32[32,8,8,128]{3,0,2,1:T(8,128)S(1)} %fusion.95, f32[32,6,8,128]{3,0,2,1:T(8,128)S(1)} %collective-permute-done.55, f32[32,6,8,128]{3,0,2,1:T(8,128)} %collective-permute-done.54, ...), kind=kLoop, calls=%fused_computation.147 | loop fusion | flops 32243712 | bytes 22929408 | tf_op jit(solution)/shard_map/sub | solution.py:100
  1144.0 67.0 %psum.7 = f32[32,32]{0,1:T(8,128)S(1)} all-reduce(f32[32,32]{0,1:T(8,128)S(1)} %convolution_bitcast_fusion.1), channel_id=1, replica_groups=mesh['gx'=8,'gy'=8,'gz'=2] {'gx','gy','gz'}, use_global_device_ids=true, to_apply=%region_12.14 | all-reduce | flops 1024 | bytes 8192 | tf_op jit(solution)/shard_map/psum | solution.py:105
  (332 shorter events, 464.2 us)
Async XLA Ops:
  1.8 50.8 %collective-permute-start.1 = (f32[32,6,8,128]{3,0,2,1:T(8,128)S(1)}, f32[32,6,8,128]{3,0,2,1:T(8,128)}, u32[]{:S(2)}, u32[]{:S(2)}) collective-permute-start(f32[32,6,8,128]{3,0,2,1:T(8,128)S(1)} %copy.159), channel_id=1, source_target_pairs={{0,16},{16,32},{32,48},{48,64},{64,80},{80,96},{96,112},{112,0},{1... | collective-permute-start | bytes 2359304 | tf_op jit(solution)/shard_map/ppermute | solution.py:29
  5.2 50.7 %collective-permute-start = (f32[32,6,8,128]{3,0,2,1:T(8,128)}, f32[32,6,8,128]{3,0,2,1:T(8,128)}, u32[]{:S(2)}, u32[]{:S(2)}) collective-permute-start(f32[32,6,8,128]{3,0,2,1:T(8,128)} %copy.160), channel_id=1, source_target_pairs={{16,0},{32,16},{48,32},{64,48},{80,64},{96,80},{112,96},{0,112},{1... | collective-permute-start | bytes 2359304 | tf_op jit(solution)/shard_map/ppermute | solution.py:31
  61.6 45.2 %collective-permute-start.2 = (f32[32,20,6,128]{3,0,2,1:T(8,128)}, f32[32,20,6,128]{3,0,2,1:T(8,128)}, u32[]{:S(2)}, u32[]{:S(2)}) collective-permute-start(f32[32,20,6,128]{3,0,2,1:T(8,128)} %get-tuple-element.29), channel_id=1, source_target_pairs={{2,0},{4,2},{6,4},{8,6},{10,8},{12,10},{14,12},{0,14},{3,1},{5,3},... | collective-permute-start | bytes 5898248 | tf_op jit(solution)/shard_map/ppermute | solution.py:31
  62.6 44.2 %collective-permute-start.3 = (f32[32,20,6,128]{3,0,2,1:T(8,128)}, f32[32,20,6,128]{3,0,2,1:T(8,128)}, u32[]{:S(2)}, u32[]{:S(2)}) collective-permute-start(f32[32,20,6,128]{3,0,2,1:T(8,128)} %get-tuple-element.28), channel_id=1, source_target_pairs={{0,2},{2,4},{4,6},{6,8},{8,10},{10,12},{12,14},{14,0},{1,3},{3,5},... | collective-permute-start | bytes 5898248 | tf_op jit(solution)/shard_map/ppermute | solution.py:29
  71.6 15.3 %collective-permute-start.9 = (f32[5,1,3,256]{3,2,1,0:T(4,128)S(1)}, f32[5,1,3,256]{3,2,1,0:T(4,128)S(1)}, u32[]{:S(2)}, u32[]{:S(2)}) collective-permute-start(f32[5,1,3,256]{3,2,1,0:T(4,128)S(1)} %get-tuple-element.60), channel_id=1, source_target_pairs={{2,0},{4,2},{6,4},{8,6},{10,8},{12,10},{14,12},{0,14},{3,1},{5,3},... | collective-permute-start | bytes 46088 | tf_op jit(solution)/shard_map/ppermute | solution.py:31
  100.8 39.1 %collective-permute-start.15 = (f32[3,1,1,256]{3,2,1,0:T(1,128)S(1)}, f32[3,1,1,256]{3,2,1,0:T(1,128)S(1)}, u32[]{:S(2)}, u32[]{:S(2)}) collective-permute-start(f32[3,1,1,256]{3,2,1,0:T(1,128)S(1)} %pad_maximum_fusion.78), channel_id=1, source_target_pairs={{2,0},{4,2},{6,4},{8,6},{10,8},{12,10},{14,12},{0,14},{3,1},{5,3},... | collective-permute-start | bytes 9224 | tf_op jit(solution)/shard_map/ppermute | solution.py:31
  106.8 33.2 %collective-permute-start.14 = (f32[3,1,1,256]{3,2,1,0:T(1,128)S(1)}, f32[3,1,1,256]{3,2,1,0:T(1,128)S(1)}, u32[]{:S(2)}, u32[]{:S(2)}) collective-permute-start(f32[3,1,1,256]{3,2,1,0:T(1,128)S(1)} %pad_maximum_fusion.78), channel_id=1, source_target_pairs={{0,2},{2,4},{4,6},{6,8},{8,10},{10,12},{12,14},{14,0},{1,3},{3,5},... | collective-permute-start | bytes 9224 | tf_op jit(solution)/shard_map/ppermute | solution.py:29
  130.4 121.6 %collective-permute-start.5 = (f32[32,20,20,6]{0,2,3,1:T(8,128)S(1)}, f32[32,20,20,6]{0,2,3,1:T(8,128)}, u32[]{:S(2)}, u32[]{:S(2)}) collective-permute-start(f32[32,20,20,6]{0,2,3,1:T(8,128)S(1)} %copy.104), channel_id=1, source_target_pairs={{0,1},{1,0},{2,3},{3,2},{4,5},{5,4},{6,7},{7,6},{8,9},{9,8},{10,11... | collective-permute-start | bytes 921608 | tf_op jit(solution)/shard_map/ppermute | solution.py:29
  137.8 119.8 %collective-permute-start.4 = (f32[32,20,20,6]{0,2,3,1:T(8,128)}, f32[32,20,20,6]{0,2,3,1:T(8,128)}, u32[]{:S(2)}, u32[]{:S(2)}) collective-permute-start(f32[32,20,20,6]{0,2,3,1:T(8,128)} %copy.102), channel_id=1, source_target_pairs={{1,0},{0,1},{3,2},{2,3},{5,4},{4,5},{7,6},{6,7},{9,8},{8,9},{11,10... | collective-permute-start | bytes 921608 | tf_op jit(solution)/shard_map/ppermute | solution.py:31
  140.0 57.3 %collective-permute-start.17 = (f32[3,3,1,256]{3,2,1,0:T(1,128)S(1)}, f32[3,3,1,256]{3,2,1,0:T(1,128)S(1)}, u32[]{:S(2)}, u32[]{:S(2)}) collective-permute-start(f32[3,3,1,256]{3,2,1,0:T(1,128)S(1)} %pad_maximum_fusion.74), channel_id=1, source_target_pairs={{1,0},{0,1},{3,2},{2,3},{5,4},{4,5},{7,6},{6,7},{9,8},{8,9},{11,10... | collective-permute-start | bytes 27656 | tf_op jit(solution)/shard_map/ppermute | solution.py:31
  140.9 56.5 %collective-permute-start.16 = (f32[3,3,1,256]{3,2,1,0:T(1,128)S(1)}, f32[3,3,1,256]{3,2,1,0:T(1,128)S(1)}, u32[]{:S(2)}, u32[]{:S(2)}) collective-permute-start(f32[3,3,1,256]{3,2,1,0:T(1,128)S(1)} %pad_maximum_fusion.74), channel_id=1, source_target_pairs={{0,1},{1,0},{2,3},{3,2},{4,5},{5,4},{6,7},{7,6},{8,9},{9,8},{10,11... | collective-permute-start | bytes 27656 | tf_op jit(solution)/shard_map/ppermute | solution.py:29
  331.9 20.1 %collective-permute-start.19 = (f32[32,6,8,128]{3,0,2,1:T(8,128)}, f32[32,6,8,128]{3,0,2,1:T(8,128)S(1)}, u32[]{:S(2)}, u32[]{:S(2)}) collective-permute-start(f32[32,6,8,128]{3,0,2,1:T(8,128)} %get-tuple-element.35), channel_id=1, source_target_pairs={{0,16},{16,32},{32,48},{48,64},{64,80},{80,96},{96,112},{112,0},{1... | collective-permute-start | bytes 2359304 | tf_op jit(solution)/shard_map/ppermute | solution.py:29
  331.9 20.1 %collective-permute-start.18 = (f32[32,6,8,128]{3,0,2,1:T(8,128)}, f32[32,6,8,128]{3,0,2,1:T(8,128)S(1)}, u32[]{:S(2)}, u32[]{:S(2)}) collective-permute-start(f32[32,6,8,128]{3,0,2,1:T(8,128)} %get-tuple-element.34), channel_id=1, source_target_pairs={{16,0},{32,16},{48,32},{64,48},{80,64},{96,80},{112,96},{0,112},{1... | collective-permute-start | bytes 2359304 | tf_op jit(solution)/shard_map/ppermute | solution.py:31
  354.8 113.7 %collective-permute-start.20 = (f32[32,20,6,128]{3,0,2,1:T(8,128)}, f32[32,20,6,128]{3,0,2,1:T(8,128)}, u32[]{:S(2)}, u32[]{:S(2)}) collective-permute-start(f32[32,20,6,128]{3,0,2,1:T(8,128)} %get-tuple-element.27), channel_id=1, source_target_pairs={{2,0},{4,2},{6,4},{8,6},{10,8},{12,10},{14,12},{0,14},{3,1},{5,3},... | collective-permute-start | bytes 5898248 | tf_op jit(solution)/shard_map/ppermute | solution.py:31
  357.0 111.5 %collective-permute-start.21 = (f32[32,20,6,128]{3,0,2,1:T(8,128)}, f32[32,20,6,128]{3,0,2,1:T(8,128)}, u32[]{:S(2)}, u32[]{:S(2)}) collective-permute-start(f32[32,20,6,128]{3,0,2,1:T(8,128)} %get-tuple-element.26), channel_id=1, source_target_pairs={{0,2},{2,4},{4,6},{6,8},{8,10},{10,12},{12,14},{14,0},{1,3},{3,5},... | collective-permute-start | bytes 5898248 | tf_op jit(solution)/shard_map/ppermute | solution.py:29
  364.4 15.7 %collective-permute-start.27 = (f32[5,1,3,256]{3,2,1,0:T(4,128)S(1)}, f32[5,1,3,256]{3,2,1,0:T(4,128)S(1)}, u32[]{:S(2)}, u32[]{:S(2)}) collective-permute-start(f32[5,1,3,256]{3,2,1,0:T(4,128)S(1)} %get-tuple-element.58), channel_id=1, source_target_pairs={{2,0},{4,2},{6,4},{8,6},{10,8},{12,10},{14,12},{0,14},{3,1},{5,3},... | collective-permute-start | bytes 46088 | tf_op jit(solution)/shard_map/ppermute | solution.py:31
  366.1 14.0 %collective-permute-start.26 = (f32[5,1,3,256]{3,2,1,0:T(4,128)S(1)}, f32[5,1,3,256]{3,2,1,0:T(4,128)S(1)}, u32[]{:S(2)}, u32[]{:S(2)}) collective-permute-start(f32[5,1,3,256]{3,2,1,0:T(4,128)S(1)} %get-tuple-element.57), channel_id=1, source_target_pairs={{0,2},{2,4},{4,6},{6,8},{8,10},{10,12},{12,14},{14,0},{1,3},{3,5},... | collective-permute-start | bytes 46088 | tf_op jit(solution)/shard_map/ppermute | solution.py:29
  491.1 31.1 %collective-permute-start.23 = (f32[32,20,20,6]{0,2,3,1:T(8,128)}, f32[32,20,20,6]{0,2,3,1:T(8,128)}, u32[]{:S(2)}, u32[]{:S(2)}) collective-permute-start(f32[32,20,20,6]{0,2,3,1:T(8,128)} %copy.115), channel_id=1, source_target_pairs={{0,1},{1,0},{2,3},{3,2},{4,5},{5,4},{6,7},{7,6},{8,9},{9,8},{10,11... | collective-permute-start | bytes 921608 | tf_op jit(solution)/shard_map/ppermute | solution.py:29
  497.6 56.1 %collective-permute-start.22 = (f32[32,20,20,6]{0,2,3,1:T(8,128)}, f32[32,20,20,6]{0,2,3,1:T(8,128)}, u32[]{:S(2)}, u32[]{:S(2)}) collective-permute-start(f32[32,20,20,6]{0,2,3,1:T(8,128)} %copy.113), channel_id=1, source_target_pairs={{1,0},{0,1},{3,2},{2,3},{5,4},{4,5},{7,6},{6,7},{9,8},{8,9},{11,10... | collective-permute-start | bytes 921608 | tf_op jit(solution)/shard_map/ppermute | solution.py:31
  610.4 15.9 %collective-permute-start.37 = (f32[32,6,8,128]{3,0,2,1:T(8,128)}, f32[32,6,8,128]{3,0,2,1:T(8,128)S(1)}, u32[]{:S(2)}, u32[]{:S(2)}) collective-permute-start(f32[32,6,8,128]{3,0,2,1:T(8,128)} %get-tuple-element.33), channel_id=1, source_target_pairs={{0,16},{16,32},{32,48},{48,64},{64,80},{80,96},{96,112},{112,0},{1... | collective-permute-start | bytes 2359304 | tf_op jit(solution)/shard_map/ppermute | solution.py:29
  610.4 15.9 %collective-permute-start.36 = (f32[32,6,8,128]{3,0,2,1:T(8,128)}, f32[32,6,8,128]{3,0,2,1:T(8,128)S(1)}, u32[]{:S(2)}, u32[]{:S(2)}) collective-permute-start(f32[32,6,8,128]{3,0,2,1:T(8,128)} %get-tuple-element.32), channel_id=1, source_target_pairs={{16,0},{32,16},{48,32},{64,48},{80,64},{96,80},{112,96},{0,112},{1... | collective-permute-start | bytes 2359304 | tf_op jit(solution)/shard_map/ppermute | solution.py:31
  629.1 124.0 %collective-permute-start.38 = (f32[32,20,6,128]{3,0,2,1:T(8,128)}, f32[32,20,6,128]{3,0,2,1:T(8,128)S(1)}, u32[]{:S(2)}, u32[]{:S(2)}) collective-permute-start(f32[32,20,6,128]{3,0,2,1:T(8,128)} %get-tuple-element.23), channel_id=1, source_target_pairs={{2,0},{4,2},{6,4},{8,6},{10,8},{12,10},{14,12},{0,14},{3,1},{5,3},... | collective-permute-start | bytes 5898248 | tf_op jit(solution)/shard_map/ppermute | solution.py:31
  635.5 117.7 %collective-permute-start.39 = (f32[32,20,6,128]{3,0,2,1:T(8,128)}, f32[32,20,6,128]{3,0,2,1:T(8,128)}, u32[]{:S(2)}, u32[]{:S(2)}) collective-permute-start(f32[32,20,6,128]{3,0,2,1:T(8,128)} %get-tuple-element.22), channel_id=1, source_target_pairs={{0,2},{2,4},{4,6},{6,8},{8,10},{10,12},{12,14},{14,0},{1,3},{3,5},... | collective-permute-start | bytes 5898248 | tf_op jit(solution)/shard_map/ppermute | solution.py:29
  643.7 15.2 %collective-permute-start.45 = (f32[5,1,3,256]{3,2,1,0:T(4,128)S(1)}, f32[5,1,3,256]{3,2,1,0:T(4,128)S(1)}, u32[]{:S(2)}, u32[]{:S(2)}) collective-permute-start(f32[5,1,3,256]{3,2,1,0:T(4,128)S(1)} %get-tuple-element.56), channel_id=1, source_target_pairs={{2,0},{4,2},{6,4},{8,6},{10,8},{12,10},{14,12},{0,14},{3,1},{5,3},... | collective-permute-start | bytes 46088 | tf_op jit(solution)/shard_map/ppermute | solution.py:31
  776.3 31.1 %collective-permute-start.41 = (f32[32,20,20,6]{0,2,3,1:T(8,128)}, f32[32,20,20,6]{0,2,3,1:T(8,128)}, u32[]{:S(2)}, u32[]{:S(2)}) collective-permute-start(f32[32,20,20,6]{0,2,3,1:T(8,128)} %copy.125), channel_id=1, source_target_pairs={{0,1},{1,0},{2,3},{3,2},{4,5},{5,4},{6,7},{7,6},{8,9},{9,8},{10,11... | collective-permute-start | bytes 921608 | tf_op jit(solution)/shard_map/ppermute | solution.py:29
  782.9 56.1 %collective-permute-start.40 = (f32[32,20,20,6]{0,2,3,1:T(8,128)}, f32[32,20,20,6]{0,2,3,1:T(8,128)}, u32[]{:S(2)}, u32[]{:S(2)}) collective-permute-start(f32[32,20,20,6]{0,2,3,1:T(8,128)} %copy.123), channel_id=1, source_target_pairs={{1,0},{0,1},{3,2},{2,3},{5,4},{4,5},{7,6},{6,7},{9,8},{8,9},{11,10... | collective-permute-start | bytes 921608 | tf_op jit(solution)/shard_map/ppermute | solution.py:31
  894.8 15.9 %collective-permute-start.55 = (f32[32,6,8,128]{3,0,2,1:T(8,128)}, f32[32,6,8,128]{3,0,2,1:T(8,128)S(1)}, u32[]{:S(2)}, u32[]{:S(2)}) collective-permute-start(f32[32,6,8,128]{3,0,2,1:T(8,128)} %get-tuple-element.31), channel_id=1, source_target_pairs={{0,16},{16,32},{32,48},{48,64},{64,80},{80,96},{96,112},{112,0},{1... | collective-permute-start | bytes 2359304 | tf_op jit(solution)/shard_map/ppermute | solution.py:29
  894.8 15.9 %collective-permute-start.54 = (f32[32,6,8,128]{3,0,2,1:T(8,128)}, f32[32,6,8,128]{3,0,2,1:T(8,128)}, u32[]{:S(2)}, u32[]{:S(2)}) collective-permute-start(f32[32,6,8,128]{3,0,2,1:T(8,128)} %get-tuple-element.30), channel_id=1, source_target_pairs={{16,0},{32,16},{48,32},{64,48},{80,64},{96,80},{112,96},{0,112},{1... | collective-permute-start | bytes 2359304 | tf_op jit(solution)/shard_map/ppermute | solution.py:31
  914.5 121.7 %collective-permute-start.56 = (f32[32,20,6,128]{3,0,2,1:T(8,128)}, f32[32,20,6,128]{3,0,2,1:T(8,128)}, u32[]{:S(2)}, u32[]{:S(2)}) collective-permute-start(f32[32,20,6,128]{3,0,2,1:T(8,128)} %get-tuple-element.19), channel_id=1, source_target_pairs={{2,0},{4,2},{6,4},{8,6},{10,8},{12,10},{14,12},{0,14},{3,1},{5,3},... | collective-permute-start | bytes 5898248 | tf_op jit(solution)/shard_map/ppermute | solution.py:31
  920.8 115.3 %collective-permute-start.57 = (f32[32,20,6,128]{3,0,2,1:T(8,128)}, f32[32,20,6,128]{3,0,2,1:T(8,128)}, u32[]{:S(2)}, u32[]{:S(2)}) collective-permute-start(f32[32,20,6,128]{3,0,2,1:T(8,128)} %get-tuple-element.18), channel_id=1, source_target_pairs={{0,2},{2,4},{4,6},{6,8},{8,10},{10,12},{12,14},{14,0},{1,3},{3,5},... | collective-permute-start | bytes 5898248 | tf_op jit(solution)/shard_map/ppermute | solution.py:29
  1058.9 31.1 %collective-permute-start.59 = (f32[32,20,20,6]{0,2,3,1:T(8,128)}, f32[32,20,20,6]{0,2,3,1:T(8,128)}, u32[]{:S(2)}, u32[]{:S(2)}) collective-permute-start(f32[32,20,20,6]{0,2,3,1:T(8,128)} %copy.134), channel_id=1, source_target_pairs={{0,1},{1,0},{2,3},{3,2},{4,5},{5,4},{6,7},{7,6},{8,9},{9,8},{10,11... | collective-permute-start | bytes 921608 | tf_op jit(solution)/shard_map/ppermute | solution.py:29
  1065.4 56.1 %collective-permute-start.58 = (f32[32,20,20,6]{0,2,3,1:T(8,128)}, f32[32,20,20,6]{0,2,3,1:T(8,128)}, u32[]{:S(2)}, u32[]{:S(2)}) collective-permute-start(f32[32,20,20,6]{0,2,3,1:T(8,128)} %copy.132), channel_id=1, source_target_pairs={{1,0},{0,1},{3,2},{2,3},{5,4},{4,5},{7,6},{6,7},{9,8},{8,9},{11,10... | collective-permute-start | bytes 921608 | tf_op jit(solution)/shard_map/ppermute | solution.py:31
  (59 other events, 566.4 us)
where the time goes:
time: 1230 us; the launch traced here: 1220 us
  local copies, waits for them, and re-layouts  354 us (29%)
  other arithmetic  340 us (28%)
  waiting for transfers between devices  287 us (23%)
  starting transfers between devices  149 us (12%)
  blocking collectives  67 us (5%)
  matrix products  23.8 us (2%)
    scatter-add x4, other arithmetic, nonlocal_term(): added = jnp.zeros((bands, cells), jnp.float32).at[:, point_cell].add(values)  186 us
    ppermute x36, waiting for transfers between devices, extended(): lax.ppermute(head, axis, [((i + 1) % count, i) for i in range(count)])  186 us
    ppermute x36, starting transfers between devices, extended(): lax.ppermute(head, axis, [((i + 1) % count, i) for i in range(count)])  133 us
    gather x4, local copies, waits for them, and re-layouts, nonlocal_term(): at_points = jnp.take(flattened, point_cell, axis=1)  120 us
    ppermute x36, waiting for transfers between devices, extended(): lax.ppermute(tail, axis, [(i, (i + 1) % count) for i in range(count)])  101 us
    slice x20, local copies, waits for them, and re-layouts, extended(): head = lax.slice_in_dim(cells, 0, width, axis=dim)  77.4 us
    psum x1, blocking collectives, local(): gram_matrix = lax.psum(local_gram, ('gx', 'gy', 'gz')) / float(total_cells)  67 us
    sub x3, other arithmetic, local(): 2.0 * (hamiltonian(current) - FILTER_CENTRE * current) / FILTER_HALF  48.1 us
  transfers between devices with their start and end apart: 72, of which 48 were waited for; matrix products, arithmetic and copies ran while one was open for 34% of the time, Pallas kernels for 0%

commit v1 on v0

v1 whole, which is shorter than its diff:
```python
import functools

import jax
import jax.numpy as jnp
import numpy as np
from jax import lax
from jax.experimental import pallas as pl
from jax.experimental.pallas import tpu as pltpu
from jax.sharding import PartitionSpec as P

DEGREE = 4
STENCIL = (
    -5369.0 / 1800.0,
    12.0 / 7.0,
    -15.0 / 56.0,
    10.0 / 189.0,
    -1.0 / 112.0,
    2.0 / 1925.0,
    -1.0 / 16632.0,
)
FILTER_CENTRE = 9.5
FILTER_HALF = 5.5
REACH = 6

NB = 32
SX = 8
SY = 8
SZ = 128
ROWS = SX * SY
PAIRS = ROWS // 2
FACE = REACH * SY
NPJ = 4
SLOTS = 8192
TGT = 40
CH = NPJ * TGT
GROUPS = ROWS // 4
ZROWS = GROUPS * 16
LANES = 128
F32 = jnp.float32
BF16 = jnp.bfloat16
NN = (((1,), (0,)), ((), ()))
NT = (((1,), (1,)), ((), ()))
VMEM_LIMIT = 40 * 1024 * 1024


def dot(a, b, dims=NN):
    return lax.dot_general(a, b, dims, preferred_element_type=F32)


def split2(v):
    hi = v.astype(BF16)
    return hi, (v - hi.astype(F32)).astype(BF16)


def split3(v):
    hi = v.astype(BF16)
    rest = v - hi.astype(F32)
    mid = rest.astype(BF16)
    return hi, mid, (rest - mid.astype(F32)).astype(BF16)


def z_matrices():
    half = [0.0] + [-0.5 * c for c in STENCIL[1:]]
    inner = np.zeros((SZ, SZ), np.float32)
    face = np.zeros((16, SZ), np.float32)
    for z in range(SZ):
        for source in range(SZ):
            if 1 <= abs(z - source) <= REACH:
                inner[source, z] = half[abs(z - source)]
        for e in range(8):
            if 1 <= abs(SZ + e - z) <= REACH:
                face[e, z] = half[abs(SZ + e - z)]
            if 1 <= abs(z + 8 - e) <= REACH:
                face[8 + e, z] = half[abs(z + 8 - e)]

    def split(m):
        hi = m.astype(jnp.bfloat16)
        return hi, (m - hi.astype(np.float32)).astype(jnp.bfloat16)

    inner_hi, inner_lo = split(inner)
    face_hi, face_lo = split(face)
    first = np.concatenate([inner_hi, inner_hi], axis=0)
    second = np.concatenate(
        [inner_lo, face_hi, face_hi, face_lo, np.zeros((SZ - 48, SZ), jnp.bfloat16)], axis=0
    )
    return jnp.asarray(first), jnp.asarray(second)


def any_specs(count):
    return [pl.BlockSpec(memory_space=pl.ANY)] * count


def vmem_specs(count):
    return [pl.BlockSpec(memory_space=pltpu.VMEM)] * count


PARAMS = pltpu.CompilerParams(vmem_limit_bytes=VMEM_LIMIT)


def rearrange_kernel(src, field, x_low, x_high, y_low, y_high, held, in_sem, out_sem):
    loads = [
        pltpu.make_async_copy(src.at[:, row, :], held.at[row], in_sem.at[row]) for row in range(ROWS)
    ]
    for load in loads:
        load.start()
    for load in loads:
        load.wait()
    held4 = held.reshape(SX, SY, NB, SZ)
    stores = [
        pltpu.make_async_copy(held.at[pl.ds(0, FACE)], x_low, out_sem.at[0]),
        pltpu.make_async_copy(held.at[pl.ds(ROWS - FACE, FACE)], x_high, out_sem.at[1]),
        pltpu.make_async_copy(held4.at[:, pl.ds(0, REACH)], y_low, out_sem.at[2]),
        pltpu.make_async_copy(held4.at[:, pl.ds(SY - REACH, REACH)], y_high, out_sem.at[3]),
        pltpu.make_async_copy(held, field, out_sem.at[4]),
    ]
    for store in stores:
        store.start()
    for store in stores:
        store.wait()


def rearrange(orbitals):
    return pl.pallas_call(
        rearrange_kernel,
        out_shape=[
            jax.ShapeDtypeStruct((ROWS, NB, SZ), F32),
            jax.ShapeDtypeStruct((FACE, NB, SZ), F32),
            jax.ShapeDtypeStruct((FACE, NB, SZ), F32),
            jax.ShapeDtypeStruct((SX, REACH, NB, SZ), F32),
            jax.ShapeDtypeStruct((SX, REACH, NB, SZ), F32),
        ],
        in_specs=any_specs(1),
        out_specs=any_specs(5),
        scratch_shapes=[
            pltpu.VMEM((ROWS, NB, SZ), F32),
            pltpu.SemaphoreType.DMA((ROWS,)),
            pltpu.SemaphoreType.DMA((5,)),
        ],
        compiler_params=PARAMS,
        name="rearrange",
    )(orbitals)


def build_kernel(starts, keys, w0, w1, w2, w3, out, held, weights):
    held[pl.ds(0, SLOTS // LANES), :] = keys[...]
    held[pl.ds(SLOTS // LANES, 8), :] = jnp.full((8, LANES), ROWS * SZ * 64, jnp.int32)
    for j, w in enumerate((w0, w1, w2, w3)):
        weights[j, pl.ds(0, SLOTS // LANES), :] = w[...]
        weights[j, pl.ds(SLOTS // LANES, 8), :] = jnp.zeros((8, LANES), F32)
    target_at = lax.broadcasted_iota(jnp.int32, (TGT, 2 * LANES), 0)
    z_at = lax.broadcasted_iota(jnp.int32, (SZ, 2 * LANES), 0)

    def window(row, block):
        key = jnp.concatenate([held[pl.ds(block, 1), :], held[pl.ds(block + 1, 1), :]], axis=1)
        target = jnp.where((key >> 13) == row, key & 63, 63)
        chosen = target_at == target
        parts = []
        for j in range(NPJ):
            w = jnp.concatenate(
                [weights[j, pl.ds(block, 1), :], weights[j, pl.ds(block + 1, 1), :]], axis=1
            )
            parts.append(jnp.where(chosen, w, 0.0))
        hi, lo = split2(jnp.concatenate(parts, axis=0))
        place = jnp.where(z_at == ((key >> 6) & 127), 1.0, 0.0).astype(BF16)
        both = dot(jnp.concatenate([hi, lo], axis=0), place, NT)
        return both[:CH] + both[CH:]

    @pl.loop(0, PAIRS)
    def _(pair):
        for parity in range(2):
            row = 2 * pair + parity
            low = starts[row]
            high = starts[row + 1]
            base = low // LANES
            windows = (high - base * LANES + 2 * LANES - 1) // (2 * LANES)
            total = window(row, base)

            total = lax.fori_loop(
                1, windows, lambda i, acc: acc + window(row, base + 2 * i), total
            )
            hi, lo = split2(total)
            out[pair, :, pl.ds(parity * SZ, SZ)] = jnp.concatenate([hi, lo], axis=0)


def build(starts, keys, weights):
    return pl.pallas_call(
        build_kernel,
        out_shape=jax.ShapeDtypeStruct((PAIRS, 2 * CH, 2 * SZ), BF16),
        in_specs=[pl.BlockSpec(memory_space=pltpu.SMEM)] + vmem_specs(5),
        out_specs=pl.BlockSpec(memory_space=pltpu.VMEM),
        scratch_shapes=[
            pltpu.VMEM((SLOTS // LANES + 8, LANES), jnp.int32),
            pltpu.VMEM((NPJ, SLOTS // LANES + 8, LANES), F32),
        ],
        compiler_params=PARAMS,
        name="build",
    )(starts, keys, *weights)


def partial_of(mat, values):
    hi, lo = split2(values)
    return dot(mat, jnp.concatenate([hi, lo], axis=0), NT)


def packed_partial(total):
    joined = total[:CH, :NB] + total[:CH, NB:] + total[CH:, :NB]
    return jnp.concatenate([joined[j * TGT : (j + 1) * TGT] for j in range(NPJ)], axis=1)


def z_faces(rows):
    turned = jnp.concatenate(rows, axis=0).T
    return jnp.concatenate([turned[:8], turned[SZ - 8 :]], axis=0)


def first_kernel(field, mat, message, total):
    total[...] = jnp.zeros_like(total)

    @pl.loop(0, SX)
    def _(x):
        acc = total[...]
        for half in range(2):
            rows = [field[x * SY + 4 * half + i] for i in range(4)]
            message[pl.ds((2 * x + half) * 16, 16), :] = z_faces(rows)
            for p in range(2):
                values = jnp.concatenate(rows[2 * p : 2 * p + 2], axis=1)
                acc = acc + partial_of(mat[x * 4 + 2 * half + p], values)
        total[...] = acc

    message[pl.ds(ZROWS, TGT), :] = packed_partial(total[...])


def first(field, mat):
    return pl.pallas_call(
        first_kernel,
        out_shape=jax.ShapeDtypeStruct((ZROWS + TGT, LANES), F32),
        in_specs=vmem_specs(2),
        out_specs=pl.BlockSpec(memory_space=pltpu.VMEM),
        scratch_shapes=[pltpu.VMEM((2 * CH, 2 * NB), F32)],
        compiler_params=PARAMS,
        name="first",
    )(field, mat)


def spread(frame, me, out, at, step, stride):
    row = lax.broadcasted_iota(jnp.int32, (TGT, LANES), 0)
    digit = (row // stride) % 3
    for distance in range(-3, 5):
        slot = (me + distance + 8) % 8
        if abs(distance) > 2:
            piece = jnp.zeros((TGT, LANES), F32)
        else:
            moved = frame if distance == 0 else pltpu.roll(frame, (-stride * distance) % TGT, 0)
            valid = (digit + distance >= 0) & (digit + distance <= 2) & (row < 36)
            piece = jnp.where(valid, moved, 0.0)
        out[slot, pl.ds(at, TGT), :] = piece


def spread_z_kernel(frames, me, mine, other, out):
    row = lax.broadcasted_iota(jnp.int32, (TGT, LANES), 0)
    for f in range(frames):
        theirs = other[pl.ds(f * TGT, TGT), :]
        swapped = jnp.where(
            row & 2 == 0, pltpu.roll(theirs, TGT - 2, 0), pltpu.roll(theirs, 2, 0)
        )
        spread(mine[pl.ds(f * TGT, TGT), :] + swapped, me[0], out, f * TGT, 1, 4)


def spread_x_kernel(frames, me, came, out):
    for f in range(frames):
        frame = came[0, pl.ds(f * TGT, TGT), :]
        for slot in range(1, 8):
            frame = frame + came[slot, pl.ds(f * TGT, TGT), :]
        spread(frame, me[0], out, f * TGT, 1, 12)


def spread_call(kernel, frames, me, *arrays):
    return pl.pallas_call(
        functools.partial(kernel, frames),
        out_shape=jax.ShapeDtypeStruct((8, frames * TGT, LANES), F32),
        in_specs=[pl.BlockSpec(memory_space=pltpu.SMEM)] + vmem_specs(len(arrays)),
        out_specs=pl.BlockSpec(memory_space=pltpu.VMEM),
        compiler_params=PARAMS,
        name="spread",
    )(me, *arrays)


def step_kernel(
    first_step, last_step,
    field, previous, x_left, x_right, y_left, y_right, faces, came, coupling, potential, mat, first_z, second_z,
    *rest,
):
    if last_step:
        (new, gram), rest = rest[:2], rest[2:]
    else:
        (new, x_low, x_high, y_low, y_high, message), rest = rest[:6], rest[6:]
    (
        wide, y_left_v, y_right_v, old, faces_v, came_v, coupling_v, potential_v, mat_v, first_v, second_v,
        made, message_v, total, coef, in_sem, mat_sem, out_sem,
    ) = rest
    shifted = 0 if first_step else 1
    alpha = (1.0 if first_step else 2.0) / FILTER_HALF
    half = [0.0] + [-0.5 * c for c in STENCIL[1:]]
    diagonal = -1.5 * STENCIL[0] - FILTER_CENTRE

    loads = [
        pltpu.make_async_copy(came, came_v, in_sem.at[0]),
        pltpu.make_async_copy(coupling, coupling_v, in_sem.at[1]),
        pltpu.make_async_copy(field, wide.at[pl.ds(FACE, ROWS)], in_sem.at[2]),
        pltpu.make_async_copy(x_left, wide.at[pl.ds(0, FACE)], in_sem.at[3]),
        pltpu.make_async_copy(x_right, wide.at[pl.ds(FACE + ROWS, FACE)], in_sem.at[4]),
        pltpu.make_async_copy(y_left, y_left_v, in_sem.at[5]),
        pltpu.make_async_copy(y_right, y_right_v, in_sem.at[6]),
        pltpu.make_async_copy(faces.at[pl.ds(0, ZROWS)], faces_v, in_sem.at[7]),
        pltpu.make_async_copy(potential, potential_v, in_sem.at[8]),
        pltpu.make_async_copy(first_z, first_v, in_sem.at[9]),
        pltpu.make_async_copy(second_z, second_v, in_sem.at[10]),
    ]
    if shifted:
        loads.append(pltpu.make_async_copy(previous, old, in_sem.at[11]))
    mat_loads = [
        pltpu.make_async_copy(mat.at[pl.ds(4 * x, 4)], mat_v.at[pl.ds(4 * x, 4)], mat_sem.at[x])
        for x in range(SX)
    ]
    for load in loads:
        load.start()
    for load in mat_loads:
        load.start()
    loads[0].wait()
    loads[1].wait()
    frame = came_v[0]
    for slot in range(1, 8):
        frame = frame + came_v[slot]
    frame = frame * coupling_v[...]
    stacked = jnp.concatenate([frame[:, j * NB : (j + 1) * NB] for j in range(NPJ)], axis=0)
    turned = stacked.T
    coef_hi = turned.astype(BF16).astype(F32)
    coef[pl.ds(0, NB), :] = jnp.concatenate([coef_hi, coef_hi], axis=1).astype(BF16)
    coef[pl.ds(NB, NB), pl.ds(0, CH)] = (turned - coef_hi).astype(BF16)
    total[...] = jnp.zeros_like(total)
    for load in loads[2:]:
        load.wait()

    def out_copies(x):
        rows = made.at[pl.ds(x * SY, SY)]
        copies = [pltpu.make_async_copy(rows, new.at[pl.ds(x * SY, SY)], out_sem.at[0, x])]
        if not last_step:
            copies += [
                pltpu.make_async_copy(made.at[pl.ds(x * SY, REACH)], y_low.at[x], out_sem.at[1, x]),
                pltpu.make_async_copy(
                    made.at[pl.ds(x * SY + SY - REACH, REACH)], y_high.at[x], out_sem.at[2, x]
                ),
            ]
        return copies

    def x_low_copy(x):
        return pltpu.make_async_copy(
            made.at[pl.ds(x * SY, SY)], x_low.at[pl.ds(x * SY, SY)], out_sem.at[3, x]
        )

    def x_high_copy(x):
        return pltpu.make_async_copy(
            made.at[pl.ds(x * SY, SY)],
            x_high.at[pl.ds((x - (SX - REACH)) * SY, SY)],
            out_sem.at[4, x],
        )

    @pl.loop(0, SX)
    def _(x):
        pltpu.make_async_copy(
            mat.at[pl.ds(4 * x, 4)], mat_v.at[pl.ds(4 * x, 4)], mat_sem.at[x]
        ).wait()
        c_hi = coef[pl.ds(0, NB), :]
        c_lo = coef[pl.ds(NB, NB), pl.ds(0, CH)]
        middle = (x + REACH) * SY

        def row_at(y):
            if y < 0:
                return y_left_v[x, y + REACH]
            if y >= SY:
                return y_right_v[x, y - SY]
            return wide[middle + y]

        acc = None
        for part in range(2):
            rows = [row_at(4 * part + i) for i in range(4)]
            block = jnp.concatenate(rows, axis=0)
            hi, lo = split2(block)
            face = faces_v[pl.ds((2 * x + part) * 16, 16), :]
            face_hi = face.astype(BF16).astype(F32)
            side = jnp.concatenate(
                [face_hi, face - face_hi, face_hi, jnp.zeros((LANES - 48, LANES), F32)], axis=0
            ).T.astype(BF16)
            along_z = dot(jnp.concatenate([hi, lo], axis=1), first_v[...]) + dot(
                jnp.concatenate([hi, side], axis=1), second_v[...]
            )
            made_rows = []
            for p in range(2):
                pair_mat = mat_v[x * 4 + 2 * part + p]
                nonlocal_part = dot(c_hi, pair_mat) + dot(c_lo, pair_mat[:CH])
                for q in range(2):
                    i = 2 * p + q
                    y = 4 * part + i
                    value = rows[i]
                    summed = along_z[i * NB : (i + 1) * NB] + nonlocal_part[:, q * SZ : (q + 1) * SZ]
                    for m in range(1, REACH + 1):
                        around = (wide[middle + y + m * SY] + wide[middle + y - m * SY]) + (
                            row_at(y + m) + row_at(y - m)
                        )
                        summed = summed + half[m] * around
                    summed = summed + (potential_v[pl.ds(x * SY + y, 1), :] + diagonal) * value
                    result = alpha * summed
                    if shifted:
                        result = result - old[x * SY + y]
                    made[x * SY + y] = result
                    made_rows.append(result)
            if last_step:
                for p in range(2):
                    parts = split3(jnp.concatenate(made_rows[2 * p : 2 * p + 2], axis=1))
                    joined = jnp.concatenate(parts, axis=0)
                    here = dot(joined, joined, NT)
                    acc = here if acc is None else acc + here
            else:
                message_v[pl.ds((2 * x + part) * 16, 16), :] = z_faces(made_rows)
                for p in range(2):
                    values = jnp.concatenate(made_rows[2 * p : 2 * p + 2], axis=1)
                    here = partial_of(mat_v[x * 4 + 2 * part + p], values)
                    acc = here if acc is None else acc + here
        total[...] = total[...] + acc
        for copy in out_copies(x):
            copy.start()
        if not last_step:

            @pl.when(x < REACH)
            def _():
                x_low_copy(x).start()

            @pl.when(x >= SX - REACH)
            def _():
                x_high_copy(x).start()

    if last_step:
        t = total[...]
        summed = t[2 * NB :, :NB] + t[:NB, 2 * NB :] + t[NB : 2 * NB, NB : 2 * NB]
        summed = summed + (t[NB : 2 * NB, :NB] + t[:NB, NB : 2 * NB]) + t[:NB, :NB]
        message_v[...] = jnp.concatenate([summed[8 * q : 8 * q + 8] for q in range(4)], axis=1)
        final = pltpu.make_async_copy(message_v, gram, in_sem.at[12])
    else:
        message_v[pl.ds(ZROWS, TGT), :] = packed_partial(total[...])
        final = pltpu.make_async_copy(message_v, message, in_sem.at[12])
    final.start()
    for x in range(SX):
        for copy in out_copies(x):
            copy.wait()
        if not last_step:
            if x < REACH:
                x_low_copy(x).wait()
            if x >= SX - REACH:
                x_high_copy(x).wait()
    final.wait()


def step(first_step, last_step, *arrays):
    block = jax.ShapeDtypeStruct((ROWS, NB, SZ), F32)
    x_face = jax.ShapeDtypeStruct((FACE, NB, SZ), F32)
    y_face = jax.ShapeDtypeStruct((SX, REACH, NB, SZ), F32)
    if last_step:
        message_rows = 8
        total = (3 * NB, 3 * NB)
        outs = [block, jax.ShapeDtypeStruct((message_rows, LANES), F32)]
    else:
        message_rows = ZROWS + TGT
        total = (2 * CH, 2 * NB)
        outs = [block, x_face, x_face, y_face, y_face, jax.ShapeDtypeStruct((message_rows, LANES), F32)]
    return pl.pallas_call(
        functools.partial(step_kernel, first_step, last_step),
        out_shape=outs,
        in_specs=any_specs(len(arrays)),
        out_specs=any_specs(len(outs)),
        scratch_shapes=[
            pltpu.VMEM((ROWS + 2 * FACE, NB, SZ), F32),
            pltpu.VMEM((SX, REACH, NB, SZ), F32),
            pltpu.VMEM((SX, REACH, NB, SZ), F32),
            pltpu.VMEM((ROWS, NB, SZ), F32),
            pltpu.VMEM((ZROWS, LANES), F32),
            pltpu.VMEM((8, TGT, LANES), F32),
            pltpu.VMEM((TGT, LANES), F32),
            pltpu.VMEM((ROWS, SZ), F32),
            pltpu.VMEM((PAIRS, 2 * CH, 2 * SZ), BF16),
            pltpu.VMEM((2 * SZ, SZ), BF16),
            pltpu.VMEM((2 * SZ, SZ), BF16),
            pltpu.VMEM((ROWS, NB, SZ), F32),
            pltpu.VMEM((message_rows, LANES), F32),
            pltpu.VMEM(total, F32),
            pltpu.VMEM((2 * NB, 2 * CH), BF16),
            pltpu.SemaphoreType.DMA((13,)),
            pltpu.SemaphoreType.DMA((SX,)),
            pltpu.SemaphoreType.DMA((5, SX)),
        ],
        compiler_params=PARAMS,
        name="step",
    )(*arrays)


def finish_kernel(scale, field, grams, out, held, made, inverse, in_sem, out_sem):
    loads = [
        pltpu.make_async_copy(field.at[pl.ds(x * SY, SY)], held.at[pl.ds(x * SY, SY)], in_sem.at[x])
        for x in range(SX)
    ]
    for load in loads:
        load.start()
    packed = grams[0]
    for slot in range(1, grams.shape[0]):
        packed = packed + grams[slot]
    packed = packed * scale
    gram = jnp.concatenate([packed[:, q * NB : (q + 1) * NB] for q in range(4)], axis=0)
    row = lax.broadcasted_iota(jnp.int32, (NB, NB), 0)
    column = lax.broadcasted_iota(jnp.int32, (NB, NB), 1)
    eye = jnp.where(row == column, 1.0, 0.0)
    work = jnp.concatenate([gram, eye], axis=1)
    below = lax.broadcasted_iota(jnp.int32, (NB, 2 * NB), 0)
    for k in range(NB):
        root = 1.0 / jnp.sqrt(work[k : k + 1, k : k + 1])
        line = work[k : k + 1, :] * root
        inverse[pl.ds(k, 1), :] = line[:, NB:]
        if k < NB - 1:
            factor = work[:, k : k + 1] * root
            work = work - jnp.where(below > k, factor * line, 0.0)
    hi, mid, lo = split3(inverse[...])
    left = jnp.concatenate([lo, mid, hi, mid, hi, hi], axis=1)

    @pl.loop(0, SX)
    def _(x):
        pltpu.make_async_copy(
            field.at[pl.ds(x * SY, SY)], held.at[pl.ds(x * SY, SY)], in_sem.at[x]
        ).wait()
        for p in range(SY // 2):
            at = x * SY + 2 * p
            values = jnp.concatenate([held[at], held[at + 1]], axis=1)
            f_hi, f_mid, f_lo = split3(values)
            right = jnp.concatenate([f_hi, f_mid, f_lo, f_hi, f_mid, f_hi], axis=0)
            result = dot(left, right)
            made[at] = result[:, :SZ]
            made[at + 1] = result[:, SZ:]
            for q in range(2):
                pltpu.make_async_copy(made.at[at + q], out.at[:, at + q, :], out_sem.at[at + q]).start()

    for r in range(ROWS):
        pltpu.make_async_copy(made.at[r], out.at[:, r, :], out_sem.at[r]).wait()


def finish(scale, field, grams):
    return pl.pallas_call(
        functools.partial(finish_kernel, scale),
        out_shape=jax.ShapeDtypeStruct((NB, ROWS, SZ), F32),
        in_specs=any_specs(1) + vmem_specs(1),
        out_specs=pl.BlockSpec(memory_space=pl.ANY),
        scratch_shapes=[
            pltpu.VMEM((ROWS, NB, SZ), F32),
            pltpu.VMEM((ROWS, NB, SZ), F32),
            pltpu.VMEM((NB, NB), F32),
            pltpu.SemaphoreType.DMA((SX,)),
            pltpu.SemaphoreType.DMA((ROWS,)),
        ],
        compiler_params=PARAMS,
        name="finish",
    )(field, grams)


def shift(value, axis, by):
    count = lax.axis_size(axis)
    return lax.ppermute(value, axis, [(i, (i + by) % count) for i in range(count)])


def local(orbitals, potential, projector, point_cell, target, point_count, coupling):
    bands, size_x, size_y, size_z = orbitals.shape
    me_x = lax.axis_index("gx").astype(jnp.int32).reshape(1)
    me_y = lax.axis_index("gy").astype(jnp.int32).reshape(1)

    field, x_low, x_high, y_low, y_high = rearrange(orbitals.reshape(NB, ROWS, SZ))
    pot = potential.reshape(ROWS, SZ)
    first_z, second_z = z_matrices()

    alive = lax.iota(jnp.int32, SLOTS) < point_count.reshape(())
    code = target // 2
    z_other = (code % 3 != 1).astype(jnp.int32)
    wanted = ((code // 3) * 2 + z_other) * 2 + target % 2
    key = jnp.where(alive, point_cell * 64 + wanted, ROWS * SZ * 64)
    starts = jnp.sum(
        (key[None, :] < (lax.iota(jnp.int32, ROWS + 1) * (SZ * 64))[:, None]).astype(jnp.int32), axis=1
    )
    ordered = lax.sort((key,) + tuple(projector[j] for j in range(NPJ)), num_keys=1, is_stable=False)
    ordered = [o.reshape(SLOTS // LANES, LANES) for o in ordered]
    mat = build(starts, ordered[0], ordered[1:])

    own = jnp.repeat(coupling, NB, axis=1)
    coupling_frame = jnp.zeros((TGT, LANES), F32).at[16:18].set(own)

    message = first(field, mat)
    previous = field
    scale_frame = None
    for k in range(DEGREE):
        x_left = shift(x_high, "gx", 1)
        x_right = shift(x_low, "gx", -1)
        y_left = shift(y_high, "gy", 1)
        y_right = shift(y_low, "gy", -1)
        if k == 0:
            message = jnp.concatenate([message, coupling_frame], axis=0)
        other = shift(message, "gz", 1)
        frames = 2 if k == 0 else 1
        sends = spread_call(spread_z_kernel, frames, me_y, message[ZROWS:], other[ZROWS:])
        came = lax.all_to_all(sends, "gy", 0, 0)
        sends = spread_call(spread_x_kernel, frames, me_x, came)
        came = lax.all_to_all(sends, "gx", 0, 0)
        if k == 0:
            scale_frame = jnp.sum(came[:, TGT:], axis=0)
            came = came[:, :TGT]
        outs = step(
            k == 0, k == DEGREE - 1,
            field, previous, x_left, x_right, y_left, y_right, other, came, scale_frame, pot, mat, first_z, second_z,
        )
        previous = field
        if k < DEGREE - 1:
            field, x_low, x_high, y_low, y_high, message = outs
        else:
            field, gram = outs
    axes = ("gx", "gy", "gz")
    devices = 1
    for axis in axes:
        devices *= lax.axis_size(axis)
    grams = lax.all_to_all(jnp.broadcast_to(gram[None], (devices,) + gram.shape), axes, 0, 0)
    result = finish(1.0 / float(devices * ROWS * SZ), field, grams)
    return result.reshape(bands, size_x, size_y, size_z)


def solution(mesh):
    in_specs = (
        P(None, "gx", "gy", "gz"),
        P("gx", "gy", "gz"),
        P(None, ("gx", "gy", "gz")),
        P(("gx", "gy", "gz")),
        P(("gx", "gy", "gz")),
        P("gx", "gy", "gz"),
        P(("gx", "gy", "gz"), None),
    )
    out_specs = P(None, "gx", "gy", "gz")
    return jax.shard_map(local, mesh=mesh, in_specs=in_specs, out_specs=out_specs, check_vma=False)
```

time: 1230 us -> 298 us (0.24)
  local copies, waits for them, and re-layouts: 354 us -> 5.91 us
  other arithmetic: 340 us -> 7.27 us
  waiting for transfers between devices: 287 us -> 57.5 us
  starting transfers between devices: 149 us -> 42.6 us
  Pallas kernels: 0 us -> 88.7 us
  blocking collectives: 67 us -> 94.1 us
  matrix products: 23.8 us -> 0 us
    ppermute x72 -> x20, waiting for transfers between devices: 287 us -> 55.8 us  [shift(): lax.ppermute(value, axis, [(i, (i + by) % count) for i in range(count)])]
    scatter-add x4 -> x0, other arithmetic: 186 us -> none  [nonlocal_term(): added = jnp.zeros((bands, cells), jnp.float32).at[:, point_cell].add(values)]
    slice x40 -> x9, local copies, waits for them, and re-layouts: 124 us -> 1.29 us  [the longest x1 1.27 us: local(): projector[j]]
    gather x4 -> x0, local copies, waits for them, and re-layouts: 120 us -> none  [nonlocal_term(): at_points = jnp.take(flattened, point_cell, axis=1)]
    ppermute x72 -> x20, starting transfers between devices: 149 us -> 37.1 us  [shift(): lax.ppermute(value, axis, [(i, (i + by) % count) for i in range(count)])]
    all_to_all x0 -> x8, blocking collectives: none -> 94.1 us  [the longest x4 48.7 us: local(): came = lax.all_to_all(sends, 'gx', 0, 0)]
    pallas_call x0 -> x16, Pallas kernels: none -> 88.7 us  [the longest x4 59.6 us: step(): pl.pallas_call(functools.partial(step_kernel, first_step, last_step), out...]
    psum x1 -> x0, blocking collectives: 67 us -> none  [local(): gram_matrix = lax.psum(local_gram, ('gx', 'gy', 'gz')) / float(total_cells)]
  transfers between devices with their start and end apart: 72 -> 21, of which waited for: 48 -> 5; matrix products, arithmetic and copies ran while one was open for 34% -> 0% of each run, Pallas kernels for 0% -> 0%
where the time goes in v1:
time: 298 us; the launch traced here: 297 us
  blocking collectives  94.1 us (32%)
  Pallas kernels  88.7 us (30%)
  waiting for transfers between devices  57.5 us (19%)
  starting transfers between devices  42.6 us (14%)
  other arithmetic  7.27 us (2%)
  local copies, waits for them, and re-layouts  5.91 us (2%)
    pallas_call x4, Pallas kernels, step(): pl.pallas_call(functools.partial(step_kernel, first_step, last_step), out...  59.6 us
    ppermute x20, waiting for transfers between devices, shift(): lax.ppermute(value, axis, [(i, (i + by) % count) for i in range(count)])  55.8 us
    all_to_all x4, blocking collectives, local(): came = lax.all_to_all(sends, 'gx', 0, 0)  48.7 us
    ppermute x20, starting transfers between devices, shift(): lax.ppermute(value, axis, [(i, (i + by) % count) for i in range(count)])  37.1 us
    all_to_all x3, blocking collectives, local(): came = lax.all_to_all(sends, 'gy', 0, 0)  27.2 us
    all_to_all x1, blocking collectives, local(): lax.all_to_all(jnp.broadcast_to(gram[None], (devices,) + gram.shape), axe...  18.2 us
    pallas_call x1, Pallas kernels, build(): pl.pallas_call(build_kernel, out_shape=jax.ShapeDtypeStruct((PAIRS, 2 * C...  15.1 us
    pallas_call x1, Pallas kernels, finish(): pl.pallas_call(functools.partial(finish_kernel, scale), out_shape=jax.Sha...  7.4 us
  transfers between devices with their start and end apart: 21, of which 5 were waited for; matrix products, arithmetic and copies ran while one was open for 0% of the time, Pallas kernels for 0%

profile of v1, /device:TPU:1, one launch (start us, length us, event | category | flops | bytes accessed | tf_op | source)
XLA Modules:
  0.0 297.2 jit_solution(3559390113034503810)
XLA Ops:
  4.0 2.8 rearrange.1
  8.2 5.9 %sort.33 = (s32[8192]{0:T(1024)S(1)}, f32[8192]{0:T(1024)S(1)}, f32[8192]{0:T(1024)S(1)}, f32[8192]{0:T(1024)S(1)}, f32[8192]{0:T(1024)S(1)}) sort(s32[8192]{0:T(1024)S(1)} %fusion.5, f32[8192]{0:T(1024)S(1)} %bitcast.30, f32[8192]{0:T(1024)S(1)} %bitcast.29, f32[8192]{0:T(1024)S(1)} %bitcast.31, f32[8192]{0:T(1024)S(1)} %bitcast.28), dimensions={0}, to_apply=%region_1.2 | sort | flops 106496 | bytes 327680 | tf_op jit(solution)/shard_map/sort | solution.py:591
  14.1 15.1 %build.1.mat = bf16[32,320,256]{2,1,0:T(8,128)(2,1)S(1)} custom-call(s32[65]{0:T(128)S(1)} %convert_reduce_fusion.starts, s32[64,128]{1,0:T(8,128)S(1)} %bitcast.23, f32[64,128]{1,0:T(8,128)S(1)} %bitcast.24, f32[64,128]{1,0:T(8,128)S(1)} %bitcast.25, f32[64,128]{1,0:T(8,128)S(1)} %bitcast.26, f32[64,128]{1,0:T(8,128)S(1)} %bitcast.27), custom_call_target="tpu_custom_call" | custom-call | tf_op jit(solution)/shard_map/build/pallas_call | solution.py:186
  29.2 2.7 first.1
  31.9 4.5 %collective-permute-start.4 = (f32[336,128]{1,0:T(8,128)S(1)}, f32[336,128]{1,0:T(8,128)S(1)}, u32[]{:S(2)}, u32[]{:S(2)}) collective-permute-start(f32[336,128]{1,0:T(8,128)S(1)} %select_maximum_fusion), channel_id=1, source_target_pairs={{0,1},{1,0},{2,3},{3,2},{4,5},{5,4},{6,7},{7,6},{8,9},{9,8},{10,11... | collective-permute-start | bytes 516104 | tf_op jit(solution)/shard_map/ppermute | solution.py:571
  36.4 4.1 %collective-permute-done.4.faces = f32[336,128]{1,0:T(8,128)S(1)} collective-permute-done((f32[336,128]{1,0:T(8,128)S(1)}, f32[336,128]{1,0:T(8,128)S(1)}, u32[]{:S(2)}, u32[]{:S(2)}) %collective-permute-start.4) | collective-permute-done | bytes 172064 | tf_op jit(solution)/shard_map/ppermute | solution.py:571
  41.4 5.5 %all-to-all-start = ((f32[8,80,128]{2,1,0:T(8,128)}), f32[8,80,128]{2,1,0:T(8,128)S(1)}, u32[]{:S(2)}, u32[]{:S(2)}) async-start(f32[8,80,128]{2,1,0:T(8,128)} %spread.8), calls=%async_computation | async-start | bytes 655360 | tf_op jit(solution)/shard_map/all_to_all | solution.py:611
  54.4 17.9 %all_to_all.45 = f32[8,80,128]{2,1,0:T(8,128)S(1)} all-to-all(f32[8,80,128]{2,1,0:T(8,128)S(1)} %spread.9), channel_id=1, replica_groups=mesh['gx'=8,'gy'=8,'gz'=2] {'gx'}, dimensions={0} | all-to-all | bytes 655360 | tf_op jit(solution)/shard_map/all_to_all | solution.py:613
  72.4 2.5 copy-done.1
  74.9 16.2 %step.4 = (f32[64,32,128]{2,1,0:T(8,128)S(1)}, f32[48,32,128]{2,1,0:T(8,128)S(1)}, f32[48,32,128]{2,1,0:T(8,128)S(1)}, f32[8,6,32,128]{3,2,1,0:T(8,128)S(1)}, f3...) custom-call(f32[64,32,128]{2,1,0:T(8,128)S(1)} %get-tuple-element.47.field.previous, ...), custom_call_target="tpu_custom_call" | custom-call | tf_op jit(solution)/shard_map/step/pallas_call | solution.py:474
  92.0 2.7 collective-permute-start.6
  94.7 3.1 %collective-permute-start.7 = (f32[8,6,32,128]{3,2,1,0:T(8,128)S(1)}, f32[8,6,32,128]{3,2,1,0:T(8,128)S(1)}, u32[]{:S(2)}, u32[]{:S(2)}) collective-permute-start(f32[8,6,32,128]{3,2,1,0:T(8,128)S(1)} %get-tuple-element.60), channel_id=1, source_target_pairs={{0,2},{2,4},{4,6},{6,8},{8,10},{10,12},{12,14},{14,0},{1,3},{3,5},... | collective-permute-start | bytes 2359304 | tf_op jit(solution)/shard_map/ppermute | solution.py:571
  97.8 3.5 %collective-permute-start.9 = (f32[296,128]{1,0:T(8,128)S(1)}, f32[296,128]{1,0:T(8,128)S(1)}, u32[]{:S(2)}, u32[]{:S(2)}) collective-permute-start(f32[296,128]{1,0:T(8,128)S(1)} %get-tuple-element.62), channel_id=1, source_target_pairs={{0,1},{1,0},{2,3},{3,2},{4,5},{5,4},{6,7},{7,6},{8,9},{9,8},{10,11... | collective-permute-start | bytes 454664 | tf_op jit(solution)/shard_map/ppermute | solution.py:571
  101.3 17.3 %collective-permute-done.9.faces = f32[296,128]{1,0:T(8,128)S(1)} collective-permute-done((f32[296,128]{1,0:T(8,128)S(1)}, f32[296,128]{1,0:T(8,128)S(1)}, u32[]{:S(2)}, u32[]{:S(2)}) %collective-permute-start.9) | collective-permute-done | bytes 151584 | tf_op jit(solution)/shard_map/ppermute | solution.py:571
  118.7 10.3 %all_to_all.46.came = f32[8,40,128]{2,1,0:T(8,128)S(1)} all-to-all(f32[8,40,128]{2,1,0:T(8,128)S(1)} %spread.10), channel_id=1, replica_groups=mesh['gx'=8,'gy'=8,'gz'=2] {'gy'}, dimensions={0} | all-to-all | bytes 327680 | tf_op jit(solution)/shard_map/all_to_all | solution.py:611
  129.0 9.9 %all_to_all.47.came = f32[8,40,128]{2,1,0:T(8,128)S(1)} all-to-all(f32[8,40,128]{2,1,0:T(8,128)S(1)} %spread.11), channel_id=1, replica_groups=mesh['gx'=8,'gy'=8,'gz'=2] {'gx'}, dimensions={0} | all-to-all | bytes 327680 | tf_op jit(solution)/shard_map/all_to_all | solution.py:613
  139.0 15.7 %step.5 = (f32[64,32,128]{2,1,0:T(8,128)S(1)}, f32[48,32,128]{2,1,0:T(8,128)S(1)}, f32[48,32,128]{2,1,0:T(8,128)S(1)}, f32[8,6,32,128]{3,2,1,0:T(8,128)S(1)}, f3...) custom-call(f32[64,32,128]{2,1,0:T(8,128)S(1)} %get-tuple-element.57.field.previous, ...), custom_call_target="tpu_custom_call" | custom-call | tf_op jit(solution)/shard_map/step/pallas_call | solution.py:474
  155.3 3.1 %collective-permute-start.11 = (f32[48,32,128]{2,1,0:T(8,128)S(1)}, f32[48,32,128]{2,1,0:T(8,128)S(1)}, u32[]{:S(2)}, u32[]{:S(2)}) collective-permute-start(f32[48,32,128]{2,1,0:T(8,128)S(1)} %get-tuple-element.65), channel_id=1, source_target_pairs={{0,112},{16,0},{32,16},{48,32},{64,48},{80,64},{96,80},{112,96},{1... | collective-permute-start | bytes 2359304 | tf_op jit(solution)/shard_map/ppermute | solution.py:571
  158.4 2.9 collective-permute-start.12
  162.1 17.2 %collective-permute-done.14.faces = f32[296,128]{1,0:T(8,128)S(1)} collective-permute-done((f32[296,128]{1,0:T(8,128)S(1)}, f32[296,128]{1,0:T(8,128)S(1)}, u32[]{:S(2)}, u32[]{:S(2)}) %collective-permute-start.14) | collective-permute-done | bytes 151584 | tf_op jit(solution)/shard_map/ppermute | solution.py:571
  179.4 8.5 %all_to_all.48.came = f32[8,40,128]{2,1,0:T(8,128)S(1)} all-to-all(f32[8,40,128]{2,1,0:T(8,128)S(1)} %spread.12), channel_id=1, replica_groups=mesh['gx'=8,'gy'=8,'gz'=2] {'gy'}, dimensions={0} | all-to-all | bytes 327680 | tf_op jit(solution)/shard_map/all_to_all | solution.py:611
  187.9 10.5 %all_to_all.49.came = f32[8,40,128]{2,1,0:T(8,128)S(1)} all-to-all(f32[8,40,128]{2,1,0:T(8,128)S(1)} %spread.13), channel_id=1, replica_groups=mesh['gx'=8,'gy'=8,'gz'=2] {'gx'}, dimensions={0} | all-to-all | bytes 327680 | tf_op jit(solution)/shard_map/all_to_all | solution.py:613
  198.4 16.2 %step.6 = (f32[64,32,128]{2,1,0:T(8,128)S(1)}, f32[48,32,128]{2,1,0:T(8,128)S(1)}, f32[48,32,128]{2,1,0:T(8,128)S(1)}, f32[8,6,32,128]{3,2,1,0:T(8,128)S(1)}, f3...) custom-call(f32[64,32,128]{2,1,0:T(8,128)S(1)} %get-tuple-element.63.field.previous, ...), custom_call_target="tpu_custom_call" | custom-call | tf_op jit(solution)/shard_map/step/pallas_call | solution.py:474
  215.2 3.1 %collective-permute-start.16 = (f32[48,32,128]{2,1,0:T(8,128)S(1)}, f32[48,32,128]{2,1,0:T(8,128)S(1)}, u32[]{:S(2)}, u32[]{:S(2)}) collective-permute-start(f32[48,32,128]{2,1,0:T(8,128)S(1)} %get-tuple-element.71), channel_id=1, source_target_pairs={{0,112},{16,0},{32,16},{48,32},{64,48},{80,64},{96,80},{112,96},{1... | collective-permute-start | bytes 2359304 | tf_op jit(solution)/shard_map/ppermute | solution.py:571
  218.3 2.9 collective-permute-start.17
  221.1 2.7 collective-permute-start.19
  223.8 17.2 %collective-permute-done.19.faces = f32[296,128]{1,0:T(8,128)S(1)} collective-permute-done((f32[296,128]{1,0:T(8,128)S(1)}, f32[296,128]{1,0:T(8,128)S(1)}, u32[]{:S(2)}, u32[]{:S(2)}) %collective-permute-start.19) | collective-permute-done | bytes 151584 | tf_op jit(solution)/shard_map/ppermute | solution.py:571
  241.1 8.5 %all_to_all.50.came = f32[8,40,128]{2,1,0:T(8,128)S(1)} all-to-all(f32[8,40,128]{2,1,0:T(8,128)S(1)} %spread.14), channel_id=1, replica_groups=mesh['gx'=8,'gy'=8,'gz'=2] {'gy'}, dimensions={0} | all-to-all | bytes 327680 | tf_op jit(solution)/shard_map/all_to_all | solution.py:611
  249.6 10.3 %all_to_all.51.came = f32[8,40,128]{2,1,0:T(8,128)S(1)} all-to-all(f32[8,40,128]{2,1,0:T(8,128)S(1)} %spread.15), channel_id=1, replica_groups=mesh['gx'=8,'gy'=8,'gz'=2] {'gx'}, dimensions={0} | all-to-all | bytes 327680 | tf_op jit(solution)/shard_map/all_to_all | solution.py:613
  260.0 11.5 %step.7 = (f32[64,32,128]{2,1,0:T(8,128)S(1)}, f32[8,128]{1,0:T(8,128)S(1)}) custom-call(f32[64,32,128]{2,1,0:T(8,128)S(1)} %get-tuple-element.69.field, f32[64,32,128]{2,1,0:T(8,128)S(1)} %get-tuple-element.63.field.previous, f32[48,32,128]{2,1,0:T(8,128)S(1)} %collective-permute-done.15.x_left, f32[48,32,128]{2,1,0:T(8,128)S(1)} %collective-permute-done.16.x_right, ...), custom_call_target="tpu_custom_call" | custom-call | tf_op jit(solution)/shard_map/step/pallas_call | solution.py:474
  271.5 18.2 %all_to_all.52.grams = f32[128,8,128]{2,1,0:T(8,128)S(1)} all-to-all(f32[128,8,128]{2,1,0:T(8,128)S(1)} %broadcast_in_dim.18), channel_id=1, replica_groups=mesh['gx'=8,'gy'=8,'gz'=2] {'gx','gy','gz'}, dimensions={0} | all-to-all | bytes 1048576 | tf_op jit(solution)/shard_map/all_to_all | solution.py:630
  289.7 7.4 %finish.1 = f32[32,64,128]{2,1,0:T(8,128)} custom-call(f32[64,32,128]{2,1,0:T(8,128)S(1)} %get-tuple-element.75.field, f32[128,8,128]{2,1,0:T(8,128)S(1)} %all_to_all.52.grams), custom_call_target="tpu_custom_call" | custom-call | tf_op jit(solution)/shard_map/finish/pallas_call | solution.py:552
  (75 shorter events, 16.4 us)
Async XLA Ops:
  2.8 1.2 copy-start.4
  6.8 1.4 copy-start.6
  6.8 1.4 copy-start.7
  6.8 1.4 copy-start.8
  29.2 2.7 copy-start
  31.9 40.5 %copy-start.2 = (bf16[256,128]{1,0:T(8,128)(2,1)S(1)}, bf16[256,128]{1,0:T(8,128)(2,1)}, u32[]{:S(2)}) copy-start(bf16[256,128]{1,0:T(8,128)(2,1)} %constant.91.clone.second_z) | copy-start | bytes 196612
  31.9 40.5 %copy-start.3 = (bf16[256,128]{1,0:T(8,128)(2,1)S(1)}, bf16[256,128]{1,0:T(8,128)(2,1)}, u32[]{:S(2)}) copy-start(bf16[256,128]{1,0:T(8,128)(2,1)} %constant.90.clone.first_z) | copy-start | bytes 196612
  31.9 40.5 %copy-start.5 = (f32[8,8,128]{2,1,0:T(8,128)S(1)}, f32[8,8,128]{2,1,0:T(8,128)}, u32[]{:S(2)}) copy-start(f32[8,8,128]{2,1,0:T(8,128)} %param.12) | copy-start | bytes 98308
  31.9 8.6 %collective-permute-start.4 = (f32[336,128]{1,0:T(8,128)S(1)}, f32[336,128]{1,0:T(8,128)S(1)}, u32[]{:S(2)}, u32[]{:S(2)}) collective-permute-start(f32[336,128]{1,0:T(8,128)S(1)} %select_maximum_fusion), channel_id=1, source_target_pairs={{0,1},{1,0},{2,3},{3,2},{4,5},{5,4},{6,7},{7,6},{8,9},{9,8},{10,11... | collective-permute-start | bytes 516104 | tf_op jit(solution)/shard_map/ppermute | solution.py:571
  41.4 12.9 %all-to-all-start = ((f32[8,80,128]{2,1,0:T(8,128)}), f32[8,80,128]{2,1,0:T(8,128)S(1)}, u32[]{:S(2)}, u32[]{:S(2)}) async-start(f32[8,80,128]{2,1,0:T(8,128)} %spread.8), calls=%async_computation | async-start | bytes 655360 | tf_op jit(solution)/shard_map/all_to_all | solution.py:611
  46.9 25.5 %collective-permute-start = (f32[48,32,128]{2,1,0:T(8,128)}, f32[48,32,128]{2,1,0:T(8,128)S(1)}, u32[]{:S(2)}, u32[]{:S(2)}) collective-permute-start(f32[48,32,128]{2,1,0:T(8,128)} %get-tuple-element.48), channel_id=1, source_target_pairs={{0,16},{16,32},{32,48},{48,64},{64,80},{80,96},{96,112},{112,0},{1... | collective-permute-start | bytes 2359304 | tf_op jit(solution)/shard_map/ppermute | solution.py:571
  48.2 24.2 %collective-permute-start.1 = (f32[48,32,128]{2,1,0:T(8,128)}, f32[48,32,128]{2,1,0:T(8,128)S(1)}, u32[]{:S(2)}, u32[]{:S(2)}) collective-permute-start(f32[48,32,128]{2,1,0:T(8,128)} %copy-done.8), channel_id=1, source_target_pairs={{0,112},{16,0},{32,16},{48,32},{64,48},{80,64},{96,80},{112,96},{1... | collective-permute-start | bytes 2359304 | tf_op jit(solution)/shard_map/ppermute | solution.py:571
  50.4 21.9 %collective-permute-start.2 = (f32[8,6,32,128]{3,2,1,0:T(8,128)}, f32[8,6,32,128]{3,2,1,0:T(8,128)}, u32[]{:S(2)}, u32[]{:S(2)}) collective-permute-start(f32[8,6,32,128]{3,2,1,0:T(8,128)} %copy-done.7), channel_id=1, source_target_pairs={{0,2},{2,4},{4,6},{6,8},{8,10},{10,12},{12,14},{14,0},{1,3},{3,5},... | collective-permute-start | bytes 2359304 | tf_op jit(solution)/shard_map/ppermute | solution.py:571
  52.6 19.7 %collective-permute-start.3 = (f32[8,6,32,128]{3,2,1,0:T(8,128)}, f32[8,6,32,128]{3,2,1,0:T(8,128)}, u32[]{:S(2)}, u32[]{:S(2)}) collective-permute-start(f32[8,6,32,128]{3,2,1,0:T(8,128)} %copy-done.6), channel_id=1, source_target_pairs={{0,14},{2,0},{4,2},{6,4},{8,6},{10,8},{12,10},{14,12},{1,15},{3,1}... | collective-permute-start | bytes 2359304 | tf_op jit(solution)/shard_map/ppermute | solution.py:571
  72.4 2.5 copy-start.1
  91.1 47.9 %collective-permute-start.5 = (f32[48,32,128]{2,1,0:T(8,128)S(1)}, f32[48,32,128]{2,1,0:T(8,128)S(1)}, u32[]{:S(2)}, u32[]{:S(2)}) collective-permute-start(f32[48,32,128]{2,1,0:T(8,128)S(1)} %get-tuple-element.58), channel_id=1, source_target_pairs={{0,16},{16,32},{32,48},{48,64},{64,80},{80,96},{96,112},{112,0},{1... | collective-permute-start | bytes 2359304 | tf_op jit(solution)/shard_map/ppermute | solution.py:571
  92.0 46.9 %collective-permute-start.6 = (f32[48,32,128]{2,1,0:T(8,128)S(1)}, f32[48,32,128]{2,1,0:T(8,128)S(1)}, u32[]{:S(2)}, u32[]{:S(2)}) collective-permute-start(f32[48,32,128]{2,1,0:T(8,128)S(1)} %get-tuple-element.59), channel_id=1, source_target_pairs={{0,112},{16,0},{32,16},{48,32},{64,48},{80,64},{96,80},{112,96},{1... | collective-permute-start | bytes 2359304 | tf_op jit(solution)/shard_map/ppermute | solution.py:571
  94.7 44.2 %collective-permute-start.7 = (f32[8,6,32,128]{3,2,1,0:T(8,128)S(1)}, f32[8,6,32,128]{3,2,1,0:T(8,128)S(1)}, u32[]{:S(2)}, u32[]{:S(2)}) collective-permute-start(f32[8,6,32,128]{3,2,1,0:T(8,128)S(1)} %get-tuple-element.60), channel_id=1, source_target_pairs={{0,2},{2,4},{4,6},{6,8},{8,10},{10,12},{12,14},{14,0},{1,3},{3,5},... | collective-permute-start | bytes 2359304 | tf_op jit(solution)/shard_map/ppermute | solution.py:571
  97.8 41.2 %collective-permute-start.8 = (f32[8,6,32,128]{3,2,1,0:T(8,128)S(1)}, f32[8,6,32,128]{3,2,1,0:T(8,128)S(1)}, u32[]{:S(2)}, u32[]{:S(2)}) collective-permute-start(f32[8,6,32,128]{3,2,1,0:T(8,128)S(1)} %get-tuple-element.61), channel_id=1, source_target_pairs={{0,14},{2,0},{4,2},{6,4},{8,6},{10,8},{12,10},{14,12},{1,15},{3,1}... | collective-permute-start | bytes 2359304 | tf_op jit(solution)/shard_map/ppermute | solution.py:571
  97.8 20.8 %collective-permute-start.9 = (f32[296,128]{1,0:T(8,128)S(1)}, f32[296,128]{1,0:T(8,128)S(1)}, u32[]{:S(2)}, u32[]{:S(2)}) collective-permute-start(f32[296,128]{1,0:T(8,128)S(1)} %get-tuple-element.62), channel_id=1, source_target_pairs={{0,1},{1,0},{2,3},{3,2},{4,5},{5,4},{6,7},{7,6},{8,9},{9,8},{10,11... | collective-permute-start | bytes 454664 | tf_op jit(solution)/shard_map/ppermute | solution.py:571
  154.7 43.6 %collective-permute-start.10 = (f32[48,32,128]{2,1,0:T(8,128)S(1)}, f32[48,32,128]{2,1,0:T(8,128)S(1)}, u32[]{:S(2)}, u32[]{:S(2)}) collective-permute-start(f32[48,32,128]{2,1,0:T(8,128)S(1)} %get-tuple-element.64), channel_id=1, source_target_pairs={{0,16},{16,32},{32,48},{48,64},{64,80},{80,96},{96,112},{112,0},{1... | collective-permute-start | bytes 2359304 | tf_op jit(solution)/shard_map/ppermute | solution.py:571
  155.3 43.1 %collective-permute-start.11 = (f32[48,32,128]{2,1,0:T(8,128)S(1)}, f32[48,32,128]{2,1,0:T(8,128)S(1)}, u32[]{:S(2)}, u32[]{:S(2)}) collective-permute-start(f32[48,32,128]{2,1,0:T(8,128)S(1)} %get-tuple-element.65), channel_id=1, source_target_pairs={{0,112},{16,0},{32,16},{48,32},{64,48},{80,64},{96,80},{112,96},{1... | collective-permute-start | bytes 2359304 | tf_op jit(solution)/shard_map/ppermute | solution.py:571
  158.4 40.0 %collective-permute-start.12 = (f32[8,6,32,128]{3,2,1,0:T(8,128)S(1)}, f32[8,6,32,128]{3,2,1,0:T(8,128)S(1)}, u32[]{:S(2)}, u32[]{:S(2)}) collective-permute-start(f32[8,6,32,128]{3,2,1,0:T(8,128)S(1)} %get-tuple-element.66), channel_id=1, source_target_pairs={{0,2},{2,4},{4,6},{6,8},{8,10},{10,12},{12,14},{14,0},{1,3},{3,5},... | collective-permute-start | bytes 2359304 | tf_op jit(solution)/shard_map/ppermute | solution.py:571
  161.2 37.1 %collective-permute-start.13 = (f32[8,6,32,128]{3,2,1,0:T(8,128)S(1)}, f32[8,6,32,128]{3,2,1,0:T(8,128)S(1)}, u32[]{:S(2)}, u32[]{:S(2)}) collective-permute-start(f32[8,6,32,128]{3,2,1,0:T(8,128)S(1)} %get-tuple-element.67), channel_id=1, source_target_pairs={{0,14},{2,0},{4,2},{6,4},{8,6},{10,8},{12,10},{14,12},{1,15},{3,1}... | collective-permute-start | bytes 2359304 | tf_op jit(solution)/shard_map/ppermute | solution.py:571
  161.2 18.1 %collective-permute-start.14 = (f32[296,128]{1,0:T(8,128)S(1)}, f32[296,128]{1,0:T(8,128)S(1)}, u32[]{:S(2)}, u32[]{:S(2)}) collective-permute-start(f32[296,128]{1,0:T(8,128)S(1)} %get-tuple-element.68), channel_id=1, source_target_pairs={{0,1},{1,0},{2,3},{3,2},{4,5},{5,4},{6,7},{7,6},{8,9},{9,8},{10,11... | collective-permute-start | bytes 454664 | tf_op jit(solution)/shard_map/ppermute | solution.py:571
  198.4 61.6 %slice-start = ((s8[5242880]{0:T(1024)(128)(4,1)}), s8[4194304]{0:T(1024)(128)(4,1)S(1)}, s32[]{:S(2)}) async-start(s8[5242880]{0:T(1024)(128)(4,1)} %bitcast.16), calls=%async_computation.9 | async-start | bytes 8388608
  198.4 61.6 %slice-start.1 = ((s8[5242880]{0:T(1024)(128)(4,1)}), s8[1048576]{0:T(1024)(128)(4,1)S(1)}, s32[]{:S(2)}) async-start(s8[5242880]{0:T(1024)(128)(4,1)} %bitcast.16), calls=%async_computation.10 | async-start | bytes 2097152
  214.6 45.3 %collective-permute-start.15 = (f32[48,32,128]{2,1,0:T(8,128)S(1)}, f32[48,32,128]{2,1,0:T(8,128)S(1)}, u32[]{:S(2)}, u32[]{:S(2)}) collective-permute-start(f32[48,32,128]{2,1,0:T(8,128)S(1)} %get-tuple-element.70), channel_id=1, source_target_pairs={{0,16},{16,32},{32,48},{48,64},{64,80},{80,96},{96,112},{112,0},{1... | collective-permute-start | bytes 2359304 | tf_op jit(solution)/shard_map/ppermute | solution.py:571
  215.2 44.7 %collective-permute-start.16 = (f32[48,32,128]{2,1,0:T(8,128)S(1)}, f32[48,32,128]{2,1,0:T(8,128)S(1)}, u32[]{:S(2)}, u32[]{:S(2)}) collective-permute-start(f32[48,32,128]{2,1,0:T(8,128)S(1)} %get-tuple-element.71), channel_id=1, source_target_pairs={{0,112},{16,0},{32,16},{48,32},{64,48},{80,64},{96,80},{112,96},{1... | collective-permute-start | bytes 2359304 | tf_op jit(solution)/shard_map/ppermute | solution.py:571
  218.3 41.6 %collective-permute-start.17 = (f32[8,6,32,128]{3,2,1,0:T(8,128)S(1)}, f32[8,6,32,128]{3,2,1,0:T(8,128)S(1)}, u32[]{:S(2)}, u32[]{:S(2)}) collective-permute-start(f32[8,6,32,128]{3,2,1,0:T(8,128)S(1)} %get-tuple-element.72), channel_id=1, source_target_pairs={{0,2},{2,4},{4,6},{6,8},{8,10},{10,12},{12,14},{14,0},{1,3},{3,5},... | collective-permute-start | bytes 2359304 | tf_op jit(solution)/shard_map/ppermute | solution.py:571
  221.1 38.8 %collective-permute-start.18 = (f32[8,6,32,128]{3,2,1,0:T(8,128)S(1)}, f32[8,6,32,128]{3,2,1,0:T(8,128)S(1)}, u32[]{:S(2)}, u32[]{:S(2)}) collective-permute-start(f32[8,6,32,128]{3,2,1,0:T(8,128)S(1)} %get-tuple-element.73), channel_id=1, source_target_pairs={{0,14},{2,0},{4,2},{6,4},{8,6},{10,8},{12,10},{14,12},{1,15},{3,1}... | collective-permute-start | bytes 2359304 | tf_op jit(solution)/shard_map/ppermute | solution.py:571
  221.1 19.9 %collective-permute-start.19 = (f32[296,128]{1,0:T(8,128)S(1)}, f32[296,128]{1,0:T(8,128)S(1)}, u32[]{:S(2)}, u32[]{:S(2)}) collective-permute-start(f32[296,128]{1,0:T(8,128)S(1)} %get-tuple-element.74), channel_id=1, source_target_pairs={{0,1},{1,0},{2,3},{3,2},{4,5},{5,4},{6,7},{7,6},{8,9},{9,8},{10,11... | collective-permute-start | bytes 454664 | tf_op jit(solution)/shard_map/ppermute | solution.py:571

commit v2 on v1

v2 whole, which is shorter than its diff:
```python
import functools

import jax
import jax.numpy as jnp
import numpy as np
from jax import lax
from jax.experimental import pallas as pl
from jax.experimental.pallas import tpu as pltpu
from jax.sharding import PartitionSpec as P

DEGREE = 4
STENCIL = (
    -5369.0 / 1800.0,
    12.0 / 7.0,
    -15.0 / 56.0,
    10.0 / 189.0,
    -1.0 / 112.0,
    2.0 / 1925.0,
    -1.0 / 16632.0,
)
FILTER_CENTRE = 9.5
FILTER_HALF = 5.5
REACH = 6

NB = 32
SX = 8
SY = 8
SZ = 128
ROWS = SX * SY
PAIRS = ROWS // 2
FACE = REACH * SY
NPJ = 4
SLOTS = 8192
TGT = 40
CH = NPJ * TGT
GROUPS = ROWS // 4
TOTAL = (2 * CH, 2 * NB)
ZROWS = GROUPS * 16
LANES = 128
F32 = jnp.float32
BF16 = jnp.bfloat16
NN = (((1,), (0,)), ((), ()))
NT = (((1,), (1,)), ((), ()))
VMEM_LIMIT = 32 * 1024 * 1024


def dot(a, b, dims=NN):
    return lax.dot_general(a, b, dims, preferred_element_type=F32)


def split2(v):
    hi = v.astype(BF16)
    return hi, (v - hi.astype(F32)).astype(BF16)


def split3(v):
    hi = v.astype(BF16)
    rest = v - hi.astype(F32)
    mid = rest.astype(BF16)
    return hi, mid, (rest - mid.astype(F32)).astype(BF16)


def z_matrices():
    half = [0.0] + [-0.5 * c for c in STENCIL[1:]]
    inner = np.zeros((SZ, SZ), np.float32)
    face = np.zeros((16, SZ), np.float32)
    for z in range(SZ):
        for source in range(SZ):
            if 1 <= abs(z - source) <= REACH:
                inner[source, z] = half[abs(z - source)]
        for e in range(8):
            if 1 <= abs(SZ + e - z) <= REACH:
                face[e, z] = half[abs(SZ + e - z)]
            if 1 <= abs(z + 8 - e) <= REACH:
                face[8 + e, z] = half[abs(z + 8 - e)]

    def split(m):
        hi = m.astype(jnp.bfloat16)
        return hi, (m - hi.astype(np.float32)).astype(jnp.bfloat16)

    inner_hi, inner_lo = split(inner)
    face_hi, face_lo = split(face)
    first = np.concatenate([inner_hi, inner_hi], axis=0)
    second = np.concatenate(
        [inner_lo, face_hi, face_hi, face_lo, np.zeros((SZ - 48, SZ), jnp.bfloat16)], axis=0
    )
    return jnp.asarray(first), jnp.asarray(second)


def any_specs(count):
    return [pl.BlockSpec(memory_space=pl.ANY)] * count


def vmem_specs(count):
    return [pl.BlockSpec(memory_space=pltpu.VMEM)] * count


PARAMS = pltpu.CompilerParams(vmem_limit_bytes=VMEM_LIMIT)


def cost(us):
    return pl.CostEstimate(flops=0, bytes_accessed=int(us * 3.5e6), transcendentals=0)


def z_faces(rows):
    turned = jnp.concatenate(rows, axis=0).T
    return jnp.concatenate([turned[:8], turned[SZ - 8 :]], axis=0)


def write_faces(field, x_low, x_high, y_low, y_high):
    x_low[...] = field[pl.ds(0, FACE)]
    x_high[...] = field[pl.ds(ROWS - FACE, FACE)]
    for x in range(SX):
        y_low[x] = field[pl.ds(x * SY, REACH)]
        y_high[x] = field[pl.ds(x * SY + SY - REACH, REACH)]


BLOCK = jax.ShapeDtypeStruct((ROWS, NB, SZ), F32)
X_FACE = jax.ShapeDtypeStruct((FACE, NB, SZ), F32)
Y_FACE = jax.ShapeDtypeStruct((SX, REACH, NB, SZ), F32)
Z_FACE = jax.ShapeDtypeStruct((ZROWS, LANES), F32)
FACES = [X_FACE, X_FACE, Y_FACE, Y_FACE, Z_FACE]


def rearrange_kernel(src, field, x_low, x_high, y_low, y_high, z_face, in_sem):
    loads = [
        pltpu.make_async_copy(src.at[:, row, :], field.at[row], in_sem.at[row]) for row in range(ROWS)
    ]
    for load in loads:
        load.start()
    for load in loads:
        load.wait()
    write_faces(field, x_low, x_high, y_low, y_high)
    for g in range(GROUPS):
        z_face[pl.ds(16 * g, 16), :] = z_faces([field[4 * g + i] for i in range(4)])


def rearrange(orbitals):
    return pl.pallas_call(
        rearrange_kernel,
        out_shape=[BLOCK] + FACES,
        in_specs=any_specs(1),
        out_specs=vmem_specs(6),
        scratch_shapes=[pltpu.SemaphoreType.DMA((ROWS,))],
        compiler_params=PARAMS,
        cost_estimate=cost(3),
        name="rearrange",
    )(orbitals)


def build_kernel(starts, keys, w0, w1, w2, w3, out, held, weights):
    held[pl.ds(0, SLOTS // LANES), :] = keys[...]
    held[pl.ds(SLOTS // LANES, 8), :] = jnp.full((8, LANES), ROWS * SZ * 64, jnp.int32)
    for j, w in enumerate((w0, w1, w2, w3)):
        weights[j, pl.ds(0, SLOTS // LANES), :] = w[...]
        weights[j, pl.ds(SLOTS // LANES, 8), :] = jnp.zeros((8, LANES), F32)
    target_at = lax.broadcasted_iota(jnp.int32, (TGT, 2 * LANES), 0)
    z_at = lax.broadcasted_iota(jnp.int32, (SZ, 2 * LANES), 0)

    def window(row, block):
        key = jnp.concatenate([held[pl.ds(block, 1), :], held[pl.ds(block + 1, 1), :]], axis=1)
        target = jnp.where((key >> 13) == row, key & 63, 63)
        chosen = target_at == target
        parts = []
        for j in range(NPJ):
            w = jnp.concatenate(
                [weights[j, pl.ds(block, 1), :], weights[j, pl.ds(block + 1, 1), :]], axis=1
            )
            parts.append(jnp.where(chosen, w, 0.0))
        hi, lo = split2(jnp.concatenate(parts, axis=0))
        place = jnp.where(z_at == ((key >> 6) & 127), 1.0, 0.0).astype(BF16)
        both = dot(jnp.concatenate([hi, lo], axis=0), place, NT)
        return both[:CH] + both[CH:]

    @pl.loop(0, PAIRS)
    def _(pair):
        for parity in range(2):
            row = 2 * pair + parity
            low = starts[row]
            high = starts[row + 1]
            base = low // LANES
            windows = (high - base * LANES + 2 * LANES - 1) // (2 * LANES)
            total = window(row, base)

            total = lax.fori_loop(
                1, windows, lambda i, acc: acc + window(row, base + 2 * i), total
            )
            hi, lo = split2(total)
            out[pair, :, pl.ds(parity * SZ, SZ)] = jnp.concatenate([hi, lo], axis=0)


def build(starts, keys, weights):
    return pl.pallas_call(
        build_kernel,
        out_shape=jax.ShapeDtypeStruct((PAIRS, 2 * CH, 2 * SZ), BF16),
        in_specs=[pl.BlockSpec(memory_space=pltpu.SMEM)] + vmem_specs(5),
        out_specs=pl.BlockSpec(memory_space=pltpu.VMEM),
        scratch_shapes=[
            pltpu.VMEM((SLOTS // LANES + 8, LANES), jnp.int32),
            pltpu.VMEM((NPJ, SLOTS // LANES + 8, LANES), F32),
        ],
        compiler_params=PARAMS,
        cost_estimate=cost(15),
        name="build",
    )(starts, keys, *weights)


def partial_of(mat, values):
    hi, lo = split2(values)
    return dot(mat, jnp.concatenate([hi, lo], axis=0), NT)


def packed_partial(total):
    joined = total[:CH, :NB] + total[:CH, NB:] + total[CH:, :NB]
    return jnp.concatenate([joined[j * TGT : (j + 1) * TGT] for j in range(NPJ)], axis=1)


def first_kernel(field, mat, out, total):
    total[...] = jnp.zeros_like(total)

    @pl.loop(0, SX)
    def _(x):
        acc = total[...]
        for p in range(4):
            at = x * SY + 2 * p
            values = jnp.concatenate([field[at], field[at + 1]], axis=1)
            acc = acc + partial_of(mat[x * 4 + p], values)
        total[...] = acc

    out[...] = packed_partial(total[...])


def first(field, mat):
    return pl.pallas_call(
        first_kernel,
        out_shape=jax.ShapeDtypeStruct((TGT, LANES), F32),
        in_specs=vmem_specs(2),
        out_specs=pl.BlockSpec(memory_space=pltpu.VMEM),
        scratch_shapes=[pltpu.VMEM(TOTAL, F32)],
        compiler_params=PARAMS,
        cost_estimate=cost(3),
        name="first",
    )(field, mat)


def pieces(frame, stride):
    row = lax.broadcasted_iota(jnp.int32, (TGT, LANES), 0)
    digit = (row // stride) % 3
    for distance in range(-2, 3):
        moved = frame if distance == 0 else pltpu.roll(frame, (-stride * distance) % TGT, 0)
        valid = (digit + distance >= 0) & (digit + distance <= 2) & (row < 36)
        yield distance, jnp.where(valid, moved, 0.0)


def spread_y_kernel(frames, me, mine, out):
    for f in range(frames):
        at = pl.ds(f * TGT, TGT)
        for distance in (-3, 3, 4):
            out[(me[0] + distance + 8) % 8, at, :] = jnp.zeros((TGT, LANES), F32)
        for distance, piece in pieces(mine[at, :], 4):
            out[(me[0] + distance + 8) % 8, at, :] = piece


def spread_xz_kernel(frames, me, came, out):
    row = lax.broadcasted_iota(jnp.int32, (TGT, LANES), 0)
    for f in range(frames):
        at = pl.ds(f * TGT, TGT)
        frame = came[0, at, :]
        for slot in range(1, 8):
            frame = frame + came[slot, at, :]
        for distance in (-3, 3, 4):
            for z in range(2):
                out[((me[0] + distance + 8) % 8) * 2 + z, at, :] = jnp.zeros((TGT, LANES), F32)
        for distance, piece in pieces(frame, 12):
            swapped = jnp.where(
                row & 2 == 0, pltpu.roll(piece, TGT - 2, 0), pltpu.roll(piece, 2, 0)
            )
            slot = ((me[0] + distance + 8) % 8) * 2
            out[slot + me[1], at, :] = piece
            out[slot + 1 - me[1], at, :] = swapped


def spread_call(kernel, slots, frames, me, array):
    return pl.pallas_call(
        functools.partial(kernel, frames),
        out_shape=jax.ShapeDtypeStruct((slots, frames * TGT, LANES), F32),
        in_specs=[pl.BlockSpec(memory_space=pltpu.SMEM)] + vmem_specs(1),
        out_specs=pl.BlockSpec(memory_space=pltpu.VMEM),
        compiler_params=PARAMS,
        cost_estimate=cost(0.7),
        name="spread",
    )(me, array)


def local_kernel(first_step, *refs):
    if first_step:
        field, x_left, x_right, y_left, y_right, faces, potential, first_z, second_z, out = refs
        previous = None
    else:
        field, previous, x_left, x_right, y_left, y_right, faces, potential, first_z, second_z, out = refs
    alpha = (1.0 if first_step else 2.0) / FILTER_HALF
    half = [0.0] + [-0.5 * c for c in STENCIL[1:]]
    diagonal = -1.5 * STENCIL[0] - FILTER_CENTRE

    def at(x, y):
        if x < 0:
            return x_left[(x + REACH) * SY + y]
        if x >= SX:
            return x_right[(x - SX) * SY + y]
        if y < 0:
            return y_left[x, y + REACH]
        if y >= SY:
            return y_right[x, y - SY]
        return field[x * SY + y]

    for g in range(GROUPS):
        rows = [field[4 * g + i] for i in range(4)]
        hi, lo = split2(jnp.concatenate(rows, axis=0))
        face = faces[pl.ds(g * 16, 16), :]
        face_hi = face.astype(BF16).astype(F32)
        side = jnp.concatenate(
            [face_hi, face - face_hi, face_hi, jnp.zeros((LANES - 48, LANES), F32)], axis=0
        ).T.astype(BF16)
        along_z = dot(jnp.concatenate([hi, lo], axis=1), first_z[...]) + dot(
            jnp.concatenate([hi, side], axis=1), second_z[...]
        )
        for i in range(4):
            x, y = divmod(4 * g + i, SY)
            summed = along_z[i * NB : (i + 1) * NB]
            for m in range(1, REACH + 1):
                around = (at(x + m, y) + at(x - m, y)) + (at(x, y + m) + at(x, y - m))
                summed = summed + half[m] * around
            summed = summed + (potential[pl.ds(4 * g + i, 1), :] + diagonal) * rows[i]
            result = alpha * summed
            if not first_step:
                result = result - previous[4 * g + i]
            out[4 * g + i] = result


def local_part(first_step, *arrays):
    return pl.pallas_call(
        functools.partial(local_kernel, first_step),
        out_shape=BLOCK,
        in_specs=vmem_specs(len(arrays)),
        out_specs=pl.BlockSpec(memory_space=pltpu.VMEM),
        compiler_params=PARAMS,
        cost_estimate=cost(4),
        name="local",
    )(*arrays)


def coupled_kernel(first_step, last_step, *refs):
    if first_step:
        (base, came, mat), refs = refs[:3], refs[3:]
    else:
        (base, came, mat, coupling), refs = refs[:4], refs[4:]
    if last_step:
        new, gram, total, coef = refs
    else:
        (new, x_low, x_high, y_low, y_high, z_face, partial), refs = refs[:7], refs[7:]
        if first_step:
            coupling, refs = refs[0], refs[1:]
        total, coef = refs
    alpha = (1.0 if first_step else 2.0) / FILTER_HALF
    frame = came[0]
    for slot in range(1, came.shape[0]):
        frame = frame + came[slot]
    if first_step:
        coupling[...] = frame[TGT:]
        frame = frame[:TGT]
    frame = frame * (alpha * coupling[...])
    stacked = jnp.concatenate([frame[:, j * NB : (j + 1) * NB] for j in range(NPJ)], axis=0)
    turned = stacked.T
    coef_hi = turned.astype(BF16).astype(F32)
    coef[pl.ds(0, NB), :] = jnp.concatenate([coef_hi, coef_hi], axis=1).astype(BF16)
    coef[pl.ds(NB, NB), pl.ds(0, CH)] = (turned - coef_hi).astype(BF16)
    total[...] = jnp.zeros_like(total)

    @pl.loop(0, SX)
    def _(x):
        c_hi = coef[pl.ds(0, NB), :]
        c_lo = coef[pl.ds(NB, NB), pl.ds(0, CH)]
        acc = total[...]
        for part in range(2):
            rows = []
            for p in range(2):
                pair_mat = mat[x * 4 + 2 * part + p]
                added = dot(c_hi, pair_mat) + dot(c_lo, pair_mat[:CH])
                for q in range(2):
                    at = x * SY + 4 * part + 2 * p + q
                    result = base[at] + added[:, q * SZ : (q + 1) * SZ]
                    new[at] = result
                    rows.append(result)
            for p in range(2):
                values = jnp.concatenate(rows[2 * p : 2 * p + 2], axis=1)
                if last_step:
                    joined = jnp.concatenate(split3(values), axis=0)
                    acc = acc + dot(joined, joined, NT)
                else:
                    acc = acc + partial_of(mat[x * 4 + 2 * part + p], values)
            if not last_step:
                z_face[pl.ds((2 * x + part) * 16, 16), :] = z_faces(rows)
        total[...] = acc

    if last_step:
        t = total[...]
        summed = t[2 * NB :, :NB] + t[:NB, 2 * NB :] + t[NB : 2 * NB, NB : 2 * NB]
        summed = summed + (t[NB : 2 * NB, :NB] + t[:NB, NB : 2 * NB]) + t[:NB, :NB]
        gram[...] = jnp.concatenate([summed[8 * q : 8 * q + 8] for q in range(4)], axis=1)
    else:
        partial[...] = packed_partial(total[...])
        write_faces(new, x_low, x_high, y_low, y_high)


def coupled_part(first_step, last_step, *arrays):
    frame = jax.ShapeDtypeStruct((TGT, LANES), F32)
    if last_step:
        outs, total = [BLOCK, jax.ShapeDtypeStruct((8, LANES), F32)], (3 * NB, 3 * NB)
    else:
        outs, total = [BLOCK] + FACES + [frame], TOTAL
        if first_step:
            outs.append(frame)
    return pl.pallas_call(
        functools.partial(coupled_kernel, first_step, last_step),
        out_shape=outs,
        in_specs=vmem_specs(len(arrays)),
        out_specs=vmem_specs(len(outs)),
        scratch_shapes=[pltpu.VMEM(total, F32), pltpu.VMEM((2 * NB, 2 * CH), BF16)],
        compiler_params=PARAMS,
        cost_estimate=cost(6),
        name="coupled",
    )(*arrays)


def finish_kernel(scale, field, grams, out, held, made, inverse, in_sem, out_sem):
    loads = [
        pltpu.make_async_copy(field.at[pl.ds(x * SY, SY)], held.at[pl.ds(x * SY, SY)], in_sem.at[x])
        for x in range(SX)
    ]
    for load in loads:
        load.start()
    packed = grams[0]
    for slot in range(1, grams.shape[0]):
        packed = packed + grams[slot]
    packed = packed * scale
    gram = jnp.concatenate([packed[:, q * NB : (q + 1) * NB] for q in range(4)], axis=0)
    row = lax.broadcasted_iota(jnp.int32, (NB, NB), 0)
    column = lax.broadcasted_iota(jnp.int32, (NB, NB), 1)
    eye = jnp.where(row == column, 1.0, 0.0)
    work = jnp.concatenate([gram, eye], axis=1)
    below = lax.broadcasted_iota(jnp.int32, (NB, 2 * NB), 0)
    for k in range(NB):
        root = 1.0 / jnp.sqrt(work[k : k + 1, k : k + 1])
        line = work[k : k + 1, :] * root
        inverse[pl.ds(k, 1), :] = line[:, NB:]
        if k < NB - 1:
            factor = work[:, k : k + 1] * root
            work = work - jnp.where(below > k, factor * line, 0.0)
    hi, mid, lo = split3(inverse[...])
    left = jnp.concatenate([lo, mid, hi, mid, hi, hi], axis=1)

    @pl.loop(0, SX)
    def _(x):
        pltpu.make_async_copy(
            field.at[pl.ds(x * SY, SY)], held.at[pl.ds(x * SY, SY)], in_sem.at[x]
        ).wait()
        for p in range(SY // 2):
            at = x * SY + 2 * p
            values = jnp.concatenate([held[at], held[at + 1]], axis=1)
            f_hi, f_mid, f_lo = split3(values)
            right = jnp.concatenate([f_hi, f_mid, f_lo, f_hi, f_mid, f_hi], axis=0)
            result = dot(left, right)
            made[at] = result[:, :SZ]
            made[at + 1] = result[:, SZ:]
            for q in range(2):
                pltpu.make_async_copy(made.at[at + q], out.at[:, at + q, :], out_sem.at[at + q]).start()

    for r in range(ROWS):
        pltpu.make_async_copy(made.at[r], out.at[:, r, :], out_sem.at[r]).wait()


def finish(scale, field, grams):
    return pl.pallas_call(
        functools.partial(finish_kernel, scale),
        out_shape=jax.ShapeDtypeStruct((NB, ROWS, SZ), F32),
        in_specs=any_specs(1) + vmem_specs(1),
        out_specs=pl.BlockSpec(memory_space=pl.ANY),
        scratch_shapes=[
            pltpu.VMEM((ROWS, NB, SZ), F32),
            pltpu.VMEM((ROWS, NB, SZ), F32),
            pltpu.VMEM((NB, NB), F32),
            pltpu.SemaphoreType.DMA((SX,)),
            pltpu.SemaphoreType.DMA((ROWS,)),
        ],
        compiler_params=PARAMS,
        name="finish",
    )(field, grams)


def shift(value, axis, by):
    count = lax.axis_size(axis)
    return lax.ppermute(value, axis, [(i, (i + by) % count) for i in range(count)])


def local(orbitals, potential, projector, point_cell, target, point_count, coupling):
    bands, size_x, size_y, size_z = orbitals.shape
    me_x = lax.axis_index("gx").astype(jnp.int32).reshape(1)
    me_y = lax.axis_index("gy").astype(jnp.int32).reshape(1)
    me_z = lax.axis_index("gz").astype(jnp.int32).reshape(1)
    me_xz = jnp.concatenate([me_x, me_z])

    field, x_low, x_high, y_low, y_high, z_face = rearrange(orbitals.reshape(NB, ROWS, SZ))
    pot = potential.reshape(ROWS, SZ)
    first_z, second_z = z_matrices()

    alive = lax.iota(jnp.int32, SLOTS) < point_count.reshape(())
    code = target // 2
    z_other = (code % 3 != 1).astype(jnp.int32)
    wanted = ((code // 3) * 2 + z_other) * 2 + target % 2
    key = jnp.where(alive, point_cell * 64 + wanted, ROWS * SZ * 64)
    starts = jnp.sum(
        (key[None, :] < (lax.iota(jnp.int32, ROWS + 1) * (SZ * 64))[:, None]).astype(jnp.int32), axis=1
    )
    ordered = lax.sort((key,) + tuple(projector[j] for j in range(NPJ)), num_keys=1, is_stable=False)
    ordered = [o.reshape(SLOTS // LANES, LANES) for o in ordered]
    mat = build(starts, ordered[0], ordered[1:])

    own = jnp.repeat(coupling, NB, axis=1)
    coupling_frame = jnp.zeros((TGT, LANES), F32).at[16:18].set(own)

    previous = ()
    scales = ()
    for k in range(DEGREE):
        start, last = k == 0, k == DEGREE - 1
        x_left = shift(x_high, "gx", 1)
        x_right = shift(x_low, "gx", -1)
        if start:
            y_left = shift(y_high, "gy", 1)
            y_right = shift(y_low, "gy", -1)
            faces = shift(z_face, "gz", 1)
            mat, field, x_left, x_right, y_left, y_right, faces = lax.optimization_barrier(
                (mat, field, x_left, x_right, y_left, y_right, faces)
            )
            partial = first(field, mat)
            partial = jnp.concatenate([partial, coupling_frame], axis=0)
        frames = 2 if start else 1
        sends = spread_call(spread_y_kernel, 8, frames, me_y, partial)
        came = lax.all_to_all(sends, "gy", 0, 0)
        if not start:
            came, y_low, y_high, z_face = lax.optimization_barrier((came, y_low, y_high, z_face))
            y_left = shift(y_high, "gy", 1)
            y_right = shift(y_low, "gy", -1)
            faces = shift(z_face, "gz", 1)
        sends = spread_call(spread_xz_kernel, 16, frames, me_xz, came)
        came = lax.all_to_all(sends, ("gx", "gz"), 0, 0)
        base = local_part(
            start, field, *previous, x_left, x_right, y_left, y_right, faces, pot, first_z, second_z
        )
        outs = coupled_part(start, last, base, came, mat, *scales)
        previous = (field,)
        if last:
            field, gram = outs
        else:
            field, x_low, x_high, y_low, y_high, z_face, partial = outs[:7]
            if start:
                scales = (outs[7],)
    axes = ("gx", "gy", "gz")
    devices = 1
    for axis in axes:
        devices *= lax.axis_size(axis)
    grams = lax.all_to_all(jnp.broadcast_to(gram[None], (devices,) + gram.shape), axes, 0, 0)
    result = finish(1.0 / float(devices * ROWS * SZ), field, grams)
    return result.reshape(bands, size_x, size_y, size_z)


def solution(mesh):
    in_specs = (
        P(None, "gx", "gy", "gz"),
        P("gx", "gy", "gz"),
        P(None, ("gx", "gy", "gz")),
        P(("gx", "gy", "gz")),
        P(("gx", "gy", "gz")),
        P("gx", "gy", "gz"),
        P(("gx", "gy", "gz"), None),
    )
    out_specs = P(None, "gx", "gy", "gz")
    return jax.shard_map(local, mesh=mesh, in_specs=in_specs, out_specs=out_specs, check_vma=False)
```

time: 298 us -> 293 us (0.983)
  blocking collectives: 94.1 us -> 21.3 us
  local copies, waits for them, and re-layouts: 5.91 us -> 50.1 us
  starting transfers between devices: 42.6 us -> 71.7 us
  Pallas kernels: 88.7 us -> 77.1 us
    all_to_all x7 -> x0, blocking collectives: 75.9 us -> none  [the longest x4 48.7 us: local(): came = lax.all_to_all(sends, 'gx', 0, 0)]
    unnamed x22 -> x110, local copies, waits for them, and re-layouts: 3.75 us -> 47.2 us
    pallas_call x6 -> x10, Pallas kernels: 65.1 us -> 46.2 us  [the longest x4 26 us: coupled_part(): pl.pallas_call(functools.partial(coupled_kernel, first_step, last_step),...]
    all_to_all x0 -> x4, starting transfers between devices: none -> 18.2 us  [local(): came = lax.all_to_all(sends, ('gx', 'gz'), 0, 0)]
    ppermute x20, waiting for transfers between devices: 55.8 us -> 40 us  [shift(): lax.ppermute(value, axis, [(i, (i + by) % count) for i in range(count)])]
    all_to_all x1 -> x4, starting transfers between devices: 5.52 us -> 21.1 us  [local(): came = lax.all_to_all(sends, 'gy', 0, 0)]
    all_to_all x1 -> x4, waiting for transfers between devices: 1.64 us -> 14 us  [local(): came = lax.all_to_all(sends, 'gy', 0, 0)]
    pallas_call x8, Pallas kernels: 1.15 us -> 8.35 us  [spread_call(): pl.pallas_call(functools.partial(kernel, frames), out_shape=jax.ShapeDtyp...]
  transfers between devices with their start and end apart: 21 -> 28, of which waited for: 5 -> 8; matrix products, arithmetic and copies ran while one was open for 0% -> 4% of each run, Pallas kernels for 0% -> 11%
where the time goes in v2:
time: 293 us; the launch traced here: 290 us
  Pallas kernels  77.1 us (26%)
  starting transfers between devices  71.7 us (24%)
  waiting for transfers between devices  58.6 us (20%)
  local copies, waits for them, and re-layouts  50.1 us (17%)
  blocking collectives  21.3 us (7%)
  other arithmetic  10 us (3%)
    unnamed x110, local copies, waits for them, and re-layouts  47.2 us
    ppermute x20, waiting for transfers between devices, shift(): lax.ppermute(value, axis, [(i, (i + by) % count) for i in range(count)])  40 us
    ppermute x20, starting transfers between devices, shift(): lax.ppermute(value, axis, [(i, (i + by) % count) for i in range(count)])  32.4 us
    pallas_call x4, Pallas kernels, coupled_part(): pl.pallas_call(functools.partial(coupled_kernel, first_step, last_step),...  26 us
    all_to_all x1, blocking collectives, local(): lax.all_to_all(jnp.broadcast_to(gram[None], (devices,) + gram.shape), axe...  21.3 us
    all_to_all x4, starting transfers between devices, local(): came = lax.all_to_all(sends, 'gy', 0, 0)  21.1 us
    all_to_all x4, starting transfers between devices, local(): came = lax.all_to_all(sends, ('gx', 'gz'), 0, 0)  18.2 us
    pallas_call x1, Pallas kernels, build(): pl.pallas_call(build_kernel, out_shape=jax.ShapeDtypeStruct((PAIRS, 2 * C...  15.1 us
  transfers between devices with their start and end apart: 28, of which 8 were waited for; matrix products, arithmetic and copies ran while one was open for 4% of the time, Pallas kernels for 11%

profile of v2, /device:TPU:1, one launch (start us, length us, event | category | flops | bytes accessed | tf_op | source)
XLA Modules:
  0.0 290.1 jit_solution(5789975017956401300)
XLA Ops:
  1.2 3.8 %rearrange.1 = (f32[64,32,128]{2,1,0:T(8,128)S(1)}, f32[48,32,128]{2,1,0:T(8,128)}, f32[48,32,128]{2,1,0:T(8,128)}, f32[8,6,32,128]{3,2,1,0:T(8,128)}, f32[8,6,32,128]{3,2,1,0:T(8,128)}, /*index=5*/f32[256,128]{1,0:T(8,128)}) custom-call(f32[32,64,128]{2,1,0:T(8,128)S(1)} %bitcast.17), custom_call_target="tpu_custom_call" | custom-call | bytes 10500000 | tf_op jit(solution)/shard_map/rearrange/pallas_call | solution.py:139
  5.0 4.5 %collective-permute-start.4 = (f32[256,128]{1,0:T(8,128)}, f32[256,128]{1,0:T(8,128)S(1)}, u32[]{:S(2)}, u32[]{:S(2)}) collective-permute-start(f32[256,128]{1,0:T(8,128)} %get-tuple-element.81), channel_id=1, source_target_pairs={{0,1},{1,0},{2,3},{3,2},{4,5},{5,4},{6,7},{7,6},{8,9},{9,8},{10,11... | collective-permute-start | bytes 393224 | tf_op jit(solution)/shard_map/ppermute | solution.py:502
  20.6 7.3 %sort.33 = (s32[8192]{0:T(1024)}, f32[8192]{0:T(1024)}, f32[8192]{0:T(1024)}, f32[8192]{0:T(1024)}, f32[8192]{0:T(1024)}) sort(s32[8192]{0:T(1024)} %fusion.5, f32[8192]{0:T(1024)} %bitcast.29, f32[8192]{0:T(1024)} %bitcast.28, f32[8192]{0:T(1024)} %bitcast.30, f32[8192]{0:T(1024)} %bitcast.27), dimensions={0}, to_apply=%region_1.2 | sort | flops 106496 | bytes 327680 | tf_op jit(solution)/shard_map/sort | solution.py:524
  32.9 15.1 %build.1.mat.refs_2_ = bf16[32,320,256]{2,1,0:T(8,128)(2,1)S(1)} custom-call(s32[65]{0:T(128)S(1)} %convert_reduce_fusion.starts, s32[64,128]{1,0:T(8,128)S(1)} %bitcast.22, f32[64,128]{1,0:T(8,128)S(1)} %bitcast.23, f32[64,128]{1,0:T(8,128)S(1)} %bitcast.24, f32[64,128]{1,0:T(8,128)S(1)} %bitcast.25, f32[64,128]{1,0:T(8,128)S(1)} %bitcast.26), custom_call_target="tpu_custom_call" | custom-call | bytes 52500000 | tf_op jit(solution)/shard_map/build/pallas_call | solution.py:193
  54.8 5.2 %all-to-all-start = ((f32[8,80,128]{2,1,0:T(8,128)}), f32[8,80,128]{2,1,0:T(8,128)S(1)}, u32[]{:S(2)}, u32[]{:S(2)}) async-start(f32[8,80,128]{2,1,0:T(8,128)} %spread.8), calls=%async_computation | async-start | bytes 655360 | tf_op jit(solution)/shard_map/all_to_all | solution.py:548
  60.1 7.1 %all-to-all-done.came = f32[8,80,128]{2,1,0:T(8,128)S(1)} async-done(((f32[8,80,128]{2,1,0:T(8,128)}), f32[8,80,128]{2,1,0:T(8,128)S(1)}, u32[]{:S(2)}, u32[]{:S(2)}) %all-to-all-start) | async-done | bytes 327712 | tf_op jit(solution)/shard_map/all_to_all | solution.py:548
  68.6 3.6 %all-to-all-start.1 = ((f32[16,80,128]{2,1,0:T(8,128)}), f32[16,80,128]{2,1,0:T(8,128)S(1)}, u32[]{:S(2)}, u32[]{:S(2)}) async-start(f32[16,80,128]{2,1,0:T(8,128)} %spread.9), calls=%async_computation.1 | async-start | bytes 1310720 | tf_op jit(solution)/shard_map/all_to_all | solution.py:555
  75.7 3.1 %local.4.refs_0_ = f32[64,32,128]{2,1,0:T(8,128)S(1)} custom-call(f32[64,32,128]{2,1,0:T(8,128)S(1)} %get-tuple-element.82.refs_0_.field.refs_1_, f32[48,32,128]{2,1,0:T(8,128)S(1)} %copy-done.20, f32[48,32,128]{2,1,0:T(8,128)S(1)} %copy-done.22, f32[8,6,32,128]{3,2,1,0:T(8,128)S(1)} %copy-done.24, f32[8,6,32,128]{3,2,1,0:T(8,128)} %collective-permute-done.3.refs_4_, ...), custom_call_target="tpu_custom_call" | custom-call | bytes 14000000 | tf_op jit(solution)/shard_map/local/pallas_call | solution.py:341
  78.8 4.6 %all-to-all-done.1.refs_1_ = f32[16,80,128]{2,1,0:T(8,128)S(1)} async-done(((f32[16,80,128]{2,1,0:T(8,128)}), f32[16,80,128]{2,1,0:T(8,128)S(1)}, u32[]{:S(2)}, u32[]{:S(2)}) %all-to-all-start.1) | async-done | bytes 655392 | tf_op jit(solution)/shard_map/all_to_all | solution.py:555
  87.8 6.9 %coupled.4 = (f32[64,32,128]{2,1,0:T(8,128)S(1)}, f32[48,32,128]{2,1,0:T(8,128)S(1)}, f32[48,32,128]{2,1,0:T(8,128)S(1)}, f32[8,6,32,128]{3,2,1,0:T(8,128)S(1)},...) custom-call(f32[64,32,128]{2,1,0:T(8,128)S(1)} %local.4.refs_0_, ...), custom_call_target="tpu_custom_call" | custom-call | bytes 21000000 | tf_op jit(solution)/shard_map/coupled/pallas_call | solution.py:423
  99.1 6.0 %all-to-all-start.2 = ((f32[8,40,128]{2,1,0:T(8,128)}), f32[8,40,128]{2,1,0:T(8,128)S(1)}, u32[]{:S(2)}, u32[]{:S(2)}) async-start(f32[8,40,128]{2,1,0:T(8,128)} %spread.10), calls=%async_computation.2 | async-start | bytes 327680 | tf_op jit(solution)/shard_map/all_to_all | solution.py:548
  105.5 3.1 %collective-permute-start.6 = (f32[48,32,128]{2,1,0:T(8,128)}, f32[48,32,128]{2,1,0:T(8,128)}, u32[]{:S(2)}, u32[]{:S(2)}) collective-permute-start(f32[48,32,128]{2,1,0:T(8,128)} %copy-done.47), channel_id=1, source_target_pairs={{0,112},{16,0},{32,16},{48,32},{64,48},{80,64},{96,80},{112,96},{1... | collective-permute-start | bytes 2359304 | tf_op jit(solution)/shard_map/ppermute | solution.py:502
  113.1 3.6 %all-to-all-start.3 = ((f32[16,40,128]{2,1,0:T(8,128)}), f32[16,40,128]{2,1,0:T(8,128)S(1)}, u32[]{:S(2)}, u32[]{:S(2)}) async-start(f32[16,40,128]{2,1,0:T(8,128)} %spread.11), calls=%async_computation.3 | async-start | bytes 655360 | tf_op jit(solution)/shard_map/all_to_all | solution.py:555
  116.8 2.9 collective-permute-start.9
  119.6 14.1 %collective-permute-done.9.refs_6_ = f32[256,128]{1,0:T(8,128)S(1)} collective-permute-done((f32[256,128]{1,0:T(8,128)}, f32[256,128]{1,0:T(8,128)S(1)}, u32[]{:S(2)}, u32[]{:S(2)}) %collective-permute-start.9) | collective-permute-done | bytes 131104 | tf_op jit(solution)/shard_map/ppermute | solution.py:502
  137.4 3.6 %local.5.refs_0_ = f32[64,32,128]{2,1,0:T(8,128)S(1)} custom-call(f32[64,32,128]{2,1,0:T(8,128)S(1)} %get-tuple-element.89.refs_0_.refs_1_, f32[64,32,128]{2,1,0:T(8,128)S(1)} %get-tuple-element.82.refs_0_.field.refs_1_, f32[48,32,128]{2,1,0:T(8,128)S(1)} %copy-done.18, f32[48,32,128]{2,1,0:T(8,128)} %collective-permute-done.6.refs_3_, ...), custom_call_target="tpu_custom_call" | custom-call | bytes 14000000 | tf_op jit(solution)/shard_map/local/pallas_call | solution.py:341
  144.2 6.9 %coupled.5 = (f32[64,32,128]{2,1,0:T(8,128)S(1)}, f32[48,32,128]{2,1,0:T(8,128)S(1)}, f32[48,32,128]{2,1,0:T(8,128)S(1)}, f32[8,6,32,128]{3,2,1,0:T(8,128)S(1)},...) custom-call(f32[64,32,128]{2,1,0:T(8,128)S(1)} %local.5.refs_0_, ...), custom_call_target="tpu_custom_call" | custom-call | bytes 21000000 | tf_op jit(solution)/shard_map/coupled/pallas_call | solution.py:423
  156.1 5.0 %all-to-all-start.4 = ((f32[8,40,128]{2,1,0:T(8,128)}), f32[8,40,128]{2,1,0:T(8,128)S(1)}, u32[]{:S(2)}, u32[]{:S(2)}) async-start(f32[8,40,128]{2,1,0:T(8,128)} %spread.12), calls=%async_computation.4 | async-start | bytes 327680 | tf_op jit(solution)/shard_map/all_to_all | solution.py:548
  161.0 3.6 %collective-permute-start.11 = (f32[48,32,128]{2,1,0:T(8,128)}, f32[48,32,128]{2,1,0:T(8,128)}, u32[]{:S(2)}, u32[]{:S(2)}) collective-permute-start(f32[48,32,128]{2,1,0:T(8,128)} %copy-done.48), channel_id=1, source_target_pairs={{0,112},{16,0},{32,16},{48,32},{64,48},{80,64},{96,80},{112,96},{1... | collective-permute-start | bytes 2359304 | tf_op jit(solution)/shard_map/ppermute | solution.py:502
  169.0 5.9 %all-to-all-start.5 = ((f32[16,40,128]{2,1,0:T(8,128)}), f32[16,40,128]{2,1,0:T(8,128)S(1)}, u32[]{:S(2)}, u32[]{:S(2)}) async-start(f32[16,40,128]{2,1,0:T(8,128)} %spread.13), calls=%async_computation.5 | async-start | bytes 655360 | tf_op jit(solution)/shard_map/all_to_all | solution.py:555
  177.8 12.9 %collective-permute-done.14.refs_6_ = f32[256,128]{1,0:T(8,128)S(1)} collective-permute-done((f32[256,128]{1,0:T(8,128)}, f32[256,128]{1,0:T(8,128)S(1)}, u32[]{:S(2)}, u32[]{:S(2)}) %collective-permute-start.14) | collective-permute-done | bytes 131104 | tf_op jit(solution)/shard_map/ppermute | solution.py:502
  194.3 3.6 %local.6.refs_0_ = f32[64,32,128]{2,1,0:T(8,128)S(1)} custom-call(f32[64,32,128]{2,1,0:T(8,128)S(1)} %get-tuple-element.101.refs_0_.refs_1_, f32[64,32,128]{2,1,0:T(8,128)S(1)} %get-tuple-element.89.refs_0_.refs_1_, f32[48,32,128]{2,1,0:T(8,128)S(1)} %copy-done.16, f32[48,32,128]{2,1,0:T(8,128)} %collective-permute-done.11.refs_3_, ...), custom_call_target="tpu_custom_call" | custom-call | bytes 14000000 | tf_op jit(solution)/shard_map/local/pallas_call | solution.py:341
  201.1 6.9 %coupled.6 = (f32[64,32,128]{2,1,0:T(8,128)S(1)}, f32[48,32,128]{2,1,0:T(8,128)S(1)}, f32[48,32,128]{2,1,0:T(8,128)S(1)}, f32[8,6,32,128]{3,2,1,0:T(8,128)S(1)},...) custom-call(f32[64,32,128]{2,1,0:T(8,128)S(1)} %local.6.refs_0_, ...), custom_call_target="tpu_custom_call" | custom-call | bytes 21000000 | tf_op jit(solution)/shard_map/coupled/pallas_call | solution.py:423
  213.1 5.0 %all-to-all-start.6 = ((f32[8,40,128]{2,1,0:T(8,128)}), f32[8,40,128]{2,1,0:T(8,128)S(1)}, u32[]{:S(2)}, u32[]{:S(2)}) async-start(f32[8,40,128]{2,1,0:T(8,128)} %spread.14), calls=%async_computation.6 | async-start | bytes 327680 | tf_op jit(solution)/shard_map/all_to_all | solution.py:548
  218.0 3.6 %collective-permute-start.16 = (f32[48,32,128]{2,1,0:T(8,128)}, f32[48,32,128]{2,1,0:T(8,128)}, u32[]{:S(2)}, u32[]{:S(2)}) collective-permute-start(f32[48,32,128]{2,1,0:T(8,128)} %copy-done.46), channel_id=1, source_target_pairs={{0,112},{16,0},{32,16},{48,32},{64,48},{80,64},{96,80},{112,96},{1... | collective-permute-start | bytes 2359304 | tf_op jit(solution)/shard_map/ppermute | solution.py:502
  226.0 5.0 %all-to-all-start.7 = ((f32[16,40,128]{2,1,0:T(8,128)}), f32[16,40,128]{2,1,0:T(8,128)S(1)}, u32[]{:S(2)}, u32[]{:S(2)}) async-start(f32[16,40,128]{2,1,0:T(8,128)} %spread.15), calls=%async_computation.7 | async-start | bytes 655360 | tf_op jit(solution)/shard_map/all_to_all | solution.py:555
  231.1 2.9 collective-permute-start.19
  233.9 12.9 %collective-permute-done.19.refs_6_ = f32[256,128]{1,0:T(8,128)S(1)} collective-permute-done((f32[256,128]{1,0:T(8,128)}, f32[256,128]{1,0:T(8,128)S(1)}, u32[]{:S(2)}, u32[]{:S(2)}) %collective-permute-start.19) | collective-permute-done | bytes 131104 | tf_op jit(solution)/shard_map/ppermute | solution.py:502
  249.7 3.6 %local.7.refs_0_ = f32[64,32,128]{2,1,0:T(8,128)S(1)} custom-call(f32[64,32,128]{2,1,0:T(8,128)S(1)} %copy-done.13, f32[64,32,128]{2,1,0:T(8,128)S(1)} %get-tuple-element.101.refs_0_.refs_1_, f32[48,32,128]{2,1,0:T(8,128)S(1)} %collective-permute-done.15.refs_2_, f32[48,32,128]{2,1,0:T(8,128)} %collective-permute-done.16.refs_3_, ...), custom_call_target="tpu_custom_call" | custom-call | bytes 14000000 | tf_op jit(solution)/shard_map/local/pallas_call | solution.py:341
  255.8 5.3 %coupled.7 = (f32[64,32,128]{2,1,0:T(8,128)S(1)}, f32[8,128]{1,0:T(8,128)S(1)}) custom-call(f32[64,32,128]{2,1,0:T(8,128)S(1)} %local.7.refs_0_, f32[16,40,128]{2,1,0:T(8,128)S(1)} %all-to-all-done.7.refs_1_, bf16[32,320,256]{2,1,0:T(8,128)(2,1)S(1)} %copy-done.4, f32[40,128]{1,0:T(8,128)S(1)} %copy-done.32), custom_call_target="tpu_custom_call" | custom-call | bytes 21000000 | tf_op jit(solution)/shard_map/coupled/pallas_call | solution.py:423
  261.2 21.3 %all_to_all.45.grams = f32[128,8,128]{2,1,0:T(8,128)S(1)} all-to-all(f32[128,8,128]{2,1,0:T(8,128)S(1)} %broadcast_in_dim.18), channel_id=1, replica_groups=mesh['gx'=8,'gy'=8,'gz'=2] {'gx','gy','gz'}, dimensions={0} | all-to-all | bytes 1048576 | tf_op jit(solution)/shard_map/all_to_all | solution.py:571
  282.5 7.4 %finish.1 = f32[32,64,128]{2,1,0:T(8,128)} custom-call(f32[64,32,128]{2,1,0:T(8,128)S(1)} %get-tuple-element.123.field, f32[128,8,128]{2,1,0:T(8,128)S(1)} %all_to_all.45.grams), custom_call_target="tpu_custom_call" | custom-call | tf_op jit(solution)/shard_map/finish/pallas_call | solution.py:483
  (165 shorter events, 82.6 us)
Async XLA Ops:
  5.0 43.0 %collective-permute-start.4 = (f32[256,128]{1,0:T(8,128)}, f32[256,128]{1,0:T(8,128)S(1)}, u32[]{:S(2)}, u32[]{:S(2)}) collective-permute-start(f32[256,128]{1,0:T(8,128)} %get-tuple-element.81), channel_id=1, source_target_pairs={{0,1},{1,0},{2,3},{3,2},{4,5},{5,4},{6,7},{7,6},{8,9},{9,8},{10,11... | collective-permute-start | bytes 393224 | tf_op jit(solution)/shard_map/ppermute | solution.py:502
  9.5 39.2 %collective-permute-start = (f32[48,32,128]{2,1,0:T(8,128)}, f32[48,32,128]{2,1,0:T(8,128)S(1)}, u32[]{:S(2)}, u32[]{:S(2)}) collective-permute-start(f32[48,32,128]{2,1,0:T(8,128)} %get-tuple-element.77), channel_id=1, source_target_pairs={{0,16},{16,32},{32,48},{48,64},{64,80},{80,96},{96,112},{112,0},{1... | collective-permute-start | bytes 2359304 | tf_op jit(solution)/shard_map/ppermute | solution.py:502
  10.8 37.9 %collective-permute-start.1 = (f32[48,32,128]{2,1,0:T(8,128)}, f32[48,32,128]{2,1,0:T(8,128)S(1)}, u32[]{:S(2)}, u32[]{:S(2)}) collective-permute-start(f32[48,32,128]{2,1,0:T(8,128)} %get-tuple-element.78), channel_id=1, source_target_pairs={{0,112},{16,0},{32,16},{48,32},{64,48},{80,64},{96,80},{112,96},{1... | collective-permute-start | bytes 2359304 | tf_op jit(solution)/shard_map/ppermute | solution.py:502
  13.1 37.0 %collective-permute-start.2 = (f32[8,6,32,128]{3,2,1,0:T(8,128)}, f32[8,6,32,128]{3,2,1,0:T(8,128)S(1)}, u32[]{:S(2)}, u32[]{:S(2)}) collective-permute-start(f32[8,6,32,128]{3,2,1,0:T(8,128)} %get-tuple-element.79), channel_id=1, source_target_pairs={{0,2},{2,4},{4,6},{6,8},{8,10},{10,12},{12,14},{14,0},{1,3},{3,5},... | collective-permute-start | bytes 2359304 | tf_op jit(solution)/shard_map/ppermute | solution.py:502
  15.7 35.6 %collective-permute-start.3 = (f32[8,6,32,128]{3,2,1,0:T(8,128)}, f32[8,6,32,128]{3,2,1,0:T(8,128)}, u32[]{:S(2)}, u32[]{:S(2)}) collective-permute-start(f32[8,6,32,128]{3,2,1,0:T(8,128)} %get-tuple-element.80), channel_id=1, source_target_pairs={{0,14},{2,0},{4,2},{6,4},{8,6},{10,8},{12,10},{14,12},{1,15},{3,1}... | collective-permute-start | bytes 2359304 | tf_op jit(solution)/shard_map/ppermute | solution.py:502
  54.0 18.3 %copy-start.7 = (bf16[256,128]{1,0:T(8,128)(2,1)S(1)}, bf16[256,128]{1,0:T(8,128)(2,1)}, u32[]{:S(2)}) copy-start(bf16[256,128]{1,0:T(8,128)(2,1)} %constant.92.clone.refs_8_.refs_9_) | copy-start | bytes 196612
  54.0 18.3 %copy-start.8 = (bf16[256,128]{1,0:T(8,128)(2,1)S(1)}, bf16[256,128]{1,0:T(8,128)(2,1)}, u32[]{:S(2)}) copy-start(bf16[256,128]{1,0:T(8,128)(2,1)} %constant.91.clone.refs_7_.refs_8_) | copy-start | bytes 196612
  54.0 18.3 %copy-start.25 = (f32[8,8,128]{2,1,0:T(8,128)S(1)}, f32[8,8,128]{2,1,0:T(8,128)}, u32[]{:S(2)}) copy-start(f32[8,8,128]{2,1,0:T(8,128)} %param.12) | copy-start | bytes 98308
  54.8 12.3 %all-to-all-start = ((f32[8,80,128]{2,1,0:T(8,128)}), f32[8,80,128]{2,1,0:T(8,128)S(1)}, u32[]{:S(2)}, u32[]{:S(2)}) async-start(f32[8,80,128]{2,1,0:T(8,128)} %spread.8), calls=%async_computation | async-start | bytes 655360 | tf_op jit(solution)/shard_map/all_to_all | solution.py:548
  68.6 14.8 %all-to-all-start.1 = ((f32[16,80,128]{2,1,0:T(8,128)}), f32[16,80,128]{2,1,0:T(8,128)S(1)}, u32[]{:S(2)}, u32[]{:S(2)}) async-start(f32[16,80,128]{2,1,0:T(8,128)} %spread.9), calls=%async_computation.1 | async-start | bytes 1310720 | tf_op jit(solution)/shard_map/all_to_all | solution.py:555
  99.1 11.9 %all-to-all-start.2 = ((f32[8,40,128]{2,1,0:T(8,128)}), f32[8,40,128]{2,1,0:T(8,128)S(1)}, u32[]{:S(2)}, u32[]{:S(2)}) async-start(f32[8,40,128]{2,1,0:T(8,128)} %spread.10), calls=%async_computation.2 | async-start | bytes 327680 | tf_op jit(solution)/shard_map/all_to_all | solution.py:548
  105.1 28.7 %collective-permute-start.5 = (f32[48,32,128]{2,1,0:T(8,128)}, f32[48,32,128]{2,1,0:T(8,128)S(1)}, u32[]{:S(2)}, u32[]{:S(2)}) collective-permute-start(f32[48,32,128]{2,1,0:T(8,128)} %copy-done.50), channel_id=1, source_target_pairs={{0,16},{16,32},{32,48},{48,64},{64,80},{80,96},{96,112},{112,0},{1... | collective-permute-start | bytes 2359304 | tf_op jit(solution)/shard_map/ppermute | solution.py:502
  105.5 29.1 %collective-permute-start.6 = (f32[48,32,128]{2,1,0:T(8,128)}, f32[48,32,128]{2,1,0:T(8,128)}, u32[]{:S(2)}, u32[]{:S(2)}) collective-permute-start(f32[48,32,128]{2,1,0:T(8,128)} %copy-done.47), channel_id=1, source_target_pairs={{0,112},{16,0},{32,16},{48,32},{64,48},{80,64},{96,80},{112,96},{1... | collective-permute-start | bytes 2359304 | tf_op jit(solution)/shard_map/ppermute | solution.py:502
  111.0 23.7 %collective-permute-start.7 = (f32[8,6,32,128]{3,2,1,0:T(8,128)}, f32[8,6,32,128]{3,2,1,0:T(8,128)}, u32[]{:S(2)}, u32[]{:S(2)}) collective-permute-start(f32[8,6,32,128]{3,2,1,0:T(8,128)} %copy-done.44), channel_id=1, source_target_pairs={{0,2},{2,4},{4,6},{6,8},{8,10},{10,12},{12,14},{14,0},{1,3},{3,5},... | collective-permute-start | bytes 2359304 | tf_op jit(solution)/shard_map/ppermute | solution.py:502
  111.8 22.9 %collective-permute-start.8 = (f32[8,6,32,128]{3,2,1,0:T(8,128)}, f32[8,6,32,128]{3,2,1,0:T(8,128)}, u32[]{:S(2)}, u32[]{:S(2)}) collective-permute-start(f32[8,6,32,128]{3,2,1,0:T(8,128)} %copy-done.41), channel_id=1, source_target_pairs={{0,14},{2,0},{4,2},{6,4},{8,6},{10,8},{12,10},{14,12},{1,15},{3,1}... | collective-permute-start | bytes 2359304 | tf_op jit(solution)/shard_map/ppermute | solution.py:502
  113.1 27.8 %all-to-all-start.3 = ((f32[16,40,128]{2,1,0:T(8,128)}), f32[16,40,128]{2,1,0:T(8,128)S(1)}, u32[]{:S(2)}, u32[]{:S(2)}) async-start(f32[16,40,128]{2,1,0:T(8,128)} %spread.11), calls=%async_computation.3 | async-start | bytes 655360 | tf_op jit(solution)/shard_map/all_to_all | solution.py:555
  116.8 17.0 %collective-permute-start.9 = (f32[256,128]{1,0:T(8,128)}, f32[256,128]{1,0:T(8,128)S(1)}, u32[]{:S(2)}, u32[]{:S(2)}) collective-permute-start(f32[256,128]{1,0:T(8,128)} %copy-done.53), channel_id=1, source_target_pairs={{0,1},{1,0},{2,3},{3,2},{4,5},{5,4},{6,7},{7,6},{8,9},{9,8},{10,11... | collective-permute-start | bytes 393224 | tf_op jit(solution)/shard_map/ppermute | solution.py:502
  156.1 10.8 %all-to-all-start.4 = ((f32[8,40,128]{2,1,0:T(8,128)}), f32[8,40,128]{2,1,0:T(8,128)S(1)}, u32[]{:S(2)}, u32[]{:S(2)}) async-start(f32[8,40,128]{2,1,0:T(8,128)} %spread.12), calls=%async_computation.4 | async-start | bytes 327680 | tf_op jit(solution)/shard_map/all_to_all | solution.py:548
  161.0 29.6 %collective-permute-start.10 = (f32[48,32,128]{2,1,0:T(8,128)}, f32[48,32,128]{2,1,0:T(8,128)S(1)}, u32[]{:S(2)}, u32[]{:S(2)}) collective-permute-start(f32[48,32,128]{2,1,0:T(8,128)} %copy-done.51), channel_id=1, source_target_pairs={{0,16},{16,32},{32,48},{48,64},{64,80},{80,96},{96,112},{112,0},{1... | collective-permute-start | bytes 2359304 | tf_op jit(solution)/shard_map/ppermute | solution.py:502
  161.0 30.5 %collective-permute-start.11 = (f32[48,32,128]{2,1,0:T(8,128)}, f32[48,32,128]{2,1,0:T(8,128)}, u32[]{:S(2)}, u32[]{:S(2)}) collective-permute-start(f32[48,32,128]{2,1,0:T(8,128)} %copy-done.48), channel_id=1, source_target_pairs={{0,112},{16,0},{32,16},{48,32},{64,48},{80,64},{96,80},{112,96},{1... | collective-permute-start | bytes 2359304 | tf_op jit(solution)/shard_map/ppermute | solution.py:502
  166.9 24.7 %collective-permute-start.12 = (f32[8,6,32,128]{3,2,1,0:T(8,128)}, f32[8,6,32,128]{3,2,1,0:T(8,128)}, u32[]{:S(2)}, u32[]{:S(2)}) collective-permute-start(f32[8,6,32,128]{3,2,1,0:T(8,128)} %copy-done.45), channel_id=1, source_target_pairs={{0,2},{2,4},{4,6},{6,8},{8,10},{10,12},{12,14},{14,0},{1,3},{3,5},... | collective-permute-start | bytes 2359304 | tf_op jit(solution)/shard_map/ppermute | solution.py:502
  167.7 23.9 %collective-permute-start.13 = (f32[8,6,32,128]{3,2,1,0:T(8,128)}, f32[8,6,32,128]{3,2,1,0:T(8,128)}, u32[]{:S(2)}, u32[]{:S(2)}) collective-permute-start(f32[8,6,32,128]{3,2,1,0:T(8,128)} %copy-done.42), channel_id=1, source_target_pairs={{0,14},{2,0},{4,2},{6,4},{8,6},{10,8},{12,10},{14,12},{1,15},{3,1}... | collective-permute-start | bytes 2359304 | tf_op jit(solution)/shard_map/ppermute | solution.py:502
  169.0 28.9 %all-to-all-start.5 = ((f32[16,40,128]{2,1,0:T(8,128)}), f32[16,40,128]{2,1,0:T(8,128)S(1)}, u32[]{:S(2)}, u32[]{:S(2)}) async-start(f32[16,40,128]{2,1,0:T(8,128)} %spread.13), calls=%async_computation.5 | async-start | bytes 655360 | tf_op jit(solution)/shard_map/all_to_all | solution.py:555
  174.9 15.7 %collective-permute-start.14 = (f32[256,128]{1,0:T(8,128)}, f32[256,128]{1,0:T(8,128)S(1)}, u32[]{:S(2)}, u32[]{:S(2)}) collective-permute-start(f32[256,128]{1,0:T(8,128)} %copy-done.54), channel_id=1, source_target_pairs={{0,1},{1,0},{2,3},{3,2},{4,5},{5,4},{6,7},{7,6},{8,9},{9,8},{10,11... | collective-permute-start | bytes 393224 | tf_op jit(solution)/shard_map/ppermute | solution.py:502
  211.4 35.5 %copy-start.12 = (f32[64,32,128]{2,1,0:T(8,128)}, f32[64,32,128]{2,1,0:T(8,128)S(1)}, u32[]{:S(2)}) copy-start(f32[64,32,128]{2,1,0:T(8,128)S(1)} %get-tuple-element.112.refs_0_) | copy-start | bytes 3145732
  213.1 10.9 %all-to-all-start.6 = ((f32[8,40,128]{2,1,0:T(8,128)}), f32[8,40,128]{2,1,0:T(8,128)S(1)}, u32[]{:S(2)}, u32[]{:S(2)}) async-start(f32[8,40,128]{2,1,0:T(8,128)} %spread.14), calls=%async_computation.6 | async-start | bytes 327680 | tf_op jit(solution)/shard_map/all_to_all | solution.py:548
  218.0 28.9 %collective-permute-start.15 = (f32[48,32,128]{2,1,0:T(8,128)}, f32[48,32,128]{2,1,0:T(8,128)S(1)}, u32[]{:S(2)}, u32[]{:S(2)}) collective-permute-start(f32[48,32,128]{2,1,0:T(8,128)} %copy-done.49), channel_id=1, source_target_pairs={{0,16},{16,32},{32,48},{48,64},{64,80},{80,96},{96,112},{112,0},{1... | collective-permute-start | bytes 2359304 | tf_op jit(solution)/shard_map/ppermute | solution.py:502
  218.0 28.9 %collective-permute-start.16 = (f32[48,32,128]{2,1,0:T(8,128)}, f32[48,32,128]{2,1,0:T(8,128)}, u32[]{:S(2)}, u32[]{:S(2)}) collective-permute-start(f32[48,32,128]{2,1,0:T(8,128)} %copy-done.46), channel_id=1, source_target_pairs={{0,112},{16,0},{32,16},{48,32},{64,48},{80,64},{96,80},{112,96},{1... | collective-permute-start | bytes 2359304 | tf_op jit(solution)/shard_map/ppermute | solution.py:502
  223.9 23.0 %collective-permute-start.17 = (f32[8,6,32,128]{3,2,1,0:T(8,128)}, f32[8,6,32,128]{3,2,1,0:T(8,128)}, u32[]{:S(2)}, u32[]{:S(2)}) collective-permute-start(f32[8,6,32,128]{3,2,1,0:T(8,128)} %copy-done.43), channel_id=1, source_target_pairs={{0,2},{2,4},{4,6},{6,8},{8,10},{10,12},{12,14},{14,0},{1,3},{3,5},... | collective-permute-start | bytes 2359304 | tf_op jit(solution)/shard_map/ppermute | solution.py:502
  224.7 22.2 %collective-permute-start.18 = (f32[8,6,32,128]{3,2,1,0:T(8,128)}, f32[8,6,32,128]{3,2,1,0:T(8,128)}, u32[]{:S(2)}, u32[]{:S(2)}) collective-permute-start(f32[8,6,32,128]{3,2,1,0:T(8,128)} %copy-done.40), channel_id=1, source_target_pairs={{0,14},{2,0},{4,2},{6,4},{8,6},{10,8},{12,10},{14,12},{1,15},{3,1}... | collective-permute-start | bytes 2359304 | tf_op jit(solution)/shard_map/ppermute | solution.py:502
  226.0 27.3 %all-to-all-start.7 = ((f32[16,40,128]{2,1,0:T(8,128)}), f32[16,40,128]{2,1,0:T(8,128)S(1)}, u32[]{:S(2)}, u32[]{:S(2)}) async-start(f32[16,40,128]{2,1,0:T(8,128)} %spread.15), calls=%async_computation.7 | async-start | bytes 655360 | tf_op jit(solution)/shard_map/all_to_all | solution.py:555
  231.1 15.8 %collective-permute-start.19 = (f32[256,128]{1,0:T(8,128)}, f32[256,128]{1,0:T(8,128)S(1)}, u32[]{:S(2)}, u32[]{:S(2)}) collective-permute-start(f32[256,128]{1,0:T(8,128)} %copy-done.52), channel_id=1, source_target_pairs={{0,1},{1,0},{2,3},{3,2},{4,5},{5,4},{6,7},{7,6},{8,9},{9,8},{10,11... | collective-permute-start | bytes 393224 | tf_op jit(solution)/shard_map/ppermute | solution.py:502
  (51 other events, 109.8 us)

commit v3 on v2

--- a/solution.py
+++ b/solution.py
@@ -35,13 +35,14 @@
 CH = NPJ * TGT
 GROUPS = ROWS // 4
 TOTAL = (2 * CH, 2 * NB)
+BATCH = 4
 ZROWS = GROUPS * 16
 LANES = 128
 F32 = jnp.float32
 BF16 = jnp.bfloat16
 NN = (((1,), (0,)), ((), ()))
 NT = (((1,), (1,)), ((), ()))
-VMEM_LIMIT = 32 * 1024 * 1024
+VMEM_LIMIT = 16 * 1024 * 1024
 
 
 def dot(a, b, dims=NN):
@@ -107,9 +108,12 @@
     return jnp.concatenate([turned[:8], turned[SZ - 8 :]], axis=0)
 
 
-def write_faces(field, x_low, x_high, y_low, y_high):
+def write_x_faces(field, x_low, x_high):
     x_low[...] = field[pl.ds(0, FACE)]
     x_high[...] = field[pl.ds(ROWS - FACE, FACE)]
+
+
+def write_y_faces(field, y_low, y_high):
     for x in range(SX):
         y_low[x] = field[pl.ds(x * SY, REACH)]
         y_high[x] = field[pl.ds(x * SY + SY - REACH, REACH)]
@@ -119,7 +123,7 @@
 X_FACE = jax.ShapeDtypeStruct((FACE, NB, SZ), F32)
 Y_FACE = jax.ShapeDtypeStruct((SX, REACH, NB, SZ), F32)
 Z_FACE = jax.ShapeDtypeStruct((ZROWS, LANES), F32)
-FACES = [X_FACE, X_FACE, Y_FACE, Y_FACE, Z_FACE]
+FRAME = jax.ShapeDtypeStruct((TGT, LANES), F32)
 
 
 def rearrange_kernel(src, field, x_low, x_high, y_low, y_high, z_face, in_sem):
@@ -130,7 +134,8 @@
         load.start()
     for load in loads:
         load.wait()
-    write_faces(field, x_low, x_high, y_low, y_high)
+    write_x_faces(field, x_low, x_high)
+    write_y_faces(field, y_low, y_high)
     for g in range(GROUPS):
         z_face[pl.ds(16 * g, 16), :] = z_faces([field[4 * g + i] for i in range(4)])
 
@@ -138,7 +143,7 @@
 def rearrange(orbitals):
     return pl.pallas_call(
         rearrange_kernel,
-        out_shape=[BLOCK] + FACES,
+        out_shape=[BLOCK, X_FACE, X_FACE, Y_FACE, Y_FACE, Z_FACE],
         in_specs=any_specs(1),
         out_specs=vmem_specs(6),
         scratch_shapes=[pltpu.SemaphoreType.DMA((ROWS,))],
@@ -148,12 +153,18 @@
     )(orbitals)
 
 
-def build_kernel(starts, keys, w0, w1, w2, w3, out, held, weights):
-    held[pl.ds(0, SLOTS // LANES), :] = keys[...]
+def build_kernel(starts, keys, w0, w1, w2, w3, out, held, weights, sem):
+    full = pl.ds(0, SLOTS // LANES)
+    loads = [pltpu.make_async_copy(keys, held.at[full], sem.at[NPJ])]
+    for j, w in enumerate((w0, w1, w2, w3)):
+        loads.append(pltpu.make_async_copy(w, weights.at[j, full], sem.at[j]))
+    for load in loads:
+        load.start()
     held[pl.ds(SLOTS // LANES, 8), :] = jnp.full((8, LANES), ROWS * SZ * 64, jnp.int32)
-    for j, w in enumerate((w0, w1, w2, w3)):
-        weights[j, pl.ds(0, SLOTS // LANES), :] = w[...]
+    for j in range(NPJ):
         weights[j, pl.ds(SLOTS // LANES, 8), :] = jnp.zeros((8, LANES), F32)
+    for load in loads:
+        load.wait()
     target_at = lax.broadcasted_iota(jnp.int32, (TGT, 2 * LANES), 0)
     z_at = lax.broadcasted_iota(jnp.int32, (SZ, 2 * LANES), 0)
 
@@ -172,35 +183,45 @@
         both = dot(jnp.concatenate([hi, lo], axis=0), place, NT)
         return both[:CH] + both[CH:]
 
-    @pl.loop(0, PAIRS)
-    def _(pair):
-        for parity in range(2):
-            row = 2 * pair + parity
-            low = starts[row]
-            high = starts[row + 1]
-            base = low // LANES
-            windows = (high - base * LANES + 2 * LANES - 1) // (2 * LANES)
-            total = window(row, base)
-
-            total = lax.fori_loop(
-                1, windows, lambda i, acc: acc + window(row, base + 2 * i), total
-            )
-            hi, lo = split2(total)
-            out[pair, :, pl.ds(parity * SZ, SZ)] = jnp.concatenate([hi, lo], axis=0)
+    @pl.loop(0, ROWS // BATCH)
+    def _(step):
+        first_row = step * BATCH
+        bases = [starts[first_row + i] // LANES for i in range(BATCH)]
+        for i in range(BATCH):
+            hi, lo = split2(window(first_row + i, bases[i]))
+            at = (step * (BATCH // 2) + i // 2, slice(None), pl.ds((i % 2) * SZ, SZ))
+            out[at] = jnp.concatenate([hi, lo], axis=0)
+
+        for i in range(BATCH):
+            row = first_row + i
+            windows = (starts[row + 1] - bases[i] * LANES + 2 * LANES - 1) // (2 * LANES)
+
+            @pl.when(windows > 1)
+            def _():
+                total = lax.fori_loop(
+                    0,
+                    windows,
+                    lambda k, acc: acc + window(row, bases[i] + 2 * k),
+                    jnp.zeros((CH, SZ), F32),
+                )
+                hi, lo = split2(total)
+                at = (step * (BATCH // 2) + i // 2, slice(None), pl.ds((i % 2) * SZ, SZ))
+                out[at] = jnp.concatenate([hi, lo], axis=0)
 
 
 def build(starts, keys, weights):
     return pl.pallas_call(
         build_kernel,
         out_shape=jax.ShapeDtypeStruct((PAIRS, 2 * CH, 2 * SZ), BF16),
-        in_specs=[pl.BlockSpec(memory_space=pltpu.SMEM)] + vmem_specs(5),
+        in_specs=[pl.BlockSpec(memory_space=pltpu.SMEM)] + any_specs(5),
         out_specs=pl.BlockSpec(memory_space=pltpu.VMEM),
         scratch_shapes=[
             pltpu.VMEM((SLOTS // LANES + 8, LANES), jnp.int32),
             pltpu.VMEM((NPJ, SLOTS // LANES + 8, LANES), F32),
+            pltpu.SemaphoreType.DMA((NPJ + 1,)),
         ],
         compiler_params=PARAMS,
-        cost_estimate=cost(15),
+        cost_estimate=cost(10),
         name="build",
     )(starts, keys, *weights)
 
@@ -215,7 +236,11 @@
     return jnp.concatenate([joined[j * TGT : (j + 1) * TGT] for j in range(NPJ)], axis=1)
 
 
-def first_kernel(field, mat, out, total):
+def partial_kernel(with_faces, *refs):
+    if with_faces:
+        field, mat, out, y_low, y_high, z_face, total = refs
+    else:
+        field, mat, out, total = refs
     total[...] = jnp.zeros_like(total)
 
     @pl.loop(0, SX)
@@ -226,20 +251,28 @@
             values = jnp.concatenate([field[at], field[at + 1]], axis=1)
             acc = acc + partial_of(mat[x * 4 + p], values)
         total[...] = acc
+        if with_faces:
+            for part in range(2):
+                z_face[pl.ds((2 * x + part) * 16, 16), :] = z_faces(
+                    [field[x * SY + 4 * part + i] for i in range(4)]
+                )
 
     out[...] = packed_partial(total[...])
-
-
-def first(field, mat):
+    if with_faces:
+        write_y_faces(field, y_low, y_high)
+
+
+def partial_part(with_faces, field, mat):
+    outs = [FRAME] + ([Y_FACE, Y_FACE, Z_FACE] if with_faces else [])
     return pl.pallas_call(
-        first_kernel,
-        out_shape=jax.ShapeDtypeStruct((TGT, LANES), F32),
+        functools.partial(partial_kernel, with_faces),
+        out_shape=outs,
         in_specs=vmem_specs(2),
-        out_specs=pl.BlockSpec(memory_space=pltpu.VMEM),
+        out_specs=vmem_specs(len(outs)),
         scratch_shapes=[pltpu.VMEM(TOTAL, F32)],
         compiler_params=PARAMS,
-        cost_estimate=cost(3),
-        name="first",
+        cost_estimate=cost(0.1),
+        name="partial",
     )(field, mat)
 
 
@@ -287,7 +320,7 @@
         in_specs=[pl.BlockSpec(memory_space=pltpu.SMEM)] + vmem_specs(1),
         out_specs=pl.BlockSpec(memory_space=pltpu.VMEM),
         compiler_params=PARAMS,
-        cost_estimate=cost(0.7),
+        cost_estimate=cost(0.1),
         name="spread",
     )(me, array)
 
@@ -344,23 +377,19 @@
         in_specs=vmem_specs(len(arrays)),
         out_specs=pl.BlockSpec(memory_space=pltpu.VMEM),
         compiler_params=PARAMS,
-        cost_estimate=cost(4),
+        cost_estimate=cost(0.1),
         name="local",
     )(*arrays)
 
 
 def coupled_kernel(first_step, last_step, *refs):
     if first_step:
-        (base, came, mat), refs = refs[:3], refs[3:]
+        base, came, mat, new, x_low, x_high, coupling, coef = refs
+    elif last_step:
+        base, came, mat, coupling, new, gram, total, coef = refs
+        total[...] = jnp.zeros_like(total)
     else:
-        (base, came, mat, coupling), refs = refs[:4], refs[4:]
-    if last_step:
-        new, gram, total, coef = refs
-    else:
-        (new, x_low, x_high, y_low, y_high, z_face, partial), refs = refs[:7], refs[7:]
-        if first_step:
-            coupling, refs = refs[0], refs[1:]
-        total, coef = refs
+        base, came, mat, coupling, new, x_low, x_high, coef = refs
     alpha = (1.0 if first_step else 2.0) / FILTER_HALF
     frame = came[0]
     for slot in range(1, came.shape[0]):
@@ -374,33 +403,26 @@
     coef_hi = turned.astype(BF16).astype(F32)
     coef[pl.ds(0, NB), :] = jnp.concatenate([coef_hi, coef_hi], axis=1).astype(BF16)
     coef[pl.ds(NB, NB), pl.ds(0, CH)] = (turned - coef_hi).astype(BF16)
-    total[...] = jnp.zeros_like(total)
 
     @pl.loop(0, SX)
     def _(x):
         c_hi = coef[pl.ds(0, NB), :]
         c_lo = coef[pl.ds(NB, NB), pl.ds(0, CH)]
-        acc = total[...]
-        for part in range(2):
+        if last_step:
+            acc = total[...]
+        for p in range(4):
+            pair_mat = mat[x * 4 + p]
+            added = dot(c_hi, pair_mat) + dot(c_lo, pair_mat[:CH])
             rows = []
-            for p in range(2):
-                pair_mat = mat[x * 4 + 2 * part + p]
-                added = dot(c_hi, pair_mat) + dot(c_lo, pair_mat[:CH])
-                for q in range(2):
-                    at = x * SY + 4 * part + 2 * p + q
-                    result = base[at] + added[:, q * SZ : (q + 1) * SZ]
-                    new[at] = result
-                    rows.append(result)
-            for p in range(2):
-                values = jnp.concatenate(rows[2 * p : 2 * p + 2], axis=1)
-                if last_step:
-                    joined = jnp.concatenate(split3(values), axis=0)
-                    acc = acc + dot(joined, joined, NT)
-                else:
-                    acc = acc + partial_of(mat[x * 4 + 2 * part + p], values)
-            if not last_step:
-                z_face[pl.ds((2 * x + part) * 16, 16), :] = z_faces(rows)
-        total[...] = acc
+            for q in range(2):
+                at = x * SY + 2 * p + q
+                rows.append(base[at] + added[:, q * SZ : (q + 1) * SZ])
+                new[at] = rows[q]
+            if last_step:
+                joined = jnp.concatenate(split3(jnp.concatenate(rows, axis=1)), axis=0)
+                acc = acc + dot(joined, joined, NT)
+        if last_step:
+            total[...] = acc
 
     if last_step:
         t = total[...]
@@ -408,26 +430,24 @@
         summed = summed + (t[NB : 2 * NB, :NB] + t[:NB, NB : 2 * NB]) + t[:NB, :NB]
         gram[...] = jnp.concatenate([summed[8 * q : 8 * q + 8] for q in range(4)], axis=1)
     else:
-        partial[...] = packed_partial(total[...])
-        write_faces(new, x_low, x_high, y_low, y_high)
+        write_x_faces(new, x_low, x_high)
 
 
 def coupled_part(first_step, last_step, *arrays):
-    frame = jax.ShapeDtypeStruct((TGT, LANES), F32)
+    scratch = [pltpu.VMEM((2 * NB, 2 * CH), BF16)]
     if last_step:
-        outs, total = [BLOCK, jax.ShapeDtypeStruct((8, LANES), F32)], (3 * NB, 3 * NB)
+        outs = [BLOCK, jax.ShapeDtypeStruct((8, LANES), F32)]
+        scratch = [pltpu.VMEM((3 * NB, 3 * NB), F32)] + scratch
     else:
-        outs, total = [BLOCK] + FACES + [frame], TOTAL
-        if first_step:
-            outs.append(frame)
+        outs = [BLOCK, X_FACE, X_FACE] + ([FRAME] if first_step else [])
     return pl.pallas_call(
         functools.partial(coupled_kernel, first_step, last_step),
         out_shape=outs,
         in_specs=vmem_specs(len(arrays)),
         out_specs=vmem_specs(len(outs)),
-        scratch_shapes=[pltpu.VMEM(total, F32), pltpu.VMEM((2 * NB, 2 * CH), BF16)],
+        scratch_shapes=scratch,
         compiler_params=PARAMS,
-        cost_estimate=cost(6),
+        cost_estimate=cost(0.1),
         name="coupled",
     )(*arrays)
 
@@ -541,16 +561,18 @@
             mat, field, x_left, x_right, y_left, y_right, faces = lax.optimization_barrier(
                 (mat, field, x_left, x_right, y_left, y_right, faces)
             )
-            partial = first(field, mat)
+            (partial,) = partial_part(False, field, mat)
             partial = jnp.concatenate([partial, coupling_frame], axis=0)
+        else:
+            partial, y_low, y_high, z_face = partial_part(True, field, mat)
         frames = 2 if start else 1
         sends = spread_call(spread_y_kernel, 8, frames, me_y, partial)
-        came = lax.all_to_all(sends, "gy", 0, 0)
         if not start:
-            came, y_low, y_high, z_face = lax.optimization_barrier((came, y_low, y_high, z_face))
+            sends, y_low, y_high, z_face = lax.optimization_barrier((sends, y_low, y_high, z_face))
             y_left = shift(y_high, "gy", 1)
             y_right = shift(y_low, "gy", -1)
             faces = shift(z_face, "gz", 1)
+        came = lax.all_to_all(sends, "gy", 0, 0)
         sends = spread_call(spread_xz_kernel, 16, frames, me_xz, came)
         came = lax.all_to_all(sends, ("gx", "gz"), 0, 0)
         base = local_part(
@@ -561,9 +583,9 @@
         if last:
             field, gram = outs
         else:
-            field, x_low, x_high, y_low, y_high, z_face, partial = outs[:7]
+            field, x_low, x_high = outs[:3]
             if start:
-                scales = (outs[7],)
+                scales = (outs[3],)
     axes = ("gx", "gy", "gz")
     devices = 1
     for axis in axes:

time: 293 us -> 267 us (0.911)
  blocking collectives: 21.3 us -> 54.4 us
  waiting for transfers between devices: 58.6 us -> 32.1 us
  starting transfers between devices: 71.7 us -> 58.2 us
  local copies, waits for them, and re-layouts: 50.1 us -> 39.3 us
  Pallas kernels: 77.1 us -> 69.7 us
    all_to_all x0 -> x3, blocking collectives: none -> 34.4 us  [local(): came = lax.all_to_all(sends, 'gy', 0, 0)]
    ppermute x20, waiting for transfers between devices: 40 us -> 20.8 us  [shift(): lax.ppermute(value, axis, [(i, (i + by) % count) for i in range(count)])]
    all_to_all x4 -> x1, starting transfers between devices: 21.1 us -> 5.49 us  [local(): came = lax.all_to_all(sends, 'gy', 0, 0)]
    pallas_call x2 -> x5, Pallas kernels: 6.44 us -> 18.2 us  [the longest x4 14.4 us: partial_part(): pl.pallas_call(functools.partial(partial_kernel, with_faces), out_shape=o...]
    unnamed x110 -> x88, local copies, waits for them, and re-layouts: 47.2 us -> 36.5 us
    pallas_call x4, Pallas kernels: 26 us -> 16.5 us  [coupled_part(): pl.pallas_call(functools.partial(coupled_kernel, first_step, last_step),...]
    pallas_call x1, Pallas kernels: 15.1 us -> 7.41 us  [build(): pl.pallas_call(build_kernel, out_shape=jax.ShapeDtypeStruct((PAIRS, 2 * C...]
    all_to_all x4 -> x1, waiting for transfers between devices: 14 us -> 7.06 us  [local(): came = lax.all_to_all(sends, 'gy', 0, 0)]
  transfers between devices with their start and end apart: 28 -> 25, of which waited for: 8 -> 5; matrix products, arithmetic and copies ran while one was open for 4% -> 5% of each run, Pallas kernels for 11% -> 10%
where the time goes in v3:
time: 267 us; the launch traced here: 265 us
  Pallas kernels  69.7 us (26%)
  starting transfers between devices  58.2 us (22%)
  blocking collectives  54.4 us (20%)
  local copies, waits for them, and re-layouts  39.3 us (15%)
  waiting for transfers between devices  32.1 us (12%)
  other arithmetic  10 us (4%)
    ppermute x20, starting transfers between devices, shift(): lax.ppermute(value, axis, [(i, (i + by) % count) for i in range(count)])  37.5 us
    unnamed x88, local copies, waits for them, and re-layouts  36.5 us
    all_to_all x3, blocking collectives, local(): came = lax.all_to_all(sends, 'gy', 0, 0)  34.4 us
    ppermute x20, waiting for transfers between devices, shift(): lax.ppermute(value, axis, [(i, (i + by) % count) for i in range(count)])  20.8 us
    all_to_all x1, blocking collectives, local(): lax.all_to_all(jnp.broadcast_to(gram[None], (devices,) + gram.shape), axe...  20.1 us
    pallas_call x4, Pallas kernels, coupled_part(): pl.pallas_call(functools.partial(coupled_kernel, first_step, last_step),...  16.5 us
    all_to_all x4, starting transfers between devices, local(): came = lax.all_to_all(sends, ('gx', 'gz'), 0, 0)  15.1 us
    pallas_call x4, Pallas kernels, partial_part(): pl.pallas_call(functools.partial(partial_kernel, with_faces), out_shape=o...  14.4 us
  transfers between devices with their start and end apart: 25, of which 5 were waited for; matrix products, arithmetic and copies ran while one was open for 5% of the time, Pallas kernels for 10%

profile of v3, /device:TPU:1, one launch (start us, length us, event | category | flops | bytes accessed | tf_op | source)
XLA Modules:
  0.0 265.0 jit_solution(15730294104195580379)
XLA Ops:
  1.2 3.8 %rearrange.1 = (f32[64,32,128]{2,1,0:T(8,128)S(1)}, f32[48,32,128]{2,1,0:T(8,128)}, f32[48,32,128]{2,1,0:T(8,128)}, f32[8,6,32,128]{3,2,1,0:T(8,128)}, f32[8,6,32,128]{3,2,1,0:T(8,128)}, /*index=5*/f32[256,128]{1,0:T(8,128)}) custom-call(f32[32,64,128]{2,1,0:T(8,128)S(1)} %bitcast.17), custom_call_target="tpu_custom_call" | custom-call | bytes 10500000 | tf_op jit(solution)/shard_map/rearrange/pallas_call | solution.py:144
  12.1 3.3 %collective-permute-start.4 = (f32[256,128]{1,0:T(8,128)}, f32[256,128]{1,0:T(8,128)S(1)}, u32[]{:S(2)}, u32[]{:S(2)}) collective-permute-start(f32[256,128]{1,0:T(8,128)} %get-tuple-element.81), channel_id=1, source_target_pairs={{0,1},{1,0},{2,3},{3,2},{4,5},{5,4},{6,7},{7,6},{8,9},{9,8},{10,11... | collective-permute-start | bytes 393224 | tf_op jit(solution)/shard_map/ppermute | solution.py:522
  20.3 7.3 %sort.33 = (s32[8192]{0:T(1024)}, f32[8192]{0:T(1024)}, f32[8192]{0:T(1024)}, f32[8192]{0:T(1024)}, f32[8192]{0:T(1024)}) sort(s32[8192]{0:T(1024)} %fusion.5, f32[8192]{0:T(1024)} %bitcast.29, f32[8192]{0:T(1024)} %bitcast.28, f32[8192]{0:T(1024)} %bitcast.30, f32[8192]{0:T(1024)} %bitcast.27), dimensions={0}, to_apply=%region_1.2 | sort | flops 106496 | bytes 327680 | tf_op jit(solution)/shard_map/sort | solution.py:544
  32.6 7.4 %build.1.refs_1_.refs_2_ = bf16[32,320,256]{2,1,0:T(8,128)(2,1)S(1)} custom-call(s32[65]{0:T(128)S(1)} %convert_reduce_fusion.starts, s32[64,128]{1,0:T(8,128)S(1)} %bitcast.22, f32[64,128]{1,0:T(8,128)S(1)} %bitcast.23, f32[64,128]{1,0:T(8,128)S(1)} %bitcast.24, f32[64,128]{1,0:T(8,128)S(1)} %bitcast.25, f32[64,128]{1,0:T(8,128)S(1)} %bitcast.26), custom_call_target="tpu_custom_call" | custom-call | bytes 35000000 | tf_op jit(solution)/shard_map/build/pallas_call | solution.py:213
  46.8 5.5 %all-to-all-start = ((f32[8,80,128]{2,1,0:T(8,128)}), f32[8,80,128]{2,1,0:T(8,128)S(1)}, u32[]{:S(2)}, u32[]{:S(2)}) async-start(f32[8,80,128]{2,1,0:T(8,128)} %spread.8), calls=%async_computation | async-start | bytes 655360 | tf_op jit(solution)/shard_map/all_to_all | solution.py:575
  52.3 7.1 %all-to-all-done.came = f32[8,80,128]{2,1,0:T(8,128)S(1)} async-done(((f32[8,80,128]{2,1,0:T(8,128)}), f32[8,80,128]{2,1,0:T(8,128)S(1)}, u32[]{:S(2)}, u32[]{:S(2)}) %all-to-all-start) | async-done | bytes 327712 | tf_op jit(solution)/shard_map/all_to_all | solution.py:575
  60.9 3.9 %all-to-all-start.1 = ((f32[16,80,128]{2,1,0:T(8,128)}), f32[16,80,128]{2,1,0:T(8,128)S(1)}, u32[]{:S(2)}, u32[]{:S(2)}) async-start(f32[16,80,128]{2,1,0:T(8,128)} %spread.9), calls=%async_computation.1 | async-start | bytes 1310720 | tf_op jit(solution)/shard_map/all_to_all | solution.py:577
  68.2 3.1 %local.4.refs_0_ = f32[64,32,128]{2,1,0:T(8,128)S(1)} custom-call(f32[64,32,128]{2,1,0:T(8,128)S(1)} %get-tuple-element.82.refs_0_.refs_1_, f32[48,32,128]{2,1,0:T(8,128)S(1)} %copy-done.21, f32[48,32,128]{2,1,0:T(8,128)S(1)} %copy-done.23, f32[8,6,32,128]{3,2,1,0:T(8,128)S(1)} %copy-done.25, f32[8,6,32,128]{3,2,1,0:T(8,128)} %collective-permute-done.3.refs_4_, ...), custom_call_target="tpu_custom_call" | custom-call | bytes 350000 | tf_op jit(solution)/shard_map/local/pallas_call | solution.py:374
  71.3 4.3 %all-to-all-done.1.refs_1_ = f32[16,80,128]{2,1,0:T(8,128)S(1)} async-done(((f32[16,80,128]{2,1,0:T(8,128)}), f32[16,80,128]{2,1,0:T(8,128)S(1)}, u32[]{:S(2)}, u32[]{:S(2)}) %all-to-all-start.1) | async-done | bytes 655392 | tf_op jit(solution)/shard_map/all_to_all | solution.py:577
  80.0 3.7 %coupled.4 = (f32[64,32,128]{2,1,0:T(8,128)S(1)}, f32[48,32,128]{2,1,0:T(8,128)}, f32[48,32,128]{2,1,0:T(8,128)}, f32[40,128]{1,0:T(8,128)S(1)}) custom-call(f32[64,32,128]{2,1,0:T(8,128)S(1)} %local.4.refs_0_, f32[16,80,128]{2,1,0:T(8,128)S(1)} %copy-done.7, bf16[32,320,256]{2,1,0:T(8,128)(2,1)S(1)} %copy-done.1), custom_call_target="tpu_custom_call" | custom-call | bytes 350000 | tf_op jit(solution)/shard_map/coupled/pallas_call | solution.py:443
  83.8 3.9 %partial.5 = (f32[40,128]{1,0:T(8,128)S(1)}, f32[8,6,32,128]{3,2,1,0:T(8,128)}, f32[8,6,32,128]{3,2,1,0:T(8,128)}, f32[256,128]{1,0:T(8,128)S(1)}) custom-call(f32[64,32,128]{2,1,0:T(8,128)S(1)} %get-tuple-element.89.refs_0_.refs_1_, bf16[32,320,256]{2,1,0:T(8,128)(2,1)S(1)} %copy-done.2), custom_call_target="tpu_custom_call" | custom-call | bytes 350000 | tf_op jit(solution)/shard_map/partial/pallas_call | solution.py:267
  87.7 3.2 %collective-permute-start.7 = (f32[8,6,32,128]{3,2,1,0:T(8,128)}, f32[8,6,32,128]{3,2,1,0:T(8,128)S(1)}, u32[]{:S(2)}, u32[]{:S(2)}) collective-permute-start(f32[8,6,32,128]{3,2,1,0:T(8,128)} %get-tuple-element.96), channel_id=1, source_target_pairs={{0,2},{2,4},{4,6},{6,8},{8,10},{10,12},{12,14},{14,0},{1,3},{3,5},... | collective-permute-start | bytes 2359304 | tf_op jit(solution)/shard_map/ppermute | solution.py:522
  91.3 3.2 %collective-permute-start.6 = (f32[48,32,128]{2,1,0:T(8,128)}, f32[48,32,128]{2,1,0:T(8,128)}, u32[]{:S(2)}, u32[]{:S(2)}) collective-permute-start(f32[48,32,128]{2,1,0:T(8,128)} %get-tuple-element.91), channel_id=1, source_target_pairs={{0,112},{16,0},{32,16},{48,32},{64,48},{80,64},{96,80},{112,96},{1... | collective-permute-start | bytes 2359304 | tf_op jit(solution)/shard_map/ppermute | solution.py:522
  94.5 11.7 %all_to_all.45.came = f32[8,40,128]{2,1,0:T(8,128)S(1)} all-to-all(f32[8,40,128]{2,1,0:T(8,128)S(1)} %spread.10), channel_id=1, replica_groups=mesh['gx'=8,'gy'=8,'gz'=2] {'gy'}, dimensions={0} | all-to-all | bytes 327680 | tf_op jit(solution)/shard_map/all_to_all | solution.py:575
  107.5 3.5 %all-to-all-start.3 = ((f32[16,40,128]{2,1,0:T(8,128)}), f32[16,40,128]{2,1,0:T(8,128)S(1)}, u32[]{:S(2)}, u32[]{:S(2)}) async-start(f32[16,40,128]{2,1,0:T(8,128)} %spread.11), calls=%async_computation.3 | async-start | bytes 655360 | tf_op jit(solution)/shard_map/all_to_all | solution.py:577
  113.8 6.1 %collective-permute-done.9.refs_6_ = f32[256,128]{1,0:T(8,128)S(1)} collective-permute-done((f32[256,128]{1,0:T(8,128)}, f32[256,128]{1,0:T(8,128)S(1)}, u32[]{:S(2)}, u32[]{:S(2)}) %collective-permute-start.9) | collective-permute-done | bytes 131104 | tf_op jit(solution)/shard_map/ppermute | solution.py:522
  123.6 3.5 %local.5.refs_0_ = f32[64,32,128]{2,1,0:T(8,128)S(1)} custom-call(f32[64,32,128]{2,1,0:T(8,128)S(1)} %get-tuple-element.89.refs_0_.refs_1_, f32[64,32,128]{2,1,0:T(8,128)S(1)} %get-tuple-element.82.refs_0_.refs_1_, f32[48,32,128]{2,1,0:T(8,128)} %collective-permute-done.5.refs_2_, f32[48,32,128]{2,1,0:T(8,128)} %collective-permute-done.6.refs_3_, ...), custom_call_target="tpu_custom_call" | custom-call | bytes 350000 | tf_op jit(solution)/shard_map/local/pallas_call | solution.py:374
  130.4 3.7 %coupled.5 = (f32[64,32,128]{2,1,0:T(8,128)S(1)}, f32[48,32,128]{2,1,0:T(8,128)}, f32[48,32,128]{2,1,0:T(8,128)}) custom-call(f32[64,32,128]{2,1,0:T(8,128)S(1)} %local.5.refs_0_, f32[16,40,128]{2,1,0:T(8,128)S(1)} %all-to-all-done.3.refs_1_, bf16[32,320,256]{2,1,0:T(8,128)(2,1)S(1)} %copy-done.3, f32[40,128]{1,0:T(8,128)S(1)} %copy-done.31), custom_call_target="tpu_custom_call" | custom-call | bytes 350000 | tf_op jit(solution)/shard_map/coupled/pallas_call | solution.py:443
  134.2 3.9 %partial.6 = (f32[40,128]{1,0:T(8,128)S(1)}, f32[8,6,32,128]{3,2,1,0:T(8,128)}, f32[8,6,32,128]{3,2,1,0:T(8,128)}, f32[256,128]{1,0:T(8,128)S(1)}) custom-call(f32[64,32,128]{2,1,0:T(8,128)S(1)} %get-tuple-element.101.refs_0_.refs_1_, bf16[32,320,256]{2,1,0:T(8,128)(2,1)S(1)} %copy-done.3), custom_call_target="tpu_custom_call" | custom-call | bytes 350000 | tf_op jit(solution)/shard_map/partial/pallas_call | solution.py:267
  144.1 11.6 %all_to_all.46.came = f32[8,40,128]{2,1,0:T(8,128)S(1)} all-to-all(f32[8,40,128]{2,1,0:T(8,128)S(1)} %spread.12), channel_id=1, replica_groups=mesh['gx'=8,'gy'=8,'gz'=2] {'gy'}, dimensions={0} | all-to-all | bytes 327680 | tf_op jit(solution)/shard_map/all_to_all | solution.py:575
  157.1 3.8 %all-to-all-start.5 = ((f32[16,40,128]{2,1,0:T(8,128)}), f32[16,40,128]{2,1,0:T(8,128)S(1)}, u32[]{:S(2)}, u32[]{:S(2)}) async-start(f32[16,40,128]{2,1,0:T(8,128)} %spread.13), calls=%async_computation.5 | async-start | bytes 655360 | tf_op jit(solution)/shard_map/all_to_all | solution.py:577
  163.8 7.2 %collective-permute-done.14.refs_6_ = f32[256,128]{1,0:T(8,128)S(1)} collective-permute-done((f32[256,128]{1,0:T(8,128)}, f32[256,128]{1,0:T(8,128)S(1)}, u32[]{:S(2)}, u32[]{:S(2)}) %collective-permute-start.14) | collective-permute-done | bytes 131104 | tf_op jit(solution)/shard_map/ppermute | solution.py:522
  174.7 3.5 %local.6.refs_0_ = f32[64,32,128]{2,1,0:T(8,128)S(1)} custom-call(f32[64,32,128]{2,1,0:T(8,128)S(1)} %get-tuple-element.101.refs_0_.refs_1_, f32[64,32,128]{2,1,0:T(8,128)S(1)} %get-tuple-element.89.refs_0_.refs_1_, f32[48,32,128]{2,1,0:T(8,128)} %collective-permute-done.10.refs_2_, f32[48,32,128]{2,1,0:T(8,128)} %collective-permute-done.11.refs_3_, ...), custom_call_target="tpu_custom_call" | custom-call | bytes 350000 | tf_op jit(solution)/shard_map/local/pallas_call | solution.py:374
  181.5 3.7 %coupled.6 = (f32[64,32,128]{2,1,0:T(8,128)S(1)}, f32[48,32,128]{2,1,0:T(8,128)}, f32[48,32,128]{2,1,0:T(8,128)}) custom-call(f32[64,32,128]{2,1,0:T(8,128)S(1)} %local.6.refs_0_, f32[16,40,128]{2,1,0:T(8,128)S(1)} %all-to-all-done.5.refs_1_, bf16[32,320,256]{2,1,0:T(8,128)(2,1)S(1)} %copy-done.4, f32[40,128]{1,0:T(8,128)S(1)} %copy-done.32), custom_call_target="tpu_custom_call" | custom-call | bytes 350000 | tf_op jit(solution)/shard_map/coupled/pallas_call | solution.py:443
  185.2 4.0 %partial.7 = (f32[40,128]{1,0:T(8,128)S(1)}, f32[8,6,32,128]{3,2,1,0:T(8,128)}, f32[8,6,32,128]{3,2,1,0:T(8,128)}, f32[256,128]{1,0:T(8,128)S(1)}) custom-call(f32[64,32,128]{2,1,0:T(8,128)S(1)} %get-tuple-element.112.refs_0_, bf16[32,320,256]{2,1,0:T(8,128)(2,1)S(1)} %copy-done.4), custom_call_target="tpu_custom_call" | custom-call | bytes 350000 | tf_op jit(solution)/shard_map/partial/pallas_call | solution.py:267
  195.0 11.0 %all_to_all.47.came = f32[8,40,128]{2,1,0:T(8,128)S(1)} all-to-all(f32[8,40,128]{2,1,0:T(8,128)S(1)} %spread.14), channel_id=1, replica_groups=mesh['gx'=8,'gy'=8,'gz'=2] {'gy'}, dimensions={0} | all-to-all | bytes 327680 | tf_op jit(solution)/shard_map/all_to_all | solution.py:575
  207.4 3.9 %all-to-all-start.7 = ((f32[16,40,128]{2,1,0:T(8,128)}), f32[16,40,128]{2,1,0:T(8,128)S(1)}, u32[]{:S(2)}, u32[]{:S(2)}) async-start(f32[16,40,128]{2,1,0:T(8,128)} %spread.15), calls=%async_computation.7 | async-start | bytes 655360 | tf_op jit(solution)/shard_map/all_to_all | solution.py:577
  214.2 7.3 %collective-permute-done.19.refs_6_ = f32[256,128]{1,0:T(8,128)S(1)} collective-permute-done((f32[256,128]{1,0:T(8,128)}, f32[256,128]{1,0:T(8,128)S(1)}, u32[]{:S(2)}, u32[]{:S(2)}) %collective-permute-start.19) | collective-permute-done | bytes 131104 | tf_op jit(solution)/shard_map/ppermute | solution.py:522
  225.2 3.5 %local.7.refs_0_ = f32[64,32,128]{2,1,0:T(8,128)S(1)} custom-call(f32[64,32,128]{2,1,0:T(8,128)S(1)} %get-tuple-element.112.refs_0_, f32[64,32,128]{2,1,0:T(8,128)S(1)} %get-tuple-element.101.refs_0_.refs_1_, f32[48,32,128]{2,1,0:T(8,128)} %collective-permute-done.15.refs_2_, f32[48,32,128]{2,1,0:T(8,128)} %collective-permute-done.16.refs_3_, ...), custom_call_target="tpu_custom_call" | custom-call | bytes 350000 | tf_op jit(solution)/shard_map/local/pallas_call | solution.py:374
  232.0 5.3 %coupled.7 = (f32[64,32,128]{2,1,0:T(8,128)S(1)}, f32[8,128]{1,0:T(8,128)S(1)}) custom-call(f32[64,32,128]{2,1,0:T(8,128)S(1)} %local.7.refs_0_, f32[16,40,128]{2,1,0:T(8,128)S(1)} %all-to-all-done.7.refs_1_, bf16[32,320,256]{2,1,0:T(8,128)(2,1)S(1)} %copy-done.5, f32[40,128]{1,0:T(8,128)S(1)} %copy-done.33), custom_call_target="tpu_custom_call" | custom-call | bytes 350000 | tf_op jit(solution)/shard_map/coupled/pallas_call | solution.py:443
  237.4 20.1 %all_to_all.48.grams = f32[128,8,128]{2,1,0:T(8,128)S(1)} all-to-all(f32[128,8,128]{2,1,0:T(8,128)S(1)} %broadcast_in_dim.18), channel_id=1, replica_groups=mesh['gx'=8,'gy'=8,'gz'=2] {'gx','gy','gz'}, dimensions={0} | all-to-all | bytes 1048576 | tf_op jit(solution)/shard_map/all_to_all | solution.py:593
  257.4 7.4 %finish.1 = f32[32,64,128]{2,1,0:T(8,128)} custom-call(f32[64,32,128]{2,1,0:T(8,128)S(1)} %get-tuple-element.123.field, f32[128,8,128]{2,1,0:T(8,128)S(1)} %all_to_all.48.grams), custom_call_target="tpu_custom_call" | custom-call | tf_op jit(solution)/shard_map/finish/pallas_call | solution.py:503
  (143 shorter events, 79.0 us)
Async XLA Ops:
  5.0 35.8 %collective-permute-start = (f32[48,32,128]{2,1,0:T(8,128)}, f32[48,32,128]{2,1,0:T(8,128)S(1)}, u32[]{:S(2)}, u32[]{:S(2)}) collective-permute-start(f32[48,32,128]{2,1,0:T(8,128)} %get-tuple-element.77), channel_id=1, source_target_pairs={{0,16},{16,32},{32,48},{48,64},{64,80},{80,96},{96,112},{112,0},{1... | collective-permute-start | bytes 2359304 | tf_op jit(solution)/shard_map/ppermute | solution.py:522
  7.2 33.6 %collective-permute-start.1 = (f32[48,32,128]{2,1,0:T(8,128)}, f32[48,32,128]{2,1,0:T(8,128)S(1)}, u32[]{:S(2)}, u32[]{:S(2)}) collective-permute-start(f32[48,32,128]{2,1,0:T(8,128)} %get-tuple-element.78), channel_id=1, source_target_pairs={{0,112},{16,0},{32,16},{48,32},{64,48},{80,64},{96,80},{112,96},{1... | collective-permute-start | bytes 2359304 | tf_op jit(solution)/shard_map/ppermute | solution.py:522
  10.1 32.0 %collective-permute-start.2 = (f32[8,6,32,128]{3,2,1,0:T(8,128)}, f32[8,6,32,128]{3,2,1,0:T(8,128)S(1)}, u32[]{:S(2)}, u32[]{:S(2)}) collective-permute-start(f32[8,6,32,128]{3,2,1,0:T(8,128)} %get-tuple-element.79), channel_id=1, source_target_pairs={{0,2},{2,4},{4,6},{6,8},{8,10},{10,12},{12,14},{14,0},{1,3},{3,5},... | collective-permute-start | bytes 2359304 | tf_op jit(solution)/shard_map/ppermute | solution.py:522
  12.1 31.1 %collective-permute-start.3 = (f32[8,6,32,128]{3,2,1,0:T(8,128)}, f32[8,6,32,128]{3,2,1,0:T(8,128)}, u32[]{:S(2)}, u32[]{:S(2)}) collective-permute-start(f32[8,6,32,128]{3,2,1,0:T(8,128)} %get-tuple-element.80), channel_id=1, source_target_pairs={{0,14},{2,0},{4,2},{6,4},{8,6},{10,8},{12,10},{14,12},{1,15},{3,1}... | collective-permute-start | bytes 2359304 | tf_op jit(solution)/shard_map/ppermute | solution.py:522
  12.1 27.9 %collective-permute-start.4 = (f32[256,128]{1,0:T(8,128)}, f32[256,128]{1,0:T(8,128)S(1)}, u32[]{:S(2)}, u32[]{:S(2)}) collective-permute-start(f32[256,128]{1,0:T(8,128)} %get-tuple-element.81), channel_id=1, source_target_pairs={{0,1},{1,0},{2,3},{3,2},{4,5},{5,4},{6,7},{7,6},{8,9},{9,8},{10,11... | collective-permute-start | bytes 393224 | tf_op jit(solution)/shard_map/ppermute | solution.py:522
  45.9 18.8 %copy-start.8 = (bf16[256,128]{1,0:T(8,128)(2,1)S(1)}, bf16[256,128]{1,0:T(8,128)(2,1)}, u32[]{:S(2)}) copy-start(bf16[256,128]{1,0:T(8,128)(2,1)} %constant.91.clone.refs_7_.refs_8_) | copy-start | bytes 196612
  45.9 18.8 %copy-start.9 = (bf16[256,128]{1,0:T(8,128)(2,1)S(1)}, bf16[256,128]{1,0:T(8,128)(2,1)}, u32[]{:S(2)}) copy-start(bf16[256,128]{1,0:T(8,128)(2,1)} %constant.92.clone.refs_8_.refs_9_) | copy-start | bytes 196612
  45.9 18.8 %copy-start.26 = (f32[8,8,128]{2,1,0:T(8,128)S(1)}, f32[8,8,128]{2,1,0:T(8,128)}, u32[]{:S(2)}) copy-start(f32[8,8,128]{2,1,0:T(8,128)} %param.12) | copy-start | bytes 98308
  45.9 18.8 %copy-start.35 = (f32[256,128]{1,0:T(8,128)S(1)}, f32[256,128]{1,0:T(8,128)}, u32[]{:S(2)}) copy-start(f32[256,128]{1,0:T(8,128)} %copy-done.34) | copy-start | bytes 393220
  46.8 12.6 %all-to-all-start = ((f32[8,80,128]{2,1,0:T(8,128)}), f32[8,80,128]{2,1,0:T(8,128)S(1)}, u32[]{:S(2)}, u32[]{:S(2)}) async-start(f32[8,80,128]{2,1,0:T(8,128)} %spread.8), calls=%async_computation | async-start | bytes 655360 | tf_op jit(solution)/shard_map/all_to_all | solution.py:575
  60.9 14.7 %all-to-all-start.1 = ((f32[16,80,128]{2,1,0:T(8,128)}), f32[16,80,128]{2,1,0:T(8,128)S(1)}, u32[]{:S(2)}, u32[]{:S(2)}) async-start(f32[16,80,128]{2,1,0:T(8,128)} %spread.9), calls=%async_computation.1 | async-start | bytes 1310720 | tf_op jit(solution)/shard_map/all_to_all | solution.py:577
  87.7 19.8 %copy-start.43 = (f32[256,128]{1,0:T(8,128)}, f32[256,128]{1,0:T(8,128)S(1)}, u32[]{:S(2)}) copy-start(f32[256,128]{1,0:T(8,128)S(1)} %get-tuple-element.98) | copy-start | bytes 393220
  87.7 32.2 %collective-permute-start.7 = (f32[8,6,32,128]{3,2,1,0:T(8,128)}, f32[8,6,32,128]{3,2,1,0:T(8,128)S(1)}, u32[]{:S(2)}, u32[]{:S(2)}) collective-permute-start(f32[8,6,32,128]{3,2,1,0:T(8,128)} %get-tuple-element.96), channel_id=1, source_target_pairs={{0,2},{2,4},{4,6},{6,8},{8,10},{10,12},{12,14},{14,0},{1,3},{3,5},... | collective-permute-start | bytes 2359304 | tf_op jit(solution)/shard_map/ppermute | solution.py:522
  90.9 30.0 %collective-permute-start.8 = (f32[8,6,32,128]{3,2,1,0:T(8,128)}, f32[8,6,32,128]{3,2,1,0:T(8,128)}, u32[]{:S(2)}, u32[]{:S(2)}) collective-permute-start(f32[8,6,32,128]{3,2,1,0:T(8,128)} %get-tuple-element.97), channel_id=1, source_target_pairs={{0,14},{2,0},{4,2},{6,4},{8,6},{10,8},{12,10},{14,12},{1,15},{3,1}... | collective-permute-start | bytes 2359304 | tf_op jit(solution)/shard_map/ppermute | solution.py:522
  90.9 30.0 %collective-permute-start.5 = (f32[48,32,128]{2,1,0:T(8,128)}, f32[48,32,128]{2,1,0:T(8,128)}, u32[]{:S(2)}, u32[]{:S(2)}) collective-permute-start(f32[48,32,128]{2,1,0:T(8,128)} %get-tuple-element.90), channel_id=1, source_target_pairs={{0,16},{16,32},{32,48},{48,64},{64,80},{80,96},{96,112},{112,0},{1... | collective-permute-start | bytes 2359304 | tf_op jit(solution)/shard_map/ppermute | solution.py:522
  91.3 29.6 %collective-permute-start.6 = (f32[48,32,128]{2,1,0:T(8,128)}, f32[48,32,128]{2,1,0:T(8,128)}, u32[]{:S(2)}, u32[]{:S(2)}) collective-permute-start(f32[48,32,128]{2,1,0:T(8,128)} %get-tuple-element.91), channel_id=1, source_target_pairs={{0,112},{16,0},{32,16},{48,32},{64,48},{80,64},{96,80},{112,96},{1... | collective-permute-start | bytes 2359304 | tf_op jit(solution)/shard_map/ppermute | solution.py:522
  107.5 19.7 %all-to-all-start.3 = ((f32[16,40,128]{2,1,0:T(8,128)}), f32[16,40,128]{2,1,0:T(8,128)S(1)}, u32[]{:S(2)}, u32[]{:S(2)}) async-start(f32[16,40,128]{2,1,0:T(8,128)} %spread.11), calls=%async_computation.3 | async-start | bytes 655360 | tf_op jit(solution)/shard_map/all_to_all | solution.py:577
  111.1 8.9 %collective-permute-start.9 = (f32[256,128]{1,0:T(8,128)}, f32[256,128]{1,0:T(8,128)S(1)}, u32[]{:S(2)}, u32[]{:S(2)}) collective-permute-start(f32[256,128]{1,0:T(8,128)} %copy-done.43), channel_id=1, source_target_pairs={{0,1},{1,0},{2,3},{3,2},{4,5},{5,4},{6,7},{7,6},{8,9},{9,8},{10,11... | collective-permute-start | bytes 393224 | tf_op jit(solution)/shard_map/ppermute | solution.py:522
  138.0 19.1 %copy-start.42 = (f32[256,128]{1,0:T(8,128)}, f32[256,128]{1,0:T(8,128)S(1)}, u32[]{:S(2)}) copy-start(f32[256,128]{1,0:T(8,128)S(1)} %get-tuple-element.110) | copy-start | bytes 393220
  138.1 33.0 %collective-permute-start.12 = (f32[8,6,32,128]{3,2,1,0:T(8,128)}, f32[8,6,32,128]{3,2,1,0:T(8,128)S(1)}, u32[]{:S(2)}, u32[]{:S(2)}) collective-permute-start(f32[8,6,32,128]{3,2,1,0:T(8,128)} %get-tuple-element.108), channel_id=1, source_target_pairs={{0,2},{2,4},{4,6},{6,8},{8,10},{10,12},{12,14},{14,0},{1,3},{3,5},... | collective-permute-start | bytes 2359304 | tf_op jit(solution)/shard_map/ppermute | solution.py:522
  140.6 31.4 %collective-permute-start.13 = (f32[8,6,32,128]{3,2,1,0:T(8,128)}, f32[8,6,32,128]{3,2,1,0:T(8,128)}, u32[]{:S(2)}, u32[]{:S(2)}) collective-permute-start(f32[8,6,32,128]{3,2,1,0:T(8,128)} %get-tuple-element.109), channel_id=1, source_target_pairs={{0,14},{2,0},{4,2},{6,4},{8,6},{10,8},{12,10},{14,12},{1,15},{3,1}... | collective-permute-start | bytes 2359304 | tf_op jit(solution)/shard_map/ppermute | solution.py:522
  140.6 31.4 %collective-permute-start.10 = (f32[48,32,128]{2,1,0:T(8,128)}, f32[48,32,128]{2,1,0:T(8,128)}, u32[]{:S(2)}, u32[]{:S(2)}) collective-permute-start(f32[48,32,128]{2,1,0:T(8,128)} %get-tuple-element.102), channel_id=1, source_target_pairs={{0,16},{16,32},{32,48},{48,64},{64,80},{80,96},{96,112},{112,0},{1... | collective-permute-start | bytes 2359304 | tf_op jit(solution)/shard_map/ppermute | solution.py:522
  142.0 30.0 %collective-permute-start.11 = (f32[48,32,128]{2,1,0:T(8,128)}, f32[48,32,128]{2,1,0:T(8,128)}, u32[]{:S(2)}, u32[]{:S(2)}) collective-permute-start(f32[48,32,128]{2,1,0:T(8,128)} %get-tuple-element.103), channel_id=1, source_target_pairs={{0,112},{16,0},{32,16},{48,32},{64,48},{80,64},{96,80},{112,96},{1... | collective-permute-start | bytes 2359304 | tf_op jit(solution)/shard_map/ppermute | solution.py:522
  157.1 21.1 %all-to-all-start.5 = ((f32[16,40,128]{2,1,0:T(8,128)}), f32[16,40,128]{2,1,0:T(8,128)S(1)}, u32[]{:S(2)}, u32[]{:S(2)}) async-start(f32[16,40,128]{2,1,0:T(8,128)} %spread.13), calls=%async_computation.5 | async-start | bytes 655360 | tf_op jit(solution)/shard_map/all_to_all | solution.py:577
  160.9 10.1 %collective-permute-start.14 = (f32[256,128]{1,0:T(8,128)}, f32[256,128]{1,0:T(8,128)S(1)}, u32[]{:S(2)}, u32[]{:S(2)}) collective-permute-start(f32[256,128]{1,0:T(8,128)} %copy-done.42), channel_id=1, source_target_pairs={{0,1},{1,0},{2,3},{3,2},{4,5},{5,4},{6,7},{7,6},{8,9},{9,8},{10,11... | collective-permute-start | bytes 393224 | tf_op jit(solution)/shard_map/ppermute | solution.py:522
  189.2 18.2 %copy-start.41 = (f32[256,128]{1,0:T(8,128)}, f32[256,128]{1,0:T(8,128)S(1)}, u32[]{:S(2)}) copy-start(f32[256,128]{1,0:T(8,128)S(1)} %get-tuple-element.121) | copy-start | bytes 393220
  189.2 32.4 %collective-permute-start.17 = (f32[8,6,32,128]{3,2,1,0:T(8,128)}, f32[8,6,32,128]{3,2,1,0:T(8,128)S(1)}, u32[]{:S(2)}, u32[]{:S(2)}) collective-permute-start(f32[8,6,32,128]{3,2,1,0:T(8,128)} %get-tuple-element.119), channel_id=1, source_target_pairs={{0,2},{2,4},{4,6},{6,8},{8,10},{10,12},{12,14},{14,0},{1,3},{3,5},... | collective-permute-start | bytes 2359304 | tf_op jit(solution)/shard_map/ppermute | solution.py:522
  191.5 31.0 %collective-permute-start.18 = (f32[8,6,32,128]{3,2,1,0:T(8,128)}, f32[8,6,32,128]{3,2,1,0:T(8,128)}, u32[]{:S(2)}, u32[]{:S(2)}) collective-permute-start(f32[8,6,32,128]{3,2,1,0:T(8,128)} %get-tuple-element.120), channel_id=1, source_target_pairs={{0,14},{2,0},{4,2},{6,4},{8,6},{10,8},{12,10},{14,12},{1,15},{3,1}... | collective-permute-start | bytes 2359304 | tf_op jit(solution)/shard_map/ppermute | solution.py:522
  191.5 31.0 %collective-permute-start.15 = (f32[48,32,128]{2,1,0:T(8,128)}, f32[48,32,128]{2,1,0:T(8,128)}, u32[]{:S(2)}, u32[]{:S(2)}) collective-permute-start(f32[48,32,128]{2,1,0:T(8,128)} %get-tuple-element.113), channel_id=1, source_target_pairs={{0,16},{16,32},{32,48},{48,64},{64,80},{80,96},{96,112},{112,0},{1... | collective-permute-start | bytes 2359304 | tf_op jit(solution)/shard_map/ppermute | solution.py:522
  192.8 29.7 %collective-permute-start.16 = (f32[48,32,128]{2,1,0:T(8,128)}, f32[48,32,128]{2,1,0:T(8,128)}, u32[]{:S(2)}, u32[]{:S(2)}) collective-permute-start(f32[48,32,128]{2,1,0:T(8,128)} %get-tuple-element.114), channel_id=1, source_target_pairs={{0,112},{16,0},{32,16},{48,32},{64,48},{80,64},{96,80},{112,96},{1... | collective-permute-start | bytes 2359304 | tf_op jit(solution)/shard_map/ppermute | solution.py:522
  207.4 21.4 %all-to-all-start.7 = ((f32[16,40,128]{2,1,0:T(8,128)}), f32[16,40,128]{2,1,0:T(8,128)S(1)}, u32[]{:S(2)}, u32[]{:S(2)}) async-start(f32[16,40,128]{2,1,0:T(8,128)} %spread.15), calls=%async_computation.7 | async-start | bytes 655360 | tf_op jit(solution)/shard_map/all_to_all | solution.py:577
  211.4 10.2 %collective-permute-start.19 = (f32[256,128]{1,0:T(8,128)}, f32[256,128]{1,0:T(8,128)S(1)}, u32[]{:S(2)}, u32[]{:S(2)}) collective-permute-start(f32[256,128]{1,0:T(8,128)} %copy-done.41), channel_id=1, source_target_pairs={{0,1},{1,0},{2,3},{3,2},{4,5},{5,4},{6,7},{7,6},{8,9},{9,8},{10,11... | collective-permute-start | bytes 393224 | tf_op jit(solution)/shard_map/ppermute | solution.py:522
  (37 other events, 55.2 us)

commit v4 on v3

--- a/solution.py
+++ b/solution.py
@@ -42,7 +42,7 @@
 BF16 = jnp.bfloat16
 NN = (((1,), (0,)), ((), ()))
 NT = (((1,), (1,)), ((), ()))
-VMEM_LIMIT = 16 * 1024 * 1024
+VMEM_LIMIT = 60 * 1024 * 1024
 
 
 def dot(a, b, dims=NN):
@@ -97,26 +97,12 @@
 
 
 PARAMS = pltpu.CompilerParams(vmem_limit_bytes=VMEM_LIMIT)
-
-
-def cost(us):
-    return pl.CostEstimate(flops=0, bytes_accessed=int(us * 3.5e6), transcendentals=0)
+SMALL = pltpu.CompilerParams(vmem_limit_bytes=52 * 1024 * 1024)
 
 
 def z_faces(rows):
     turned = jnp.concatenate(rows, axis=0).T
     return jnp.concatenate([turned[:8], turned[SZ - 8 :]], axis=0)
-
-
-def write_x_faces(field, x_low, x_high):
-    x_low[...] = field[pl.ds(0, FACE)]
-    x_high[...] = field[pl.ds(ROWS - FACE, FACE)]
-
-
-def write_y_faces(field, y_low, y_high):
-    for x in range(SX):
-        y_low[x] = field[pl.ds(x * SY, REACH)]
-        y_high[x] = field[pl.ds(x * SY + SY - REACH, REACH)]
 
 
 BLOCK = jax.ShapeDtypeStruct((ROWS, NB, SZ), F32)
@@ -126,18 +112,73 @@
 FRAME = jax.ShapeDtypeStruct((TGT, LANES), F32)
 
 
-def rearrange_kernel(src, field, x_low, x_high, y_low, y_high, z_face, in_sem):
-    loads = [
-        pltpu.make_async_copy(src.at[:, row, :], field.at[row], in_sem.at[row]) for row in range(ROWS)
+def face_copies(x, field, x_low, x_high, y_low, y_high, sem):
+    copies = [
+        pltpu.make_async_copy(field.at[pl.ds(x * SY, REACH)], y_low.at[x], sem.at[0, x]),
+        pltpu.make_async_copy(field.at[pl.ds(x * SY + SY - REACH, REACH)], y_high.at[x], sem.at[1, x]),
     ]
-    for load in loads:
-        load.start()
-    for load in loads:
-        load.wait()
-    write_x_faces(field, x_low, x_high)
-    write_y_faces(field, y_low, y_high)
-    for g in range(GROUPS):
-        z_face[pl.ds(16 * g, 16), :] = z_faces([field[4 * g + i] for i in range(4)])
+    return copies
+
+
+def low_copy(x, field, x_low, sem):
+    rows = pl.ds(x * SY, SY)
+    return pltpu.make_async_copy(field.at[rows], x_low.at[rows], sem.at[2, x])
+
+
+def high_copy(x, field, x_high, sem):
+    to = pl.ds((x - (SX - REACH)) * SY, SY)
+    return pltpu.make_async_copy(field.at[pl.ds(x * SY, SY)], x_high.at[to], sem.at[3, x])
+
+
+def block_copy(x, field, out, sem):
+    rows = pl.ds(x * SY, SY)
+    return pltpu.make_async_copy(field.at[rows], out.at[rows], sem.at[4, x])
+
+
+def start_faces(x, field, outs, sem):
+    new, x_low, x_high, y_low, y_high = outs
+    for copy in face_copies(x, field, x_low, x_high, y_low, y_high, sem):
+        copy.start()
+    block_copy(x, field, new, sem).start()
+
+    @pl.when(x < REACH)
+    def _():
+        low_copy(x, field, x_low, sem).start()
+
+    @pl.when(x >= SX - REACH)
+    def _():
+        high_copy(x, field, x_high, sem).start()
+
+
+def wait_faces(field, outs, sem):
+    new, x_low, x_high, y_low, y_high = outs
+    for x in range(SX):
+        for copy in face_copies(x, field, x_low, x_high, y_low, y_high, sem):
+            copy.wait()
+        block_copy(x, field, new, sem).wait()
+        if x < REACH:
+            low_copy(x, field, x_low, sem).wait()
+        if x >= SX - REACH:
+            high_copy(x, field, x_high, sem).wait()
+
+
+def rearrange_kernel(src, *refs):
+    outs, (z_face, field, in_sem, out_sem) = refs[:5], refs[5:]
+    for row in range(ROWS):
+        pltpu.make_async_copy(src.at[:, row, :], field.at[row], in_sem.at[row]).start()
+
+    @pl.loop(0, SX)
+    def _(x):
+        for y in range(SY):
+            row = x * SY + y
+            pltpu.make_async_copy(src.at[:, row, :], field.at[row], in_sem.at[row]).wait()
+        start_faces(x, field, outs, out_sem)
+        for part in range(2):
+            z_face[pl.ds((2 * x + part) * 16, 16), :] = z_faces(
+                [field[x * SY + 4 * part + i] for i in range(4)]
+            )
+
+    wait_faces(field, outs, out_sem)
 
 
 def rearrange(orbitals):
@@ -145,15 +186,18 @@
         rearrange_kernel,
         out_shape=[BLOCK, X_FACE, X_FACE, Y_FACE, Y_FACE, Z_FACE],
         in_specs=any_specs(1),
-        out_specs=vmem_specs(6),
-        scratch_shapes=[pltpu.SemaphoreType.DMA((ROWS,))],
+        out_specs=any_specs(5) + vmem_specs(1),
+        scratch_shapes=[
+            pltpu.VMEM((ROWS, NB, SZ), F32),
+            pltpu.SemaphoreType.DMA((ROWS,)),
+            pltpu.SemaphoreType.DMA((5, SX)),
+        ],
         compiler_params=PARAMS,
-        cost_estimate=cost(3),
         name="rearrange",
     )(orbitals)
 
 
-def build_kernel(starts, keys, w0, w1, w2, w3, out, held, weights, sem):
+def build_kernel(starts, keys, w0, w1, w2, w3, out_hbm, held, weights, out, sem, out_sem):
     full = pl.ds(0, SLOTS // LANES)
     loads = [pltpu.make_async_copy(keys, held.at[full], sem.at[NPJ])]
     for j, w in enumerate((w0, w1, w2, w3)):
@@ -183,6 +227,10 @@
         both = dot(jnp.concatenate([hi, lo], axis=0), place, NT)
         return both[:CH] + both[CH:]
 
+    def store_of(step):
+        done = pl.ds(step * (BATCH // 2), BATCH // 2)
+        return pltpu.make_async_copy(out.at[done], out_hbm.at[done], out_sem.at[step])
+
     @pl.loop(0, ROWS // BATCH)
     def _(step):
         first_row = step * BATCH
@@ -208,20 +256,26 @@
                 at = (step * (BATCH // 2) + i // 2, slice(None), pl.ds((i % 2) * SZ, SZ))
                 out[at] = jnp.concatenate([hi, lo], axis=0)
 
+        store_of(step).start()
+
+    for step in range(ROWS // BATCH):
+        store_of(step).wait()
+
 
 def build(starts, keys, weights):
     return pl.pallas_call(
         build_kernel,
         out_shape=jax.ShapeDtypeStruct((PAIRS, 2 * CH, 2 * SZ), BF16),
         in_specs=[pl.BlockSpec(memory_space=pltpu.SMEM)] + any_specs(5),
-        out_specs=pl.BlockSpec(memory_space=pltpu.VMEM),
+        out_specs=pl.BlockSpec(memory_space=pl.ANY),
         scratch_shapes=[
             pltpu.VMEM((SLOTS // LANES + 8, LANES), jnp.int32),
             pltpu.VMEM((NPJ, SLOTS // LANES + 8, LANES), F32),
+            pltpu.VMEM((PAIRS, 2 * CH, 2 * SZ), BF16),
             pltpu.SemaphoreType.DMA((NPJ + 1,)),
+            pltpu.SemaphoreType.DMA((ROWS // BATCH,)),
         ],
         compiler_params=PARAMS,
-        cost_estimate=cost(10),
         name="build",
     )(starts, keys, *weights)
 
@@ -234,46 +288,6 @@
 def packed_partial(total):
     joined = total[:CH, :NB] + total[:CH, NB:] + total[CH:, :NB]
     return jnp.concatenate([joined[j * TGT : (j + 1) * TGT] for j in range(NPJ)], axis=1)
-
-
-def partial_kernel(with_faces, *refs):
-    if with_faces:
-        field, mat, out, y_low, y_high, z_face, total = refs
-    else:
-        field, mat, out, total = refs
-    total[...] = jnp.zeros_like(total)
-
-    @pl.loop(0, SX)
-    def _(x):
-        acc = total[...]
-        for p in range(4):
-            at = x * SY + 2 * p
-            values = jnp.concatenate([field[at], field[at + 1]], axis=1)
-            acc = acc + partial_of(mat[x * 4 + p], values)
-        total[...] = acc
-        if with_faces:
-            for part in range(2):
-                z_face[pl.ds((2 * x + part) * 16, 16), :] = z_faces(
-                    [field[x * SY + 4 * part + i] for i in range(4)]
-                )
-
-    out[...] = packed_partial(total[...])
-    if with_faces:
-        write_y_faces(field, y_low, y_high)
-
-
-def partial_part(with_faces, field, mat):
-    outs = [FRAME] + ([Y_FACE, Y_FACE, Z_FACE] if with_faces else [])
-    return pl.pallas_call(
-        functools.partial(partial_kernel, with_faces),
-        out_shape=outs,
-        in_specs=vmem_specs(2),
-        out_specs=vmem_specs(len(outs)),
-        scratch_shapes=[pltpu.VMEM(TOTAL, F32)],
-        compiler_params=PARAMS,
-        cost_estimate=cost(0.1),
-        name="partial",
-    )(field, mat)
 
 
 def pieces(frame, stride):
@@ -285,13 +299,60 @@
         yield distance, jnp.where(valid, moved, 0.0)
 
 
-def spread_y_kernel(frames, me, mine, out):
-    for f in range(frames):
-        at = pl.ds(f * TGT, TGT)
-        for distance in (-3, 3, 4):
-            out[(me[0] + distance + 8) % 8, at, :] = jnp.zeros((TGT, LANES), F32)
-        for distance, piece in pieces(mine[at, :], 4):
-            out[(me[0] + distance + 8) % 8, at, :] = piece
+def spread_y(frame, me, out, at):
+    for distance in (-3, 3, 4):
+        out[(me[0] + distance + 8) % 8, at, :] = jnp.zeros((TGT, LANES), F32)
+    for distance, piece in pieces(frame, 4):
+        out[(me[0] + distance + 8) % 8, at, :] = piece
+
+
+def first_kernel(me, field, mat, own, out, field_v, mat_v, total, in_sem, mat_sem):
+    def load(x):
+        rows = pl.ds(x * SY, SY)
+        some = pl.ds(x * 4, 4)
+        return [
+            pltpu.make_async_copy(field.at[rows], field_v.at[rows], in_sem.at[x]),
+            pltpu.make_async_copy(mat.at[some], mat_v.at[some], mat_sem.at[x]),
+        ]
+
+    for x in range(SX):
+        for copy in load(x):
+            copy.start()
+    row = lax.broadcasted_iota(jnp.int32, (TGT, LANES), 0)
+    couplings = jnp.where(row == 16, own[pl.ds(0, 1), :], jnp.where(row == 17, own[pl.ds(1, 1), :], 0.0))
+    spread_y(couplings, me, out, pl.ds(TGT, TGT))
+    total[...] = jnp.zeros_like(total)
+
+    @pl.loop(0, SX)
+    def _(x):
+        for copy in load(x):
+            copy.wait()
+        acc = total[...]
+        for p in range(4):
+            at = x * SY + 2 * p
+            values = jnp.concatenate([field_v[at], field_v[at + 1]], axis=1)
+            acc = acc + partial_of(mat_v[x * 4 + p], values)
+        total[...] = acc
+
+    spread_y(packed_partial(total[...]), me, out, pl.ds(0, TGT))
+
+
+def first(me, field, mat, own):
+    return pl.pallas_call(
+        first_kernel,
+        out_shape=jax.ShapeDtypeStruct((8, 2 * TGT, LANES), F32),
+        in_specs=[pl.BlockSpec(memory_space=pltpu.SMEM)] + any_specs(2) + vmem_specs(1),
+        out_specs=pl.BlockSpec(memory_space=pltpu.VMEM),
+        scratch_shapes=[
+            pltpu.VMEM((ROWS, NB, SZ), F32),
+            pltpu.VMEM((PAIRS, 2 * CH, 2 * SZ), BF16),
+            pltpu.VMEM(TOTAL, F32),
+            pltpu.SemaphoreType.DMA((SX,)),
+            pltpu.SemaphoreType.DMA((SX,)),
+        ],
+        compiler_params=PARAMS,
+        name="first",
+    )(me, field, mat, own)
 
 
 def spread_xz_kernel(frames, me, came, out):
@@ -313,40 +374,32 @@
             out[slot + 1 - me[1], at, :] = swapped
 
 
-def spread_call(kernel, slots, frames, me, array):
+def spread_xz(frames, me, array):
     return pl.pallas_call(
-        functools.partial(kernel, frames),
-        out_shape=jax.ShapeDtypeStruct((slots, frames * TGT, LANES), F32),
+        functools.partial(spread_xz_kernel, frames),
+        out_shape=jax.ShapeDtypeStruct((16, frames * TGT, LANES), F32),
         in_specs=[pl.BlockSpec(memory_space=pltpu.SMEM)] + vmem_specs(1),
         out_specs=pl.BlockSpec(memory_space=pltpu.VMEM),
-        compiler_params=PARAMS,
-        cost_estimate=cost(0.1),
+        compiler_params=SMALL,
         name="spread",
     )(me, array)
 
 
 def local_kernel(first_step, *refs):
-    if first_step:
-        field, x_left, x_right, y_left, y_right, faces, potential, first_z, second_z, out = refs
-        previous = None
-    else:
-        field, previous, x_left, x_right, y_left, y_right, faces, potential, first_z, second_z, out = refs
+    count = 9 if first_step else 10
+    inputs, out, held, made, in_sem, out_sem = refs[:count], refs[count], refs[count + 1 : -3], *refs[-3:]
+    loads = [pltpu.make_async_copy(inputs[i], held[i], in_sem.at[i]) for i in range(count)]
+    for load in loads:
+        load.start()
+    field, faces, potential, first_z, second_z, x_left, x_right, y_left, y_right = held[:9]
     alpha = (1.0 if first_step else 2.0) / FILTER_HALF
     half = [0.0] + [-0.5 * c for c in STENCIL[1:]]
     diagonal = -1.5 * STENCIL[0] - FILTER_CENTRE
-
-    def at(x, y):
-        if x < 0:
-            return x_left[(x + REACH) * SY + y]
-        if x >= SX:
-            return x_right[(x - SX) * SY + y]
-        if y < 0:
-            return y_left[x, y + REACH]
-        if y >= SY:
-            return y_right[x, y - SY]
-        return field[x * SY + y]
-
-    for g in range(GROUPS):
+    for load in loads[:5]:
+        load.wait()
+
+    @pl.loop(0, GROUPS)
+    def _(g):
         rows = [field[4 * g + i] for i in range(4)]
         hi, lo = split2(jnp.concatenate(rows, axis=0))
         face = faces[pl.ds(g * 16, 16), :]
@@ -358,42 +411,91 @@
             jnp.concatenate([hi, side], axis=1), second_z[...]
         )
         for i in range(4):
-            x, y = divmod(4 * g + i, SY)
-            summed = along_z[i * NB : (i + 1) * NB]
+            own = (potential[pl.ds(4 * g + i, 1), :] + diagonal) * rows[i]
+            made[4 * g + i] = along_z[i * NB : (i + 1) * NB] + own
+
+    for load in loads[5:]:
+        load.wait()
+
+    def at(x, y):
+        if x < 0:
+            return x_left[(x + REACH) * SY + y]
+        if x >= SX:
+            return x_right[(x - SX) * SY + y]
+        if y < 0:
+            return y_left[x, y + REACH]
+        if y >= SY:
+            return y_right[x, y - SY]
+        return field[x * SY + y]
+
+    stores = []
+    for x in range(SX):
+        for y in range(SY):
+            row = x * SY + y
+            summed = made[row]
             for m in range(1, REACH + 1):
                 around = (at(x + m, y) + at(x - m, y)) + (at(x, y + m) + at(x, y - m))
                 summed = summed + half[m] * around
-            summed = summed + (potential[pl.ds(4 * g + i, 1), :] + diagonal) * rows[i]
             result = alpha * summed
             if not first_step:
-                result = result - previous[4 * g + i]
-            out[4 * g + i] = result
+                result = result - held[9][row]
+            made[row] = result
+        rows = pl.ds(x * SY, SY)
+        stores.append(pltpu.make_async_copy(made.at[rows], out.at[rows], out_sem.at[x]))
+        stores[-1].start()
+    for store in stores:
+        store.wait()
 
 
 def local_part(first_step, *arrays):
     return pl.pallas_call(
         functools.partial(local_kernel, first_step),
         out_shape=BLOCK,
-        in_specs=vmem_specs(len(arrays)),
-        out_specs=pl.BlockSpec(memory_space=pltpu.VMEM),
-        compiler_params=PARAMS,
-        cost_estimate=cost(0.1),
+        in_specs=any_specs(len(arrays)),
+        out_specs=pl.BlockSpec(memory_space=pl.ANY),
+        scratch_shapes=[pltpu.VMEM(a.shape, a.dtype) for a in arrays]
+        + [
+            pltpu.VMEM((ROWS, NB, SZ), F32),
+            pltpu.SemaphoreType.DMA((len(arrays),)),
+            pltpu.SemaphoreType.DMA((SX,)),
+        ],
+        compiler_params=SMALL,
         name="local",
     )(*arrays)
 
 
-def coupled_kernel(first_step, last_step, *refs):
-    if first_step:
-        base, came, mat, new, x_low, x_high, coupling, coef = refs
-    elif last_step:
-        base, came, mat, coupling, new, gram, total, coef = refs
-        total[...] = jnp.zeros_like(total)
+def coupled_kernel(first_step, last_step, me, base, came, mat, *refs):
+    coupling = None
+    if not first_step:
+        coupling, refs = refs[0], refs[1:]
+    if last_step:
+        (new, gram), refs = refs[:2], refs[2:]
     else:
-        base, came, mat, coupling, new, x_low, x_high, coef = refs
+        (new, x_low, x_high, y_low, y_high, z_face, sends), refs = refs[:7], refs[7:]
+        if first_step:
+            coupling, refs = refs[0], refs[1:]
+        outs = (new, x_low, x_high, y_low, y_high)
+    made, came_v, mat_v, total, coef, came_sem, in_sem, mat_sem, out_sem = refs
     alpha = (1.0 if first_step else 2.0) / FILTER_HALF
-    frame = came[0]
+    arrive = pltpu.make_async_copy(came, came_v, came_sem)
+    arrive.start()
+
+    def load(x):
+        rows = pl.ds(x * SY, SY)
+        some = pl.ds(x * 4, 4)
+        return [
+            pltpu.make_async_copy(base.at[rows], made.at[rows], in_sem.at[x]),
+            pltpu.make_async_copy(mat.at[some], mat_v.at[some], mat_sem.at[x]),
+        ]
+
+    for x in range(SX):
+        for copy in load(x):
+            copy.start()
+    total[...] = jnp.zeros_like(total)
+    arrive.wait()
+    frame = came_v[0]
     for slot in range(1, came.shape[0]):
-        frame = frame + came[slot]
+        frame = frame + came_v[slot]
     if first_step:
         coupling[...] = frame[TGT:]
         frame = frame[:TGT]
@@ -406,50 +508,77 @@
 
     @pl.loop(0, SX)
     def _(x):
+        for copy in load(x):
+            copy.wait()
         c_hi = coef[pl.ds(0, NB), :]
         c_lo = coef[pl.ds(NB, NB), pl.ds(0, CH)]
-        if last_step:
-            acc = total[...]
+        acc = total[...]
+        rows = []
         for p in range(4):
-            pair_mat = mat[x * 4 + p]
+            pair_mat = mat_v[x * 4 + p]
             added = dot(c_hi, pair_mat) + dot(c_lo, pair_mat[:CH])
-            rows = []
             for q in range(2):
                 at = x * SY + 2 * p + q
-                rows.append(base[at] + added[:, q * SZ : (q + 1) * SZ])
-                new[at] = rows[q]
+                rows.append(made[at] + added[:, q * SZ : (q + 1) * SZ])
+                made[at] = rows[-1]
+        if last_step:
+            block_copy(x, made, new, out_sem).start()
+        else:
+            start_faces(x, made, outs, out_sem)
+        for p in range(4):
+            values = jnp.concatenate(rows[2 * p : 2 * p + 2], axis=1)
             if last_step:
-                joined = jnp.concatenate(split3(jnp.concatenate(rows, axis=1)), axis=0)
+                joined = jnp.concatenate(split3(values), axis=0)
                 acc = acc + dot(joined, joined, NT)
-        if last_step:
-            total[...] = acc
+            else:
+                acc = acc + partial_of(mat_v[x * 4 + p], values)
+        total[...] = acc
+        if not last_step:
+            for part in range(2):
+                z_face[pl.ds((2 * x + part) * 16, 16), :] = z_faces(rows[4 * part : 4 * part + 4])
 
     if last_step:
         t = total[...]
         summed = t[2 * NB :, :NB] + t[:NB, 2 * NB :] + t[NB : 2 * NB, NB : 2 * NB]
         summed = summed + (t[NB : 2 * NB, :NB] + t[:NB, NB : 2 * NB]) + t[:NB, :NB]
         gram[...] = jnp.concatenate([summed[8 * q : 8 * q + 8] for q in range(4)], axis=1)
+        for x in range(SX):
+            block_copy(x, made, new, out_sem).wait()
     else:
-        write_x_faces(new, x_low, x_high)
-
-
-def coupled_part(first_step, last_step, *arrays):
-    scratch = [pltpu.VMEM((2 * NB, 2 * CH), BF16)]
+        spread_y(packed_partial(total[...]), me, sends, pl.ds(0, TGT))
+        wait_faces(made, outs, out_sem)
+
+
+def coupled_part(first_step, last_step, me, base, came, mat, *scales):
+    total = (3 * NB, 3 * NB) if last_step else TOTAL
     if last_step:
         outs = [BLOCK, jax.ShapeDtypeStruct((8, LANES), F32)]
-        scratch = [pltpu.VMEM((3 * NB, 3 * NB), F32)] + scratch
+        specs = any_specs(1) + vmem_specs(1)
     else:
-        outs = [BLOCK, X_FACE, X_FACE] + ([FRAME] if first_step else [])
+        outs = [BLOCK, X_FACE, X_FACE, Y_FACE, Y_FACE, Z_FACE, jax.ShapeDtypeStruct((8, TGT, LANES), F32)]
+        specs = any_specs(5) + vmem_specs(2)
+        if first_step:
+            outs.append(FRAME)
+            specs = specs + vmem_specs(1)
     return pl.pallas_call(
         functools.partial(coupled_kernel, first_step, last_step),
         out_shape=outs,
-        in_specs=vmem_specs(len(arrays)),
-        out_specs=vmem_specs(len(outs)),
-        scratch_shapes=scratch,
+        in_specs=[pl.BlockSpec(memory_space=pltpu.SMEM)] + any_specs(3) + vmem_specs(len(scales)),
+        out_specs=specs,
+        scratch_shapes=[
+            pltpu.VMEM((ROWS, NB, SZ), F32),
+            pltpu.VMEM(came.shape, F32),
+            pltpu.VMEM((PAIRS, 2 * CH, 2 * SZ), BF16),
+            pltpu.VMEM(total, F32),
+            pltpu.VMEM((2 * NB, 2 * CH), BF16),
+            pltpu.SemaphoreType.DMA(()),
+            pltpu.SemaphoreType.DMA((SX,)),
+            pltpu.SemaphoreType.DMA((SX,)),
+            pltpu.SemaphoreType.DMA((5, SX)),
+        ],
         compiler_params=PARAMS,
-        cost_estimate=cost(0.1),
         name="coupled",
-    )(*arrays)
+    )(me, base, came, mat, *scales)
 
 
 def finish_kernel(scale, field, grams, out, held, made, inverse, in_sem, out_sem):
@@ -546,10 +675,9 @@
     mat = build(starts, ordered[0], ordered[1:])
 
     own = jnp.repeat(coupling, NB, axis=1)
-    coupling_frame = jnp.zeros((TGT, LANES), F32).at[16:18].set(own)
-
     previous = ()
     scales = ()
+    sends = None
     for k in range(DEGREE):
         start, last = k == 0, k == DEGREE - 1
         x_left = shift(x_high, "gx", 1)
@@ -561,31 +689,27 @@
             mat, field, x_left, x_right, y_left, y_right, faces = lax.optimization_barrier(
                 (mat, field, x_left, x_right, y_left, y_right, faces)
             )
-            (partial,) = partial_part(False, field, mat)
-            partial = jnp.concatenate([partial, coupling_frame], axis=0)
-        else:
-            partial, y_low, y_high, z_face = partial_part(True, field, mat)
-        frames = 2 if start else 1
-        sends = spread_call(spread_y_kernel, 8, frames, me_y, partial)
+            sends = first(me_y, field, mat, own)
         if not start:
-            sends, y_low, y_high, z_face = lax.optimization_barrier((sends, y_low, y_high, z_face))
+            faces = shift(z_face, "gz", 1)
+            sends, faces, y_low, y_high = lax.optimization_barrier((sends, faces, y_low, y_high))
+        came = lax.all_to_all(sends, "gy", 0, 0)
+        if not start:
             y_left = shift(y_high, "gy", 1)
             y_right = shift(y_low, "gy", -1)
-            faces = shift(z_face, "gz", 1)
-        came = lax.all_to_all(sends, "gy", 0, 0)
-        sends = spread_call(spread_xz_kernel, 16, frames, me_xz, came)
+        sends = spread_xz(2 if start else 1, me_xz, came)
         came = lax.all_to_all(sends, ("gx", "gz"), 0, 0)
         base = local_part(
-            start, field, *previous, x_left, x_right, y_left, y_right, faces, pot, first_z, second_z
+            start, field, faces, pot, first_z, second_z, x_left, x_right, y_left, y_right, *previous
         )
-        outs = coupled_part(start, last, base, came, mat, *scales)
+        outs = coupled_part(start, last, me_y, base, came, mat, *scales)
         previous = (field,)
         if last:
             field, gram = outs
         else:
-            field, x_low, x_high = outs[:3]
+            field, x_low, x_high, y_low, y_high, z_face, sends = outs[:7]
             if start:
-                scales = (outs[3],)
+                scales = (outs[7],)
     axes = ("gx", "gy", "gz")
     devices = 1
     for axis in axes:

time: 267 us -> 304 us (1.14)
  starting transfers between devices: 58.2 us -> 108 us
  local copies, waits for them, and re-layouts: 39.3 us -> 9.34 us
  Pallas kernels: 69.7 us -> 97.8 us
  waiting for transfers between devices: 32.1 us -> 13.8 us
  blocking collectives: 54.4 us -> 63.7 us
    ppermute x20, starting transfers between devices: 37.5 us -> 88.6 us  [shift(): lax.ppermute(value, axis, [(i, (i + by) % count) for i in range(count)])]
    unnamed x88 -> x22, local copies, waits for them, and re-layouts: 36.5 us -> 5.94 us
    pallas_call x4, Pallas kernels: 16.5 us -> 38.6 us  [coupled_part(): pl.pallas_call(functools.partial(coupled_kernel, first_step, last_step),...]
    ppermute x20, waiting for transfers between devices: 20.8 us -> 0.82 us  [shift(): lax.ppermute(value, axis, [(i, (i + by) % count) for i in range(count)])]
    pallas_call x4, Pallas kernels: 13.8 us -> 27.7 us  [local_part(): pl.pallas_call(functools.partial(local_kernel, first_step), out_shape=BLO...]
    pallas_call x12 -> x5, Pallas kernels: 20.9 us -> 11 us  [the longest x4 5.52 us: spread_xz(): pl.pallas_call(functools.partial(spread_xz_kernel, frames), out_shape=jax...]
    all_to_all x3, blocking collectives: 34.4 us -> 41.5 us  [local(): came = lax.all_to_all(sends, 'gy', 0, 0)]
  transfers between devices with their start and end apart: 25 -> 25, of which waited for: 5 -> 6; matrix products, arithmetic and copies ran while one was open for 5% -> 4% of each run, Pallas kernels for 10% -> 13%
where the time goes in v4:
time: 304 us; the launch traced here: 303 us
  starting transfers between devices  108 us (36%)
  Pallas kernels  97.8 us (32%)
  blocking collectives  63.7 us (21%)
  waiting for transfers between devices  13.8 us (5%)
  local copies, waits for them, and re-layouts  9.34 us (3%)
  other arithmetic  8.39 us (3%)
    ppermute x20, starting transfers between devices, shift(): lax.ppermute(value, axis, [(i, (i + by) % count) for i in range(count)])  88.6 us
    all_to_all x3, blocking collectives, local(): came = lax.all_to_all(sends, 'gy', 0, 0)  41.5 us
    pallas_call x4, Pallas kernels, coupled_part(): pl.pallas_call(functools.partial(coupled_kernel, first_step, last_step),...  38.6 us
    pallas_call x4, Pallas kernels, local_part(): pl.pallas_call(functools.partial(local_kernel, first_step), out_shape=BLO...  27.7 us
    all_to_all x1, blocking collectives, local(): lax.all_to_all(jnp.broadcast_to(gram[None], (devices,) + gram.shape), axe...  22.1 us
    all_to_all x4, starting transfers between devices, local(): came = lax.all_to_all(sends, ('gx', 'gz'), 0, 0)  14.4 us
    pallas_call x1, Pallas kernels, build(): pl.pallas_call(build_kernel, out_shape=jax.ShapeDtypeStruct((PAIRS, 2 * C...  9.06 us
    pallas_call x1, Pallas kernels, finish(): pl.pallas_call(functools.partial(finish_kernel, scale), out_shape=jax.Sha...  7.11 us
  transfers between devices with their start and end apart: 25, of which 6 were waited for; matrix products, arithmetic and copies ran while one was open for 4% of the time, Pallas kernels for 13%

profile of v4, /device:TPU:1, one launch (start us, length us, event | category | flops | bytes accessed | tf_op | source)
XLA Modules:
  0.0 302.6 jit_solution(17444489838999937318)
XLA Ops:
  0.0 4.4 %rearrange.1 = (f32[64,32,128]{2,1,0:T(8,128)}, f32[48,32,128]{2,1,0:T(8,128)}, f32[48,32,128]{2,1,0:T(8,128)}, f32[8,6,32,128]{3,2,1,0:T(8,128)}, f32[8,6,32,128]{3,2,1,0:T(8,128)}, /*index=5*/f32[256,128]{1,0:T(8,128)}) custom-call(f32[32,64,128]{2,1,0:T(8,128)} %bitcast.21), custom_call_target="tpu_custom_call" | custom-call | tf_op jit(solution)/shard_map/rearrange/pallas_call | solution.py:185
  4.4 4.5 %collective-permute-start.4 = (f32[256,128]{1,0:T(8,128)}, f32[256,128]{1,0:T(8,128)S(1)}, u32[]{:S(2)}, u32[]{:S(2)}) collective-permute-start(f32[256,128]{1,0:T(8,128)} %get-tuple-element.69), channel_id=1, source_target_pairs={{0,1},{1,0},{2,3},{3,2},{4,5},{5,4},{6,7},{7,6},{8,9},{9,8},{10,11... | collective-permute-start | bytes 393224 | tf_op jit(solution)/shard_map/ppermute | solution.py:651
  12.5 2.6 collective-permute-start.2
  19.3 6.5 %sort.33 = (s32[8192]{0:T(1024)}, f32[8192]{0:T(1024)}, f32[8192]{0:T(1024)}, f32[8192]{0:T(1024)}, f32[8192]{0:T(1024)}) sort(s32[8192]{0:T(1024)S(1)} %fusion.5, f32[8192]{0:T(1024)S(1)} %bitcast.24, f32[8192]{0:T(1024)S(1)} %bitcast.23, f32[8192]{0:T(1024)S(1)} %bitcast.25, f32[8192]{0:T(1024)S(1)} %bitcast.22), dimensions={0}, to_apply=%region_1.2 | sort | flops 106496 | bytes 327680 | tf_op jit(solution)/shard_map/sort | solution.py:673
  26.8 9.1 %build.1.mat = bf16[32,320,256]{2,1,0:T(8,128)(2,1)} custom-call(s32[65]{0:T(128)} %convert_reduce_fusion.starts, s32[64,128]{1,0:T(8,128)} %bitcast.26, f32[64,128]{1,0:T(8,128)} %bitcast.27, f32[64,128]{1,0:T(8,128)} %bitcast.28, f32[64,128]{1,0:T(8,128)} %bitcast.29, f32[64,128]{1,0:T(8,128)} %bitcast.30), custom_call_target="tpu_custom_call" | custom-call | tf_op jit(solution)/shard_map/build/pallas_call | solution.py:266
  35.9 5.5 %first.1 = f32[8,80,128]{2,1,0:T(8,128)} custom-call(s32[1]{0:T(128)} %bitcast.me, f32[64,32,128]{2,1,0:T(8,128)} %get-tuple-element.70.refs_0_.field.refs_9_, bf16[32,320,256]{2,1,0:T(8,128)(2,1)} %build.1.mat, f32[2,128]{1,0:T(2,128)} %reshape.56.own), custom_call_target="tpu_custom_call" | custom-call | tf_op jit(solution)/shard_map/first/pallas_call | solution.py:341
  41.4 5.3 %all-to-all-start = ((f32[8,80,128]{2,1,0:T(8,128)}), f32[8,80,128]{2,1,0:T(8,128)S(1)}, u32[]{:S(2)}, u32[]{:S(2)}) async-start(f32[8,80,128]{2,1,0:T(8,128)} %first.1), calls=%async_computation | async-start | bytes 655360 | tf_op jit(solution)/shard_map/all_to_all | solution.py:696
  46.8 7.1 %all-to-all-done.came = f32[8,80,128]{2,1,0:T(8,128)S(1)} async-done(((f32[8,80,128]{2,1,0:T(8,128)}), f32[8,80,128]{2,1,0:T(8,128)S(1)}, u32[]{:S(2)}, u32[]{:S(2)}) %all-to-all-start) | async-done | bytes 327712 | tf_op jit(solution)/shard_map/all_to_all | solution.py:696
  55.4 3.6 %all-to-all-start.1 = ((f32[16,80,128]{2,1,0:T(8,128)}), f32[16,80,128]{2,1,0:T(8,128)S(1)}, u32[]{:S(2)}, u32[]{:S(2)}) async-start(f32[16,80,128]{2,1,0:T(8,128)} %spread.4), calls=%async_computation.1 | async-start | bytes 1310720 | tf_op jit(solution)/shard_map/all_to_all | solution.py:701
  59.1 6.9 %local.4.base = f32[64,32,128]{2,1,0:T(8,128)} custom-call(f32[64,32,128]{2,1,0:T(8,128)} %get-tuple-element.70.refs_0_.field.refs_9_, f32[256,128]{1,0:T(8,128)S(1)} %collective-permute-done.4.refs_1_, f32[64,128]{1,0:T(8,128)S(1)} %bitcast.17, bf16[256,128]{1,0:T(8,128)(2,1)S(1)} %copy-done.1, bf16[256,128]{1,0:T(8,128)(2,1)S(1)} %copy-done, ...), custom_call_target="tpu_custom_call" | custom-call | tf_op jit(solution)/shard_map/local/pallas_call | solution.py:451
  66.0 4.2 %all-to-all-done.1.came = f32[16,80,128]{2,1,0:T(8,128)S(1)} async-done(((f32[16,80,128]{2,1,0:T(8,128)}), f32[16,80,128]{2,1,0:T(8,128)S(1)}, u32[]{:S(2)}, u32[]{:S(2)}) %all-to-all-start.1) | async-done | bytes 655392 | tf_op jit(solution)/shard_map/all_to_all | solution.py:701
  71.1 9.4 %coupled.4 = (f32[64,32,128]{2,1,0:T(8,128)}, f32[48,32,128]{2,1,0:T(8,128)}, f32[48,32,128]{2,1,0:T(8,128)}, f32[8,6,32,128]{3,2,1,0:T(8,128)}, f32[8,6,32,128]...) custom-call(s32[1]{0:T(128)} %bitcast.me, f32[64,32,128]{2,1,0:T(8,128)} %local.4.base, ...), custom_call_target="tpu_custom_call" | custom-call | tf_op jit(solution)/shard_map/coupled/pallas_call | solution.py:563
  82.1 3.6 %collective-permute-start.7 = (f32[48,32,128]{2,1,0:T(8,128)}, f32[48,32,128]{2,1,0:T(8,128)S(1)}, u32[]{:S(2)}, u32[]{:S(2)}) collective-permute-start(f32[48,32,128]{2,1,0:T(8,128)} %get-tuple-element.84), channel_id=1, source_target_pairs={{0,112},{16,0},{32,16},{48,32},{64,48},{80,64},{96,80},{112,96},{1... | collective-permute-start | bytes 2359304 | tf_op jit(solution)/shard_map/ppermute | solution.py:651
  86.1 20.7 %collective-permute-start.8 = (f32[8,6,32,128]{3,2,1,0:T(8,128)}, f32[8,6,32,128]{3,2,1,0:T(8,128)S(1)}, u32[]{:S(2)}, u32[]{:S(2)}) collective-permute-start(f32[8,6,32,128]{3,2,1,0:T(8,128)} %get-tuple-element.85), channel_id=1, source_target_pairs={{0,2},{2,4},{4,6},{6,8},{8,10},{10,12},{12,14},{14,0},{1,3},{3,5},... | collective-permute-start | bytes 2359304 | tf_op jit(solution)/shard_map/ppermute | solution.py:651
  106.8 13.6 %all_to_all.45.came = f32[8,40,128]{2,1,0:T(8,128)S(1)} all-to-all(f32[8,40,128]{2,1,0:T(8,128)} %get-tuple-element.87), channel_id=1, replica_groups=mesh['gx'=8,'gy'=8,'gz'=2] {'gy'}, dimensions={0} | all-to-all | bytes 327680 | tf_op jit(solution)/shard_map/all_to_all | solution.py:696
  121.7 3.7 %all-to-all-start.3 = ((f32[16,40,128]{2,1,0:T(8,128)}), f32[16,40,128]{2,1,0:T(8,128)S(1)}, u32[]{:S(2)}, u32[]{:S(2)}) async-start(f32[16,40,128]{2,1,0:T(8,128)} %spread.5), calls=%async_computation.3 | async-start | bytes 655360 | tf_op jit(solution)/shard_map/all_to_all | solution.py:701
  126.5 6.9 %local.5.base = f32[64,32,128]{2,1,0:T(8,128)} custom-call(f32[64,32,128]{2,1,0:T(8,128)} %get-tuple-element.77.refs_0_.refs_9_, f32[256,128]{1,0:T(8,128)S(1)} %collective-permute-done.5.refs_1_, f32[64,128]{1,0:T(8,128)S(1)} %bitcast.18, bf16[256,128]{1,0:T(8,128)(2,1)S(1)} %copy-done.1, bf16[256,128]{1,0:T(8,128)(2,1)S(1)} %copy-done, ...), custom_call_target="tpu_custom_call" | custom-call | tf_op jit(solution)/shard_map/local/pallas_call | solution.py:451
  134.2 10.1 %coupled.5 = (f32[64,32,128]{2,1,0:T(8,128)}, f32[48,32,128]{2,1,0:T(8,128)}, f32[48,32,128]{2,1,0:T(8,128)}, f32[8,6,32,128]{3,2,1,0:T(8,128)}, f32[8,6,32,128]...) custom-call(s32[1]{0:T(128)} %bitcast.me, f32[64,32,128]{2,1,0:T(8,128)} %local.5.base, ...), custom_call_target="tpu_custom_call" | custom-call | tf_op jit(solution)/shard_map/coupled/pallas_call | solution.py:563
  144.3 2.7 collective-permute-start.10
  150.5 20.2 %collective-permute-start.13 = (f32[8,6,32,128]{3,2,1,0:T(8,128)}, f32[8,6,32,128]{3,2,1,0:T(8,128)S(1)}, u32[]{:S(2)}, u32[]{:S(2)}) collective-permute-start(f32[8,6,32,128]{3,2,1,0:T(8,128)} %get-tuple-element.97), channel_id=1, source_target_pairs={{0,2},{2,4},{4,6},{6,8},{8,10},{10,12},{12,14},{14,0},{1,3},{3,5},... | collective-permute-start | bytes 2359304 | tf_op jit(solution)/shard_map/ppermute | solution.py:651
  170.7 15.0 %all_to_all.46.came = f32[8,40,128]{2,1,0:T(8,128)S(1)} all-to-all(f32[8,40,128]{2,1,0:T(8,128)} %get-tuple-element.99), channel_id=1, replica_groups=mesh['gx'=8,'gy'=8,'gz'=2] {'gy'}, dimensions={0} | all-to-all | bytes 327680 | tf_op jit(solution)/shard_map/all_to_all | solution.py:696
  186.9 3.5 %all-to-all-start.5 = ((f32[16,40,128]{2,1,0:T(8,128)}), f32[16,40,128]{2,1,0:T(8,128)S(1)}, u32[]{:S(2)}, u32[]{:S(2)}) async-start(f32[16,40,128]{2,1,0:T(8,128)} %spread.6), calls=%async_computation.5 | async-start | bytes 655360 | tf_op jit(solution)/shard_map/all_to_all | solution.py:701
  191.5 6.9 %local.6.base = f32[64,32,128]{2,1,0:T(8,128)} custom-call(f32[64,32,128]{2,1,0:T(8,128)} %get-tuple-element.89.refs_0_.refs_9_, f32[256,128]{1,0:T(8,128)S(1)} %collective-permute-done.10.refs_1_, f32[64,128]{1,0:T(8,128)S(1)} %bitcast.19, bf16[256,128]{1,0:T(8,128)(2,1)S(1)} %copy-done.1, bf16[256,128]{1,0:T(8,128)(2,1)S(1)} %copy-done, ...), custom_call_target="tpu_custom_call" | custom-call | tf_op jit(solution)/shard_map/local/pallas_call | solution.py:451
  200.3 10.1 %coupled.6 = (f32[64,32,128]{2,1,0:T(8,128)}, f32[48,32,128]{2,1,0:T(8,128)}, f32[48,32,128]{2,1,0:T(8,128)}, f32[8,6,32,128]{3,2,1,0:T(8,128)}, f32[8,6,32,128]...) custom-call(s32[1]{0:T(128)} %bitcast.me, f32[64,32,128]{2,1,0:T(8,128)} %local.6.base, ...), custom_call_target="tpu_custom_call" | custom-call | tf_op jit(solution)/shard_map/coupled/pallas_call | solution.py:563
  213.3 2.4 collective-permute-start.17
  216.0 20.4 %collective-permute-start.18 = (f32[8,6,32,128]{3,2,1,0:T(8,128)}, f32[8,6,32,128]{3,2,1,0:T(8,128)S(1)}, u32[]{:S(2)}, u32[]{:S(2)}) collective-permute-start(f32[8,6,32,128]{3,2,1,0:T(8,128)} %get-tuple-element.108), channel_id=1, source_target_pairs={{0,2},{2,4},{4,6},{6,8},{8,10},{10,12},{12,14},{14,0},{1,3},{3,5},... | collective-permute-start | bytes 2359304 | tf_op jit(solution)/shard_map/ppermute | solution.py:651
  236.4 13.0 %all_to_all.47.came = f32[8,40,128]{2,1,0:T(8,128)S(1)} all-to-all(f32[8,40,128]{2,1,0:T(8,128)} %get-tuple-element.110), channel_id=1, replica_groups=mesh['gx'=8,'gy'=8,'gz'=2] {'gy'}, dimensions={0} | all-to-all | bytes 327680 | tf_op jit(solution)/shard_map/all_to_all | solution.py:696
  250.7 3.5 %all-to-all-start.7 = ((f32[16,40,128]{2,1,0:T(8,128)}), f32[16,40,128]{2,1,0:T(8,128)S(1)}, u32[]{:S(2)}, u32[]{:S(2)}) async-start(f32[16,40,128]{2,1,0:T(8,128)} %spread.7), calls=%async_computation.7 | async-start | bytes 655360 | tf_op jit(solution)/shard_map/all_to_all | solution.py:701
  255.2 6.9 %local.7.base = f32[64,32,128]{2,1,0:T(8,128)} custom-call(f32[64,32,128]{2,1,0:T(8,128)} %get-tuple-element.100.refs_0_, f32[256,128]{1,0:T(8,128)S(1)} %collective-permute-done.15.refs_1_, f32[64,128]{1,0:T(8,128)S(1)} %bitcast.20, bf16[256,128]{1,0:T(8,128)(2,1)S(1)} %copy-done.1, bf16[256,128]{1,0:T(8,128)(2,1)S(1)} %copy-done, ...), custom_call_target="tpu_custom_call" | custom-call | tf_op jit(solution)/shard_map/local/pallas_call | solution.py:451
  263.5 9.0 %coupled.7 = (f32[64,32,128]{2,1,0:T(8,128)}, f32[8,128]{1,0:T(8,128)}) custom-call(s32[1]{0:T(128)} %bitcast.me, f32[64,32,128]{2,1,0:T(8,128)} %local.7.base, f32[16,40,128]{2,1,0:T(8,128)} %copy-done.4, bf16[32,320,256]{2,1,0:T(8,128)(2,1)} %build.1.mat, f32[40,128]{1,0:T(8,128)} %get-tuple-element.88.refs_0_), custom_call_target="tpu_custom_call" | custom-call | tf_op jit(solution)/shard_map/coupled/pallas_call | solution.py:563
  273.2 22.1 %all_to_all.48.grams = f32[128,8,128]{2,1,0:T(8,128)} all-to-all(f32[128,8,128]{2,1,0:T(8,128)S(1)} %broadcast_in_dim.17), channel_id=1, replica_groups=mesh['gx'=8,'gy'=8,'gz'=2] {'gx','gy','gz'}, dimensions={0} | all-to-all | bytes 1048576 | tf_op jit(solution)/shard_map/all_to_all | solution.py:717
  295.4 7.1 %finish.1 = f32[32,64,128]{2,1,0:T(8,128)} custom-call(f32[64,32,128]{2,1,0:T(8,128)} %get-tuple-element.111.field, f32[128,8,128]{2,1,0:T(8,128)} %all_to_all.48.grams), custom_call_target="tpu_custom_call" | custom-call | tf_op jit(solution)/shard_map/finish/pallas_call | solution.py:632
  (69 shorter events, 31.0 us)
Async XLA Ops:
  4.4 31.4 %collective-permute-start.4 = (f32[256,128]{1,0:T(8,128)}, f32[256,128]{1,0:T(8,128)S(1)}, u32[]{:S(2)}, u32[]{:S(2)}) collective-permute-start(f32[256,128]{1,0:T(8,128)} %get-tuple-element.69), channel_id=1, source_target_pairs={{0,1},{1,0},{2,3},{3,2},{4,5},{5,4},{6,7},{7,6},{8,9},{9,8},{10,11... | collective-permute-start | bytes 393224 | tf_op jit(solution)/shard_map/ppermute | solution.py:651
  8.9 26.9 %collective-permute-start = (f32[48,32,128]{2,1,0:T(8,128)}, f32[48,32,128]{2,1,0:T(8,128)S(1)}, u32[]{:S(2)}, u32[]{:S(2)}) collective-permute-start(f32[48,32,128]{2,1,0:T(8,128)} %get-tuple-element.65), channel_id=1, source_target_pairs={{0,16},{16,32},{32,48},{48,64},{64,80},{80,96},{96,112},{112,0},{1... | collective-permute-start | bytes 2359304 | tf_op jit(solution)/shard_map/ppermute | solution.py:651
  10.2 25.7 %collective-permute-start.1 = (f32[48,32,128]{2,1,0:T(8,128)}, f32[48,32,128]{2,1,0:T(8,128)S(1)}, u32[]{:S(2)}, u32[]{:S(2)}) collective-permute-start(f32[48,32,128]{2,1,0:T(8,128)} %get-tuple-element.66), channel_id=1, source_target_pairs={{0,112},{16,0},{32,16},{48,32},{64,48},{80,64},{96,80},{112,96},{1... | collective-permute-start | bytes 2359304 | tf_op jit(solution)/shard_map/ppermute | solution.py:651
  12.5 23.4 %collective-permute-start.2 = (f32[8,6,32,128]{3,2,1,0:T(8,128)}, f32[8,6,32,128]{3,2,1,0:T(8,128)S(1)}, u32[]{:S(2)}, u32[]{:S(2)}) collective-permute-start(f32[8,6,32,128]{3,2,1,0:T(8,128)} %get-tuple-element.67), channel_id=1, source_target_pairs={{0,2},{2,4},{4,6},{6,8},{8,10},{10,12},{12,14},{14,0},{1,3},{3,5},... | collective-permute-start | bytes 2359304 | tf_op jit(solution)/shard_map/ppermute | solution.py:651
  15.1 20.8 %collective-permute-start.3 = (f32[8,6,32,128]{3,2,1,0:T(8,128)}, f32[8,6,32,128]{3,2,1,0:T(8,128)}, u32[]{:S(2)}, u32[]{:S(2)}) collective-permute-start(f32[8,6,32,128]{3,2,1,0:T(8,128)} %get-tuple-element.68), channel_id=1, source_target_pairs={{0,14},{2,0},{4,2},{6,4},{8,6},{10,8},{12,10},{14,12},{1,15},{3,1}... | collective-permute-start | bytes 2359304 | tf_op jit(solution)/shard_map/ppermute | solution.py:651
  35.9 5.5 %copy-start.10 = (f32[8,6,32,128]{3,2,1,0:T(8,128)}, f32[8,6,32,128]{3,2,1,0:T(8,128)S(1)}, u32[]{:S(2)}) copy-start(f32[8,6,32,128]{3,2,1,0:T(8,128)S(1)} %collective-permute-done.2.refs_7_) | copy-start | bytes 2359300
  41.4 17.7 %copy-start = (bf16[256,128]{1,0:T(8,128)(2,1)S(1)}, bf16[256,128]{1,0:T(8,128)(2,1)}, u32[]{:S(2)}) copy-start(bf16[256,128]{1,0:T(8,128)(2,1)} %constant.64.clone.refs_4_) | copy-start | bytes 196612
  41.4 17.7 %copy-start.1 = (bf16[256,128]{1,0:T(8,128)(2,1)S(1)}, bf16[256,128]{1,0:T(8,128)(2,1)}, u32[]{:S(2)}) copy-start(bf16[256,128]{1,0:T(8,128)(2,1)} %constant.63.clone.refs_3_) | copy-start | bytes 196612
  41.4 17.7 %copy-start.2 = (f32[8,8,128]{2,1,0:T(8,128)S(1)}, f32[8,8,128]{2,1,0:T(8,128)}, u32[]{:S(2)}) copy-start(f32[8,8,128]{2,1,0:T(8,128)} %param.10) | copy-start | bytes 98308
  41.4 12.5 %all-to-all-start = ((f32[8,80,128]{2,1,0:T(8,128)}), f32[8,80,128]{2,1,0:T(8,128)S(1)}, u32[]{:S(2)}, u32[]{:S(2)}) async-start(f32[8,80,128]{2,1,0:T(8,128)} %first.1), calls=%async_computation | async-start | bytes 655360 | tf_op jit(solution)/shard_map/all_to_all | solution.py:696
  55.4 14.8 %all-to-all-start.1 = ((f32[16,80,128]{2,1,0:T(8,128)}), f32[16,80,128]{2,1,0:T(8,128)S(1)}, u32[]{:S(2)}, u32[]{:S(2)}) async-start(f32[16,80,128]{2,1,0:T(8,128)} %spread.4), calls=%async_computation.1 | async-start | bytes 1310720 | tf_op jit(solution)/shard_map/all_to_all | solution.py:701
  80.5 5.6 %collective-permute-start.5 = (f32[256,128]{1,0:T(8,128)}, f32[256,128]{1,0:T(8,128)S(1)}, u32[]{:S(2)}, u32[]{:S(2)}) collective-permute-start(f32[256,128]{1,0:T(8,128)} %get-tuple-element.79), channel_id=1, source_target_pairs={{0,1},{1,0},{2,3},{3,2},{4,5},{5,4},{6,7},{7,6},{8,9},{9,8},{10,11... | collective-permute-start | bytes 393224 | tf_op jit(solution)/shard_map/ppermute | solution.py:651
  82.1 43.4 %collective-permute-start.6 = (f32[48,32,128]{2,1,0:T(8,128)}, f32[48,32,128]{2,1,0:T(8,128)S(1)}, u32[]{:S(2)}, u32[]{:S(2)}) collective-permute-start(f32[48,32,128]{2,1,0:T(8,128)} %get-tuple-element.83), channel_id=1, source_target_pairs={{0,16},{16,32},{32,48},{48,64},{64,80},{80,96},{96,112},{112,0},{1... | collective-permute-start | bytes 2359304 | tf_op jit(solution)/shard_map/ppermute | solution.py:651
  82.1 43.4 %collective-permute-start.7 = (f32[48,32,128]{2,1,0:T(8,128)}, f32[48,32,128]{2,1,0:T(8,128)S(1)}, u32[]{:S(2)}, u32[]{:S(2)}) collective-permute-start(f32[48,32,128]{2,1,0:T(8,128)} %get-tuple-element.84), channel_id=1, source_target_pairs={{0,112},{16,0},{32,16},{48,32},{64,48},{80,64},{96,80},{112,96},{1... | collective-permute-start | bytes 2359304 | tf_op jit(solution)/shard_map/ppermute | solution.py:651
  86.1 39.4 %collective-permute-start.8 = (f32[8,6,32,128]{3,2,1,0:T(8,128)}, f32[8,6,32,128]{3,2,1,0:T(8,128)S(1)}, u32[]{:S(2)}, u32[]{:S(2)}) collective-permute-start(f32[8,6,32,128]{3,2,1,0:T(8,128)} %get-tuple-element.85), channel_id=1, source_target_pairs={{0,2},{2,4},{4,6},{6,8},{8,10},{10,12},{12,14},{14,0},{1,3},{3,5},... | collective-permute-start | bytes 2359304 | tf_op jit(solution)/shard_map/ppermute | solution.py:651
  106.8 18.7 %collective-permute-start.9 = (f32[8,6,32,128]{3,2,1,0:T(8,128)}, f32[8,6,32,128]{3,2,1,0:T(8,128)}, u32[]{:S(2)}, u32[]{:S(2)}) collective-permute-start(f32[8,6,32,128]{3,2,1,0:T(8,128)} %get-tuple-element.86), channel_id=1, source_target_pairs={{0,14},{2,0},{4,2},{6,4},{8,6},{10,8},{12,10},{14,12},{1,15},{3,1}... | collective-permute-start | bytes 2359304 | tf_op jit(solution)/shard_map/ppermute | solution.py:651
  121.7 11.7 %all-to-all-start.3 = ((f32[16,40,128]{2,1,0:T(8,128)}), f32[16,40,128]{2,1,0:T(8,128)S(1)}, u32[]{:S(2)}, u32[]{:S(2)}) async-start(f32[16,40,128]{2,1,0:T(8,128)} %spread.5), calls=%async_computation.3 | async-start | bytes 655360 | tf_op jit(solution)/shard_map/all_to_all | solution.py:701
  125.5 1.0 copy-start.9
  144.3 6.2 %collective-permute-start.10 = (f32[256,128]{1,0:T(8,128)}, f32[256,128]{1,0:T(8,128)S(1)}, u32[]{:S(2)}, u32[]{:S(2)}) collective-permute-start(f32[256,128]{1,0:T(8,128)} %get-tuple-element.91), channel_id=1, source_target_pairs={{0,1},{1,0},{2,3},{3,2},{4,5},{5,4},{6,7},{7,6},{8,9},{9,8},{10,11... | collective-permute-start | bytes 393224 | tf_op jit(solution)/shard_map/ppermute | solution.py:651
  146.9 43.6 %collective-permute-start.11 = (f32[48,32,128]{2,1,0:T(8,128)}, f32[48,32,128]{2,1,0:T(8,128)S(1)}, u32[]{:S(2)}, u32[]{:S(2)}) collective-permute-start(f32[48,32,128]{2,1,0:T(8,128)} %get-tuple-element.95), channel_id=1, source_target_pairs={{0,16},{16,32},{32,48},{48,64},{64,80},{80,96},{96,112},{112,0},{1... | collective-permute-start | bytes 2359304 | tf_op jit(solution)/shard_map/ppermute | solution.py:651
  148.1 42.4 %collective-permute-start.12 = (f32[48,32,128]{2,1,0:T(8,128)}, f32[48,32,128]{2,1,0:T(8,128)S(1)}, u32[]{:S(2)}, u32[]{:S(2)}) collective-permute-start(f32[48,32,128]{2,1,0:T(8,128)} %get-tuple-element.96), channel_id=1, source_target_pairs={{0,112},{16,0},{32,16},{48,32},{64,48},{80,64},{96,80},{112,96},{1... | collective-permute-start | bytes 2359304 | tf_op jit(solution)/shard_map/ppermute | solution.py:651
  150.5 40.0 %collective-permute-start.13 = (f32[8,6,32,128]{3,2,1,0:T(8,128)}, f32[8,6,32,128]{3,2,1,0:T(8,128)S(1)}, u32[]{:S(2)}, u32[]{:S(2)}) collective-permute-start(f32[8,6,32,128]{3,2,1,0:T(8,128)} %get-tuple-element.97), channel_id=1, source_target_pairs={{0,2},{2,4},{4,6},{6,8},{8,10},{10,12},{12,14},{14,0},{1,3},{3,5},... | collective-permute-start | bytes 2359304 | tf_op jit(solution)/shard_map/ppermute | solution.py:651
  170.7 19.9 %collective-permute-start.14 = (f32[8,6,32,128]{3,2,1,0:T(8,128)}, f32[8,6,32,128]{3,2,1,0:T(8,128)}, u32[]{:S(2)}, u32[]{:S(2)}) collective-permute-start(f32[8,6,32,128]{3,2,1,0:T(8,128)} %get-tuple-element.98), channel_id=1, source_target_pairs={{0,14},{2,0},{4,2},{6,4},{8,6},{10,8},{12,10},{14,12},{1,15},{3,1}... | collective-permute-start | bytes 2359304 | tf_op jit(solution)/shard_map/ppermute | solution.py:651
  186.9 12.6 %all-to-all-start.5 = ((f32[16,40,128]{2,1,0:T(8,128)}), f32[16,40,128]{2,1,0:T(8,128)S(1)}, u32[]{:S(2)}, u32[]{:S(2)}) async-start(f32[16,40,128]{2,1,0:T(8,128)} %spread.6), calls=%async_computation.5 | async-start | bytes 655360 | tf_op jit(solution)/shard_map/all_to_all | solution.py:701
  190.5 1.0 copy-start.8
  210.4 5.6 %collective-permute-start.15 = (f32[256,128]{1,0:T(8,128)}, f32[256,128]{1,0:T(8,128)S(1)}, u32[]{:S(2)}, u32[]{:S(2)}) collective-permute-start(f32[256,128]{1,0:T(8,128)} %get-tuple-element.102), channel_id=1, source_target_pairs={{0,1},{1,0},{2,3},{3,2},{4,5},{5,4},{6,7},{7,6},{8,9},{9,8},{10,11... | collective-permute-start | bytes 393224 | tf_op jit(solution)/shard_map/ppermute | solution.py:651
  212.1 42.1 %collective-permute-start.16 = (f32[48,32,128]{2,1,0:T(8,128)}, f32[48,32,128]{2,1,0:T(8,128)S(1)}, u32[]{:S(2)}, u32[]{:S(2)}) collective-permute-start(f32[48,32,128]{2,1,0:T(8,128)} %get-tuple-element.106), channel_id=1, source_target_pairs={{0,16},{16,32},{32,48},{48,64},{64,80},{80,96},{96,112},{112,0},{1... | collective-permute-start | bytes 2359304 | tf_op jit(solution)/shard_map/ppermute | solution.py:651
  213.3 41.0 %collective-permute-start.17 = (f32[48,32,128]{2,1,0:T(8,128)}, f32[48,32,128]{2,1,0:T(8,128)S(1)}, u32[]{:S(2)}, u32[]{:S(2)}) collective-permute-start(f32[48,32,128]{2,1,0:T(8,128)} %get-tuple-element.107), channel_id=1, source_target_pairs={{0,112},{16,0},{32,16},{48,32},{64,48},{80,64},{96,80},{112,96},{1... | collective-permute-start | bytes 2359304 | tf_op jit(solution)/shard_map/ppermute | solution.py:651
  216.0 38.3 %collective-permute-start.18 = (f32[8,6,32,128]{3,2,1,0:T(8,128)}, f32[8,6,32,128]{3,2,1,0:T(8,128)S(1)}, u32[]{:S(2)}, u32[]{:S(2)}) collective-permute-start(f32[8,6,32,128]{3,2,1,0:T(8,128)} %get-tuple-element.108), channel_id=1, source_target_pairs={{0,2},{2,4},{4,6},{6,8},{8,10},{10,12},{12,14},{14,0},{1,3},{3,5},... | collective-permute-start | bytes 2359304 | tf_op jit(solution)/shard_map/ppermute | solution.py:651
  236.4 17.9 %collective-permute-start.19 = (f32[8,6,32,128]{3,2,1,0:T(8,128)}, f32[8,6,32,128]{3,2,1,0:T(8,128)}, u32[]{:S(2)}, u32[]{:S(2)}) collective-permute-start(f32[8,6,32,128]{3,2,1,0:T(8,128)} %get-tuple-element.109), channel_id=1, source_target_pairs={{0,14},{2,0},{4,2},{6,4},{8,6},{10,8},{12,10},{14,12},{1,15},{3,1}... | collective-permute-start | bytes 2359304 | tf_op jit(solution)/shard_map/ppermute | solution.py:651
  250.7 12.1 %all-to-all-start.7 = ((f32[16,40,128]{2,1,0:T(8,128)}), f32[16,40,128]{2,1,0:T(8,128)S(1)}, u32[]{:S(2)}, u32[]{:S(2)}) async-start(f32[16,40,128]{2,1,0:T(8,128)} %spread.7), calls=%async_computation.7 | async-start | bytes 655360 | tf_op jit(solution)/shard_map/all_to_all | solution.py:701
  254.3 1.0 copy-start.7
  (4 other events, 3.1 us)

commit v5 on v3

v5 whole, which is shorter than its diff:
```python
import functools

import jax
import jax.numpy as jnp
from jax import lax
from jax.experimental import pallas as pl
from jax.experimental.pallas import tpu as pltpu
from jax.sharding import PartitionSpec as P

DEGREE = 4
STENCIL = (
    -5369.0 / 1800.0,
    12.0 / 7.0,
    -15.0 / 56.0,
    10.0 / 189.0,
    -1.0 / 112.0,
    2.0 / 1925.0,
    -1.0 / 16632.0,
)
FILTER_CENTRE = 9.5
FILTER_HALF = 5.5
REACH = 6

NB = 32
SX = 8
SY = 8
SZ = 128
ROWS = SX * SY
PAIRS = ROWS // 2
FACE = REACH * SY
NPJ = 4
SLOTS = 8192
TGT = 40
CH = NPJ * TGT
GROUPS = ROWS // 4
TOTAL = (2 * CH, 2 * NB)
BATCH = 4
ZROWS = GROUPS * 16
LANES = 128
F32 = jnp.float32
BF16 = jnp.bfloat16
NN = (((1,), (0,)), ((), ()))
NT = (((1,), (1,)), ((), ()))
VMEM_LIMIT = 16 * 1024 * 1024


def dot(a, b, dims=NN):
    return lax.dot_general(a, b, dims, preferred_element_type=F32)


def split2(v):
    hi = v.astype(BF16)
    return hi, (v - hi.astype(F32)).astype(BF16)


def split3(v):
    hi = v.astype(BF16)
    rest = v - hi.astype(F32)
    mid = rest.astype(BF16)
    return hi, mid, (rest - mid.astype(F32)).astype(BF16)


def band(distance):
    found = jnp.zeros(distance.shape, F32)
    for m in range(1, REACH + 1):
        found = jnp.where(jnp.abs(distance) == m, -0.5 * STENCIL[m], found)
    return found


def write_z_matrices(first, second):
    source = lax.broadcasted_iota(jnp.int32, (SZ, SZ), 0)
    z = lax.broadcasted_iota(jnp.int32, (SZ, SZ), 1)
    inner_hi, inner_lo = split2(band(source - z))
    e = lax.broadcasted_iota(jnp.int32, (16, SZ), 0)
    z = lax.broadcasted_iota(jnp.int32, (16, SZ), 1)
    face_hi, face_lo = split2(band(jnp.where(e < 8, SZ + e - z, z + 16 - e)))
    first[...] = jnp.concatenate([inner_hi, inner_hi], axis=0)
    unused = jnp.zeros((SZ - 48, SZ), BF16)
    second[...] = jnp.concatenate([inner_lo, face_hi, face_hi, face_lo, unused], axis=0)


def any_specs(count):
    return [pl.BlockSpec(memory_space=pl.ANY)] * count


def vmem_specs(count):
    return [pl.BlockSpec(memory_space=pltpu.VMEM)] * count


PARAMS = pltpu.CompilerParams(vmem_limit_bytes=VMEM_LIMIT)


def z_faces(rows):
    turned = jnp.concatenate(rows, axis=0).T
    return jnp.concatenate([turned[:8], turned[SZ - 8 :]], axis=0)


BLOCK = jax.ShapeDtypeStruct((ROWS, NB, SZ), F32)
X_FACE = jax.ShapeDtypeStruct((FACE, NB, SZ), F32)
Y_FACE = jax.ShapeDtypeStruct((SX, REACH, NB, SZ), F32)
MESSAGE = jax.ShapeDtypeStruct((ZROWS + TGT, LANES), F32)
FRAME = jax.ShapeDtypeStruct((TGT, LANES), F32)
MATRIX = jax.ShapeDtypeStruct((PAIRS, 2 * CH, 2 * SZ), BF16)


def face_copies(x, field, x_low, x_high, y_low, y_high, sem):
    copies = [
        pltpu.make_async_copy(field.at[pl.ds(x * SY, REACH)], y_low.at[x], sem.at[0, x]),
        pltpu.make_async_copy(field.at[pl.ds(x * SY + SY - REACH, REACH)], y_high.at[x], sem.at[1, x]),
    ]
    return copies


def low_copy(x, field, x_low, sem):
    rows = pl.ds(x * SY, SY)
    return pltpu.make_async_copy(field.at[rows], x_low.at[rows], sem.at[2, x])


def high_copy(x, field, x_high, sem):
    to = pl.ds((x - (SX - REACH)) * SY, SY)
    return pltpu.make_async_copy(field.at[pl.ds(x * SY, SY)], x_high.at[to], sem.at[3, x])


def start_faces(x, field, outs, sem):
    x_low, x_high, y_low, y_high = outs
    for copy in face_copies(x, field, x_low, x_high, y_low, y_high, sem):
        copy.start()

    @pl.when(x < REACH)
    def _():
        low_copy(x, field, x_low, sem).start()

    @pl.when(x >= SX - REACH)
    def _():
        high_copy(x, field, x_high, sem).start()


def wait_faces(field, outs, sem):
    x_low, x_high, y_low, y_high = outs
    for x in range(SX):
        for copy in face_copies(x, field, x_low, x_high, y_low, y_high, sem):
            copy.wait()
        if x < REACH:
            low_copy(x, field, x_low, sem).wait()
        if x >= SX - REACH:
            high_copy(x, field, x_high, sem).wait()


def rearrange_kernel(src, *refs):
    field, outs, (z_face, in_sem, out_sem) = refs[0], refs[1:5], refs[5:]
    for row in range(ROWS):
        pltpu.make_async_copy(src.at[:, row, :], field.at[row], in_sem.at[row]).start()

    @pl.loop(0, SX)
    def _(x):
        for y in range(SY):
            row = x * SY + y
            pltpu.make_async_copy(src.at[:, row, :], field.at[row], in_sem.at[row]).wait()
        start_faces(x, field, outs, out_sem)
        for part in range(2):
            z_face[pl.ds((2 * x + part) * 16, 16), :] = z_faces(
                [field[x * SY + 4 * part + i] for i in range(4)]
            )

    wait_faces(field, outs, out_sem)


def rearrange(orbitals):
    return pl.pallas_call(
        rearrange_kernel,
        out_shape=[BLOCK, X_FACE, X_FACE, Y_FACE, Y_FACE, jax.ShapeDtypeStruct((ZROWS, LANES), F32)],
        in_specs=any_specs(1),
        out_specs=vmem_specs(6),
        scratch_shapes=[
            pltpu.SemaphoreType.DMA((ROWS,)),
            pltpu.SemaphoreType.DMA((4, SX)),
        ],
        compiler_params=PARAMS,
        name="rearrange",
    )(orbitals)


def build_kernel(starts, keys, w0, w1, w2, w3, out, held, weights, sem):
    full = pl.ds(0, SLOTS // LANES)
    loads = [pltpu.make_async_copy(keys, held.at[full], sem.at[NPJ])]
    for j, w in enumerate((w0, w1, w2, w3)):
        loads.append(pltpu.make_async_copy(w, weights.at[j, full], sem.at[j]))
    for load in loads:
        load.start()
    held[pl.ds(SLOTS // LANES, 8), :] = jnp.full((8, LANES), ROWS * SZ * 64, jnp.int32)
    for j in range(NPJ):
        weights[j, pl.ds(SLOTS // LANES, 8), :] = jnp.zeros((8, LANES), F32)
    for load in loads:
        load.wait()
    target_at = lax.broadcasted_iota(jnp.int32, (TGT, 2 * LANES), 0)
    z_at = lax.broadcasted_iota(jnp.int32, (SZ, 2 * LANES), 0)

    def window(row, block):
        key = jnp.concatenate([held[pl.ds(block, 1), :], held[pl.ds(block + 1, 1), :]], axis=1)
        target = jnp.where((key >> 13) == row, key & 63, 63)
        chosen = target_at == target
        parts = []
        for j in range(NPJ):
            w = jnp.concatenate(
                [weights[j, pl.ds(block, 1), :], weights[j, pl.ds(block + 1, 1), :]], axis=1
            )
            parts.append(jnp.where(chosen, w, 0.0))
        hi, lo = split2(jnp.concatenate(parts, axis=0))
        place = jnp.where(z_at == ((key >> 6) & 127), 1.0, 0.0).astype(BF16)
        both = dot(jnp.concatenate([hi, lo], axis=0), place, NT)
        return both[:CH] + both[CH:]

    @pl.loop(0, ROWS // BATCH)
    def _(step):
        first_row = step * BATCH
        bases = [starts[first_row + i] // LANES for i in range(BATCH)]
        for i in range(BATCH):
            hi, lo = split2(window(first_row + i, bases[i]))
            at = (step * (BATCH // 2) + i // 2, slice(None), pl.ds((i % 2) * SZ, SZ))
            out[at] = jnp.concatenate([hi, lo], axis=0)

        for i in range(BATCH):
            row = first_row + i
            windows = (starts[row + 1] - bases[i] * LANES + 2 * LANES - 1) // (2 * LANES)

            @pl.when(windows > 1)
            def _():
                total = lax.fori_loop(
                    0,
                    windows,
                    lambda k, acc: acc + window(row, bases[i] + 2 * k),
                    jnp.zeros((CH, SZ), F32),
                )
                hi, lo = split2(total)
                at = (step * (BATCH // 2) + i // 2, slice(None), pl.ds((i % 2) * SZ, SZ))
                out[at] = jnp.concatenate([hi, lo], axis=0)


def build(starts, keys, weights):
    return pl.pallas_call(
        build_kernel,
        out_shape=MATRIX,
        in_specs=[pl.BlockSpec(memory_space=pltpu.SMEM)] + any_specs(5),
        out_specs=pl.BlockSpec(memory_space=pltpu.VMEM),
        scratch_shapes=[
            pltpu.VMEM((SLOTS // LANES + 8, LANES), jnp.int32),
            pltpu.VMEM((NPJ, SLOTS // LANES + 8, LANES), F32),
            pltpu.SemaphoreType.DMA((NPJ + 1,)),
        ],
        compiler_params=PARAMS,
        name="build",
    )(starts, keys, *weights)


def partial_of(mat, values):
    hi, lo = split2(values)
    return dot(mat, jnp.concatenate([hi, lo], axis=0), NT)


def packed_partial(total):
    joined = total[:CH, :NB] + total[:CH, NB:] + total[CH:, :NB]
    return jnp.concatenate([joined[j * TGT : (j + 1) * TGT] for j in range(NPJ)], axis=1)


def first_kernel(field, mat, own, out, total):
    row = lax.broadcasted_iota(jnp.int32, (TGT, LANES), 0)
    couplings = jnp.where(row == 16, own[pl.ds(0, 1), :], jnp.where(row == 17, own[pl.ds(1, 1), :], 0.0))
    out[pl.ds(TGT, TGT), :] = couplings
    total[...] = jnp.zeros_like(total)

    @pl.loop(0, SX)
    def _(x):
        acc = total[...]
        for p in range(4):
            at = x * SY + 2 * p
            values = jnp.concatenate([field[at], field[at + 1]], axis=1)
            acc = acc + partial_of(mat[x * 4 + p], values)
        total[...] = acc

    out[pl.ds(0, TGT), :] = packed_partial(total[...])


def first(field, mat, own):
    return pl.pallas_call(
        first_kernel,
        out_shape=jax.ShapeDtypeStruct((2 * TGT, LANES), F32),
        in_specs=vmem_specs(3),
        out_specs=pl.BlockSpec(memory_space=pltpu.VMEM),
        scratch_shapes=[pltpu.VMEM(TOTAL, F32)],
        compiler_params=PARAMS,
        name="first",
    )(field, mat, own)


def spread(frame, axis, stride, out, at):
    me = lax.axis_index(axis)
    row = lax.broadcasted_iota(jnp.int32, (TGT, LANES), 0)
    digit = (row // stride) % 3
    for distance in range(-3, 5):
        if abs(distance) > 2:
            piece = jnp.zeros((TGT, LANES), F32)
        else:
            moved = frame if distance == 0 else pltpu.roll(frame, (-stride * distance) % TGT, 0)
            valid = (digit + distance >= 0) & (digit + distance <= 2) & (row < 36)
            piece = jnp.where(valid, moved, 0.0)
        out[(me + distance + 8) % 8, at, :] = piece


def spread_zy_kernel(frames, mine, other, out):
    row = lax.broadcasted_iota(jnp.int32, (TGT, LANES), 0)
    start = mine.shape[0] - frames * TGT
    for f in range(frames):
        at = pl.ds(start + f * TGT, TGT)
        theirs = other[at, :]
        swapped = jnp.where(row & 2 == 0, pltpu.roll(theirs, TGT - 2, 0), pltpu.roll(theirs, 2, 0))
        spread(mine[at, :] + swapped, "gy", 4, out, pl.ds(f * TGT, TGT))


def spread_x_kernel(frames, came, out):
    for f in range(frames):
        at = pl.ds(f * TGT, TGT)
        frame = came[0, at, :]
        for slot in range(1, 8):
            frame = frame + came[slot, at, :]
        spread(frame, "gx", 12, out, at)


def spread_call(kernel, frames, *arrays):
    return pl.pallas_call(
        functools.partial(kernel, frames),
        out_shape=jax.ShapeDtypeStruct((8, frames * TGT, LANES), F32),
        in_specs=vmem_specs(len(arrays)),
        out_specs=pl.BlockSpec(memory_space=pltpu.VMEM),
        compiler_params=PARAMS,
        name="spread",
    )(*arrays)


def step_kernel(first_step, last_step, *refs):
    count = 9 if first_step else 11
    field, faces, x_left, x_right, y_left, y_right, potential, came, mat = refs[:9]
    if not first_step:
        previous, coupling = refs[9:11]
    refs = refs[count:]
    if last_step:
        (new, gram), refs = refs[:2], refs[2:]
    else:
        (new, x_low, x_high, y_low, y_high, message), refs = refs[:6], refs[6:]
        outs = (x_low, x_high, y_low, y_high)
        if first_step:
            coupling, refs = refs[0], refs[1:]
    total, coef, first_z, second_z, out_sem = refs
    alpha = (1.0 if first_step else 2.0) / FILTER_HALF
    half = [0.0] + [-0.5 * c for c in STENCIL[1:]]
    diagonal = -1.5 * STENCIL[0] - FILTER_CENTRE
    write_z_matrices(first_z, second_z)

    def at(x, y):
        if x < 0:
            return x_left[(x + REACH) * SY + y]
        if x >= SX:
            return x_right[(x - SX) * SY + y]
        if y < 0:
            return y_left[x, y + REACH]
        if y >= SY:
            return y_right[x, y - SY]
        return field[x * SY + y]

    for g in range(GROUPS):
        rows = [field[4 * g + i] for i in range(4)]
        hi, lo = split2(jnp.concatenate(rows, axis=0))
        face = faces[pl.ds(g * 16, 16), :]
        face_hi = face.astype(BF16).astype(F32)
        side = jnp.concatenate(
            [face_hi, face - face_hi, face_hi, jnp.zeros((LANES - 48, LANES), F32)], axis=0
        ).T.astype(BF16)
        along_z = dot(jnp.concatenate([hi, lo], axis=1), first_z[...]) + dot(
            jnp.concatenate([hi, side], axis=1), second_z[...]
        )
        for i in range(4):
            x, y = divmod(4 * g + i, SY)
            summed = along_z[i * NB : (i + 1) * NB]
            for m in range(1, REACH + 1):
                around = (at(x + m, y) + at(x - m, y)) + (at(x, y + m) + at(x, y - m))
                summed = summed + half[m] * around
            summed = summed + (potential[pl.ds(4 * g + i, 1), :] + diagonal) * rows[i]
            result = alpha * summed
            if not first_step:
                result = result - previous[4 * g + i]
            new[4 * g + i] = result

    total[...] = jnp.zeros_like(total)
    frame = came[0]
    for slot in range(1, came.shape[0]):
        frame = frame + came[slot]
    if first_step:
        coupling[...] = frame[TGT:]
        frame = frame[:TGT]
    frame = frame * (alpha * coupling[...])
    stacked = jnp.concatenate([frame[:, j * NB : (j + 1) * NB] for j in range(NPJ)], axis=0)
    turned = stacked.T
    coef_hi = turned.astype(BF16).astype(F32)
    coef[pl.ds(0, NB), :] = jnp.concatenate([coef_hi, coef_hi], axis=1).astype(BF16)
    coef[pl.ds(NB, NB), pl.ds(0, CH)] = (turned - coef_hi).astype(BF16)

    @pl.loop(0, SX)
    def _(x):
        c_hi = coef[pl.ds(0, NB), :]
        c_lo = coef[pl.ds(NB, NB), pl.ds(0, CH)]
        acc = total[...]
        rows = []
        for p in range(4):
            pair_mat = mat[x * 4 + p]
            added = dot(c_hi, pair_mat) + dot(c_lo, pair_mat[:CH])
            for q in range(2):
                here = x * SY + 2 * p + q
                rows.append(new[here] + added[:, q * SZ : (q + 1) * SZ])
                new[here] = rows[-1]
        if not last_step:
            start_faces(x, new, outs, out_sem)
        for p in range(4):
            values = jnp.concatenate(rows[2 * p : 2 * p + 2], axis=1)
            if last_step:
                joined = jnp.concatenate(split3(values), axis=0)
                acc = acc + dot(joined, joined, NT)
            else:
                acc = acc + partial_of(mat[x * 4 + p], values)
        total[...] = acc
        if not last_step:
            for part in range(2):
                message[pl.ds((2 * x + part) * 16, 16), :] = z_faces(rows[4 * part : 4 * part + 4])

    if last_step:
        t = total[...]
        summed = t[2 * NB :, :NB] + t[:NB, 2 * NB :] + t[NB : 2 * NB, NB : 2 * NB]
        summed = summed + (t[NB : 2 * NB, :NB] + t[:NB, NB : 2 * NB]) + t[:NB, :NB]
        gram[...] = jnp.concatenate([summed[8 * q : 8 * q + 8] for q in range(4)], axis=1)
    else:
        message[pl.ds(ZROWS, TGT), :] = packed_partial(total[...])
        wait_faces(new, outs, out_sem)


def step(first_step, last_step, *arrays):
    total = (3 * NB, 3 * NB) if last_step else TOTAL
    if last_step:
        outs = [BLOCK, jax.ShapeDtypeStruct((8, LANES), F32)]
    else:
        outs = [BLOCK, X_FACE, X_FACE, Y_FACE, Y_FACE, MESSAGE] + ([FRAME] if first_step else [])
    return pl.pallas_call(
        functools.partial(step_kernel, first_step, last_step),
        out_shape=outs,
        in_specs=vmem_specs(len(arrays)),
        out_specs=vmem_specs(len(outs)),
        scratch_shapes=[
            pltpu.VMEM(total, F32),
            pltpu.VMEM((2 * NB, 2 * CH), BF16),
            pltpu.VMEM((2 * SZ, SZ), BF16),
            pltpu.VMEM((2 * SZ, SZ), BF16),
            pltpu.SemaphoreType.DMA((4, SX)),
        ],
        compiler_params=PARAMS,
        name="step",
    )(*arrays)


def finish_kernel(scale, field, grams, out, made, inverse, out_sem):
    packed = grams[0]
    for slot in range(1, grams.shape[0]):
        packed = packed + grams[slot]
    packed = packed * scale
    gram = jnp.concatenate([packed[:, q * NB : (q + 1) * NB] for q in range(4)], axis=0)
    row = lax.broadcasted_iota(jnp.int32, (NB, NB), 0)
    column = lax.broadcasted_iota(jnp.int32, (NB, NB), 1)
    eye = jnp.where(row == column, 1.0, 0.0)
    work = jnp.concatenate([gram, eye], axis=1)
    below = lax.broadcasted_iota(jnp.int32, (NB, 2 * NB), 0)
    for k in range(NB):
        root = 1.0 / jnp.sqrt(work[k : k + 1, k : k + 1])
        line = work[k : k + 1, :] * root
        inverse[pl.ds(k, 1), :] = line[:, NB:]
        if k < NB - 1:
            factor = work[:, k : k + 1] * root
            work = work - jnp.where(below > k, factor * line, 0.0)
    hi, mid, lo = split3(inverse[...])
    left = jnp.concatenate([lo, mid, hi, mid, hi, hi], axis=1)

    @pl.loop(0, SX)
    def _(x):
        for p in range(SY // 2):
            at = x * SY + 2 * p
            values = jnp.concatenate([field[at], field[at + 1]], axis=1)
            f_hi, f_mid, f_lo = split3(values)
            right = jnp.concatenate([f_hi, f_mid, f_lo, f_hi, f_mid, f_hi], axis=0)
            result = dot(left, right)
            made[at] = result[:, :SZ]
            made[at + 1] = result[:, SZ:]
            for q in range(2):
                pltpu.make_async_copy(made.at[at + q], out.at[:, at + q, :], out_sem.at[at + q]).start()

    for r in range(ROWS):
        pltpu.make_async_copy(made.at[r], out.at[:, r, :], out_sem.at[r]).wait()


def finish(scale, field, grams):
    return pl.pallas_call(
        functools.partial(finish_kernel, scale),
        out_shape=jax.ShapeDtypeStruct((NB, ROWS, SZ), F32),
        in_specs=vmem_specs(2),
        out_specs=pl.BlockSpec(memory_space=pl.ANY),
        scratch_shapes=[
            pltpu.VMEM((ROWS, NB, SZ), F32),
            pltpu.VMEM((NB, NB), F32),
            pltpu.SemaphoreType.DMA((ROWS,)),
        ],
        compiler_params=PARAMS,
        name="finish",
    )(field, grams)


def shift(value, axis, by):
    count = lax.axis_size(axis)
    return lax.ppermute(value, axis, [(i, (i + by) % count) for i in range(count)])


def local(orbitals, potential, projector, point_cell, target, point_count, coupling):
    bands, size_x, size_y, size_z = orbitals.shape
    field, x_low, x_high, y_low, y_high, z_face = rearrange(orbitals.reshape(NB, ROWS, SZ))
    pot = potential.reshape(ROWS, SZ)

    alive = lax.iota(jnp.int32, SLOTS) < point_count.reshape(())
    code = target // 2
    z_other = (code % 3 != 1).astype(jnp.int32)
    wanted = ((code // 3) * 2 + z_other) * 2 + target % 2
    key = jnp.where(alive, point_cell * 64 + wanted, ROWS * SZ * 64)
    starts = jnp.sum(
        (key[None, :] < (lax.iota(jnp.int32, ROWS + 1) * (SZ * 64))[:, None]).astype(jnp.int32), axis=1
    )
    ordered = lax.sort((key,) + tuple(projector[j] for j in range(NPJ)), num_keys=1, is_stable=False)
    ordered = [o.reshape(SLOTS // LANES, LANES) for o in ordered]
    mat = build(starts, ordered[0], ordered[1:])

    own = jnp.repeat(coupling, NB, axis=1)
    other = ()
    for k in range(DEGREE):
        start, last = k == 0, k == DEGREE - 1
        if start:
            faces = shift(z_face, "gz", 1)
        else:
            came = shift(message, "gz", 1)
            came, x_low, x_high, y_low, y_high = lax.optimization_barrier(
                (came, x_low, x_high, y_low, y_high)
            )
            faces = came
        x_left = shift(x_high, "gx", 1)
        x_right = shift(x_low, "gx", -1)
        y_left = shift(y_high, "gy", 1)
        y_right = shift(y_low, "gy", -1)
        if start:
            mat, field, faces, x_left, x_right, y_left, y_right = lax.optimization_barrier(
                (mat, field, faces, x_left, x_right, y_left, y_right)
            )
            message = first(field, mat, own)
            came = shift(message, "gz", 1)
        frames = 2 if start else 1
        sends = spread_call(spread_zy_kernel, frames, message, came)
        came = lax.all_to_all(sends, "gy", 0, 0)
        sends = spread_call(spread_x_kernel, frames, came)
        came = lax.all_to_all(sends, "gx", 0, 0)
        outs = step(start, last, field, faces, x_left, x_right, y_left, y_right, pot, came, mat, *other)
        previous = field
        if last:
            field, gram = outs
        else:
            field, x_low, x_high, y_low, y_high, message = outs[:6]
            if start:
                scales = outs[6]
            other = (previous, scales)
    axes = ("gx", "gy", "gz")
    devices = 1
    for axis in axes:
        devices *= lax.axis_size(axis)
    grams = lax.all_to_all(jnp.broadcast_to(gram[None], (devices,) + gram.shape), axes, 0, 0)
    result = finish(1.0 / float(devices * ROWS * SZ), field, grams)
    return result.reshape(bands, size_x, size_y, size_z)


def solution(mesh):
    in_specs = (
        P(None, "gx", "gy", "gz"),
        P("gx", "gy", "gz"),
        P(None, ("gx", "gy", "gz")),
        P(("gx", "gy", "gz")),
        P(("gx", "gy", "gz")),
        P("gx", "gy", "gz"),
        P(("gx", "gy", "gz"), None),
    )
    out_specs = P(None, "gx", "gy", "gz")
    return jax.shard_map(local, mesh=mesh, in_specs=in_specs, out_specs=out_specs, check_vma=False)
```

time: 267 us -> 253 us (0.948)
  blocking collectives: 54.4 us -> 109 us
  local copies, waits for them, and re-layouts: 39.3 us -> 7.87 us
  starting transfers between devices: 58.2 us -> 34.2 us
  waiting for transfers between devices: 32.1 us -> 20.2 us
    all_to_all x0 -> x4, blocking collectives: none -> 35.1 us  [local(): came = lax.all_to_all(sends, 'gx', 0, 0)]
    unnamed x88 -> x14, local copies, waits for them, and re-layouts: 36.5 us -> 5.02 us
    all_to_all x5 -> x0, starting transfers between devices: 20.6 us -> none  [the longest x4 15.1 us: local(): came = lax.all_to_all(sends, ('gx', 'gz'), 0, 0)]
    all_to_all x3 -> x4, blocking collectives: 34.4 us -> 54.8 us  [local(): came = lax.all_to_all(sends, 'gy', 0, 0)]
    all_to_all x5 -> x0, waiting for transfers between devices: 11.4 us -> none  [the longest x1 7.06 us: local(): came = lax.all_to_all(sends, 'gy', 0, 0)]
    pallas_call x8, Pallas kernels: 6.44 us -> 0.42 us  [spread_call(): pl.pallas_call(functools.partial(kernel, frames), out_shape=jax.ShapeDtyp...]
    pallas_call x1, Pallas kernels: 3.76 us -> 8.65 us  [rearrange(): pl.pallas_call(rearrange_kernel, out_shape=[BLOCK, X_FACE, X_FACE, Y_FACE...]
    ppermute x20 -> x21, starting transfers between devices: 37.5 us -> 34.2 us  [shift(): lax.ppermute(value, axis, [(i, (i + by) % count) for i in range(count)])]
  transfers between devices with their start and end apart: 25 -> 21, of which waited for: 5 -> 4; matrix products, arithmetic and copies ran while one was open for 5% -> 5% of each run, Pallas kernels for 10% -> 3%
where the time goes in v5:
time: 253 us; the launch traced here: 251 us
  blocking collectives  109 us (43%)
  Pallas kernels  68.2 us (27%)
  starting transfers between devices  34.2 us (14%)
  waiting for transfers between devices  20.2 us (8%)
  other arithmetic  9.94 us (4%)
  local copies, waits for them, and re-layouts  7.87 us (3%)
    all_to_all x4, blocking collectives, local(): came = lax.all_to_all(sends, 'gy', 0, 0)  54.8 us
    pallas_call x4, Pallas kernels, step(): pl.pallas_call(functools.partial(step_kernel, first_step, last_step), out...  43.1 us
    all_to_all x4, blocking collectives, local(): came = lax.all_to_all(sends, 'gx', 0, 0)  35.1 us
    ppermute x21, starting transfers between devices, shift(): lax.ppermute(value, axis, [(i, (i + by) % count) for i in range(count)])  34.2 us
    ppermute x21, waiting for transfers between devices, shift(): lax.ppermute(value, axis, [(i, (i + by) % count) for i in range(count)])  20.2 us
    all_to_all x1, blocking collectives, local(): lax.all_to_all(jnp.broadcast_to(gram[None], (devices,) + gram.shape), axe...  19.3 us
    pallas_call x1, Pallas kernels, rearrange(): pl.pallas_call(rearrange_kernel, out_shape=[BLOCK, X_FACE, X_FACE, Y_FACE...  8.65 us
    pallas_call x1, Pallas kernels, build(): pl.pallas_call(build_kernel, out_shape=MATRIX, in_specs=[pl.BlockSpec(mem...  7.43 us
  transfers between devices with their start and end apart: 21, of which 4 were waited for; matrix products, arithmetic and copies ran while one was open for 5% of the time, Pallas kernels for 3%

profile of v5, /device:TPU:1, one launch (start us, length us, event | category | flops | bytes accessed | tf_op | source)
XLA Modules:
  0.0 250.6 jit_solution(15775477991558191366)
XLA Ops:
  1.2 8.7 %rearrange.1 = (f32[64,32,128]{2,1,0:T(8,128)S(1)}, f32[48,32,128]{2,1,0:T(8,128)}, f32[48,32,128]{2,1,0:T(8,128)}, f32[8,6,32,128]{3,2,1,0:T(8,128)}, f32[8,6,32,128]{3,2,1,0:T(8,128)}, /*index=5*/f32[256,128]{1,0:T(8,128)}) custom-call(f32[32,64,128]{2,1,0:T(8,128)S(1)} %bitcast.14), custom_call_target="tpu_custom_call" | custom-call | tf_op jit(solution)/shard_map/rearrange/pallas_call | solution.py:169
  9.9 4.5 %collective-permute-start = (f32[256,128]{1,0:T(8,128)}, f32[256,128]{1,0:T(8,128)S(1)}, u32[]{:S(2)}, u32[]{:S(2)}) collective-permute-start(f32[256,128]{1,0:T(8,128)} %get-tuple-element.65), channel_id=1, source_target_pairs={{0,1},{1,0},{2,3},{3,2},{4,5},{5,4},{6,7},{7,6},{8,9},{9,8},{10,11... | collective-permute-start | bytes 393224 | tf_op jit(solution)/shard_map/ppermute | solution.py:522
  15.7 2.3 collective-permute-start.2
  18.0 2.6 %collective-permute-start.3 = (f32[8,6,32,128]{3,2,1,0:T(8,128)}, f32[8,6,32,128]{3,2,1,0:T(8,128)S(1)}, u32[]{:S(2)}, u32[]{:S(2)}) collective-permute-start(f32[8,6,32,128]{3,2,1,0:T(8,128)} %get-tuple-element.68), channel_id=1, source_target_pairs={{0,2},{2,4},{4,6},{6,8},{8,10},{10,12},{12,14},{14,0},{1,3},{3,5},... | collective-permute-start | bytes 2359304 | tf_op jit(solution)/shard_map/ppermute | solution.py:522
  20.6 2.0 fusion.9
  25.5 7.3 %sort.33 = (s32[8192]{0:T(1024)}, f32[8192]{0:T(1024)}, f32[8192]{0:T(1024)}, f32[8192]{0:T(1024)}, f32[8192]{0:T(1024)}) sort(s32[8192]{0:T(1024)} %fusion.5, f32[8192]{0:T(1024)} %bitcast.26, f32[8192]{0:T(1024)} %bitcast.25, f32[8192]{0:T(1024)} %bitcast.27, f32[8192]{0:T(1024)} %bitcast.24), dimensions={0}, to_apply=%region_1.2 | sort | flops 106496 | bytes 327680 | tf_op jit(solution)/shard_map/sort | solution.py:538
  37.8 7.4 %build.1.mat.refs_8_ = bf16[32,320,256]{2,1,0:T(8,128)(2,1)S(1)} custom-call(s32[65]{0:T(128)S(1)} %convert_reduce_fusion.starts, s32[64,128]{1,0:T(8,128)S(1)} %bitcast.19, f32[64,128]{1,0:T(8,128)S(1)} %bitcast.20, f32[64,128]{1,0:T(8,128)S(1)} %bitcast.21, f32[64,128]{1,0:T(8,128)S(1)} %bitcast.22, f32[64,128]{1,0:T(8,128)S(1)} %bitcast.23), custom_call_target="tpu_custom_call" | custom-call | tf_op jit(solution)/shard_map/build/pallas_call | solution.py:240
  45.3 2.7 %first.1.mine = f32[80,128]{1,0:T(8,128)S(1)} custom-call(f32[64,32,128]{2,1,0:T(8,128)S(1)} %get-tuple-element.70.field.refs_0_.refs_9_, bf16[32,320,256]{2,1,0:T(8,128)(2,1)S(1)} %build.1.mat.refs_8_, f32[2,128]{1,0:T(2,128)S(1)} %reshape.44.own), custom_call_target="tpu_custom_call" | custom-call | tf_op jit(solution)/shard_map/first/pallas_call | solution.py:284
  48.3 4.2 %collective-permute-done.5.other = f32[80,128]{1,0:T(8,128)S(1)} collective-permute-done((f32[80,128]{1,0:T(8,128)S(1)}, f32[80,128]{1,0:T(8,128)S(1)}, u32[]{:S(2)}, u32[]{:S(2)}) %collective-permute-start.5) | collective-permute-done | bytes 40992 | tf_op jit(solution)/shard_map/ppermute | solution.py:522
  52.5 13.8 %all_to_all.45.came = f32[8,80,128]{2,1,0:T(8,128)S(1)} all-to-all(f32[8,80,128]{2,1,0:T(8,128)S(1)} %spread.8), channel_id=1, replica_groups=mesh['gx'=8,'gy'=8,'gz'=2] {'gy'}, dimensions={0} | all-to-all | bytes 655360 | tf_op jit(solution)/shard_map/all_to_all | solution.py:566
  66.4 10.2 %all_to_all.46.refs_7_ = f32[8,80,128]{2,1,0:T(8,128)S(1)} all-to-all(f32[8,80,128]{2,1,0:T(8,128)S(1)} %spread.9), channel_id=1, replica_groups=mesh['gx'=8,'gy'=8,'gz'=2] {'gx'}, dimensions={0} | all-to-all | bytes 655360 | tf_op jit(solution)/shard_map/all_to_all | solution.py:568
  76.6 12.4 %step.4 = (f32[64,32,128]{2,1,0:T(8,128)S(1)}, f32[48,32,128]{2,1,0:T(8,128)S(1)}, f32[48,32,128]{2,1,0:T(8,128)S(1)}, f32[8,6,32,128]{3,2,1,0:T(8,128)S(1)}, f3...) custom-call(f32[64,32,128]{2,1,0:T(8,128)S(1)} %get-tuple-element.70.field.refs_0_.refs_9_, ...), custom_call_target="tpu_custom_call" | custom-call | tf_op jit(solution)/shard_map/step/pallas_call | solution.py:449
  89.3 5.5 %collective-permute-done.6.other.refs_1_ = f32[296,128]{1,0:T(8,128)S(1)} collective-permute-done((f32[296,128]{1,0:T(8,128)S(1)}, f32[296,128]{1,0:T(8,128)S(1)}, u32[]{:S(2)}, u32[]{:S(2)}) %collective-permute-start.6) | collective-permute-done | bytes 151584 | tf_op jit(solution)/shard_map/ppermute | solution.py:522
  94.8 3.6 %collective-permute-start.8 = (f32[48,32,128]{2,1,0:T(8,128)S(1)}, f32[48,32,128]{2,1,0:T(8,128)S(1)}, u32[]{:S(2)}, u32[]{:S(2)}) collective-permute-start(f32[48,32,128]{2,1,0:T(8,128)S(1)} %get-tuple-element.85), channel_id=1, source_target_pairs={{0,112},{16,0},{32,16},{48,32},{64,48},{80,64},{96,80},{112,96},{1... | collective-permute-start | bytes 2359304 | tf_op jit(solution)/shard_map/ppermute | solution.py:522
  98.4 3.1 %collective-permute-start.9 = (f32[8,6,32,128]{3,2,1,0:T(8,128)S(1)}, f32[8,6,32,128]{3,2,1,0:T(8,128)S(1)}, u32[]{:S(2)}, u32[]{:S(2)}) collective-permute-start(f32[8,6,32,128]{3,2,1,0:T(8,128)S(1)} %get-tuple-element.86), channel_id=1, source_target_pairs={{0,2},{2,4},{4,6},{6,8},{8,10},{10,12},{12,14},{14,0},{1,3},{3,5},... | collective-permute-start | bytes 2359304 | tf_op jit(solution)/shard_map/ppermute | solution.py:522
  101.6 13.5 %all_to_all.47.came = f32[8,40,128]{2,1,0:T(8,128)S(1)} all-to-all(f32[8,40,128]{2,1,0:T(8,128)S(1)} %spread.10), channel_id=1, replica_groups=mesh['gx'=8,'gy'=8,'gz'=2] {'gy'}, dimensions={0} | all-to-all | bytes 327680 | tf_op jit(solution)/shard_map/all_to_all | solution.py:566
  115.2 8.1 %all_to_all.48.refs_7_ = f32[8,40,128]{2,1,0:T(8,128)S(1)} all-to-all(f32[8,40,128]{2,1,0:T(8,128)S(1)} %spread.11), channel_id=1, replica_groups=mesh['gx'=8,'gy'=8,'gz'=2] {'gx'}, dimensions={0} | all-to-all | bytes 327680 | tf_op jit(solution)/shard_map/all_to_all | solution.py:568
  123.3 11.9 %step.5 = (f32[64,32,128]{2,1,0:T(8,128)S(1)}, f32[48,32,128]{2,1,0:T(8,128)S(1)}, f32[48,32,128]{2,1,0:T(8,128)S(1)}, f32[8,6,32,128]{3,2,1,0:T(8,128)S(1)}, f3...) custom-call(f32[64,32,128]{2,1,0:T(8,128)S(1)} %get-tuple-element.77.refs_0_.refs_9_, ...), custom_call_target="tpu_custom_call" | custom-call | tf_op jit(solution)/shard_map/step/pallas_call | solution.py:449
  135.9 5.0 %collective-permute-done.11.other.refs_1_ = f32[296,128]{1,0:T(8,128)S(1)} collective-permute-done((f32[296,128]{1,0:T(8,128)S(1)}, f32[296,128]{1,0:T(8,128)S(1)}, u32[]{:S(2)}, u32[]{:S(2)}) %collective-permute-start.11) | collective-permute-done | bytes 151584 | tf_op jit(solution)/shard_map/ppermute | solution.py:522
  141.4 3.0 %collective-permute-start.13 = (f32[48,32,128]{2,1,0:T(8,128)S(1)}, f32[48,32,128]{2,1,0:T(8,128)S(1)}, u32[]{:S(2)}, u32[]{:S(2)}) collective-permute-start(f32[48,32,128]{2,1,0:T(8,128)S(1)} %get-tuple-element.97), channel_id=1, source_target_pairs={{0,112},{16,0},{32,16},{48,32},{64,48},{80,64},{96,80},{112,96},{1... | collective-permute-start | bytes 2359304 | tf_op jit(solution)/shard_map/ppermute | solution.py:522
  144.4 4.1 %collective-permute-start.14 = (f32[8,6,32,128]{3,2,1,0:T(8,128)S(1)}, f32[8,6,32,128]{3,2,1,0:T(8,128)S(1)}, u32[]{:S(2)}, u32[]{:S(2)}) collective-permute-start(f32[8,6,32,128]{3,2,1,0:T(8,128)S(1)} %get-tuple-element.98), channel_id=1, source_target_pairs={{0,2},{2,4},{4,6},{6,8},{8,10},{10,12},{12,14},{14,0},{1,3},{3,5},... | collective-permute-start | bytes 2359304 | tf_op jit(solution)/shard_map/ppermute | solution.py:522
  148.6 14.7 %all_to_all.49.came = f32[8,40,128]{2,1,0:T(8,128)S(1)} all-to-all(f32[8,40,128]{2,1,0:T(8,128)S(1)} %spread.12), channel_id=1, replica_groups=mesh['gx'=8,'gy'=8,'gz'=2] {'gy'}, dimensions={0} | all-to-all | bytes 327680 | tf_op jit(solution)/shard_map/all_to_all | solution.py:566
  163.3 8.7 %all_to_all.50.refs_7_ = f32[8,40,128]{2,1,0:T(8,128)S(1)} all-to-all(f32[8,40,128]{2,1,0:T(8,128)S(1)} %spread.13), channel_id=1, replica_groups=mesh['gx'=8,'gy'=8,'gz'=2] {'gx'}, dimensions={0} | all-to-all | bytes 327680 | tf_op jit(solution)/shard_map/all_to_all | solution.py:568
  172.0 11.9 %step.6 = (f32[64,32,128]{2,1,0:T(8,128)S(1)}, f32[48,32,128]{2,1,0:T(8,128)S(1)}, f32[48,32,128]{2,1,0:T(8,128)S(1)}, f32[8,6,32,128]{3,2,1,0:T(8,128)S(1)}, f3...) custom-call(f32[64,32,128]{2,1,0:T(8,128)S(1)} %get-tuple-element.89.refs_0_.refs_9_, ...), custom_call_target="tpu_custom_call" | custom-call | tf_op jit(solution)/shard_map/step/pallas_call | solution.py:449
  184.5 5.5 %collective-permute-done.16.other.refs_1_ = f32[296,128]{1,0:T(8,128)S(1)} collective-permute-done((f32[296,128]{1,0:T(8,128)S(1)}, f32[296,128]{1,0:T(8,128)S(1)}, u32[]{:S(2)}, u32[]{:S(2)}) %collective-permute-start.16) | collective-permute-done | bytes 151584 | tf_op jit(solution)/shard_map/ppermute | solution.py:522
  190.1 3.6 %collective-permute-start.18 = (f32[48,32,128]{2,1,0:T(8,128)S(1)}, f32[48,32,128]{2,1,0:T(8,128)S(1)}, u32[]{:S(2)}, u32[]{:S(2)}) collective-permute-start(f32[48,32,128]{2,1,0:T(8,128)S(1)} %get-tuple-element.108), channel_id=1, source_target_pairs={{0,112},{16,0},{32,16},{48,32},{64,48},{80,64},{96,80},{112,96},{1... | collective-permute-start | bytes 2359304 | tf_op jit(solution)/shard_map/ppermute | solution.py:522
  193.6 3.6 %collective-permute-start.19 = (f32[8,6,32,128]{3,2,1,0:T(8,128)S(1)}, f32[8,6,32,128]{3,2,1,0:T(8,128)S(1)}, u32[]{:S(2)}, u32[]{:S(2)}) collective-permute-start(f32[8,6,32,128]{3,2,1,0:T(8,128)S(1)} %get-tuple-element.109), channel_id=1, source_target_pairs={{0,2},{2,4},{4,6},{6,8},{8,10},{10,12},{12,14},{14,0},{1,3},{3,5},... | collective-permute-start | bytes 2359304 | tf_op jit(solution)/shard_map/ppermute | solution.py:522
  197.3 12.8 %all_to_all.51.came = f32[8,40,128]{2,1,0:T(8,128)S(1)} all-to-all(f32[8,40,128]{2,1,0:T(8,128)S(1)} %spread.14), channel_id=1, replica_groups=mesh['gx'=8,'gy'=8,'gz'=2] {'gy'}, dimensions={0} | all-to-all | bytes 327680 | tf_op jit(solution)/shard_map/all_to_all | solution.py:566
  210.1 8.1 %all_to_all.52.refs_7_ = f32[8,40,128]{2,1,0:T(8,128)S(1)} all-to-all(f32[8,40,128]{2,1,0:T(8,128)S(1)} %spread.15), channel_id=1, replica_groups=mesh['gx'=8,'gy'=8,'gz'=2] {'gx'}, dimensions={0} | all-to-all | bytes 327680 | tf_op jit(solution)/shard_map/all_to_all | solution.py:568
  218.3 6.9 %step.7 = (f32[64,32,128]{2,1,0:T(8,128)S(1)}, f32[8,128]{1,0:T(8,128)S(1)}) custom-call(f32[64,32,128]{2,1,0:T(8,128)S(1)} %get-tuple-element.100.refs_0_, f32[296,128]{1,0:T(8,128)S(1)} %collective-permute-done.16.other.refs_1_, f32[48,32,128]{2,1,0:T(8,128)S(1)} %collective-permute-done.17.refs_2_, f32[48,32,128]{2,1,0:T(8,128)S(1)} %collective-permute-done.18.refs_3_, ...), custom_call_target="tpu_custom_call" | custom-call | tf_op jit(solution)/shard_map/step/pallas_call | solution.py:449
  225.2 19.3 %all_to_all.53.grams = f32[128,8,128]{2,1,0:T(8,128)S(1)} all-to-all(f32[128,8,128]{2,1,0:T(8,128)S(1)} %broadcast_in_dim.17), channel_id=1, replica_groups=mesh['gx'=8,'gy'=8,'gz'=2] {'gx','gy','gz'}, dimensions={0} | all-to-all | bytes 1048576 | tf_op jit(solution)/shard_map/all_to_all | solution.py:582
  244.4 6.0 %finish.1 = f32[32,64,128]{2,1,0:T(8,128)} custom-call(f32[64,32,128]{2,1,0:T(8,128)S(1)} %get-tuple-element.111.field, f32[128,8,128]{2,1,0:T(8,128)S(1)} %all_to_all.53.grams), custom_call_target="tpu_custom_call" | custom-call | tf_op jit(solution)/shard_map/finish/pallas_call | solution.py:505
  (57 shorter events, 12.7 us)
Async XLA Ops:
  0.0 1.2 copy-start
  9.9 35.3 %collective-permute-start = (f32[256,128]{1,0:T(8,128)}, f32[256,128]{1,0:T(8,128)S(1)}, u32[]{:S(2)}, u32[]{:S(2)}) collective-permute-start(f32[256,128]{1,0:T(8,128)} %get-tuple-element.65), channel_id=1, source_target_pairs={{0,1},{1,0},{2,3},{3,2},{4,5},{5,4},{6,7},{7,6},{8,9},{9,8},{10,11... | collective-permute-start | bytes 393224 | tf_op jit(solution)/shard_map/ppermute | solution.py:522
  14.4 30.9 %collective-permute-start.1 = (f32[48,32,128]{2,1,0:T(8,128)}, f32[48,32,128]{2,1,0:T(8,128)S(1)}, u32[]{:S(2)}, u32[]{:S(2)}) collective-permute-start(f32[48,32,128]{2,1,0:T(8,128)} %get-tuple-element.66), channel_id=1, source_target_pairs={{0,16},{16,32},{32,48},{48,64},{64,80},{80,96},{96,112},{112,0},{1... | collective-permute-start | bytes 2359304 | tf_op jit(solution)/shard_map/ppermute | solution.py:522
  15.7 29.6 %collective-permute-start.2 = (f32[48,32,128]{2,1,0:T(8,128)}, f32[48,32,128]{2,1,0:T(8,128)S(1)}, u32[]{:S(2)}, u32[]{:S(2)}) collective-permute-start(f32[48,32,128]{2,1,0:T(8,128)} %get-tuple-element.67), channel_id=1, source_target_pairs={{0,112},{16,0},{32,16},{48,32},{64,48},{80,64},{96,80},{112,96},{1... | collective-permute-start | bytes 2359304 | tf_op jit(solution)/shard_map/ppermute | solution.py:522
  18.0 27.3 %collective-permute-start.3 = (f32[8,6,32,128]{3,2,1,0:T(8,128)}, f32[8,6,32,128]{3,2,1,0:T(8,128)S(1)}, u32[]{:S(2)}, u32[]{:S(2)}) collective-permute-start(f32[8,6,32,128]{3,2,1,0:T(8,128)} %get-tuple-element.68), channel_id=1, source_target_pairs={{0,2},{2,4},{4,6},{6,8},{8,10},{10,12},{12,14},{14,0},{1,3},{3,5},... | collective-permute-start | bytes 2359304 | tf_op jit(solution)/shard_map/ppermute | solution.py:522
  20.6 24.7 %collective-permute-start.4 = (f32[8,6,32,128]{3,2,1,0:T(8,128)}, f32[8,6,32,128]{3,2,1,0:T(8,128)}, u32[]{:S(2)}, u32[]{:S(2)}) collective-permute-start(f32[8,6,32,128]{3,2,1,0:T(8,128)} %get-tuple-element.69), channel_id=1, source_target_pairs={{0,14},{2,0},{4,2},{6,4},{8,6},{10,8},{12,10},{14,12},{1,15},{3,1}... | collective-permute-start | bytes 2359304 | tf_op jit(solution)/shard_map/ppermute | solution.py:522
  34.0 0.8 copy-start.2
  34.8 0.8 copy-start.3
  35.5 0.8 copy-start.4
  36.3 0.8 copy-start.5
  37.0 0.8 copy-start.6
  48.0 28.6 %copy-start.1 = (f32[8,8,128]{2,1,0:T(8,128)S(1)}, f32[8,8,128]{2,1,0:T(8,128)}, u32[]{:S(2)}) copy-start(f32[8,8,128]{2,1,0:T(8,128)} %param.8) | copy-start | bytes 98308
  48.0 4.4 %collective-permute-start.5 = (f32[80,128]{1,0:T(8,128)S(1)}, f32[80,128]{1,0:T(8,128)S(1)}, u32[]{:S(2)}, u32[]{:S(2)}) collective-permute-start(f32[80,128]{1,0:T(8,128)S(1)} %first.1.mine), channel_id=1, source_target_pairs={{0,1},{1,0},{2,3},{3,2},{4,5},{5,4},{6,7},{7,6},{8,9},{9,8},{10,11... | collective-permute-start | bytes 122888 | tf_op jit(solution)/shard_map/ppermute | solution.py:522
  89.0 5.8 %collective-permute-start.6 = (f32[296,128]{1,0:T(8,128)S(1)}, f32[296,128]{1,0:T(8,128)S(1)}, u32[]{:S(2)}, u32[]{:S(2)}) collective-permute-start(f32[296,128]{1,0:T(8,128)S(1)} %get-tuple-element.78.mine), channel_id=1, source_target_pairs={{0,1},{1,0},{2,3},{3,2},{4,5},{5,4},{6,7},{7,6},{8,9},{9,8},{10,11... | collective-permute-start | bytes 454664 | tf_op jit(solution)/shard_map/ppermute | solution.py:522
  94.8 28.5 %collective-permute-start.7 = (f32[48,32,128]{2,1,0:T(8,128)S(1)}, f32[48,32,128]{2,1,0:T(8,128)S(1)}, u32[]{:S(2)}, u32[]{:S(2)}) collective-permute-start(f32[48,32,128]{2,1,0:T(8,128)S(1)} %get-tuple-element.84), channel_id=1, source_target_pairs={{0,16},{16,32},{32,48},{48,64},{64,80},{80,96},{96,112},{112,0},{1... | collective-permute-start | bytes 2359304 | tf_op jit(solution)/shard_map/ppermute | solution.py:522
  94.8 28.5 %collective-permute-start.8 = (f32[48,32,128]{2,1,0:T(8,128)S(1)}, f32[48,32,128]{2,1,0:T(8,128)S(1)}, u32[]{:S(2)}, u32[]{:S(2)}) collective-permute-start(f32[48,32,128]{2,1,0:T(8,128)S(1)} %get-tuple-element.85), channel_id=1, source_target_pairs={{0,112},{16,0},{32,16},{48,32},{64,48},{80,64},{96,80},{112,96},{1... | collective-permute-start | bytes 2359304 | tf_op jit(solution)/shard_map/ppermute | solution.py:522
  98.4 24.9 %collective-permute-start.9 = (f32[8,6,32,128]{3,2,1,0:T(8,128)S(1)}, f32[8,6,32,128]{3,2,1,0:T(8,128)S(1)}, u32[]{:S(2)}, u32[]{:S(2)}) collective-permute-start(f32[8,6,32,128]{3,2,1,0:T(8,128)S(1)} %get-tuple-element.86), channel_id=1, source_target_pairs={{0,2},{2,4},{4,6},{6,8},{8,10},{10,12},{12,14},{14,0},{1,3},{3,5},... | collective-permute-start | bytes 2359304 | tf_op jit(solution)/shard_map/ppermute | solution.py:522
  101.5 21.8 %collective-permute-start.10 = (f32[8,6,32,128]{3,2,1,0:T(8,128)S(1)}, f32[8,6,32,128]{3,2,1,0:T(8,128)S(1)}, u32[]{:S(2)}, u32[]{:S(2)}) collective-permute-start(f32[8,6,32,128]{3,2,1,0:T(8,128)S(1)} %get-tuple-element.87), channel_id=1, source_target_pairs={{0,14},{2,0},{4,2},{6,4},{8,6},{10,8},{12,10},{14,12},{1,15},{3,1}... | collective-permute-start | bytes 2359304 | tf_op jit(solution)/shard_map/ppermute | solution.py:522
  135.2 5.6 %collective-permute-start.11 = (f32[296,128]{1,0:T(8,128)S(1)}, f32[296,128]{1,0:T(8,128)S(1)}, u32[]{:S(2)}, u32[]{:S(2)}) collective-permute-start(f32[296,128]{1,0:T(8,128)S(1)} %get-tuple-element.90.mine), channel_id=1, source_target_pairs={{0,1},{1,0},{2,3},{3,2},{4,5},{5,4},{6,7},{7,6},{8,9},{9,8},{10,11... | collective-permute-start | bytes 454664 | tf_op jit(solution)/shard_map/ppermute | solution.py:522
  140.8 31.2 %collective-permute-start.12 = (f32[48,32,128]{2,1,0:T(8,128)S(1)}, f32[48,32,128]{2,1,0:T(8,128)S(1)}, u32[]{:S(2)}, u32[]{:S(2)}) collective-permute-start(f32[48,32,128]{2,1,0:T(8,128)S(1)} %get-tuple-element.96), channel_id=1, source_target_pairs={{0,16},{16,32},{32,48},{48,64},{64,80},{80,96},{96,112},{112,0},{1... | collective-permute-start | bytes 2359304 | tf_op jit(solution)/shard_map/ppermute | solution.py:522
  141.4 30.6 %collective-permute-start.13 = (f32[48,32,128]{2,1,0:T(8,128)S(1)}, f32[48,32,128]{2,1,0:T(8,128)S(1)}, u32[]{:S(2)}, u32[]{:S(2)}) collective-permute-start(f32[48,32,128]{2,1,0:T(8,128)S(1)} %get-tuple-element.97), channel_id=1, source_target_pairs={{0,112},{16,0},{32,16},{48,32},{64,48},{80,64},{96,80},{112,96},{1... | collective-permute-start | bytes 2359304 | tf_op jit(solution)/shard_map/ppermute | solution.py:522
  144.4 27.6 %collective-permute-start.14 = (f32[8,6,32,128]{3,2,1,0:T(8,128)S(1)}, f32[8,6,32,128]{3,2,1,0:T(8,128)S(1)}, u32[]{:S(2)}, u32[]{:S(2)}) collective-permute-start(f32[8,6,32,128]{3,2,1,0:T(8,128)S(1)} %get-tuple-element.98), channel_id=1, source_target_pairs={{0,2},{2,4},{4,6},{6,8},{8,10},{10,12},{12,14},{14,0},{1,3},{3,5},... | collective-permute-start | bytes 2359304 | tf_op jit(solution)/shard_map/ppermute | solution.py:522
  148.5 23.5 %collective-permute-start.15 = (f32[8,6,32,128]{3,2,1,0:T(8,128)S(1)}, f32[8,6,32,128]{3,2,1,0:T(8,128)S(1)}, u32[]{:S(2)}, u32[]{:S(2)}) collective-permute-start(f32[8,6,32,128]{3,2,1,0:T(8,128)S(1)} %get-tuple-element.99), channel_id=1, source_target_pairs={{0,14},{2,0},{4,2},{6,4},{8,6},{10,8},{12,10},{14,12},{1,15},{3,1}... | collective-permute-start | bytes 2359304 | tf_op jit(solution)/shard_map/ppermute | solution.py:522
  183.9 6.2 %collective-permute-start.16 = (f32[296,128]{1,0:T(8,128)S(1)}, f32[296,128]{1,0:T(8,128)S(1)}, u32[]{:S(2)}, u32[]{:S(2)}) collective-permute-start(f32[296,128]{1,0:T(8,128)S(1)} %get-tuple-element.101.mine), channel_id=1, source_target_pairs={{0,1},{1,0},{2,3},{3,2},{4,5},{5,4},{6,7},{7,6},{8,9},{9,8},{10,11... | collective-permute-start | bytes 454664 | tf_op jit(solution)/shard_map/ppermute | solution.py:522
  190.1 28.2 %collective-permute-start.17 = (f32[48,32,128]{2,1,0:T(8,128)S(1)}, f32[48,32,128]{2,1,0:T(8,128)S(1)}, u32[]{:S(2)}, u32[]{:S(2)}) collective-permute-start(f32[48,32,128]{2,1,0:T(8,128)S(1)} %get-tuple-element.107), channel_id=1, source_target_pairs={{0,16},{16,32},{32,48},{48,64},{64,80},{80,96},{96,112},{112,0},{1... | collective-permute-start | bytes 2359304 | tf_op jit(solution)/shard_map/ppermute | solution.py:522
  190.1 28.2 %collective-permute-start.18 = (f32[48,32,128]{2,1,0:T(8,128)S(1)}, f32[48,32,128]{2,1,0:T(8,128)S(1)}, u32[]{:S(2)}, u32[]{:S(2)}) collective-permute-start(f32[48,32,128]{2,1,0:T(8,128)S(1)} %get-tuple-element.108), channel_id=1, source_target_pairs={{0,112},{16,0},{32,16},{48,32},{64,48},{80,64},{96,80},{112,96},{1... | collective-permute-start | bytes 2359304 | tf_op jit(solution)/shard_map/ppermute | solution.py:522
  193.6 24.6 %collective-permute-start.19 = (f32[8,6,32,128]{3,2,1,0:T(8,128)S(1)}, f32[8,6,32,128]{3,2,1,0:T(8,128)S(1)}, u32[]{:S(2)}, u32[]{:S(2)}) collective-permute-start(f32[8,6,32,128]{3,2,1,0:T(8,128)S(1)} %get-tuple-element.109), channel_id=1, source_target_pairs={{0,2},{2,4},{4,6},{6,8},{8,10},{10,12},{12,14},{14,0},{1,3},{3,5},... | collective-permute-start | bytes 2359304 | tf_op jit(solution)/shard_map/ppermute | solution.py:522
  197.3 21.0 %collective-permute-start.20 = (f32[8,6,32,128]{3,2,1,0:T(8,128)S(1)}, f32[8,6,32,128]{3,2,1,0:T(8,128)S(1)}, u32[]{:S(2)}, u32[]{:S(2)}) collective-permute-start(f32[8,6,32,128]{3,2,1,0:T(8,128)S(1)} %get-tuple-element.110), channel_id=1, source_target_pairs={{0,14},{2,0},{4,2},{6,4},{8,6},{10,8},{12,10},{14,12},{1,15},{3,1}... | collective-permute-start | bytes 2359304 | tf_op jit(solution)/shard_map/ppermute | solution.py:522

commit v6 on v5

--- a/solution.py
+++ b/solution.py
@@ -103,66 +103,33 @@
 MATRIX = jax.ShapeDtypeStruct((PAIRS, 2 * CH, 2 * SZ), BF16)
 
 
-def face_copies(x, field, x_low, x_high, y_low, y_high, sem):
-    copies = [
-        pltpu.make_async_copy(field.at[pl.ds(x * SY, REACH)], y_low.at[x], sem.at[0, x]),
-        pltpu.make_async_copy(field.at[pl.ds(x * SY + SY - REACH, REACH)], y_high.at[x], sem.at[1, x]),
-    ]
-    return copies
-
-
-def low_copy(x, field, x_low, sem):
-    rows = pl.ds(x * SY, SY)
-    return pltpu.make_async_copy(field.at[rows], x_low.at[rows], sem.at[2, x])
-
-
-def high_copy(x, field, x_high, sem):
-    to = pl.ds((x - (SX - REACH)) * SY, SY)
-    return pltpu.make_async_copy(field.at[pl.ds(x * SY, SY)], x_high.at[to], sem.at[3, x])
-
-
-def start_faces(x, field, outs, sem):
-    x_low, x_high, y_low, y_high = outs
-    for copy in face_copies(x, field, x_low, x_high, y_low, y_high, sem):
-        copy.start()
-
-    @pl.when(x < REACH)
-    def _():
-        low_copy(x, field, x_low, sem).start()
-
-    @pl.when(x >= SX - REACH)
-    def _():
-        high_copy(x, field, x_high, sem).start()
-
-
-def wait_faces(field, outs, sem):
-    x_low, x_high, y_low, y_high = outs
-    for x in range(SX):
-        for copy in face_copies(x, field, x_low, x_high, y_low, y_high, sem):
-            copy.wait()
-        if x < REACH:
-            low_copy(x, field, x_low, sem).wait()
-        if x >= SX - REACH:
-            high_copy(x, field, x_high, sem).wait()
+def write_faces(x, rows, x_low, x_high, y_low, y_high):
+    for i in range(REACH):
+        y_low[x, i] = rows[i]
+        y_high[x, i] = rows[SY - REACH + i]
+
+    if x < REACH:
+        for i in range(SY):
+            x_low[x * SY + i] = rows[i]
+
+    if x >= SX - REACH:
+        for i in range(SY):
+            x_high[(x - (SX - REACH)) * SY + i] = rows[i]
 
 
 def rearrange_kernel(src, *refs):
-    field, outs, (z_face, in_sem, out_sem) = refs[0], refs[1:5], refs[5:]
+    field, faces, (z_face, in_sem) = refs[0], refs[1:5], refs[5:]
     for row in range(ROWS):
         pltpu.make_async_copy(src.at[:, row, :], field.at[row], in_sem.at[row]).start()
 
-    @pl.loop(0, SX)
-    def _(x):
+    for x in range(SX):
         for y in range(SY):
             row = x * SY + y
             pltpu.make_async_copy(src.at[:, row, :], field.at[row], in_sem.at[row]).wait()
-        start_faces(x, field, outs, out_sem)
+        rows = [field[x * SY + y] for y in range(SY)]
+        write_faces(x, rows, *faces)
         for part in range(2):
-            z_face[pl.ds((2 * x + part) * 16, 16), :] = z_faces(
-                [field[x * SY + 4 * part + i] for i in range(4)]
-            )
-
-    wait_faces(field, outs, out_sem)
+            z_face[pl.ds((2 * x + part) * 16, 16), :] = z_faces(rows[4 * part : 4 * part + 4])
 
 
 def rearrange(orbitals):
@@ -173,7 +140,6 @@
         out_specs=vmem_specs(6),
         scratch_shapes=[
             pltpu.SemaphoreType.DMA((ROWS,)),
-            pltpu.SemaphoreType.DMA((4, SX)),
         ],
         compiler_params=PARAMS,
         name="rearrange",
@@ -267,16 +233,9 @@
     couplings = jnp.where(row == 16, own[pl.ds(0, 1), :], jnp.where(row == 17, own[pl.ds(1, 1), :], 0.0))
     out[pl.ds(TGT, TGT), :] = couplings
     total[...] = jnp.zeros_like(total)
-
-    @pl.loop(0, SX)
-    def _(x):
-        acc = total[...]
-        for p in range(4):
-            at = x * SY + 2 * p
-            values = jnp.concatenate([field[at], field[at + 1]], axis=1)
-            acc = acc + partial_of(mat[x * 4 + p], values)
-        total[...] = acc
-
+    for pair in range(PAIRS):
+        values = jnp.concatenate([field[2 * pair], field[2 * pair + 1]], axis=1)
+        total[...] = total[...] + partial_of(mat[pair], values)
     out[pl.ds(0, TGT), :] = packed_partial(total[...])
 
 
@@ -346,10 +305,10 @@
         (new, gram), refs = refs[:2], refs[2:]
     else:
         (new, x_low, x_high, y_low, y_high, message), refs = refs[:6], refs[6:]
-        outs = (x_low, x_high, y_low, y_high)
+        faces_out = (x_low, x_high, y_low, y_high)
         if first_step:
             coupling, refs = refs[0], refs[1:]
-    total, coef, first_z, second_z, out_sem = refs
+    total, coef, first_z, second_z = refs
     alpha = (1.0 if first_step else 2.0) / FILTER_HALF
     half = [0.0] + [-0.5 * c for c in STENCIL[1:]]
     diagonal = -1.5 * STENCIL[0] - FILTER_CENTRE
@@ -399,25 +358,22 @@
     frame = frame * (alpha * coupling[...])
     stacked = jnp.concatenate([frame[:, j * NB : (j + 1) * NB] for j in range(NPJ)], axis=0)
     turned = stacked.T
-    coef_hi = turned.astype(BF16).astype(F32)
-    coef[pl.ds(0, NB), :] = jnp.concatenate([coef_hi, coef_hi], axis=1).astype(BF16)
-    coef[pl.ds(NB, NB), pl.ds(0, CH)] = (turned - coef_hi).astype(BF16)
-
-    @pl.loop(0, SX)
-    def _(x):
-        c_hi = coef[pl.ds(0, NB), :]
-        c_lo = coef[pl.ds(NB, NB), pl.ds(0, CH)]
+    coef[...] = jnp.concatenate(split2(turned), axis=0)
+
+    c_both = coef[...]
+    for x in range(SX):
         acc = total[...]
         rows = []
         for p in range(4):
             pair_mat = mat[x * 4 + p]
-            added = dot(c_hi, pair_mat) + dot(c_lo, pair_mat[:CH])
+            both = dot(c_both, pair_mat[:CH])
+            added = both[:NB] + both[NB:] + dot(c_both[:NB], pair_mat[CH:])
             for q in range(2):
                 here = x * SY + 2 * p + q
                 rows.append(new[here] + added[:, q * SZ : (q + 1) * SZ])
                 new[here] = rows[-1]
         if not last_step:
-            start_faces(x, new, outs, out_sem)
+            write_faces(x, rows, *faces_out)
         for p in range(4):
             values = jnp.concatenate(rows[2 * p : 2 * p + 2], axis=1)
             if last_step:
@@ -437,7 +393,6 @@
         gram[...] = jnp.concatenate([summed[8 * q : 8 * q + 8] for q in range(4)], axis=1)
     else:
         message[pl.ds(ZROWS, TGT), :] = packed_partial(total[...])
-        wait_faces(new, outs, out_sem)
 
 
 def step(first_step, last_step, *arrays):
@@ -453,10 +408,9 @@
         out_specs=vmem_specs(len(outs)),
         scratch_shapes=[
             pltpu.VMEM(total, F32),
-            pltpu.VMEM((2 * NB, 2 * CH), BF16),
+            pltpu.VMEM((2 * NB, CH), BF16),
             pltpu.VMEM((2 * SZ, SZ), BF16),
             pltpu.VMEM((2 * SZ, SZ), BF16),
-            pltpu.SemaphoreType.DMA((4, SX)),
         ],
         compiler_params=PARAMS,
         name="step",
@@ -484,8 +438,7 @@
     hi, mid, lo = split3(inverse[...])
     left = jnp.concatenate([lo, mid, hi, mid, hi, hi], axis=1)
 
-    @pl.loop(0, SX)
-    def _(x):
+    for x in range(SX):
         for p in range(SY // 2):
             at = x * SY + 2 * p
             values = jnp.concatenate([field[at], field[at + 1]], axis=1)

time: 253 us -> 222 us (0.88)
  Pallas kernels: 68.2 us -> 38.5 us
    pallas_call x4, Pallas kernels: 43.1 us -> 19.3 us  [step(): pl.pallas_call(functools.partial(step_kernel, first_step, last_step), out...]
    pallas_call x1, Pallas kernels: 8.65 us -> 4.19 us  [rearrange(): pl.pallas_call(rearrange_kernel, out_shape=[BLOCK, X_FACE, X_FACE, Y_FACE...]
  transfers between devices with their start and end apart: 21 -> 21, of which waited for: 4 -> 4; matrix products, arithmetic and copies ran while one was open for 5% -> 6% of each run, Pallas kernels for 3% -> 3%
where the time goes in v6:
time: 222 us; the launch traced here: 221 us
  blocking collectives  109 us (49%)
  Pallas kernels  38.5 us (17%)
  starting transfers between devices  35 us (16%)
  waiting for transfers between devices  20.3 us (9%)
  other arithmetic  9.94 us (4%)
  local copies, waits for them, and re-layouts  7.88 us (4%)
    all_to_all x4, blocking collectives, local(): came = lax.all_to_all(sends, 'gy', 0, 0)  54.4 us
    all_to_all x4, blocking collectives, local(): came = lax.all_to_all(sends, 'gx', 0, 0)  35.1 us
    ppermute x21, starting transfers between devices, shift(): lax.ppermute(value, axis, [(i, (i + by) % count) for i in range(count)])  35 us
    ppermute x21, waiting for transfers between devices, shift(): lax.ppermute(value, axis, [(i, (i + by) % count) for i in range(count)])  20.3 us
    pallas_call x4, Pallas kernels, step(): pl.pallas_call(functools.partial(step_kernel, first_step, last_step), out...  19.3 us
    all_to_all x1, blocking collectives, local(): lax.all_to_all(jnp.broadcast_to(gram[None], (devices,) + gram.shape), axe...  19.2 us
    pallas_call x1, Pallas kernels, build(): pl.pallas_call(build_kernel, out_shape=MATRIX, in_specs=[pl.BlockSpec(mem...  7.41 us
    sort x1, other arithmetic, local(): lax.sort((key,) + tuple((projector[j] for j in range(NPJ))), num_keys=1,...  7.32 us
  transfers between devices with their start and end apart: 21, of which 4 were waited for; matrix products, arithmetic and copies ran while one was open for 6% of the time, Pallas kernels for 3%

profile of v6, /device:TPU:1, one launch (start us, length us, event | category | flops | bytes accessed | tf_op | source)
XLA Modules:
  0.0 221.3 jit_solution(4321562990250804245)
XLA Ops:
  1.2 4.2 %rearrange.1 = (f32[64,32,128]{2,1,0:T(8,128)S(1)}, f32[48,32,128]{2,1,0:T(8,128)}, f32[48,32,128]{2,1,0:T(8,128)}, f32[8,6,32,128]{3,2,1,0:T(8,128)}, f32[8,6,32,128]{3,2,1,0:T(8,128)}, /*index=5*/f32[256,128]{1,0:T(8,128)}) custom-call(f32[32,64,128]{2,1,0:T(8,128)S(1)} %bitcast.14), custom_call_target="tpu_custom_call" | custom-call | tf_op jit(solution)/shard_map/rearrange/pallas_call | solution.py:136
  5.4 4.5 %collective-permute-start = (f32[256,128]{1,0:T(8,128)}, f32[256,128]{1,0:T(8,128)S(1)}, u32[]{:S(2)}, u32[]{:S(2)}) collective-permute-start(f32[256,128]{1,0:T(8,128)} %get-tuple-element.65), channel_id=1, source_target_pairs={{0,1},{1,0},{2,3},{3,2},{4,5},{5,4},{6,7},{7,6},{8,9},{9,8},{10,11... | collective-permute-start | bytes 393224 | tf_op jit(solution)/shard_map/ppermute | solution.py:475
  11.2 2.3 %collective-permute-start.2 = (f32[48,32,128]{2,1,0:T(8,128)}, f32[48,32,128]{2,1,0:T(8,128)S(1)}, u32[]{:S(2)}, u32[]{:S(2)}) collective-permute-start(f32[48,32,128]{2,1,0:T(8,128)} %get-tuple-element.67), channel_id=1, source_target_pairs={{0,112},{16,0},{32,16},{48,32},{64,48},{80,64},{96,80},{112,96},{1... | collective-permute-start | bytes 2359304 | tf_op jit(solution)/shard_map/ppermute | solution.py:475
  13.5 2.6 %collective-permute-start.3 = (f32[8,6,32,128]{3,2,1,0:T(8,128)}, f32[8,6,32,128]{3,2,1,0:T(8,128)S(1)}, u32[]{:S(2)}, u32[]{:S(2)}) collective-permute-start(f32[8,6,32,128]{3,2,1,0:T(8,128)} %get-tuple-element.68), channel_id=1, source_target_pairs={{0,2},{2,4},{4,6},{6,8},{8,10},{10,12},{12,14},{14,0},{1,3},{3,5},... | collective-permute-start | bytes 2359304 | tf_op jit(solution)/shard_map/ppermute | solution.py:475
  16.1 2.0 fusion.9
  21.0 7.3 %sort.33 = (s32[8192]{0:T(1024)}, f32[8192]{0:T(1024)}, f32[8192]{0:T(1024)}, f32[8192]{0:T(1024)}, f32[8192]{0:T(1024)}) sort(s32[8192]{0:T(1024)} %fusion.5, f32[8192]{0:T(1024)} %bitcast.26, f32[8192]{0:T(1024)} %bitcast.25, f32[8192]{0:T(1024)} %bitcast.27, f32[8192]{0:T(1024)} %bitcast.24), dimensions={0}, to_apply=%region_1.2 | sort | flops 106496 | bytes 327680 | tf_op jit(solution)/shard_map/sort | solution.py:491
  33.3 7.4 %build.1.mat.refs_8_ = bf16[32,320,256]{2,1,0:T(8,128)(2,1)S(1)} custom-call(s32[65]{0:T(128)S(1)} %convert_reduce_fusion.starts, s32[64,128]{1,0:T(8,128)S(1)} %bitcast.19, f32[64,128]{1,0:T(8,128)S(1)} %bitcast.20, f32[64,128]{1,0:T(8,128)S(1)} %bitcast.21, f32[64,128]{1,0:T(8,128)S(1)} %bitcast.22, f32[64,128]{1,0:T(8,128)S(1)} %bitcast.23), custom_call_target="tpu_custom_call" | custom-call | tf_op jit(solution)/shard_map/build/pallas_call | solution.py:206
  40.8 2.1 first.1.mine
  43.2 4.1 %collective-permute-done.5.other = f32[80,128]{1,0:T(8,128)S(1)} collective-permute-done((f32[80,128]{1,0:T(8,128)S(1)}, f32[80,128]{1,0:T(8,128)S(1)}, u32[]{:S(2)}, u32[]{:S(2)}) %collective-permute-start.5) | collective-permute-done | bytes 40992 | tf_op jit(solution)/shard_map/ppermute | solution.py:475
  47.4 13.4 %all_to_all.45.came = f32[8,80,128]{2,1,0:T(8,128)S(1)} all-to-all(f32[8,80,128]{2,1,0:T(8,128)S(1)} %spread.8), channel_id=1, replica_groups=mesh['gx'=8,'gy'=8,'gz'=2] {'gy'}, dimensions={0} | all-to-all | bytes 655360 | tf_op jit(solution)/shard_map/all_to_all | solution.py:519
  60.9 10.2 %all_to_all.46.refs_7_ = f32[8,80,128]{2,1,0:T(8,128)S(1)} all-to-all(f32[8,80,128]{2,1,0:T(8,128)S(1)} %spread.9), channel_id=1, replica_groups=mesh['gx'=8,'gy'=8,'gz'=2] {'gx'}, dimensions={0} | all-to-all | bytes 655360 | tf_op jit(solution)/shard_map/all_to_all | solution.py:521
  71.1 5.2 %step.4 = (f32[64,32,128]{2,1,0:T(8,128)S(1)}, f32[48,32,128]{2,1,0:T(8,128)S(1)}, f32[48,32,128]{2,1,0:T(8,128)S(1)}, f32[8,6,32,128]{3,2,1,0:T(8,128)S(1)}, f3...) custom-call(f32[64,32,128]{2,1,0:T(8,128)S(1)} %get-tuple-element.70.field.refs_0_.refs_9_, ...), custom_call_target="tpu_custom_call" | custom-call | tf_op jit(solution)/shard_map/step/pallas_call | solution.py:404
  76.7 5.2 %collective-permute-done.6.other.refs_1_ = f32[296,128]{1,0:T(8,128)S(1)} collective-permute-done((f32[296,128]{1,0:T(8,128)S(1)}, f32[296,128]{1,0:T(8,128)S(1)}, u32[]{:S(2)}, u32[]{:S(2)}) %collective-permute-start.6) | collective-permute-done | bytes 151584 | tf_op jit(solution)/shard_map/ppermute | solution.py:475
  82.5 2.9 %collective-permute-start.8 = (f32[48,32,128]{2,1,0:T(8,128)S(1)}, f32[48,32,128]{2,1,0:T(8,128)S(1)}, u32[]{:S(2)}, u32[]{:S(2)}) collective-permute-start(f32[48,32,128]{2,1,0:T(8,128)S(1)} %get-tuple-element.85), channel_id=1, source_target_pairs={{0,112},{16,0},{32,16},{48,32},{64,48},{80,64},{96,80},{112,96},{1... | collective-permute-start | bytes 2359304 | tf_op jit(solution)/shard_map/ppermute | solution.py:475
  85.4 4.3 %collective-permute-start.9 = (f32[8,6,32,128]{3,2,1,0:T(8,128)S(1)}, f32[8,6,32,128]{3,2,1,0:T(8,128)S(1)}, u32[]{:S(2)}, u32[]{:S(2)}) collective-permute-start(f32[8,6,32,128]{3,2,1,0:T(8,128)S(1)} %get-tuple-element.86), channel_id=1, source_target_pairs={{0,2},{2,4},{4,6},{6,8},{8,10},{10,12},{12,14},{14,0},{1,3},{3,5},... | collective-permute-start | bytes 2359304 | tf_op jit(solution)/shard_map/ppermute | solution.py:475
  89.7 13.5 %all_to_all.47.came = f32[8,40,128]{2,1,0:T(8,128)S(1)} all-to-all(f32[8,40,128]{2,1,0:T(8,128)S(1)} %spread.10), channel_id=1, replica_groups=mesh['gx'=8,'gy'=8,'gz'=2] {'gy'}, dimensions={0} | all-to-all | bytes 327680 | tf_op jit(solution)/shard_map/all_to_all | solution.py:519
  103.3 8.1 %all_to_all.48.refs_7_ = f32[8,40,128]{2,1,0:T(8,128)S(1)} all-to-all(f32[8,40,128]{2,1,0:T(8,128)S(1)} %spread.11), channel_id=1, replica_groups=mesh['gx'=8,'gy'=8,'gz'=2] {'gx'}, dimensions={0} | all-to-all | bytes 327680 | tf_op jit(solution)/shard_map/all_to_all | solution.py:521
  111.5 4.9 %step.5 = (f32[64,32,128]{2,1,0:T(8,128)S(1)}, f32[48,32,128]{2,1,0:T(8,128)S(1)}, f32[48,32,128]{2,1,0:T(8,128)S(1)}, f32[8,6,32,128]{3,2,1,0:T(8,128)S(1)}, f3...) custom-call(f32[64,32,128]{2,1,0:T(8,128)S(1)} %get-tuple-element.77.refs_0_.refs_9_, ...), custom_call_target="tpu_custom_call" | custom-call | tf_op jit(solution)/shard_map/step/pallas_call | solution.py:404
  116.8 5.2 %collective-permute-done.11.other.refs_1_ = f32[296,128]{1,0:T(8,128)S(1)} collective-permute-done((f32[296,128]{1,0:T(8,128)S(1)}, f32[296,128]{1,0:T(8,128)S(1)}, u32[]{:S(2)}, u32[]{:S(2)}) %collective-permute-start.11) | collective-permute-done | bytes 151584 | tf_op jit(solution)/shard_map/ppermute | solution.py:475
  122.5 3.0 %collective-permute-start.13 = (f32[48,32,128]{2,1,0:T(8,128)S(1)}, f32[48,32,128]{2,1,0:T(8,128)S(1)}, u32[]{:S(2)}, u32[]{:S(2)}) collective-permute-start(f32[48,32,128]{2,1,0:T(8,128)S(1)} %get-tuple-element.97), channel_id=1, source_target_pairs={{0,112},{16,0},{32,16},{48,32},{64,48},{80,64},{96,80},{112,96},{1... | collective-permute-start | bytes 2359304 | tf_op jit(solution)/shard_map/ppermute | solution.py:475
  125.6 4.1 %collective-permute-start.14 = (f32[8,6,32,128]{3,2,1,0:T(8,128)S(1)}, f32[8,6,32,128]{3,2,1,0:T(8,128)S(1)}, u32[]{:S(2)}, u32[]{:S(2)}) collective-permute-start(f32[8,6,32,128]{3,2,1,0:T(8,128)S(1)} %get-tuple-element.98), channel_id=1, source_target_pairs={{0,2},{2,4},{4,6},{6,8},{8,10},{10,12},{12,14},{14,0},{1,3},{3,5},... | collective-permute-start | bytes 2359304 | tf_op jit(solution)/shard_map/ppermute | solution.py:475
  129.7 14.7 %all_to_all.49.came = f32[8,40,128]{2,1,0:T(8,128)S(1)} all-to-all(f32[8,40,128]{2,1,0:T(8,128)S(1)} %spread.12), channel_id=1, replica_groups=mesh['gx'=8,'gy'=8,'gz'=2] {'gy'}, dimensions={0} | all-to-all | bytes 327680 | tf_op jit(solution)/shard_map/all_to_all | solution.py:519
  144.5 8.7 %all_to_all.50.refs_7_ = f32[8,40,128]{2,1,0:T(8,128)S(1)} all-to-all(f32[8,40,128]{2,1,0:T(8,128)S(1)} %spread.13), channel_id=1, replica_groups=mesh['gx'=8,'gy'=8,'gz'=2] {'gx'}, dimensions={0} | all-to-all | bytes 327680 | tf_op jit(solution)/shard_map/all_to_all | solution.py:521
  153.2 4.9 %step.6 = (f32[64,32,128]{2,1,0:T(8,128)S(1)}, f32[48,32,128]{2,1,0:T(8,128)S(1)}, f32[48,32,128]{2,1,0:T(8,128)S(1)}, f32[8,6,32,128]{3,2,1,0:T(8,128)S(1)}, f3...) custom-call(f32[64,32,128]{2,1,0:T(8,128)S(1)} %get-tuple-element.89.refs_0_.refs_9_, ...), custom_call_target="tpu_custom_call" | custom-call | tf_op jit(solution)/shard_map/step/pallas_call | solution.py:404
  158.5 5.7 %collective-permute-done.16.other.refs_1_ = f32[296,128]{1,0:T(8,128)S(1)} collective-permute-done((f32[296,128]{1,0:T(8,128)S(1)}, f32[296,128]{1,0:T(8,128)S(1)}, u32[]{:S(2)}, u32[]{:S(2)}) %collective-permute-start.16) | collective-permute-done | bytes 151584 | tf_op jit(solution)/shard_map/ppermute | solution.py:475
  164.3 3.6 %collective-permute-start.18 = (f32[48,32,128]{2,1,0:T(8,128)S(1)}, f32[48,32,128]{2,1,0:T(8,128)S(1)}, u32[]{:S(2)}, u32[]{:S(2)}) collective-permute-start(f32[48,32,128]{2,1,0:T(8,128)S(1)} %get-tuple-element.108), channel_id=1, source_target_pairs={{0,112},{16,0},{32,16},{48,32},{64,48},{80,64},{96,80},{112,96},{1... | collective-permute-start | bytes 2359304 | tf_op jit(solution)/shard_map/ppermute | solution.py:475
  167.8 3.6 %collective-permute-start.19 = (f32[8,6,32,128]{3,2,1,0:T(8,128)S(1)}, f32[8,6,32,128]{3,2,1,0:T(8,128)S(1)}, u32[]{:S(2)}, u32[]{:S(2)}) collective-permute-start(f32[8,6,32,128]{3,2,1,0:T(8,128)S(1)} %get-tuple-element.109), channel_id=1, source_target_pairs={{0,2},{2,4},{4,6},{6,8},{8,10},{10,12},{12,14},{14,0},{1,3},{3,5},... | collective-permute-start | bytes 2359304 | tf_op jit(solution)/shard_map/ppermute | solution.py:475
  171.5 12.8 %all_to_all.51.came = f32[8,40,128]{2,1,0:T(8,128)S(1)} all-to-all(f32[8,40,128]{2,1,0:T(8,128)S(1)} %spread.14), channel_id=1, replica_groups=mesh['gx'=8,'gy'=8,'gz'=2] {'gy'}, dimensions={0} | all-to-all | bytes 327680 | tf_op jit(solution)/shard_map/all_to_all | solution.py:519
  184.3 8.1 %all_to_all.52.refs_7_ = f32[8,40,128]{2,1,0:T(8,128)S(1)} all-to-all(f32[8,40,128]{2,1,0:T(8,128)S(1)} %spread.15), channel_id=1, replica_groups=mesh['gx'=8,'gy'=8,'gz'=2] {'gx'}, dimensions={0} | all-to-all | bytes 327680 | tf_op jit(solution)/shard_map/all_to_all | solution.py:521
  192.4 4.3 %step.7 = (f32[64,32,128]{2,1,0:T(8,128)S(1)}, f32[8,128]{1,0:T(8,128)S(1)}) custom-call(f32[64,32,128]{2,1,0:T(8,128)S(1)} %get-tuple-element.100.refs_0_, f32[296,128]{1,0:T(8,128)S(1)} %collective-permute-done.16.other.refs_1_, f32[48,32,128]{2,1,0:T(8,128)S(1)} %collective-permute-done.17.refs_2_, f32[48,32,128]{2,1,0:T(8,128)S(1)} %collective-permute-done.18.refs_3_, ...), custom_call_target="tpu_custom_call" | custom-call | tf_op jit(solution)/shard_map/step/pallas_call | solution.py:404
  196.8 19.2 %all_to_all.53.grams = f32[128,8,128]{2,1,0:T(8,128)S(1)} all-to-all(f32[128,8,128]{2,1,0:T(8,128)S(1)} %broadcast_in_dim.17), channel_id=1, replica_groups=mesh['gx'=8,'gy'=8,'gz'=2] {'gx','gy','gz'}, dimensions={0} | all-to-all | bytes 1048576 | tf_op jit(solution)/shard_map/all_to_all | solution.py:535
  216.0 5.1 %finish.1 = f32[32,64,128]{2,1,0:T(8,128)} custom-call(f32[64,32,128]{2,1,0:T(8,128)S(1)} %get-tuple-element.111.field, f32[128,8,128]{2,1,0:T(8,128)S(1)} %all_to_all.53.grams), custom_call_target="tpu_custom_call" | custom-call | tf_op jit(solution)/shard_map/finish/pallas_call | solution.py:458
  (57 shorter events, 13.1 us)
Async XLA Ops:
  0.0 1.2 copy-start
  5.4 35.3 %collective-permute-start = (f32[256,128]{1,0:T(8,128)}, f32[256,128]{1,0:T(8,128)S(1)}, u32[]{:S(2)}, u32[]{:S(2)}) collective-permute-start(f32[256,128]{1,0:T(8,128)} %get-tuple-element.65), channel_id=1, source_target_pairs={{0,1},{1,0},{2,3},{3,2},{4,5},{5,4},{6,7},{7,6},{8,9},{9,8},{10,11... | collective-permute-start | bytes 393224 | tf_op jit(solution)/shard_map/ppermute | solution.py:475
  9.9 30.8 %collective-permute-start.1 = (f32[48,32,128]{2,1,0:T(8,128)}, f32[48,32,128]{2,1,0:T(8,128)S(1)}, u32[]{:S(2)}, u32[]{:S(2)}) collective-permute-start(f32[48,32,128]{2,1,0:T(8,128)} %get-tuple-element.66), channel_id=1, source_target_pairs={{0,16},{16,32},{32,48},{48,64},{64,80},{80,96},{96,112},{112,0},{1... | collective-permute-start | bytes 2359304 | tf_op jit(solution)/shard_map/ppermute | solution.py:475
  11.2 29.6 %collective-permute-start.2 = (f32[48,32,128]{2,1,0:T(8,128)}, f32[48,32,128]{2,1,0:T(8,128)S(1)}, u32[]{:S(2)}, u32[]{:S(2)}) collective-permute-start(f32[48,32,128]{2,1,0:T(8,128)} %get-tuple-element.67), channel_id=1, source_target_pairs={{0,112},{16,0},{32,16},{48,32},{64,48},{80,64},{96,80},{112,96},{1... | collective-permute-start | bytes 2359304 | tf_op jit(solution)/shard_map/ppermute | solution.py:475
  13.5 27.3 %collective-permute-start.3 = (f32[8,6,32,128]{3,2,1,0:T(8,128)}, f32[8,6,32,128]{3,2,1,0:T(8,128)S(1)}, u32[]{:S(2)}, u32[]{:S(2)}) collective-permute-start(f32[8,6,32,128]{3,2,1,0:T(8,128)} %get-tuple-element.68), channel_id=1, source_target_pairs={{0,2},{2,4},{4,6},{6,8},{8,10},{10,12},{12,14},{14,0},{1,3},{3,5},... | collective-permute-start | bytes 2359304 | tf_op jit(solution)/shard_map/ppermute | solution.py:475
  16.1 24.7 %collective-permute-start.4 = (f32[8,6,32,128]{3,2,1,0:T(8,128)}, f32[8,6,32,128]{3,2,1,0:T(8,128)}, u32[]{:S(2)}, u32[]{:S(2)}) collective-permute-start(f32[8,6,32,128]{3,2,1,0:T(8,128)} %get-tuple-element.69), channel_id=1, source_target_pairs={{0,14},{2,0},{4,2},{6,4},{8,6},{10,8},{12,10},{14,12},{1,15},{3,1}... | collective-permute-start | bytes 2359304 | tf_op jit(solution)/shard_map/ppermute | solution.py:475
  29.5 0.8 copy-start.2
  30.3 0.8 copy-start.3
  31.1 0.8 copy-start.4
  31.8 0.8 copy-start.5
  32.6 0.8 copy-start.6
  42.9 28.2 %copy-start.1 = (f32[8,8,128]{2,1,0:T(8,128)S(1)}, f32[8,8,128]{2,1,0:T(8,128)}, u32[]{:S(2)}) copy-start(f32[8,8,128]{2,1,0:T(8,128)} %param.8) | copy-start | bytes 98308
  42.9 4.4 %collective-permute-start.5 = (f32[80,128]{1,0:T(8,128)S(1)}, f32[80,128]{1,0:T(8,128)S(1)}, u32[]{:S(2)}, u32[]{:S(2)}) collective-permute-start(f32[80,128]{1,0:T(8,128)S(1)} %first.1.mine), channel_id=1, source_target_pairs={{0,1},{1,0},{2,3},{3,2},{4,5},{5,4},{6,7},{7,6},{8,9},{9,8},{10,11... | collective-permute-start | bytes 122888 | tf_op jit(solution)/shard_map/ppermute | solution.py:475
  76.2 5.6 %collective-permute-start.6 = (f32[296,128]{1,0:T(8,128)S(1)}, f32[296,128]{1,0:T(8,128)S(1)}, u32[]{:S(2)}, u32[]{:S(2)}) collective-permute-start(f32[296,128]{1,0:T(8,128)S(1)} %get-tuple-element.78.mine), channel_id=1, source_target_pairs={{0,1},{1,0},{2,3},{3,2},{4,5},{5,4},{6,7},{7,6},{8,9},{9,8},{10,11... | collective-permute-start | bytes 454664 | tf_op jit(solution)/shard_map/ppermute | solution.py:475
  81.9 29.6 %collective-permute-start.7 = (f32[48,32,128]{2,1,0:T(8,128)S(1)}, f32[48,32,128]{2,1,0:T(8,128)S(1)}, u32[]{:S(2)}, u32[]{:S(2)}) collective-permute-start(f32[48,32,128]{2,1,0:T(8,128)S(1)} %get-tuple-element.84), channel_id=1, source_target_pairs={{0,16},{16,32},{32,48},{48,64},{64,80},{80,96},{96,112},{112,0},{1... | collective-permute-start | bytes 2359304 | tf_op jit(solution)/shard_map/ppermute | solution.py:475
  82.5 28.9 %collective-permute-start.8 = (f32[48,32,128]{2,1,0:T(8,128)S(1)}, f32[48,32,128]{2,1,0:T(8,128)S(1)}, u32[]{:S(2)}, u32[]{:S(2)}) collective-permute-start(f32[48,32,128]{2,1,0:T(8,128)S(1)} %get-tuple-element.85), channel_id=1, source_target_pairs={{0,112},{16,0},{32,16},{48,32},{64,48},{80,64},{96,80},{112,96},{1... | collective-permute-start | bytes 2359304 | tf_op jit(solution)/shard_map/ppermute | solution.py:475
  85.4 26.0 %collective-permute-start.9 = (f32[8,6,32,128]{3,2,1,0:T(8,128)S(1)}, f32[8,6,32,128]{3,2,1,0:T(8,128)S(1)}, u32[]{:S(2)}, u32[]{:S(2)}) collective-permute-start(f32[8,6,32,128]{3,2,1,0:T(8,128)S(1)} %get-tuple-element.86), channel_id=1, source_target_pairs={{0,2},{2,4},{4,6},{6,8},{8,10},{10,12},{12,14},{14,0},{1,3},{3,5},... | collective-permute-start | bytes 2359304 | tf_op jit(solution)/shard_map/ppermute | solution.py:475
  89.7 21.8 %collective-permute-start.10 = (f32[8,6,32,128]{3,2,1,0:T(8,128)S(1)}, f32[8,6,32,128]{3,2,1,0:T(8,128)S(1)}, u32[]{:S(2)}, u32[]{:S(2)}) collective-permute-start(f32[8,6,32,128]{3,2,1,0:T(8,128)S(1)} %get-tuple-element.87), channel_id=1, source_target_pairs={{0,14},{2,0},{4,2},{6,4},{8,6},{10,8},{12,10},{14,12},{1,15},{3,1}... | collective-permute-start | bytes 2359304 | tf_op jit(solution)/shard_map/ppermute | solution.py:475
  116.4 5.6 %collective-permute-start.11 = (f32[296,128]{1,0:T(8,128)S(1)}, f32[296,128]{1,0:T(8,128)S(1)}, u32[]{:S(2)}, u32[]{:S(2)}) collective-permute-start(f32[296,128]{1,0:T(8,128)S(1)} %get-tuple-element.90.mine), channel_id=1, source_target_pairs={{0,1},{1,0},{2,3},{3,2},{4,5},{5,4},{6,7},{7,6},{8,9},{9,8},{10,11... | collective-permute-start | bytes 454664 | tf_op jit(solution)/shard_map/ppermute | solution.py:475
  122.0 31.2 %collective-permute-start.12 = (f32[48,32,128]{2,1,0:T(8,128)S(1)}, f32[48,32,128]{2,1,0:T(8,128)S(1)}, u32[]{:S(2)}, u32[]{:S(2)}) collective-permute-start(f32[48,32,128]{2,1,0:T(8,128)S(1)} %get-tuple-element.96), channel_id=1, source_target_pairs={{0,16},{16,32},{32,48},{48,64},{64,80},{80,96},{96,112},{112,0},{1... | collective-permute-start | bytes 2359304 | tf_op jit(solution)/shard_map/ppermute | solution.py:475
  122.5 30.6 %collective-permute-start.13 = (f32[48,32,128]{2,1,0:T(8,128)S(1)}, f32[48,32,128]{2,1,0:T(8,128)S(1)}, u32[]{:S(2)}, u32[]{:S(2)}) collective-permute-start(f32[48,32,128]{2,1,0:T(8,128)S(1)} %get-tuple-element.97), channel_id=1, source_target_pairs={{0,112},{16,0},{32,16},{48,32},{64,48},{80,64},{96,80},{112,96},{1... | collective-permute-start | bytes 2359304 | tf_op jit(solution)/shard_map/ppermute | solution.py:475
  125.6 27.6 %collective-permute-start.14 = (f32[8,6,32,128]{3,2,1,0:T(8,128)S(1)}, f32[8,6,32,128]{3,2,1,0:T(8,128)S(1)}, u32[]{:S(2)}, u32[]{:S(2)}) collective-permute-start(f32[8,6,32,128]{3,2,1,0:T(8,128)S(1)} %get-tuple-element.98), channel_id=1, source_target_pairs={{0,2},{2,4},{4,6},{6,8},{8,10},{10,12},{12,14},{14,0},{1,3},{3,5},... | collective-permute-start | bytes 2359304 | tf_op jit(solution)/shard_map/ppermute | solution.py:475
  129.7 23.5 %collective-permute-start.15 = (f32[8,6,32,128]{3,2,1,0:T(8,128)S(1)}, f32[8,6,32,128]{3,2,1,0:T(8,128)S(1)}, u32[]{:S(2)}, u32[]{:S(2)}) collective-permute-start(f32[8,6,32,128]{3,2,1,0:T(8,128)S(1)} %get-tuple-element.99), channel_id=1, source_target_pairs={{0,14},{2,0},{4,2},{6,4},{8,6},{10,8},{12,10},{14,12},{1,15},{3,1}... | collective-permute-start | bytes 2359304 | tf_op jit(solution)/shard_map/ppermute | solution.py:475
  158.1 6.2 %collective-permute-start.16 = (f32[296,128]{1,0:T(8,128)S(1)}, f32[296,128]{1,0:T(8,128)S(1)}, u32[]{:S(2)}, u32[]{:S(2)}) collective-permute-start(f32[296,128]{1,0:T(8,128)S(1)} %get-tuple-element.101.mine), channel_id=1, source_target_pairs={{0,1},{1,0},{2,3},{3,2},{4,5},{5,4},{6,7},{7,6},{8,9},{9,8},{10,11... | collective-permute-start | bytes 454664 | tf_op jit(solution)/shard_map/ppermute | solution.py:475
  164.3 28.2 %collective-permute-start.17 = (f32[48,32,128]{2,1,0:T(8,128)S(1)}, f32[48,32,128]{2,1,0:T(8,128)S(1)}, u32[]{:S(2)}, u32[]{:S(2)}) collective-permute-start(f32[48,32,128]{2,1,0:T(8,128)S(1)} %get-tuple-element.107), channel_id=1, source_target_pairs={{0,16},{16,32},{32,48},{48,64},{64,80},{80,96},{96,112},{112,0},{1... | collective-permute-start | bytes 2359304 | tf_op jit(solution)/shard_map/ppermute | solution.py:475
  164.3 28.2 %collective-permute-start.18 = (f32[48,32,128]{2,1,0:T(8,128)S(1)}, f32[48,32,128]{2,1,0:T(8,128)S(1)}, u32[]{:S(2)}, u32[]{:S(2)}) collective-permute-start(f32[48,32,128]{2,1,0:T(8,128)S(1)} %get-tuple-element.108), channel_id=1, source_target_pairs={{0,112},{16,0},{32,16},{48,32},{64,48},{80,64},{96,80},{112,96},{1... | collective-permute-start | bytes 2359304 | tf_op jit(solution)/shard_map/ppermute | solution.py:475
  167.8 24.6 %collective-permute-start.19 = (f32[8,6,32,128]{3,2,1,0:T(8,128)S(1)}, f32[8,6,32,128]{3,2,1,0:T(8,128)S(1)}, u32[]{:S(2)}, u32[]{:S(2)}) collective-permute-start(f32[8,6,32,128]{3,2,1,0:T(8,128)S(1)} %get-tuple-element.109), channel_id=1, source_target_pairs={{0,2},{2,4},{4,6},{6,8},{8,10},{10,12},{12,14},{14,0},{1,3},{3,5},... | collective-permute-start | bytes 2359304 | tf_op jit(solution)/shard_map/ppermute | solution.py:475
  171.5 21.0 %collective-permute-start.20 = (f32[8,6,32,128]{3,2,1,0:T(8,128)S(1)}, f32[8,6,32,128]{3,2,1,0:T(8,128)S(1)}, u32[]{:S(2)}, u32[]{:S(2)}) collective-permute-start(f32[8,6,32,128]{3,2,1,0:T(8,128)S(1)} %get-tuple-element.110), channel_id=1, source_target_pairs={{0,14},{2,0},{4,2},{6,4},{8,6},{10,8},{12,10},{14,12},{1,15},{3,1}... | collective-permute-start | bytes 2359304 | tf_op jit(solution)/shard_map/ppermute | solution.py:475

commit v7 on v6

--- a/solution.py
+++ b/solution.py
@@ -118,7 +118,7 @@
 
 
 def rearrange_kernel(src, *refs):
-    field, faces, (z_face, in_sem) = refs[0], refs[1:5], refs[5:]
+    field, faces, in_sem = refs[0], refs[1:5], refs[5]
     for row in range(ROWS):
         pltpu.make_async_copy(src.at[:, row, :], field.at[row], in_sem.at[row]).start()
 
@@ -128,16 +128,14 @@
             pltpu.make_async_copy(src.at[:, row, :], field.at[row], in_sem.at[row]).wait()
         rows = [field[x * SY + y] for y in range(SY)]
         write_faces(x, rows, *faces)
-        for part in range(2):
-            z_face[pl.ds((2 * x + part) * 16, 16), :] = z_faces(rows[4 * part : 4 * part + 4])
 
 
 def rearrange(orbitals):
     return pl.pallas_call(
         rearrange_kernel,
-        out_shape=[BLOCK, X_FACE, X_FACE, Y_FACE, Y_FACE, jax.ShapeDtypeStruct((ZROWS, LANES), F32)],
+        out_shape=[BLOCK, X_FACE, X_FACE, Y_FACE, Y_FACE],
         in_specs=any_specs(1),
-        out_specs=vmem_specs(6),
+        out_specs=vmem_specs(5),
         scratch_shapes=[
             pltpu.SemaphoreType.DMA((ROWS,)),
         ],
@@ -146,31 +144,27 @@
     )(orbitals)
 
 
-def build_kernel(starts, keys, w0, w1, w2, w3, out, held, weights, sem):
+def build_kernel(starts, points, out, held, sem):
     full = pl.ds(0, SLOTS // LANES)
-    loads = [pltpu.make_async_copy(keys, held.at[full], sem.at[NPJ])]
-    for j, w in enumerate((w0, w1, w2, w3)):
-        loads.append(pltpu.make_async_copy(w, weights.at[j, full], sem.at[j]))
-    for load in loads:
-        load.start()
-    held[pl.ds(SLOTS // LANES, 8), :] = jnp.full((8, LANES), ROWS * SZ * 64, jnp.int32)
+    load = pltpu.make_async_copy(points, held.at[:, full], sem)
+    load.start()
+    held[0, pl.ds(SLOTS // LANES, 8), :] = jnp.full((8, LANES), ROWS * SZ * 64, F32)
     for j in range(NPJ):
-        weights[j, pl.ds(SLOTS // LANES, 8), :] = jnp.zeros((8, LANES), F32)
-    for load in loads:
-        load.wait()
+        held[1 + j, pl.ds(SLOTS // LANES, 8), :] = jnp.zeros((8, LANES), F32)
+    load.wait()
     target_at = lax.broadcasted_iota(jnp.int32, (TGT, 2 * LANES), 0)
     z_at = lax.broadcasted_iota(jnp.int32, (SZ, 2 * LANES), 0)
 
     def window(row, block):
-        key = jnp.concatenate([held[pl.ds(block, 1), :], held[pl.ds(block + 1, 1), :]], axis=1)
+        def window_of(i):
+            return jnp.concatenate([held[i, pl.ds(block, 1), :], held[i, pl.ds(block + 1, 1), :]], axis=1)
+
+        key = window_of(0).astype(jnp.int32)
         target = jnp.where((key >> 13) == row, key & 63, 63)
         chosen = target_at == target
         parts = []
         for j in range(NPJ):
-            w = jnp.concatenate(
-                [weights[j, pl.ds(block, 1), :], weights[j, pl.ds(block + 1, 1), :]], axis=1
-            )
-            parts.append(jnp.where(chosen, w, 0.0))
+            parts.append(jnp.where(chosen, window_of(1 + j), 0.0))
         hi, lo = split2(jnp.concatenate(parts, axis=0))
         place = jnp.where(z_at == ((key >> 6) & 127), 1.0, 0.0).astype(BF16)
         both = dot(jnp.concatenate([hi, lo], axis=0), place, NT)
@@ -202,20 +196,19 @@
                 out[at] = jnp.concatenate([hi, lo], axis=0)
 
 
-def build(starts, keys, weights):
+def build(starts, points):
     return pl.pallas_call(
         build_kernel,
         out_shape=MATRIX,
-        in_specs=[pl.BlockSpec(memory_space=pltpu.SMEM)] + any_specs(5),
+        in_specs=[pl.BlockSpec(memory_space=pltpu.SMEM)] + any_specs(1),
         out_specs=pl.BlockSpec(memory_space=pltpu.VMEM),
         scratch_shapes=[
-            pltpu.VMEM((SLOTS // LANES + 8, LANES), jnp.int32),
-            pltpu.VMEM((NPJ, SLOTS // LANES + 8, LANES), F32),
-            pltpu.SemaphoreType.DMA((NPJ + 1,)),
+            pltpu.VMEM((1 + NPJ, SLOTS // LANES + 8, LANES), F32),
+            pltpu.SemaphoreType.DMA(()),
         ],
         compiler_params=PARAMS,
         name="build",
-    )(starts, keys, *weights)
+    )(starts, points)
 
 
 def partial_of(mat, values):
@@ -229,20 +222,20 @@
 
 
 def first_kernel(field, mat, own, out, total):
-    row = lax.broadcasted_iota(jnp.int32, (TGT, LANES), 0)
-    couplings = jnp.where(row == 16, own[pl.ds(0, 1), :], jnp.where(row == 17, own[pl.ds(1, 1), :], 0.0))
-    out[pl.ds(TGT, TGT), :] = couplings
+    for g in range(GROUPS):
+        out[pl.ds(16 * g, 16), :] = z_faces([field[4 * g + i] for i in range(4)])
     total[...] = jnp.zeros_like(total)
     for pair in range(PAIRS):
         values = jnp.concatenate([field[2 * pair], field[2 * pair + 1]], axis=1)
         total[...] = total[...] + partial_of(mat[pair], values)
-    out[pl.ds(0, TGT), :] = packed_partial(total[...])
+    out[pl.ds(ZROWS, TGT), :] = packed_partial(total[...])
+    out[pl.ds(ZROWS + TGT, 8), :] = own[...]
 
 
 def first(field, mat, own):
     return pl.pallas_call(
         first_kernel,
-        out_shape=jax.ShapeDtypeStruct((2 * TGT, LANES), F32),
+        out_shape=jax.ShapeDtypeStruct((ZROWS + TGT + 8, LANES), F32),
         in_specs=vmem_specs(3),
         out_specs=pl.BlockSpec(memory_space=pltpu.VMEM),
         scratch_shapes=[pltpu.VMEM(TOTAL, F32)],
@@ -251,43 +244,48 @@
     )(field, mat, own)
 
 
-def spread(frame, axis, stride, out, at):
+def spread(frame, axis, stride, along, out, at):
     me = lax.axis_index(axis)
-    row = lax.broadcasted_iota(jnp.int32, (TGT, LANES), 0)
-    digit = (row // stride) % 3
+    target = lax.broadcasted_iota(jnp.int32, frame.shape, along)
+    digit = (target // stride) % 3
     for distance in range(-3, 5):
         if abs(distance) > 2:
-            piece = jnp.zeros((TGT, LANES), F32)
+            piece = jnp.zeros(frame.shape, F32)
         else:
-            moved = frame if distance == 0 else pltpu.roll(frame, (-stride * distance) % TGT, 0)
-            valid = (digit + distance >= 0) & (digit + distance <= 2) & (row < 36)
+            by = (-stride * distance) % frame.shape[along]
+            moved = frame if distance == 0 else pltpu.roll(frame, by, along)
+            valid = (digit + distance >= 0) & (digit + distance <= 2) & (target < 36)
             piece = jnp.where(valid, moved, 0.0)
         out[(me + distance + 8) % 8, at, :] = piece
 
 
-def spread_zy_kernel(frames, mine, other, out):
-    row = lax.broadcasted_iota(jnp.int32, (TGT, LANES), 0)
-    start = mine.shape[0] - frames * TGT
-    for f in range(frames):
-        at = pl.ds(start + f * TGT, TGT)
+def parts_of(rows):
+    return ((0, TGT, 0),) if rows == TGT else ((0, TGT, 0), (TGT, 8, 1))
+
+
+def spread_zy_kernel(mine, other, out):
+    for start, size, along in parts_of(out.shape[1]):
+        at = pl.ds(ZROWS + start, size)
         theirs = other[at, :]
-        swapped = jnp.where(row & 2 == 0, pltpu.roll(theirs, TGT - 2, 0), pltpu.roll(theirs, 2, 0))
-        spread(mine[at, :] + swapped, "gy", 4, out, pl.ds(f * TGT, TGT))
-
-
-def spread_x_kernel(frames, came, out):
-    for f in range(frames):
-        at = pl.ds(f * TGT, TGT)
+        target = lax.broadcasted_iota(jnp.int32, theirs.shape, along)
+        up = pltpu.roll(theirs, theirs.shape[along] - 2, along)
+        swapped = jnp.where(target & 2 == 0, up, pltpu.roll(theirs, 2, along))
+        spread(mine[at, :] + swapped, "gy", 4, along, out, pl.ds(start, size))
+
+
+def spread_x_kernel(came, out):
+    for start, size, along in parts_of(out.shape[1]):
+        at = pl.ds(start, size)
         frame = came[0, at, :]
         for slot in range(1, 8):
             frame = frame + came[slot, at, :]
-        spread(frame, "gx", 12, out, at)
-
-
-def spread_call(kernel, frames, *arrays):
+        spread(frame, "gx", 12, along, out, at)
+
+
+def spread_call(kernel, rows, *arrays):
     return pl.pallas_call(
-        functools.partial(kernel, frames),
-        out_shape=jax.ShapeDtypeStruct((8, frames * TGT, LANES), F32),
+        kernel,
+        out_shape=jax.ShapeDtypeStruct((8, rows, LANES), F32),
         in_specs=vmem_specs(len(arrays)),
         out_specs=pl.BlockSpec(memory_space=pltpu.VMEM),
         compiler_params=PARAMS,
@@ -353,7 +351,9 @@
     for slot in range(1, came.shape[0]):
         frame = frame + came[slot]
     if first_step:
-        coupling[...] = frame[TGT:]
+        by_channel = jnp.concatenate([frame[TGT:], jnp.zeros((LANES - 8, LANES), F32)], axis=0).T
+        columns = [jnp.broadcast_to(by_channel[:TGT, j : j + 1], (TGT, NB)) for j in range(NPJ)]
+        coupling[...] = jnp.concatenate(columns, axis=1)
         frame = frame[:TGT]
     frame = frame * (alpha * coupling[...])
     stacked = jnp.concatenate([frame[:, j * NB : (j + 1) * NB] for j in range(NPJ)], axis=0)
@@ -477,7 +477,7 @@
 
 def local(orbitals, potential, projector, point_cell, target, point_count, coupling):
     bands, size_x, size_y, size_z = orbitals.shape
-    field, x_low, x_high, y_low, y_high, z_face = rearrange(orbitals.reshape(NB, ROWS, SZ))
+    field, x_low, x_high, y_low, y_high = rearrange(orbitals.reshape(NB, ROWS, SZ))
     pot = potential.reshape(ROWS, SZ)
 
     alive = lax.iota(jnp.int32, SLOTS) < point_count.reshape(())
@@ -489,36 +489,29 @@
         (key[None, :] < (lax.iota(jnp.int32, ROWS + 1) * (SZ * 64))[:, None]).astype(jnp.int32), axis=1
     )
     ordered = lax.sort((key,) + tuple(projector[j] for j in range(NPJ)), num_keys=1, is_stable=False)
-    ordered = [o.reshape(SLOTS // LANES, LANES) for o in ordered]
-    mat = build(starts, ordered[0], ordered[1:])
-
-    own = jnp.repeat(coupling, NB, axis=1)
+    points = jnp.stack([ordered[0].astype(F32), *ordered[1:]]).reshape(1 + NPJ, SLOTS // LANES, LANES)
+    mat = build(starts, points)
+
+    own = jnp.pad(coupling.T, ((0, 8 - NPJ), (16, LANES - 18)))
     other = ()
     for k in range(DEGREE):
         start, last = k == 0, k == DEGREE - 1
         if start:
-            faces = shift(z_face, "gz", 1)
-        else:
-            came = shift(message, "gz", 1)
-            came, x_low, x_high, y_low, y_high = lax.optimization_barrier(
-                (came, x_low, x_high, y_low, y_high)
-            )
-            faces = came
-        x_left = shift(x_high, "gx", 1)
-        x_right = shift(x_low, "gx", -1)
+            x_left = shift(x_high, "gx", 1)
+            x_right = shift(x_low, "gx", -1)
+            mat, field, x_left, x_right = lax.optimization_barrier((mat, field, x_left, x_right))
+            message = first(field, mat, own)
+            message, y_low, y_high = lax.optimization_barrier((message, y_low, y_high))
+        faces = shift(message, "gz", 1)
         y_left = shift(y_high, "gy", 1)
         y_right = shift(y_low, "gy", -1)
-        if start:
-            mat, field, faces, x_left, x_right, y_left, y_right = lax.optimization_barrier(
-                (mat, field, faces, x_left, x_right, y_left, y_right)
-            )
-            message = first(field, mat, own)
-            came = shift(message, "gz", 1)
-        frames = 2 if start else 1
-        sends = spread_call(spread_zy_kernel, frames, message, came)
-        came = lax.all_to_all(sends, "gy", 0, 0)
-        sends = spread_call(spread_x_kernel, frames, came)
-        came = lax.all_to_all(sends, "gx", 0, 0)
+        if not start:
+            faces, x_low, x_high = lax.optimization_barrier((faces, x_low, x_high))
+            x_left = shift(x_high, "gx", 1)
+            x_right = shift(x_low, "gx", -1)
+        rows = message.shape[0] - ZROWS
+        came = lax.all_to_all(spread_call(spread_zy_kernel, rows, message, faces), "gy", 0, 0)
+        came = lax.all_to_all(spread_call(spread_x_kernel, rows, came), "gx", 0, 0)
         outs = step(start, last, field, faces, x_left, x_right, y_left, y_right, pot, came, mat, *other)
         previous = field
         if last:

time: 222 us -> 199 us (0.90)
  waiting for transfers between devices: 20.3 us -> 4.21 us
  blocking collectives: 109 us -> 101 us
    ppermute x21 -> x20, waiting for transfers between devices: 20.3 us -> 4.21 us  [shift(): lax.ppermute(value, axis, [(i, (i + by) % count) for i in range(count)])]
    all_to_all x8, blocking collectives: 89.4 us -> 81.9 us  [the longest x4 48.3 us: local(): lax.all_to_all(spread_call(spread_zy_kernel, rows, message, faces), 'gy',...]
    ppermute x21 -> x20, starting transfers between devices: 35 us -> 36.8 us  [shift(): lax.ppermute(value, axis, [(i, (i + by) % count) for i in range(count)])]
    unnamed x14 -> x12, local copies, waits for them, and re-layouts: 5.02 us -> 5.2 us
  transfers between devices with their start and end apart: 21 -> 20, of which waited for: 4 -> 3; matrix products, arithmetic and copies ran while one was open for 6% -> 8% of each run, Pallas kernels for 3% -> 4%
where the time goes in v7:
time: 199 us; the launch traced here: 197 us
  blocking collectives  101 us (51%)
  starting transfers between devices  36.8 us (18%)
  Pallas kernels  36.5 us (18%)
  other arithmetic  9.32 us (5%)
  local copies, waits for them, and re-layouts  7.99 us (4%)
  waiting for transfers between devices  4.21 us (2%)
    all_to_all x4, blocking collectives, local(): lax.all_to_all(spread_call(spread_zy_kernel, rows, message, faces), 'gy',...  48.3 us
    ppermute x20, starting transfers between devices, shift(): lax.ppermute(value, axis, [(i, (i + by) % count) for i in range(count)])  36.8 us
    all_to_all x4, blocking collectives, local(): came = lax.all_to_all(spread_call(spread_x_kernel, rows, came), 'gx', 0, 0)  33.6 us
    all_to_all x1, blocking collectives, local(): lax.all_to_all(jnp.broadcast_to(gram[None], (devices,) + gram.shape), axe...  19.6 us
    pallas_call x4, Pallas kernels, step(): pl.pallas_call(functools.partial(step_kernel, first_step, last_step), out...  18.4 us
    sort x1, other arithmetic, local(): lax.sort((key,) + tuple((projector[j] for j in range(NPJ))), num_keys=1,...  7.28 us
    pallas_call x1, Pallas kernels, build(): pl.pallas_call(build_kernel, out_shape=MATRIX, in_specs=[pl.BlockSpec(mem...  7.26 us
    unnamed x12, local copies, waits for them, and re-layouts  5.2 us
  transfers between devices with their start and end apart: 20, of which 3 were waited for; matrix products, arithmetic and copies ran while one was open for 8% of the time, Pallas kernels for 4%

profile of v7, /device:TPU:1, one launch (start us, length us, event | category | flops | bytes accessed | tf_op | source)
XLA Modules:
  0.0 197.3 jit_solution(11382285487410436090)
XLA Ops:
  1.2 3.1 %rearrange.1 = (f32[64,32,128]{2,1,0:T(8,128)S(1)}, f32[48,32,128]{2,1,0:T(8,128)}, f32[48,32,128]{2,1,0:T(8,128)}, f32[8,6,32,128]{3,2,1,0:T(8,128)S(1)}, f32[8,6,32,128]{3,2,1,0:T(8,128)S(1)}) custom-call(f32[32,64,128]{2,1,0:T(8,128)S(1)} %bitcast.20), custom_call_target="tpu_custom_call" | custom-call | tf_op jit(solution)/shard_map/rearrange/pallas_call | solution.py:134
  5.3 2.1 %collective-permute-start = (f32[48,32,128]{2,1,0:T(8,128)}, f32[48,32,128]{2,1,0:T(8,128)S(1)}, u32[]{:S(2)}, u32[]{:S(2)}) collective-permute-start(f32[48,32,128]{2,1,0:T(8,128)} %get-tuple-element.58), channel_id=1, source_target_pairs={{0,16},{16,32},{32,48},{48,64},{64,80},{80,96},{96,112},{112,0},{1... | collective-permute-start | bytes 2359304 | tf_op jit(solution)/shard_map/ppermute | solution.py:475
  7.4 2.8 %collective-permute-start.1 = (f32[48,32,128]{2,1,0:T(8,128)}, f32[48,32,128]{2,1,0:T(8,128)S(1)}, u32[]{:S(2)}, u32[]{:S(2)}) collective-permute-start(f32[48,32,128]{2,1,0:T(8,128)} %get-tuple-element.59), channel_id=1, source_target_pairs={{0,112},{16,0},{32,16},{48,32},{64,48},{80,64},{96,80},{112,96},{1... | collective-permute-start | bytes 2359304 | tf_op jit(solution)/shard_map/ppermute | solution.py:475
  14.4 7.3 %sort.33 = (s32[8192]{0:T(1024)}, f32[8192]{0:T(1024)}, f32[8192]{0:T(1024)}, f32[8192]{0:T(1024)}, f32[8192]{0:T(1024)}) sort(s32[8192]{0:T(1024)S(1)} %fusion.5, f32[8192]{0:T(1024)S(1)} %bitcast.27, f32[8192]{0:T(1024)S(1)} %bitcast.26, f32[8192]{0:T(1024)} %bitcast.28, f32[8192]{0:T(1024)S(1)} %bitcast.25), dimensions={0}, to_apply=%region_1.2 | sort | flops 106496 | bytes 327680 | tf_op jit(solution)/shard_map/sort | solution.py:491
  26.0 7.3 %build.1.mat.refs_8_ = bf16[32,320,256]{2,1,0:T(8,128)(2,1)S(1)} custom-call(s32[65]{0:T(128)S(1)} %convert_reduce_fusion.starts, f32[5,64,128]{2,1,0:T(8,128)S(1)} %bitcast_dynamic-update-slice_fusion.points), custom_call_target="tpu_custom_call" | custom-call | tf_op jit(solution)/shard_map/build/pallas_call | solution.py:200
  33.3 2.1 %first.1.mine = f32[304,128]{1,0:T(8,128)S(1)} custom-call(f32[64,32,128]{2,1,0:T(8,128)S(1)} %get-tuple-element.60.field.refs_0_.refs_9_, bf16[32,320,256]{2,1,0:T(8,128)(2,1)S(1)} %build.1.mat.refs_8_, f32[8,128]{1,0:T(8,128)S(1)} %pad.4.own), custom_call_target="tpu_custom_call" | custom-call | tf_op jit(solution)/shard_map/first/pallas_call | solution.py:236
  35.4 2.1 %collective-permute-start.3 = (f32[8,6,32,128]{3,2,1,0:T(8,128)S(1)}, f32[8,6,32,128]{3,2,1,0:T(8,128)S(1)}, u32[]{:S(2)}, u32[]{:S(2)}) collective-permute-start(f32[8,6,32,128]{3,2,1,0:T(8,128)S(1)} %copy-done.3), channel_id=1, source_target_pairs={{0,2},{2,4},{4,6},{6,8},{8,10},{10,12},{12,14},{14,0},{1,3},{3,5},... | collective-permute-start | bytes 2359304 | tf_op jit(solution)/shard_map/ppermute | solution.py:475
  37.5 3.4 %collective-permute-start.2 = (f32[304,128]{1,0:T(8,128)S(1)}, f32[304,128]{1,0:T(8,128)S(1)}, u32[]{:S(2)}, u32[]{:S(2)}) collective-permute-start(f32[304,128]{1,0:T(8,128)S(1)} %first.1.mine), channel_id=1, source_target_pairs={{0,1},{1,0},{2,3},{3,2},{4,5},{5,4},{6,7},{7,6},{8,9},{9,8},{10,11... | collective-permute-start | bytes 466952 | tf_op jit(solution)/shard_map/ppermute | solution.py:475
  40.9 2.6 %collective-permute-done.2.other.refs_1_ = f32[304,128]{1,0:T(8,128)S(1)} collective-permute-done((f32[304,128]{1,0:T(8,128)S(1)}, f32[304,128]{1,0:T(8,128)S(1)}, u32[]{:S(2)}, u32[]{:S(2)}) %collective-permute-start.2) | collective-permute-done | bytes 155680 | tf_op jit(solution)/shard_map/ppermute | solution.py:475
  43.6 12.5 %all_to_all.45.came = f32[8,48,128]{2,1,0:T(8,128)S(1)} all-to-all(f32[8,48,128]{2,1,0:T(8,128)S(1)} %spread.8), channel_id=1, replica_groups=mesh['gx'=8,'gy'=8,'gz'=2] {'gy'}, dimensions={0} | all-to-all | bytes 393216 | tf_op jit(solution)/shard_map/all_to_all | solution.py:513
  56.2 8.5 %all_to_all.46.refs_7_ = f32[8,48,128]{2,1,0:T(8,128)S(1)} all-to-all(f32[8,48,128]{2,1,0:T(8,128)S(1)} %spread.9), channel_id=1, replica_groups=mesh['gx'=8,'gy'=8,'gz'=2] {'gx'}, dimensions={0} | all-to-all | bytes 393216 | tf_op jit(solution)/shard_map/all_to_all | solution.py:514
  64.7 4.3 %step.4 = (f32[64,32,128]{2,1,0:T(8,128)S(1)}, f32[48,32,128]{2,1,0:T(8,128)S(1)}, f32[48,32,128]{2,1,0:T(8,128)S(1)}, f32[8,6,32,128]{3,2,1,0:T(8,128)S(1)}, f3...) custom-call(f32[64,32,128]{2,1,0:T(8,128)S(1)} %get-tuple-element.60.field.refs_0_.refs_9_, ...), custom_call_target="tpu_custom_call" | custom-call | tf_op jit(solution)/shard_map/step/pallas_call | solution.py:404
  69.0 3.1 %collective-permute-start.5 = (f32[296,128]{1,0:T(8,128)S(1)}, f32[296,128]{1,0:T(8,128)S(1)}, u32[]{:S(2)}, u32[]{:S(2)}) collective-permute-start(f32[296,128]{1,0:T(8,128)S(1)} %get-tuple-element.70.mine), channel_id=1, source_target_pairs={{0,1},{1,0},{2,3},{3,2},{4,5},{5,4},{6,7},{7,6},{8,9},{9,8},{10,11... | collective-permute-start | bytes 454664 | tf_op jit(solution)/shard_map/ppermute | solution.py:475
  72.1 2.6 %collective-permute-start.8 = (f32[8,6,32,128]{3,2,1,0:T(8,128)S(1)}, f32[8,6,32,128]{3,2,1,0:T(8,128)S(1)}, u32[]{:S(2)}, u32[]{:S(2)}) collective-permute-start(f32[8,6,32,128]{3,2,1,0:T(8,128)S(1)} %get-tuple-element.76), channel_id=1, source_target_pairs={{0,2},{2,4},{4,6},{6,8},{8,10},{10,12},{12,14},{14,0},{1,3},{3,5},... | collective-permute-start | bytes 2359304 | tf_op jit(solution)/shard_map/ppermute | solution.py:475
  75.3 3.0 %collective-permute-start.7 = (f32[48,32,128]{2,1,0:T(8,128)S(1)}, f32[48,32,128]{2,1,0:T(8,128)S(1)}, u32[]{:S(2)}, u32[]{:S(2)}) collective-permute-start(f32[48,32,128]{2,1,0:T(8,128)S(1)} %get-tuple-element.75), channel_id=1, source_target_pairs={{0,112},{16,0},{32,16},{48,32},{64,48},{80,64},{96,80},{112,96},{1... | collective-permute-start | bytes 2359304 | tf_op jit(solution)/shard_map/ppermute | solution.py:475
  78.3 11.8 %all_to_all.47.came = f32[8,40,128]{2,1,0:T(8,128)S(1)} all-to-all(f32[8,40,128]{2,1,0:T(8,128)S(1)} %spread.10), channel_id=1, replica_groups=mesh['gx'=8,'gy'=8,'gz'=2] {'gy'}, dimensions={0} | all-to-all | bytes 327680 | tf_op jit(solution)/shard_map/all_to_all | solution.py:513
  90.2 8.1 %all_to_all.48.refs_7_ = f32[8,40,128]{2,1,0:T(8,128)S(1)} all-to-all(f32[8,40,128]{2,1,0:T(8,128)S(1)} %spread.11), channel_id=1, replica_groups=mesh['gx'=8,'gy'=8,'gz'=2] {'gx'}, dimensions={0} | all-to-all | bytes 327680 | tf_op jit(solution)/shard_map/all_to_all | solution.py:514
  98.3 4.9 %step.5 = (f32[64,32,128]{2,1,0:T(8,128)S(1)}, f32[48,32,128]{2,1,0:T(8,128)S(1)}, f32[48,32,128]{2,1,0:T(8,128)S(1)}, f32[8,6,32,128]{3,2,1,0:T(8,128)S(1)}, f3...) custom-call(f32[64,32,128]{2,1,0:T(8,128)S(1)} %get-tuple-element.69.refs_0_.refs_9_, ...), custom_call_target="tpu_custom_call" | custom-call | tf_op jit(solution)/shard_map/step/pallas_call | solution.py:404
  103.2 3.3 %collective-permute-start.10 = (f32[296,128]{1,0:T(8,128)S(1)}, f32[296,128]{1,0:T(8,128)S(1)}, u32[]{:S(2)}, u32[]{:S(2)}) collective-permute-start(f32[296,128]{1,0:T(8,128)S(1)} %get-tuple-element.80.mine), channel_id=1, source_target_pairs={{0,1},{1,0},{2,3},{3,2},{4,5},{5,4},{6,7},{7,6},{8,9},{9,8},{10,11... | collective-permute-start | bytes 454664 | tf_op jit(solution)/shard_map/ppermute | solution.py:475
  106.5 2.1 %collective-permute-start.13 = (f32[8,6,32,128]{3,2,1,0:T(8,128)S(1)}, f32[8,6,32,128]{3,2,1,0:T(8,128)S(1)}, u32[]{:S(2)}, u32[]{:S(2)}) collective-permute-start(f32[8,6,32,128]{3,2,1,0:T(8,128)S(1)} %get-tuple-element.86), channel_id=1, source_target_pairs={{0,2},{2,4},{4,6},{6,8},{8,10},{10,12},{12,14},{14,0},{1,3},{3,5},... | collective-permute-start | bytes 2359304 | tf_op jit(solution)/shard_map/ppermute | solution.py:475
  109.6 3.0 %collective-permute-start.12 = (f32[48,32,128]{2,1,0:T(8,128)S(1)}, f32[48,32,128]{2,1,0:T(8,128)S(1)}, u32[]{:S(2)}, u32[]{:S(2)}) collective-permute-start(f32[48,32,128]{2,1,0:T(8,128)S(1)} %get-tuple-element.85), channel_id=1, source_target_pairs={{0,112},{16,0},{32,16},{48,32},{64,48},{80,64},{96,80},{112,96},{1... | collective-permute-start | bytes 2359304 | tf_op jit(solution)/shard_map/ppermute | solution.py:475
  112.7 11.7 %all_to_all.49.came = f32[8,40,128]{2,1,0:T(8,128)S(1)} all-to-all(f32[8,40,128]{2,1,0:T(8,128)S(1)} %spread.12), channel_id=1, replica_groups=mesh['gx'=8,'gy'=8,'gz'=2] {'gy'}, dimensions={0} | all-to-all | bytes 327680 | tf_op jit(solution)/shard_map/all_to_all | solution.py:513
  124.5 8.7 %all_to_all.50.refs_7_ = f32[8,40,128]{2,1,0:T(8,128)S(1)} all-to-all(f32[8,40,128]{2,1,0:T(8,128)S(1)} %spread.13), channel_id=1, replica_groups=mesh['gx'=8,'gy'=8,'gz'=2] {'gx'}, dimensions={0} | all-to-all | bytes 327680 | tf_op jit(solution)/shard_map/all_to_all | solution.py:514
  133.2 4.9 %step.6 = (f32[64,32,128]{2,1,0:T(8,128)S(1)}, f32[48,32,128]{2,1,0:T(8,128)S(1)}, f32[48,32,128]{2,1,0:T(8,128)S(1)}, f32[8,6,32,128]{3,2,1,0:T(8,128)S(1)}, f3...) custom-call(f32[64,32,128]{2,1,0:T(8,128)S(1)} %get-tuple-element.79.refs_0_.refs_9_, ...), custom_call_target="tpu_custom_call" | custom-call | tf_op jit(solution)/shard_map/step/pallas_call | solution.py:404
  138.1 2.4 %collective-permute-start.15 = (f32[296,128]{1,0:T(8,128)S(1)}, f32[296,128]{1,0:T(8,128)S(1)}, u32[]{:S(2)}, u32[]{:S(2)}) collective-permute-start(f32[296,128]{1,0:T(8,128)S(1)} %get-tuple-element.89.mine), channel_id=1, source_target_pairs={{0,1},{1,0},{2,3},{3,2},{4,5},{5,4},{6,7},{7,6},{8,9},{9,8},{10,11... | collective-permute-start | bytes 454664 | tf_op jit(solution)/shard_map/ppermute | solution.py:475
  140.4 2.1 %collective-permute-start.18 = (f32[8,6,32,128]{3,2,1,0:T(8,128)S(1)}, f32[8,6,32,128]{3,2,1,0:T(8,128)S(1)}, u32[]{:S(2)}, u32[]{:S(2)}) collective-permute-start(f32[8,6,32,128]{3,2,1,0:T(8,128)S(1)} %get-tuple-element.95), channel_id=1, source_target_pairs={{0,2},{2,4},{4,6},{6,8},{8,10},{10,12},{12,14},{14,0},{1,3},{3,5},... | collective-permute-start | bytes 2359304 | tf_op jit(solution)/shard_map/ppermute | solution.py:475
  144.0 3.3 %collective-permute-start.17 = (f32[48,32,128]{2,1,0:T(8,128)S(1)}, f32[48,32,128]{2,1,0:T(8,128)S(1)}, u32[]{:S(2)}, u32[]{:S(2)}) collective-permute-start(f32[48,32,128]{2,1,0:T(8,128)S(1)} %get-tuple-element.94), channel_id=1, source_target_pairs={{0,112},{16,0},{32,16},{48,32},{64,48},{80,64},{96,80},{112,96},{1... | collective-permute-start | bytes 2359304 | tf_op jit(solution)/shard_map/ppermute | solution.py:475
  147.3 12.3 %all_to_all.51.came = f32[8,40,128]{2,1,0:T(8,128)S(1)} all-to-all(f32[8,40,128]{2,1,0:T(8,128)S(1)} %spread.14), channel_id=1, replica_groups=mesh['gx'=8,'gy'=8,'gz'=2] {'gy'}, dimensions={0} | all-to-all | bytes 327680 | tf_op jit(solution)/shard_map/all_to_all | solution.py:513
  159.6 8.4 %all_to_all.52.refs_7_ = f32[8,40,128]{2,1,0:T(8,128)S(1)} all-to-all(f32[8,40,128]{2,1,0:T(8,128)S(1)} %spread.15), channel_id=1, replica_groups=mesh['gx'=8,'gy'=8,'gz'=2] {'gx'}, dimensions={0} | all-to-all | bytes 327680 | tf_op jit(solution)/shard_map/all_to_all | solution.py:514
  168.0 4.3 %step.7 = (f32[64,32,128]{2,1,0:T(8,128)S(1)}, f32[8,128]{1,0:T(8,128)S(1)}) custom-call(f32[64,32,128]{2,1,0:T(8,128)S(1)} %get-tuple-element.88.refs_0_, f32[296,128]{1,0:T(8,128)S(1)} %collective-permute-done.15.other.refs_1_, f32[48,32,128]{2,1,0:T(8,128)S(1)} %collective-permute-done.16.refs_2_, f32[48,32,128]{2,1,0:T(8,128)S(1)} %collective-permute-done.17.refs_3_, ...), custom_call_target="tpu_custom_call" | custom-call | tf_op jit(solution)/shard_map/step/pallas_call | solution.py:404
  172.4 19.6 %all_to_all.53.grams = f32[128,8,128]{2,1,0:T(8,128)S(1)} all-to-all(f32[128,8,128]{2,1,0:T(8,128)S(1)} %broadcast_in_dim.7), channel_id=1, replica_groups=mesh['gx'=8,'gy'=8,'gz'=2] {'gx','gy','gz'}, dimensions={0} | all-to-all | bytes 1048576 | tf_op jit(solution)/shard_map/all_to_all | solution.py:528
  192.0 5.1 %finish.1 = f32[32,64,128]{2,1,0:T(8,128)} custom-call(f32[64,32,128]{2,1,0:T(8,128)S(1)} %get-tuple-element.97.field, f32[128,8,128]{2,1,0:T(8,128)S(1)} %all_to_all.53.grams), custom_call_target="tpu_custom_call" | custom-call | tf_op jit(solution)/shard_map/finish/pallas_call | solution.py:458
  (54 shorter events, 13.5 us)
Async XLA Ops:
  0.0 1.2 copy-start
  4.4 0.9 copy-start.2
  5.3 28.0 %collective-permute-start = (f32[48,32,128]{2,1,0:T(8,128)}, f32[48,32,128]{2,1,0:T(8,128)S(1)}, u32[]{:S(2)}, u32[]{:S(2)}) collective-permute-start(f32[48,32,128]{2,1,0:T(8,128)} %get-tuple-element.58), channel_id=1, source_target_pairs={{0,16},{16,32},{32,48},{48,64},{64,80},{80,96},{96,112},{112,0},{1... | collective-permute-start | bytes 2359304 | tf_op jit(solution)/shard_map/ppermute | solution.py:475
  7.4 25.9 %collective-permute-start.1 = (f32[48,32,128]{2,1,0:T(8,128)}, f32[48,32,128]{2,1,0:T(8,128)S(1)}, u32[]{:S(2)}, u32[]{:S(2)}) collective-permute-start(f32[48,32,128]{2,1,0:T(8,128)} %get-tuple-element.59), channel_id=1, source_target_pairs={{0,112},{16,0},{32,16},{48,32},{64,48},{80,64},{96,80},{112,96},{1... | collective-permute-start | bytes 2359304 | tf_op jit(solution)/shard_map/ppermute | solution.py:475
  33.3 2.2 %copy-start.3 = (f32[8,6,32,128]{3,2,1,0:T(8,128)S(1)}, f32[8,6,32,128]{3,2,1,0:T(8,128)}, u32[]{:S(2)}) copy-start(f32[8,6,32,128]{3,2,1,0:T(8,128)} %copy-done.2) | copy-start | bytes 2359300
  33.3 31.4 %copy-start.1 = (f32[8,8,128]{2,1,0:T(8,128)S(1)}, f32[8,8,128]{2,1,0:T(8,128)}, u32[]{:S(2)}) copy-start(f32[8,8,128]{2,1,0:T(8,128)} %param.8) | copy-start | bytes 98308
  35.4 29.2 %collective-permute-start.3 = (f32[8,6,32,128]{3,2,1,0:T(8,128)S(1)}, f32[8,6,32,128]{3,2,1,0:T(8,128)S(1)}, u32[]{:S(2)}, u32[]{:S(2)}) collective-permute-start(f32[8,6,32,128]{3,2,1,0:T(8,128)S(1)} %copy-done.3), channel_id=1, source_target_pairs={{0,2},{2,4},{4,6},{6,8},{8,10},{10,12},{12,14},{14,0},{1,3},{3,5},... | collective-permute-start | bytes 2359304 | tf_op jit(solution)/shard_map/ppermute | solution.py:475
  37.5 27.2 %collective-permute-start.4 = (f32[8,6,32,128]{3,2,1,0:T(8,128)S(1)}, f32[8,6,32,128]{3,2,1,0:T(8,128)S(1)}, u32[]{:S(2)}, u32[]{:S(2)}) collective-permute-start(f32[8,6,32,128]{3,2,1,0:T(8,128)S(1)} %get-tuple-element.68), channel_id=1, source_target_pairs={{0,14},{2,0},{4,2},{6,4},{8,6},{10,8},{12,10},{14,12},{1,15},{3,1}... | collective-permute-start | bytes 2359304 | tf_op jit(solution)/shard_map/ppermute | solution.py:475
  37.5 6.0 %collective-permute-start.2 = (f32[304,128]{1,0:T(8,128)S(1)}, f32[304,128]{1,0:T(8,128)S(1)}, u32[]{:S(2)}, u32[]{:S(2)}) collective-permute-start(f32[304,128]{1,0:T(8,128)S(1)} %first.1.mine), channel_id=1, source_target_pairs={{0,1},{1,0},{2,3},{3,2},{4,5},{5,4},{6,7},{7,6},{8,9},{9,8},{10,11... | collective-permute-start | bytes 466952 | tf_op jit(solution)/shard_map/ppermute | solution.py:475
  69.0 5.7 %collective-permute-start.5 = (f32[296,128]{1,0:T(8,128)S(1)}, f32[296,128]{1,0:T(8,128)S(1)}, u32[]{:S(2)}, u32[]{:S(2)}) collective-permute-start(f32[296,128]{1,0:T(8,128)S(1)} %get-tuple-element.70.mine), channel_id=1, source_target_pairs={{0,1},{1,0},{2,3},{3,2},{4,5},{5,4},{6,7},{7,6},{8,9},{9,8},{10,11... | collective-permute-start | bytes 454664 | tf_op jit(solution)/shard_map/ppermute | solution.py:475
  72.1 26.2 %collective-permute-start.8 = (f32[8,6,32,128]{3,2,1,0:T(8,128)S(1)}, f32[8,6,32,128]{3,2,1,0:T(8,128)S(1)}, u32[]{:S(2)}, u32[]{:S(2)}) collective-permute-start(f32[8,6,32,128]{3,2,1,0:T(8,128)S(1)} %get-tuple-element.76), channel_id=1, source_target_pairs={{0,2},{2,4},{4,6},{6,8},{8,10},{10,12},{12,14},{14,0},{1,3},{3,5},... | collective-permute-start | bytes 2359304 | tf_op jit(solution)/shard_map/ppermute | solution.py:475
  74.7 23.6 %collective-permute-start.9 = (f32[8,6,32,128]{3,2,1,0:T(8,128)S(1)}, f32[8,6,32,128]{3,2,1,0:T(8,128)S(1)}, u32[]{:S(2)}, u32[]{:S(2)}) collective-permute-start(f32[8,6,32,128]{3,2,1,0:T(8,128)S(1)} %get-tuple-element.77), channel_id=1, source_target_pairs={{0,14},{2,0},{4,2},{6,4},{8,6},{10,8},{12,10},{14,12},{1,15},{3,1}... | collective-permute-start | bytes 2359304 | tf_op jit(solution)/shard_map/ppermute | solution.py:475
  74.7 23.6 %collective-permute-start.6 = (f32[48,32,128]{2,1,0:T(8,128)S(1)}, f32[48,32,128]{2,1,0:T(8,128)S(1)}, u32[]{:S(2)}, u32[]{:S(2)}) collective-permute-start(f32[48,32,128]{2,1,0:T(8,128)S(1)} %get-tuple-element.74), channel_id=1, source_target_pairs={{0,16},{16,32},{32,48},{48,64},{64,80},{80,96},{96,112},{112,0},{1... | collective-permute-start | bytes 2359304 | tf_op jit(solution)/shard_map/ppermute | solution.py:475
  75.3 23.0 %collective-permute-start.7 = (f32[48,32,128]{2,1,0:T(8,128)S(1)}, f32[48,32,128]{2,1,0:T(8,128)S(1)}, u32[]{:S(2)}, u32[]{:S(2)}) collective-permute-start(f32[48,32,128]{2,1,0:T(8,128)S(1)} %get-tuple-element.75), channel_id=1, source_target_pairs={{0,112},{16,0},{32,16},{48,32},{64,48},{80,64},{96,80},{112,96},{1... | collective-permute-start | bytes 2359304 | tf_op jit(solution)/shard_map/ppermute | solution.py:475
  103.2 5.9 %collective-permute-start.10 = (f32[296,128]{1,0:T(8,128)S(1)}, f32[296,128]{1,0:T(8,128)S(1)}, u32[]{:S(2)}, u32[]{:S(2)}) collective-permute-start(f32[296,128]{1,0:T(8,128)S(1)} %get-tuple-element.80.mine), channel_id=1, source_target_pairs={{0,1},{1,0},{2,3},{3,2},{4,5},{5,4},{6,7},{7,6},{8,9},{9,8},{10,11... | collective-permute-start | bytes 454664 | tf_op jit(solution)/shard_map/ppermute | solution.py:475
  106.5 26.7 %collective-permute-start.13 = (f32[8,6,32,128]{3,2,1,0:T(8,128)S(1)}, f32[8,6,32,128]{3,2,1,0:T(8,128)S(1)}, u32[]{:S(2)}, u32[]{:S(2)}) collective-permute-start(f32[8,6,32,128]{3,2,1,0:T(8,128)S(1)} %get-tuple-element.86), channel_id=1, source_target_pairs={{0,2},{2,4},{4,6},{6,8},{8,10},{10,12},{12,14},{14,0},{1,3},{3,5},... | collective-permute-start | bytes 2359304 | tf_op jit(solution)/shard_map/ppermute | solution.py:475
  108.6 24.5 %collective-permute-start.14 = (f32[8,6,32,128]{3,2,1,0:T(8,128)S(1)}, f32[8,6,32,128]{3,2,1,0:T(8,128)S(1)}, u32[]{:S(2)}, u32[]{:S(2)}) collective-permute-start(f32[8,6,32,128]{3,2,1,0:T(8,128)S(1)} %get-tuple-element.87), channel_id=1, source_target_pairs={{0,14},{2,0},{4,2},{6,4},{8,6},{10,8},{12,10},{14,12},{1,15},{3,1}... | collective-permute-start | bytes 2359304 | tf_op jit(solution)/shard_map/ppermute | solution.py:475
  109.1 24.1 %collective-permute-start.11 = (f32[48,32,128]{2,1,0:T(8,128)S(1)}, f32[48,32,128]{2,1,0:T(8,128)S(1)}, u32[]{:S(2)}, u32[]{:S(2)}) collective-permute-start(f32[48,32,128]{2,1,0:T(8,128)S(1)} %get-tuple-element.84), channel_id=1, source_target_pairs={{0,16},{16,32},{32,48},{48,64},{64,80},{80,96},{96,112},{112,0},{1... | collective-permute-start | bytes 2359304 | tf_op jit(solution)/shard_map/ppermute | solution.py:475
  109.6 23.6 %collective-permute-start.12 = (f32[48,32,128]{2,1,0:T(8,128)S(1)}, f32[48,32,128]{2,1,0:T(8,128)S(1)}, u32[]{:S(2)}, u32[]{:S(2)}) collective-permute-start(f32[48,32,128]{2,1,0:T(8,128)S(1)} %get-tuple-element.85), channel_id=1, source_target_pairs={{0,112},{16,0},{32,16},{48,32},{64,48},{80,64},{96,80},{112,96},{1... | collective-permute-start | bytes 2359304 | tf_op jit(solution)/shard_map/ppermute | solution.py:475
  138.1 5.6 %collective-permute-start.15 = (f32[296,128]{1,0:T(8,128)S(1)}, f32[296,128]{1,0:T(8,128)S(1)}, u32[]{:S(2)}, u32[]{:S(2)}) collective-permute-start(f32[296,128]{1,0:T(8,128)S(1)} %get-tuple-element.89.mine), channel_id=1, source_target_pairs={{0,1},{1,0},{2,3},{3,2},{4,5},{5,4},{6,7},{7,6},{8,9},{9,8},{10,11... | collective-permute-start | bytes 454664 | tf_op jit(solution)/shard_map/ppermute | solution.py:475
  140.4 27.5 %collective-permute-start.18 = (f32[8,6,32,128]{3,2,1,0:T(8,128)S(1)}, f32[8,6,32,128]{3,2,1,0:T(8,128)S(1)}, u32[]{:S(2)}, u32[]{:S(2)}) collective-permute-start(f32[8,6,32,128]{3,2,1,0:T(8,128)S(1)} %get-tuple-element.95), channel_id=1, source_target_pairs={{0,2},{2,4},{4,6},{6,8},{8,10},{10,12},{12,14},{14,0},{1,3},{3,5},... | collective-permute-start | bytes 2359304 | tf_op jit(solution)/shard_map/ppermute | solution.py:475
  142.6 25.4 %collective-permute-start.19 = (f32[8,6,32,128]{3,2,1,0:T(8,128)S(1)}, f32[8,6,32,128]{3,2,1,0:T(8,128)S(1)}, u32[]{:S(2)}, u32[]{:S(2)}) collective-permute-start(f32[8,6,32,128]{3,2,1,0:T(8,128)S(1)} %get-tuple-element.96), channel_id=1, source_target_pairs={{0,14},{2,0},{4,2},{6,4},{8,6},{10,8},{12,10},{14,12},{1,15},{3,1}... | collective-permute-start | bytes 2359304 | tf_op jit(solution)/shard_map/ppermute | solution.py:475
  143.7 24.3 %collective-permute-start.16 = (f32[48,32,128]{2,1,0:T(8,128)S(1)}, f32[48,32,128]{2,1,0:T(8,128)S(1)}, u32[]{:S(2)}, u32[]{:S(2)}) collective-permute-start(f32[48,32,128]{2,1,0:T(8,128)S(1)} %get-tuple-element.93), channel_id=1, source_target_pairs={{0,16},{16,32},{32,48},{48,64},{64,80},{80,96},{96,112},{112,0},{1... | collective-permute-start | bytes 2359304 | tf_op jit(solution)/shard_map/ppermute | solution.py:475
  144.0 24.0 %collective-permute-start.17 = (f32[48,32,128]{2,1,0:T(8,128)S(1)}, f32[48,32,128]{2,1,0:T(8,128)S(1)}, u32[]{:S(2)}, u32[]{:S(2)}) collective-permute-start(f32[48,32,128]{2,1,0:T(8,128)S(1)} %get-tuple-element.94), channel_id=1, source_target_pairs={{0,112},{16,0},{32,16},{48,32},{64,48},{80,64},{96,80},{112,96},{1... | collective-permute-start | bytes 2359304 | tf_op jit(solution)/shard_map/ppermute | solution.py:475

commit v8 on v7

--- a/solution.py
+++ b/solution.py
@@ -34,7 +34,7 @@
 CH = NPJ * TGT
 GROUPS = ROWS // 4
 TOTAL = (2 * CH, 2 * NB)
-BATCH = 4
+BATCH = 16
 ZROWS = GROUPS * 16
 LANES = 128
 F32 = jnp.float32
@@ -103,68 +103,87 @@
 MATRIX = jax.ShapeDtypeStruct((PAIRS, 2 * CH, 2 * SZ), BF16)
 
 
-def write_faces(x, rows, x_low, x_high, y_low, y_high):
+def write_x_faces(x, rows, x_low, x_high):
+    if x < REACH:
+        for i in range(SY):
+            x_low[x * SY + i] = rows[i]
+    if x >= SX - REACH:
+        for i in range(SY):
+            x_high[(x - (SX - REACH)) * SY + i] = rows[i]
+
+
+def write_y_faces(x, rows, y_low, y_high):
     for i in range(REACH):
         y_low[x, i] = rows[i]
         y_high[x, i] = rows[SY - REACH + i]
 
-    if x < REACH:
-        for i in range(SY):
-            x_low[x * SY + i] = rows[i]
-
-    if x >= SX - REACH:
-        for i in range(SY):
-            x_high[(x - (SX - REACH)) * SY + i] = rows[i]
-
-
-def rearrange_kernel(src, *refs):
-    field, faces, in_sem = refs[0], refs[1:5], refs[5]
-    for row in range(ROWS):
-        pltpu.make_async_copy(src.at[:, row, :], field.at[row], in_sem.at[row]).start()
-
+
+def prepare_kernel(count, coupling, src, cells, targets, projector, *refs):
+    field, x_low, x_high, key, own = refs[:5]
+    weights, in_sem = refs[5:-1], refs[-1]
+    loads = [pltpu.make_async_copy(src.at[:, row, :], field.at[row], in_sem.at[row]) for row in range(ROWS)]
+    for load in loads:
+        load.start()
+    slot = lax.broadcasted_iota(jnp.int32, (SLOTS // LANES, LANES), 0) * LANES
+    slot = slot + lax.broadcasted_iota(jnp.int32, (SLOTS // LANES, LANES), 1)
+    target = targets[...]
+    code = target // 2
+    z_other = jnp.where(code % 3 != 1, 1, 0)
+    wanted = ((code // 3) * 2 + z_other) * 2 + target % 2
+    key[...] = jnp.where(slot < count[0], cells[...] * 64 + wanted, ROWS * SZ * 64)
+    for j in range(NPJ):
+        for i in range(SLOTS // LANES):
+            weights[j][pl.ds(i, 1), :] = projector[pl.ds(j, 1), pl.ds(i * LANES, LANES)]
+    channel = lax.broadcasted_iota(jnp.int32, (8, LANES), 0)
+    at = lax.broadcasted_iota(jnp.int32, (8, LANES), 1)
+    placed = jnp.zeros((8, LANES), F32)
+    for a in range(2):
+        for j in range(NPJ):
+            placed = jnp.where((channel == j) & (at == 16 + a), coupling[a, j], placed)
+    own[...] = placed
     for x in range(SX):
         for y in range(SY):
-            row = x * SY + y
-            pltpu.make_async_copy(src.at[:, row, :], field.at[row], in_sem.at[row]).wait()
-        rows = [field[x * SY + y] for y in range(SY)]
-        write_faces(x, rows, *faces)
-
-
-def rearrange(orbitals):
+            loads[x * SY + y].wait()
+        write_x_faces(x, [field[x * SY + y] for y in range(SY)], x_low, x_high)
+
+
+def prepare(count, coupling, orbitals, cells, targets, projector):
+    lines = (SLOTS // LANES, LANES)
     return pl.pallas_call(
-        rearrange_kernel,
-        out_shape=[BLOCK, X_FACE, X_FACE, Y_FACE, Y_FACE],
-        in_specs=any_specs(1),
-        out_specs=vmem_specs(5),
-        scratch_shapes=[
-            pltpu.SemaphoreType.DMA((ROWS,)),
-        ],
+        prepare_kernel,
+        out_shape=[
+            BLOCK,
+            X_FACE,
+            X_FACE,
+            jax.ShapeDtypeStruct(lines, jnp.int32),
+            jax.ShapeDtypeStruct((8, LANES), F32),
+        ]
+        + [jax.ShapeDtypeStruct(lines, F32)] * NPJ,
+        in_specs=[pl.BlockSpec(memory_space=pltpu.SMEM)] * 2 + any_specs(1) + vmem_specs(3),
+        out_specs=vmem_specs(5 + NPJ),
+        scratch_shapes=[pltpu.SemaphoreType.DMA((ROWS,))],
         compiler_params=PARAMS,
-        name="rearrange",
-    )(orbitals)
+        name="prepare",
+    )(count, coupling, orbitals, cells.reshape(lines), targets.reshape(lines), projector)
 
 
 def build_kernel(starts, points, out, held, sem):
-    full = pl.ds(0, SLOTS // LANES)
-    load = pltpu.make_async_copy(points, held.at[:, full], sem)
+    load = pltpu.make_async_copy(points, held.at[:, pl.ds(0, SLOTS)], sem)
     load.start()
-    held[0, pl.ds(SLOTS // LANES, 8), :] = jnp.full((8, LANES), ROWS * SZ * 64, F32)
-    for j in range(NPJ):
-        held[1 + j, pl.ds(SLOTS // LANES, 8), :] = jnp.zeros((8, LANES), F32)
+    row = lax.broadcasted_iota(jnp.int32, (1 + NPJ, 2 * LANES), 0)
     load.wait()
+    held[:, pl.ds(SLOTS, 2 * LANES)] = jnp.where(row == 0, float(ROWS * SZ * 64), 0.0)
     target_at = lax.broadcasted_iota(jnp.int32, (TGT, 2 * LANES), 0)
     z_at = lax.broadcasted_iota(jnp.int32, (SZ, 2 * LANES), 0)
 
     def window(row, block):
-        def window_of(i):
-            return jnp.concatenate([held[i, pl.ds(block, 1), :], held[i, pl.ds(block + 1, 1), :]], axis=1)
-
-        key = window_of(0).astype(jnp.int32)
+        seen = held[:, pl.ds(pl.multiple_of(block * LANES, LANES), 2 * LANES)]
+        key = seen[:1].astype(jnp.int32)
         target = jnp.where((key >> 13) == row, key & 63, 63)
         chosen = target_at == target
         parts = []
         for j in range(NPJ):
-            parts.append(jnp.where(chosen, window_of(1 + j), 0.0))
+            parts.append(jnp.where(chosen, seen[1 + j : 2 + j], 0.0))
         hi, lo = split2(jnp.concatenate(parts, axis=0))
         place = jnp.where(z_at == ((key >> 6) & 127), 1.0, 0.0).astype(BF16)
         both = dot(jnp.concatenate([hi, lo], axis=0), place, NT)
@@ -203,7 +222,7 @@
         in_specs=[pl.BlockSpec(memory_space=pltpu.SMEM)] + any_specs(1),
         out_specs=pl.BlockSpec(memory_space=pltpu.VMEM),
         scratch_shapes=[
-            pltpu.VMEM((1 + NPJ, SLOTS // LANES + 8, LANES), F32),
+            pltpu.VMEM((1 + NPJ, SLOTS + 2 * LANES), F32),
             pltpu.SemaphoreType.DMA(()),
         ],
         compiler_params=PARAMS,
@@ -221,9 +240,11 @@
     return jnp.concatenate([joined[j * TGT : (j + 1) * TGT] for j in range(NPJ)], axis=1)
 
 
-def first_kernel(field, mat, own, out, total):
+def first_kernel(field, mat, own, out, y_low, y_high, total):
     for g in range(GROUPS):
         out[pl.ds(16 * g, 16), :] = z_faces([field[4 * g + i] for i in range(4)])
+    for x in range(SX):
+        write_y_faces(x, [field[x * SY + y] for y in range(SY)], y_low, y_high)
     total[...] = jnp.zeros_like(total)
     for pair in range(PAIRS):
         values = jnp.concatenate([field[2 * pair], field[2 * pair + 1]], axis=1)
@@ -235,9 +256,9 @@
 def first(field, mat, own):
     return pl.pallas_call(
         first_kernel,
-        out_shape=jax.ShapeDtypeStruct((ZROWS + TGT + 8, LANES), F32),
+        out_shape=[jax.ShapeDtypeStruct((ZROWS + TGT + 8, LANES), F32), Y_FACE, Y_FACE],
         in_specs=vmem_specs(3),
-        out_specs=pl.BlockSpec(memory_space=pltpu.VMEM),
+        out_specs=vmem_specs(3),
         scratch_shapes=[pltpu.VMEM(TOTAL, F32)],
         compiler_params=PARAMS,
         name="first",
@@ -303,7 +324,6 @@
         (new, gram), refs = refs[:2], refs[2:]
     else:
         (new, x_low, x_high, y_low, y_high, message), refs = refs[:6], refs[6:]
-        faces_out = (x_low, x_high, y_low, y_high)
         if first_step:
             coupling, refs = refs[0], refs[1:]
     total, coef, first_z, second_z = refs
@@ -373,7 +393,8 @@
                 rows.append(new[here] + added[:, q * SZ : (q + 1) * SZ])
                 new[here] = rows[-1]
         if not last_step:
-            write_faces(x, rows, *faces_out)
+            write_x_faces(x, rows, x_low, x_high)
+            write_y_faces(x, rows, y_low, y_high)
         for p in range(4):
             values = jnp.concatenate(rows[2 * p : 2 * p + 2], axis=1)
             if last_step:
@@ -477,22 +498,18 @@
 
 def local(orbitals, potential, projector, point_cell, target, point_count, coupling):
     bands, size_x, size_y, size_z = orbitals.shape
-    field, x_low, x_high, y_low, y_high = rearrange(orbitals.reshape(NB, ROWS, SZ))
+    field, x_low, x_high, key, own, *weights = prepare(
+        point_count.reshape(1), coupling, orbitals.reshape(NB, ROWS, SZ), point_cell, target, projector
+    )
     pot = potential.reshape(ROWS, SZ)
-
-    alive = lax.iota(jnp.int32, SLOTS) < point_count.reshape(())
-    code = target // 2
-    z_other = (code % 3 != 1).astype(jnp.int32)
-    wanted = ((code // 3) * 2 + z_other) * 2 + target % 2
-    key = jnp.where(alive, point_cell * 64 + wanted, ROWS * SZ * 64)
+    key = key.reshape(SLOTS)
     starts = jnp.sum(
         (key[None, :] < (lax.iota(jnp.int32, ROWS + 1) * (SZ * 64))[:, None]).astype(jnp.int32), axis=1
     )
-    ordered = lax.sort((key,) + tuple(projector[j] for j in range(NPJ)), num_keys=1, is_stable=False)
-    points = jnp.stack([ordered[0].astype(F32), *ordered[1:]]).reshape(1 + NPJ, SLOTS // LANES, LANES)
+    ordered = lax.sort((key, *[w.reshape(SLOTS) for w in weights]), num_keys=1, is_stable=False)
+    points = jnp.stack([ordered[0].astype(F32), *ordered[1:]])
     mat = build(starts, points)
 
-    own = jnp.pad(coupling.T, ((0, 8 - NPJ), (16, LANES - 18)))
     other = ()
     for k in range(DEGREE):
         start, last = k == 0, k == DEGREE - 1
@@ -500,8 +517,7 @@
             x_left = shift(x_high, "gx", 1)
             x_right = shift(x_low, "gx", -1)
             mat, field, x_left, x_right = lax.optimization_barrier((mat, field, x_left, x_right))
-            message = first(field, mat, own)
-            message, y_low, y_high = lax.optimization_barrier((message, y_low, y_high))
+            message, y_low, y_high = first(field, mat, own)
         faces = shift(message, "gz", 1)
         y_left = shift(y_high, "gy", 1)
         y_right = shift(y_low, "gy", -1)

time: 199 us -> 198 us (level)
  waiting for transfers between devices: 4.21 us -> 9.3 us
  local copies, waits for them, and re-layouts: 7.99 us -> 4.61 us
  other arithmetic: 9.32 us -> 6.29 us
  blocking collectives: 101 us -> 103 us
    ppermute x20, waiting for transfers between devices: 4.21 us -> 9.3 us  [shift(): lax.ppermute(value, axis, [(i, (i + by) % count) for i in range(count)])]
    all_to_all x4, blocking collectives: 33.6 us -> 35.7 us  [local(): came = lax.all_to_all(spread_call(spread_x_kernel, rows, came), 'gx', 0, 0)]
  transfers between devices with their start and end apart: 20 -> 20, of which waited for: 3 -> 4; matrix products, arithmetic and copies ran while one was open for 8% -> 3% of each run, Pallas kernels for 4% -> 3%
where the time goes in v8:
time: 198 us; the launch traced here: 197 us
  blocking collectives  103 us (52%)
  starting transfers between devices  37 us (19%)
  Pallas kernels  35.6 us (18%)
  waiting for transfers between devices  9.3 us (5%)
  other arithmetic  6.29 us (3%)
  local copies, waits for them, and re-layouts  4.61 us (2%)
    all_to_all x4, blocking collectives, local(): lax.all_to_all(spread_call(spread_zy_kernel, rows, message, faces), 'gy',...  48 us
    ppermute x20, starting transfers between devices, shift(): lax.ppermute(value, axis, [(i, (i + by) % count) for i in range(count)])  37 us
    all_to_all x4, blocking collectives, local(): came = lax.all_to_all(spread_call(spread_x_kernel, rows, came), 'gx', 0, 0)  35.7 us
    all_to_all x1, blocking collectives, local(): lax.all_to_all(jnp.broadcast_to(gram[None], (devices,) + gram.shape), axe...  19.6 us
    pallas_call x4, Pallas kernels, step(): pl.pallas_call(functools.partial(step_kernel, first_step, last_step), out...  18.3 us
    ppermute x20, waiting for transfers between devices, shift(): lax.ppermute(value, axis, [(i, (i + by) % count) for i in range(count)])  9.3 us
    sort x1, other arithmetic, local(): lax.sort((key, *[w.reshape(SLOTS) for w in weights]), num_keys=1, is_stab...  5.85 us
    pallas_call x1, Pallas kernels, build(): pl.pallas_call(build_kernel, out_shape=MATRIX, in_specs=[pl.BlockSpec(mem...  5.73 us
  transfers between devices with their start and end apart: 20, of which 4 were waited for; matrix products, arithmetic and copies ran while one was open for 3% of the time, Pallas kernels for 3%

profile of v8, /device:TPU:1, one launch (start us, length us, event | category | flops | bytes accessed | tf_op | source)
XLA Modules:
  0.0 197.2 jit_solution(9623150744635907889)
XLA Ops:
  5.0 3.7 %prepare.1 = (f32[64,32,128]{2,1,0:T(8,128)S(1)}, f32[48,32,128]{2,1,0:T(8,128)}, f32[48,32,128]{2,1,0:T(8,128)}, s32[64,128]{1,0:T(8,128)S(1)}, f32[8,128]{1,0:...) custom-call(s32[1]{0:T(128)} %bitcast.16.count, ...), custom_call_target="tpu_custom_call" | custom-call | tf_op jit(solution)/shard_map/prepare/pallas_call | solution.py:152
  8.7 2.2 %collective-permute-start = (f32[48,32,128]{2,1,0:T(8,128)}, f32[48,32,128]{2,1,0:T(8,128)S(1)}, u32[]{:S(2)}, u32[]{:S(2)}) collective-permute-start(f32[48,32,128]{2,1,0:T(8,128)} %get-tuple-element.67), channel_id=1, source_target_pairs={{0,16},{16,32},{32,48},{48,64},{64,80},{80,96},{96,112},{112,0},{1... | collective-permute-start | bytes 2359304 | tf_op jit(solution)/shard_map/ppermute | solution.py:496
  10.9 2.9 %collective-permute-start.1 = (f32[48,32,128]{2,1,0:T(8,128)}, f32[48,32,128]{2,1,0:T(8,128)S(1)}, u32[]{:S(2)}, u32[]{:S(2)}) collective-permute-start(f32[48,32,128]{2,1,0:T(8,128)} %get-tuple-element.68), channel_id=1, source_target_pairs={{0,112},{16,0},{32,16},{48,32},{64,48},{80,64},{96,80},{112,96},{1... | collective-permute-start | bytes 2359304 | tf_op jit(solution)/shard_map/ppermute | solution.py:496
  13.8 5.9 %sort.33 = (s32[8192]{0:T(1024)S(1)}, f32[8192]{0:T(1024)S(1)}, f32[8192]{0:T(1024)S(1)}, f32[8192]{0:T(1024)S(1)}, f32[8192]{0:T(1024)S(1)}) sort(s32[8192]{0:T(1024)S(1)} %bitcast.22, f32[8192]{0:T(1024)S(1)} %bitcast.24, f32[8192]{0:T(1024)S(1)} %bitcast.25, f32[8192]{0:T(1024)S(1)} %bitcast.26, f32[8192]{0:T(1024)S(1)} %bitcast.27), dimensions={0}, to_apply=%region_1.0 | sort | flops 106496 | bytes 327680 | tf_op jit(solution)/shard_map/sort | solution.py:509
  20.3 5.7 %build.1.mat.refs_8_ = bf16[32,320,256]{2,1,0:T(8,128)(2,1)S(1)} custom-call(s32[65]{0:T(128)S(1)} %convert_reduce_fusion.starts, f32[5,8192]{1,0:T(8,128)S(1)} %stack.23.points), custom_call_target="tpu_custom_call" | custom-call | tf_op jit(solution)/shard_map/build/pallas_call | solution.py:219
  26.1 5.1 %collective-permute-done.refs_2_ = f32[48,32,128]{2,1,0:T(8,128)S(1)} collective-permute-done((f32[48,32,128]{2,1,0:T(8,128)}, f32[48,32,128]{2,1,0:T(8,128)S(1)}, u32[]{:S(2)}, u32[]{:S(2)}) %collective-permute-start) | collective-permute-done | bytes 786464 | tf_op jit(solution)/shard_map/ppermute | solution.py:496
  31.2 2.2 %first.1 = (f32[304,128]{1,0:T(8,128)S(1)}, f32[8,6,32,128]{3,2,1,0:T(8,128)S(1)}, f32[8,6,32,128]{3,2,1,0:T(8,128)S(1)}) custom-call(f32[64,32,128]{2,1,0:T(8,128)S(1)} %get-tuple-element.69.field.refs_0_.refs_9_, bf16[32,320,256]{2,1,0:T(8,128)(2,1)S(1)} %build.1.mat.refs_8_, f32[8,128]{1,0:T(8,128)S(1)} %get-tuple-element.71.own), custom_call_target="tpu_custom_call" | custom-call | tf_op jit(solution)/shard_map/first/pallas_call | solution.py:257
  33.4 2.4 %collective-permute-start.3 = (f32[8,6,32,128]{3,2,1,0:T(8,128)S(1)}, f32[8,6,32,128]{3,2,1,0:T(8,128)S(1)}, u32[]{:S(2)}, u32[]{:S(2)}) collective-permute-start(f32[8,6,32,128]{3,2,1,0:T(8,128)S(1)} %get-tuple-element.75), channel_id=1, source_target_pairs={{0,2},{2,4},{4,6},{6,8},{8,10},{10,12},{12,14},{14,0},{1,3},{3,5},... | collective-permute-start | bytes 2359304 | tf_op jit(solution)/shard_map/ppermute | solution.py:496
  35.8 3.3 %collective-permute-start.2 = (f32[304,128]{1,0:T(8,128)S(1)}, f32[304,128]{1,0:T(8,128)S(1)}, u32[]{:S(2)}, u32[]{:S(2)}) collective-permute-start(f32[304,128]{1,0:T(8,128)S(1)} %get-tuple-element.72.mine), channel_id=1, source_target_pairs={{0,1},{1,0},{2,3},{3,2},{4,5},{5,4},{6,7},{7,6},{8,9},{9,8},{10,11... | collective-permute-start | bytes 466952 | tf_op jit(solution)/shard_map/ppermute | solution.py:496
  39.1 2.6 %collective-permute-done.2.other.refs_1_ = f32[304,128]{1,0:T(8,128)S(1)} collective-permute-done((f32[304,128]{1,0:T(8,128)S(1)}, f32[304,128]{1,0:T(8,128)S(1)}, u32[]{:S(2)}, u32[]{:S(2)}) %collective-permute-start.2) | collective-permute-done | bytes 155680 | tf_op jit(solution)/shard_map/ppermute | solution.py:496
  41.8 12.0 %all_to_all.45.came = f32[8,48,128]{2,1,0:T(8,128)S(1)} all-to-all(f32[8,48,128]{2,1,0:T(8,128)S(1)} %spread.8), channel_id=1, replica_groups=mesh['gx'=8,'gy'=8,'gz'=2] {'gy'}, dimensions={0} | all-to-all | bytes 393216 | tf_op jit(solution)/shard_map/all_to_all | solution.py:529
  53.9 10.6 %all_to_all.46.refs_7_ = f32[8,48,128]{2,1,0:T(8,128)S(1)} all-to-all(f32[8,48,128]{2,1,0:T(8,128)S(1)} %spread.9), channel_id=1, replica_groups=mesh['gx'=8,'gy'=8,'gz'=2] {'gx'}, dimensions={0} | all-to-all | bytes 393216 | tf_op jit(solution)/shard_map/all_to_all | solution.py:530
  64.6 4.4 %step.4 = (f32[64,32,128]{2,1,0:T(8,128)S(1)}, f32[48,32,128]{2,1,0:T(8,128)S(1)}, f32[48,32,128]{2,1,0:T(8,128)S(1)}, f32[8,6,32,128]{3,2,1,0:T(8,128)S(1)}, f3...) custom-call(f32[64,32,128]{2,1,0:T(8,128)S(1)} %get-tuple-element.69.field.refs_0_.refs_9_, ...), custom_call_target="tpu_custom_call" | custom-call | tf_op jit(solution)/shard_map/step/pallas_call | solution.py:425
  69.0 3.2 %collective-permute-start.5 = (f32[296,128]{1,0:T(8,128)S(1)}, f32[296,128]{1,0:T(8,128)S(1)}, u32[]{:S(2)}, u32[]{:S(2)}) collective-permute-start(f32[296,128]{1,0:T(8,128)S(1)} %get-tuple-element.78.mine), channel_id=1, source_target_pairs={{0,1},{1,0},{2,3},{3,2},{4,5},{5,4},{6,7},{7,6},{8,9},{9,8},{10,11... | collective-permute-start | bytes 454664 | tf_op jit(solution)/shard_map/ppermute | solution.py:496
  72.2 2.6 %collective-permute-start.8 = (f32[8,6,32,128]{3,2,1,0:T(8,128)S(1)}, f32[8,6,32,128]{3,2,1,0:T(8,128)S(1)}, u32[]{:S(2)}, u32[]{:S(2)}) collective-permute-start(f32[8,6,32,128]{3,2,1,0:T(8,128)S(1)} %get-tuple-element.84), channel_id=1, source_target_pairs={{0,2},{2,4},{4,6},{6,8},{8,10},{10,12},{12,14},{14,0},{1,3},{3,5},... | collective-permute-start | bytes 2359304 | tf_op jit(solution)/shard_map/ppermute | solution.py:496
  75.3 3.0 %collective-permute-start.7 = (f32[48,32,128]{2,1,0:T(8,128)S(1)}, f32[48,32,128]{2,1,0:T(8,128)S(1)}, u32[]{:S(2)}, u32[]{:S(2)}) collective-permute-start(f32[48,32,128]{2,1,0:T(8,128)S(1)} %get-tuple-element.83), channel_id=1, source_target_pairs={{0,112},{16,0},{32,16},{48,32},{64,48},{80,64},{96,80},{112,96},{1... | collective-permute-start | bytes 2359304 | tf_op jit(solution)/shard_map/ppermute | solution.py:496
  78.3 12.0 %all_to_all.47.came = f32[8,40,128]{2,1,0:T(8,128)S(1)} all-to-all(f32[8,40,128]{2,1,0:T(8,128)S(1)} %spread.10), channel_id=1, replica_groups=mesh['gx'=8,'gy'=8,'gz'=2] {'gy'}, dimensions={0} | all-to-all | bytes 327680 | tf_op jit(solution)/shard_map/all_to_all | solution.py:529
  90.4 8.1 %all_to_all.48.refs_7_ = f32[8,40,128]{2,1,0:T(8,128)S(1)} all-to-all(f32[8,40,128]{2,1,0:T(8,128)S(1)} %spread.11), channel_id=1, replica_groups=mesh['gx'=8,'gy'=8,'gz'=2] {'gx'}, dimensions={0} | all-to-all | bytes 327680 | tf_op jit(solution)/shard_map/all_to_all | solution.py:530
  98.5 4.8 %step.5 = (f32[64,32,128]{2,1,0:T(8,128)S(1)}, f32[48,32,128]{2,1,0:T(8,128)S(1)}, f32[48,32,128]{2,1,0:T(8,128)S(1)}, f32[8,6,32,128]{3,2,1,0:T(8,128)S(1)}, f3...) custom-call(f32[64,32,128]{2,1,0:T(8,128)S(1)} %get-tuple-element.77.refs_0_.refs_9_, ...), custom_call_target="tpu_custom_call" | custom-call | tf_op jit(solution)/shard_map/step/pallas_call | solution.py:425
  103.3 3.2 %collective-permute-start.10 = (f32[296,128]{1,0:T(8,128)S(1)}, f32[296,128]{1,0:T(8,128)S(1)}, u32[]{:S(2)}, u32[]{:S(2)}) collective-permute-start(f32[296,128]{1,0:T(8,128)S(1)} %get-tuple-element.88.mine), channel_id=1, source_target_pairs={{0,1},{1,0},{2,3},{3,2},{4,5},{5,4},{6,7},{7,6},{8,9},{9,8},{10,11... | collective-permute-start | bytes 454664 | tf_op jit(solution)/shard_map/ppermute | solution.py:496
  106.5 2.1 %collective-permute-start.13 = (f32[8,6,32,128]{3,2,1,0:T(8,128)S(1)}, f32[8,6,32,128]{3,2,1,0:T(8,128)S(1)}, u32[]{:S(2)}, u32[]{:S(2)}) collective-permute-start(f32[8,6,32,128]{3,2,1,0:T(8,128)S(1)} %get-tuple-element.94), channel_id=1, source_target_pairs={{0,2},{2,4},{4,6},{6,8},{8,10},{10,12},{12,14},{14,0},{1,3},{3,5},... | collective-permute-start | bytes 2359304 | tf_op jit(solution)/shard_map/ppermute | solution.py:496
  109.6 3.0 %collective-permute-start.12 = (f32[48,32,128]{2,1,0:T(8,128)S(1)}, f32[48,32,128]{2,1,0:T(8,128)S(1)}, u32[]{:S(2)}, u32[]{:S(2)}) collective-permute-start(f32[48,32,128]{2,1,0:T(8,128)S(1)} %get-tuple-element.93), channel_id=1, source_target_pairs={{0,112},{16,0},{32,16},{48,32},{64,48},{80,64},{96,80},{112,96},{1... | collective-permute-start | bytes 2359304 | tf_op jit(solution)/shard_map/ppermute | solution.py:496
  112.7 11.7 %all_to_all.49.came = f32[8,40,128]{2,1,0:T(8,128)S(1)} all-to-all(f32[8,40,128]{2,1,0:T(8,128)S(1)} %spread.12), channel_id=1, replica_groups=mesh['gx'=8,'gy'=8,'gz'=2] {'gy'}, dimensions={0} | all-to-all | bytes 327680 | tf_op jit(solution)/shard_map/all_to_all | solution.py:529
  124.5 8.7 %all_to_all.50.refs_7_ = f32[8,40,128]{2,1,0:T(8,128)S(1)} all-to-all(f32[8,40,128]{2,1,0:T(8,128)S(1)} %spread.13), channel_id=1, replica_groups=mesh['gx'=8,'gy'=8,'gz'=2] {'gx'}, dimensions={0} | all-to-all | bytes 327680 | tf_op jit(solution)/shard_map/all_to_all | solution.py:530
  133.1 4.8 %step.6 = (f32[64,32,128]{2,1,0:T(8,128)S(1)}, f32[48,32,128]{2,1,0:T(8,128)S(1)}, f32[48,32,128]{2,1,0:T(8,128)S(1)}, f32[8,6,32,128]{3,2,1,0:T(8,128)S(1)}, f3...) custom-call(f32[64,32,128]{2,1,0:T(8,128)S(1)} %get-tuple-element.87.refs_0_.refs_9_, ...), custom_call_target="tpu_custom_call" | custom-call | tf_op jit(solution)/shard_map/step/pallas_call | solution.py:425
  137.9 2.4 %collective-permute-start.15 = (f32[296,128]{1,0:T(8,128)S(1)}, f32[296,128]{1,0:T(8,128)S(1)}, u32[]{:S(2)}, u32[]{:S(2)}) collective-permute-start(f32[296,128]{1,0:T(8,128)S(1)} %get-tuple-element.97.mine), channel_id=1, source_target_pairs={{0,1},{1,0},{2,3},{3,2},{4,5},{5,4},{6,7},{7,6},{8,9},{9,8},{10,11... | collective-permute-start | bytes 454664 | tf_op jit(solution)/shard_map/ppermute | solution.py:496
  143.8 3.3 %collective-permute-start.17 = (f32[48,32,128]{2,1,0:T(8,128)S(1)}, f32[48,32,128]{2,1,0:T(8,128)S(1)}, u32[]{:S(2)}, u32[]{:S(2)}) collective-permute-start(f32[48,32,128]{2,1,0:T(8,128)S(1)} %get-tuple-element.102), channel_id=1, source_target_pairs={{0,112},{16,0},{32,16},{48,32},{64,48},{80,64},{96,80},{112,96},{1... | collective-permute-start | bytes 2359304 | tf_op jit(solution)/shard_map/ppermute | solution.py:496
  147.2 12.3 %all_to_all.51.came = f32[8,40,128]{2,1,0:T(8,128)S(1)} all-to-all(f32[8,40,128]{2,1,0:T(8,128)S(1)} %spread.14), channel_id=1, replica_groups=mesh['gx'=8,'gy'=8,'gz'=2] {'gy'}, dimensions={0} | all-to-all | bytes 327680 | tf_op jit(solution)/shard_map/all_to_all | solution.py:529
  159.5 8.4 %all_to_all.52.refs_7_ = f32[8,40,128]{2,1,0:T(8,128)S(1)} all-to-all(f32[8,40,128]{2,1,0:T(8,128)S(1)} %spread.15), channel_id=1, replica_groups=mesh['gx'=8,'gy'=8,'gz'=2] {'gx'}, dimensions={0} | all-to-all | bytes 327680 | tf_op jit(solution)/shard_map/all_to_all | solution.py:530
  167.9 4.3 %step.7 = (f32[64,32,128]{2,1,0:T(8,128)S(1)}, f32[8,128]{1,0:T(8,128)S(1)}) custom-call(f32[64,32,128]{2,1,0:T(8,128)S(1)} %get-tuple-element.96.refs_0_, f32[296,128]{1,0:T(8,128)S(1)} %collective-permute-done.15.other.refs_1_, f32[48,32,128]{2,1,0:T(8,128)S(1)} %collective-permute-done.16.refs_2_, f32[48,32,128]{2,1,0:T(8,128)S(1)} %collective-permute-done.17.refs_3_, ...), custom_call_target="tpu_custom_call" | custom-call | tf_op jit(solution)/shard_map/step/pallas_call | solution.py:425
  172.2 19.6 %all_to_all.53.grams = f32[128,8,128]{2,1,0:T(8,128)S(1)} all-to-all(f32[128,8,128]{2,1,0:T(8,128)S(1)} %broadcast_in_dim.2), channel_id=1, replica_groups=mesh['gx'=8,'gy'=8,'gz'=2] {'gx','gy','gz'}, dimensions={0} | all-to-all | bytes 1048576 | tf_op jit(solution)/shard_map/all_to_all | solution.py:544
  191.9 5.1 %finish.1 = f32[32,64,128]{2,1,0:T(8,128)} custom-call(f32[64,32,128]{2,1,0:T(8,128)S(1)} %get-tuple-element.105.field, f32[128,8,128]{2,1,0:T(8,128)S(1)} %all_to_all.53.grams), custom_call_target="tpu_custom_call" | custom-call | tf_op jit(solution)/shard_map/finish/pallas_call | solution.py:479
  (51 shorter events, 10.7 us)
Async XLA Ops:
  0.7 1.2 copy-start
  1.9 0.9 copy-start.2
  2.8 0.8 copy-start.3
  3.5 0.8 copy-start.4
  4.3 0.7 copy-start.5
  8.7 22.5 %collective-permute-start = (f32[48,32,128]{2,1,0:T(8,128)}, f32[48,32,128]{2,1,0:T(8,128)S(1)}, u32[]{:S(2)}, u32[]{:S(2)}) collective-permute-start(f32[48,32,128]{2,1,0:T(8,128)} %get-tuple-element.67), channel_id=1, source_target_pairs={{0,16},{16,32},{32,48},{48,64},{64,80},{80,96},{96,112},{112,0},{1... | collective-permute-start | bytes 2359304 | tf_op jit(solution)/shard_map/ppermute | solution.py:496
  10.9 20.3 %collective-permute-start.1 = (f32[48,32,128]{2,1,0:T(8,128)}, f32[48,32,128]{2,1,0:T(8,128)S(1)}, u32[]{:S(2)}, u32[]{:S(2)}) collective-permute-start(f32[48,32,128]{2,1,0:T(8,128)} %get-tuple-element.68), channel_id=1, source_target_pairs={{0,112},{16,0},{32,16},{48,32},{64,48},{80,64},{96,80},{112,96},{1... | collective-permute-start | bytes 2359304 | tf_op jit(solution)/shard_map/ppermute | solution.py:496
  31.2 33.4 %copy-start.1 = (f32[8,8,128]{2,1,0:T(8,128)S(1)}, f32[8,8,128]{2,1,0:T(8,128)}, u32[]{:S(2)}) copy-start(f32[8,8,128]{2,1,0:T(8,128)} %param.8) | copy-start | bytes 98308
  33.4 31.2 %collective-permute-start.3 = (f32[8,6,32,128]{3,2,1,0:T(8,128)S(1)}, f32[8,6,32,128]{3,2,1,0:T(8,128)S(1)}, u32[]{:S(2)}, u32[]{:S(2)}) collective-permute-start(f32[8,6,32,128]{3,2,1,0:T(8,128)S(1)} %get-tuple-element.75), channel_id=1, source_target_pairs={{0,2},{2,4},{4,6},{6,8},{8,10},{10,12},{12,14},{14,0},{1,3},{3,5},... | collective-permute-start | bytes 2359304 | tf_op jit(solution)/shard_map/ppermute | solution.py:496
  35.8 28.8 %collective-permute-start.4 = (f32[8,6,32,128]{3,2,1,0:T(8,128)S(1)}, f32[8,6,32,128]{3,2,1,0:T(8,128)S(1)}, u32[]{:S(2)}, u32[]{:S(2)}) collective-permute-start(f32[8,6,32,128]{3,2,1,0:T(8,128)S(1)} %get-tuple-element.76), channel_id=1, source_target_pairs={{0,14},{2,0},{4,2},{6,4},{8,6},{10,8},{12,10},{14,12},{1,15},{3,1}... | collective-permute-start | bytes 2359304 | tf_op jit(solution)/shard_map/ppermute | solution.py:496
  35.8 5.9 %collective-permute-start.2 = (f32[304,128]{1,0:T(8,128)S(1)}, f32[304,128]{1,0:T(8,128)S(1)}, u32[]{:S(2)}, u32[]{:S(2)}) collective-permute-start(f32[304,128]{1,0:T(8,128)S(1)} %get-tuple-element.72.mine), channel_id=1, source_target_pairs={{0,1},{1,0},{2,3},{3,2},{4,5},{5,4},{6,7},{7,6},{8,9},{9,8},{10,11... | collective-permute-start | bytes 466952 | tf_op jit(solution)/shard_map/ppermute | solution.py:496
  69.0 5.8 %collective-permute-start.5 = (f32[296,128]{1,0:T(8,128)S(1)}, f32[296,128]{1,0:T(8,128)S(1)}, u32[]{:S(2)}, u32[]{:S(2)}) collective-permute-start(f32[296,128]{1,0:T(8,128)S(1)} %get-tuple-element.78.mine), channel_id=1, source_target_pairs={{0,1},{1,0},{2,3},{3,2},{4,5},{5,4},{6,7},{7,6},{8,9},{9,8},{10,11... | collective-permute-start | bytes 454664 | tf_op jit(solution)/shard_map/ppermute | solution.py:496
  72.2 26.3 %collective-permute-start.8 = (f32[8,6,32,128]{3,2,1,0:T(8,128)S(1)}, f32[8,6,32,128]{3,2,1,0:T(8,128)S(1)}, u32[]{:S(2)}, u32[]{:S(2)}) collective-permute-start(f32[8,6,32,128]{3,2,1,0:T(8,128)S(1)} %get-tuple-element.84), channel_id=1, source_target_pairs={{0,2},{2,4},{4,6},{6,8},{8,10},{10,12},{12,14},{14,0},{1,3},{3,5},... | collective-permute-start | bytes 2359304 | tf_op jit(solution)/shard_map/ppermute | solution.py:496
  74.7 23.7 %collective-permute-start.9 = (f32[8,6,32,128]{3,2,1,0:T(8,128)S(1)}, f32[8,6,32,128]{3,2,1,0:T(8,128)S(1)}, u32[]{:S(2)}, u32[]{:S(2)}) collective-permute-start(f32[8,6,32,128]{3,2,1,0:T(8,128)S(1)} %get-tuple-element.85), channel_id=1, source_target_pairs={{0,14},{2,0},{4,2},{6,4},{8,6},{10,8},{12,10},{14,12},{1,15},{3,1}... | collective-permute-start | bytes 2359304 | tf_op jit(solution)/shard_map/ppermute | solution.py:496
  74.7 23.7 %collective-permute-start.6 = (f32[48,32,128]{2,1,0:T(8,128)S(1)}, f32[48,32,128]{2,1,0:T(8,128)S(1)}, u32[]{:S(2)}, u32[]{:S(2)}) collective-permute-start(f32[48,32,128]{2,1,0:T(8,128)S(1)} %get-tuple-element.82), channel_id=1, source_target_pairs={{0,16},{16,32},{32,48},{48,64},{64,80},{80,96},{96,112},{112,0},{1... | collective-permute-start | bytes 2359304 | tf_op jit(solution)/shard_map/ppermute | solution.py:496
  75.3 23.2 %collective-permute-start.7 = (f32[48,32,128]{2,1,0:T(8,128)S(1)}, f32[48,32,128]{2,1,0:T(8,128)S(1)}, u32[]{:S(2)}, u32[]{:S(2)}) collective-permute-start(f32[48,32,128]{2,1,0:T(8,128)S(1)} %get-tuple-element.83), channel_id=1, source_target_pairs={{0,112},{16,0},{32,16},{48,32},{64,48},{80,64},{96,80},{112,96},{1... | collective-permute-start | bytes 2359304 | tf_op jit(solution)/shard_map/ppermute | solution.py:496
  103.3 5.8 %collective-permute-start.10 = (f32[296,128]{1,0:T(8,128)S(1)}, f32[296,128]{1,0:T(8,128)S(1)}, u32[]{:S(2)}, u32[]{:S(2)}) collective-permute-start(f32[296,128]{1,0:T(8,128)S(1)} %get-tuple-element.88.mine), channel_id=1, source_target_pairs={{0,1},{1,0},{2,3},{3,2},{4,5},{5,4},{6,7},{7,6},{8,9},{9,8},{10,11... | collective-permute-start | bytes 454664 | tf_op jit(solution)/shard_map/ppermute | solution.py:496
  106.5 26.7 %collective-permute-start.13 = (f32[8,6,32,128]{3,2,1,0:T(8,128)S(1)}, f32[8,6,32,128]{3,2,1,0:T(8,128)S(1)}, u32[]{:S(2)}, u32[]{:S(2)}) collective-permute-start(f32[8,6,32,128]{3,2,1,0:T(8,128)S(1)} %get-tuple-element.94), channel_id=1, source_target_pairs={{0,2},{2,4},{4,6},{6,8},{8,10},{10,12},{12,14},{14,0},{1,3},{3,5},... | collective-permute-start | bytes 2359304 | tf_op jit(solution)/shard_map/ppermute | solution.py:496
  108.6 24.5 %collective-permute-start.14 = (f32[8,6,32,128]{3,2,1,0:T(8,128)S(1)}, f32[8,6,32,128]{3,2,1,0:T(8,128)S(1)}, u32[]{:S(2)}, u32[]{:S(2)}) collective-permute-start(f32[8,6,32,128]{3,2,1,0:T(8,128)S(1)} %get-tuple-element.95), channel_id=1, source_target_pairs={{0,14},{2,0},{4,2},{6,4},{8,6},{10,8},{12,10},{14,12},{1,15},{3,1}... | collective-permute-start | bytes 2359304 | tf_op jit(solution)/shard_map/ppermute | solution.py:496
  109.0 24.1 %collective-permute-start.11 = (f32[48,32,128]{2,1,0:T(8,128)S(1)}, f32[48,32,128]{2,1,0:T(8,128)S(1)}, u32[]{:S(2)}, u32[]{:S(2)}) collective-permute-start(f32[48,32,128]{2,1,0:T(8,128)S(1)} %get-tuple-element.92), channel_id=1, source_target_pairs={{0,16},{16,32},{32,48},{48,64},{64,80},{80,96},{96,112},{112,0},{1... | collective-permute-start | bytes 2359304 | tf_op jit(solution)/shard_map/ppermute | solution.py:496
  109.6 23.6 %collective-permute-start.12 = (f32[48,32,128]{2,1,0:T(8,128)S(1)}, f32[48,32,128]{2,1,0:T(8,128)S(1)}, u32[]{:S(2)}, u32[]{:S(2)}) collective-permute-start(f32[48,32,128]{2,1,0:T(8,128)S(1)} %get-tuple-element.93), channel_id=1, source_target_pairs={{0,112},{16,0},{32,16},{48,32},{64,48},{80,64},{96,80},{112,96},{1... | collective-permute-start | bytes 2359304 | tf_op jit(solution)/shard_map/ppermute | solution.py:496
  137.9 5.6 %collective-permute-start.15 = (f32[296,128]{1,0:T(8,128)S(1)}, f32[296,128]{1,0:T(8,128)S(1)}, u32[]{:S(2)}, u32[]{:S(2)}) collective-permute-start(f32[296,128]{1,0:T(8,128)S(1)} %get-tuple-element.97.mine), channel_id=1, source_target_pairs={{0,1},{1,0},{2,3},{3,2},{4,5},{5,4},{6,7},{7,6},{8,9},{9,8},{10,11... | collective-permute-start | bytes 454664 | tf_op jit(solution)/shard_map/ppermute | solution.py:496
  140.3 27.5 %collective-permute-start.18 = (f32[8,6,32,128]{3,2,1,0:T(8,128)S(1)}, f32[8,6,32,128]{3,2,1,0:T(8,128)S(1)}, u32[]{:S(2)}, u32[]{:S(2)}) collective-permute-start(f32[8,6,32,128]{3,2,1,0:T(8,128)S(1)} %get-tuple-element.103), channel_id=1, source_target_pairs={{0,2},{2,4},{4,6},{6,8},{8,10},{10,12},{12,14},{14,0},{1,3},{3,5},... | collective-permute-start | bytes 2359304 | tf_op jit(solution)/shard_map/ppermute | solution.py:496
  142.4 25.4 %collective-permute-start.19 = (f32[8,6,32,128]{3,2,1,0:T(8,128)S(1)}, f32[8,6,32,128]{3,2,1,0:T(8,128)S(1)}, u32[]{:S(2)}, u32[]{:S(2)}) collective-permute-start(f32[8,6,32,128]{3,2,1,0:T(8,128)S(1)} %get-tuple-element.104), channel_id=1, source_target_pairs={{0,14},{2,0},{4,2},{6,4},{8,6},{10,8},{12,10},{14,12},{1,15},{3,1}... | collective-permute-start | bytes 2359304 | tf_op jit(solution)/shard_map/ppermute | solution.py:496
  143.5 24.3 %collective-permute-start.16 = (f32[48,32,128]{2,1,0:T(8,128)S(1)}, f32[48,32,128]{2,1,0:T(8,128)S(1)}, u32[]{:S(2)}, u32[]{:S(2)}) collective-permute-start(f32[48,32,128]{2,1,0:T(8,128)S(1)} %get-tuple-element.101), channel_id=1, source_target_pairs={{0,16},{16,32},{32,48},{48,64},{64,80},{80,96},{96,112},{112,0},{1... | collective-permute-start | bytes 2359304 | tf_op jit(solution)/shard_map/ppermute | solution.py:496
  143.8 24.0 %collective-permute-start.17 = (f32[48,32,128]{2,1,0:T(8,128)S(1)}, f32[48,32,128]{2,1,0:T(8,128)S(1)}, u32[]{:S(2)}, u32[]{:S(2)}) collective-permute-start(f32[48,32,128]{2,1,0:T(8,128)S(1)} %get-tuple-element.102), channel_id=1, source_target_pairs={{0,112},{16,0},{32,16},{48,32},{64,48},{80,64},{96,80},{112,96},{1... | collective-permute-start | bytes 2359304 | tf_op jit(solution)/shard_map/ppermute | solution.py:496

commit v9 on v8

--- a/solution.py
+++ b/solution.py
@@ -42,6 +42,7 @@
 NN = (((1,), (0,)), ((), ()))
 NT = (((1,), (1,)), ((), ()))
 VMEM_LIMIT = 16 * 1024 * 1024
+PREPARE_LIMIT = 64256 * 1024
 
 
 def dot(a, b, dims=NN):
@@ -119,50 +120,55 @@
 
 
 def prepare_kernel(count, coupling, src, cells, targets, projector, *refs):
-    field, x_low, x_high, key, own = refs[:5]
-    weights, in_sem = refs[5:-1], refs[-1]
-    loads = [pltpu.make_async_copy(src.at[:, row, :], field.at[row], in_sem.at[row]) for row in range(ROWS)]
+    field, key, own = refs[:3]
+    weights = refs[3 : 3 + NPJ]
+    coupling_v, cells_v, targets_v, projector_v, in_sem, row_sem = refs[3 + NPJ :]
+    pairs = ((cells, cells_v), (targets, targets_v), (projector, projector_v), (coupling, coupling_v))
+    loads = [pltpu.make_async_copy(a, b, in_sem.at[i]) for i, (a, b) in enumerate(pairs)]
+    rows = [pltpu.make_async_copy(src.at[:, row, :], field.at[row], row_sem.at[row]) for row in range(ROWS)]
+    for load in loads + rows:
+        load.start()
     for load in loads:
-        load.start()
+        load.wait()
     slot = lax.broadcasted_iota(jnp.int32, (SLOTS // LANES, LANES), 0) * LANES
     slot = slot + lax.broadcasted_iota(jnp.int32, (SLOTS // LANES, LANES), 1)
-    target = targets[...]
+    target = targets_v[...]
     code = target // 2
     z_other = jnp.where(code % 3 != 1, 1, 0)
     wanted = ((code // 3) * 2 + z_other) * 2 + target % 2
-    key[...] = jnp.where(slot < count[0], cells[...] * 64 + wanted, ROWS * SZ * 64)
+    key[...] = jnp.where(slot < count[0], cells_v[...] * 64 + wanted, ROWS * SZ * 64)
     for j in range(NPJ):
         for i in range(SLOTS // LANES):
-            weights[j][pl.ds(i, 1), :] = projector[pl.ds(j, 1), pl.ds(i * LANES, LANES)]
+            weights[j][pl.ds(i, 1), :] = projector_v[pl.ds(j, 1), pl.ds(i * LANES, LANES)]
     channel = lax.broadcasted_iota(jnp.int32, (8, LANES), 0)
     at = lax.broadcasted_iota(jnp.int32, (8, LANES), 1)
     placed = jnp.zeros((8, LANES), F32)
     for a in range(2):
         for j in range(NPJ):
-            placed = jnp.where((channel == j) & (at == 16 + a), coupling[a, j], placed)
+            value = jnp.broadcast_to(coupling_v[a : a + 1, j : j + 1], (8, LANES))
+            placed = jnp.where((channel == j) & (at == 16 + a), value, placed)
     own[...] = placed
-    for x in range(SX):
-        for y in range(SY):
-            loads[x * SY + y].wait()
-        write_x_faces(x, [field[x * SY + y] for y in range(SY)], x_low, x_high)
+    for row in rows:
+        row.wait()
 
 
 def prepare(count, coupling, orbitals, cells, targets, projector):
     lines = (SLOTS // LANES, LANES)
     return pl.pallas_call(
         prepare_kernel,
-        out_shape=[
-            BLOCK,
-            X_FACE,
-            X_FACE,
-            jax.ShapeDtypeStruct(lines, jnp.int32),
-            jax.ShapeDtypeStruct((8, LANES), F32),
-        ]
+        out_shape=[BLOCK, jax.ShapeDtypeStruct(lines, jnp.int32), jax.ShapeDtypeStruct((8, LANES), F32)]
         + [jax.ShapeDtypeStruct(lines, F32)] * NPJ,
-        in_specs=[pl.BlockSpec(memory_space=pltpu.SMEM)] * 2 + any_specs(1) + vmem_specs(3),
-        out_specs=vmem_specs(5 + NPJ),
-        scratch_shapes=[pltpu.SemaphoreType.DMA((ROWS,))],
-        compiler_params=PARAMS,
+        in_specs=[pl.BlockSpec(memory_space=pltpu.SMEM)] + any_specs(5),
+        out_specs=vmem_specs(3 + NPJ),
+        scratch_shapes=[
+            pltpu.VMEM(coupling.shape, F32),
+            pltpu.VMEM(lines, jnp.int32),
+            pltpu.VMEM(lines, jnp.int32),
+            pltpu.VMEM(projector.shape, F32),
+            pltpu.SemaphoreType.DMA((4,)),
+            pltpu.SemaphoreType.DMA((ROWS,)),
+        ],
+        compiler_params=pltpu.CompilerParams(vmem_limit_bytes=PREPARE_LIMIT),
         name="prepare",
     )(count, coupling, orbitals, cells.reshape(lines), targets.reshape(lines), projector)
 
@@ -240,11 +246,13 @@
     return jnp.concatenate([joined[j * TGT : (j + 1) * TGT] for j in range(NPJ)], axis=1)
 
 
-def first_kernel(field, mat, own, out, y_low, y_high, total):
+def first_kernel(field, mat, own, out, x_low, x_high, y_low, y_high, total):
     for g in range(GROUPS):
         out[pl.ds(16 * g, 16), :] = z_faces([field[4 * g + i] for i in range(4)])
     for x in range(SX):
-        write_y_faces(x, [field[x * SY + y] for y in range(SY)], y_low, y_high)
+        rows = [field[x * SY + y] for y in range(SY)]
+        write_x_faces(x, rows, x_low, x_high)
+        write_y_faces(x, rows, y_low, y_high)
     total[...] = jnp.zeros_like(total)
     for pair in range(PAIRS):
         values = jnp.concatenate([field[2 * pair], field[2 * pair + 1]], axis=1)
@@ -256,9 +264,9 @@
 def first(field, mat, own):
     return pl.pallas_call(
         first_kernel,
-        out_shape=[jax.ShapeDtypeStruct((ZROWS + TGT + 8, LANES), F32), Y_FACE, Y_FACE],
+        out_shape=[jax.ShapeDtypeStruct((ZROWS + TGT + 8, LANES), F32), X_FACE, X_FACE, Y_FACE, Y_FACE],
         in_specs=vmem_specs(3),
-        out_specs=vmem_specs(3),
+        out_specs=vmem_specs(5),
         scratch_shapes=[pltpu.VMEM(TOTAL, F32)],
         compiler_params=PARAMS,
         name="first",
@@ -498,7 +506,7 @@
 
 def local(orbitals, potential, projector, point_cell, target, point_count, coupling):
     bands, size_x, size_y, size_z = orbitals.shape
-    field, x_low, x_high, key, own, *weights = prepare(
+    field, key, own, *weights = prepare(
         point_count.reshape(1), coupling, orbitals.reshape(NB, ROWS, SZ), point_cell, target, projector
     )
     pot = potential.reshape(ROWS, SZ)
@@ -514,17 +522,13 @@
     for k in range(DEGREE):
         start, last = k == 0, k == DEGREE - 1
         if start:
-            x_left = shift(x_high, "gx", 1)
-            x_right = shift(x_low, "gx", -1)
-            mat, field, x_left, x_right = lax.optimization_barrier((mat, field, x_left, x_right))
-            message, y_low, y_high = first(field, mat, own)
+            message, x_low, x_high, y_low, y_high = first(field, mat, own)
         faces = shift(message, "gz", 1)
         y_left = shift(y_high, "gy", 1)
         y_right = shift(y_low, "gy", -1)
-        if not start:
-            faces, x_low, x_high = lax.optimization_barrier((faces, x_low, x_high))
-            x_left = shift(x_high, "gx", 1)
-            x_right = shift(x_low, "gx", -1)
+        faces, x_low, x_high = lax.optimization_barrier((faces, x_low, x_high))
+        x_left = shift(x_high, "gx", 1)
+        x_right = shift(x_low, "gx", -1)
         rows = message.shape[0] - ZROWS
         came = lax.all_to_all(spread_call(spread_zy_kernel, rows, message, faces), "gy", 0, 0)
         came = lax.all_to_all(spread_call(spread_x_kernel, rows, came), "gx", 0, 0)

time: 198 us -> 191 us (0.965)
  waiting for transfers between devices: 9.3 us -> 4.08 us
  local copies, waits for them, and re-layouts: 4.61 us -> 0.31 us
  blocking collectives: 103 us -> 105 us
    ppermute x20, waiting for transfers between devices: 9.3 us -> 4.08 us  [shift(): lax.ppermute(value, axis, [(i, (i + by) % count) for i in range(count)])]
    unnamed x12 -> x6, local copies, waits for them, and re-layouts: 4.32 us -> 0.02 us
    all_to_all x1, blocking collectives: 19.6 us -> 22 us  [local(): lax.all_to_all(jnp.broadcast_to(gram[None], (devices,) + gram.shape), axe...]
  transfers between devices with their start and end apart: 20 -> 20, of which waited for: 4 -> 4; matrix products, arithmetic and copies ran while one was open for 3% -> 0% of each run, Pallas kernels for 3% -> 0%
where the time goes in v9:
time: 191 us; the launch traced here: 192 us
  blocking collectives  105 us (55%)
  starting transfers between devices  37.1 us (19%)
  Pallas kernels  36.3 us (19%)
  other arithmetic  7.86 us (4%)
  waiting for transfers between devices  4.08 us (2%)
    all_to_all x4, blocking collectives, local(): lax.all_to_all(spread_call(spread_zy_kernel, rows, message, faces), 'gy',...  47.9 us
    ppermute x20, starting transfers between devices, shift(): lax.ppermute(value, axis, [(i, (i + by) % count) for i in range(count)])  37.1 us
    all_to_all x4, blocking collectives, local(): came = lax.all_to_all(spread_call(spread_x_kernel, rows, came), 'gx', 0, 0)  35 us
    all_to_all x1, blocking collectives, local(): lax.all_to_all(jnp.broadcast_to(gram[None], (devices,) + gram.shape), axe...  22 us
    pallas_call x4, Pallas kernels, step(): pl.pallas_call(functools.partial(step_kernel, first_step, last_step), out...  19.2 us
    sort x1, other arithmetic, local(): lax.sort((key, *[w.reshape(SLOTS) for w in weights]), num_keys=1, is_stab...  6.69 us
    pallas_call x1, Pallas kernels, build(): pl.pallas_call(build_kernel, out_shape=MATRIX, in_specs=[pl.BlockSpec(mem...  5.73 us
    pallas_call x1, Pallas kernels, finish(): pl.pallas_call(functools.partial(finish_kernel, scale), out_shape=jax.Sha...  5.12 us
  transfers between devices with their start and end apart: 20, of which 4 were waited for; matrix products, arithmetic and copies ran while one was open for 0% of the time, Pallas kernels for 0%

profile of v9, /device:TPU:1, one launch (start us, length us, event | category | flops | bytes accessed | tf_op | source)
XLA Modules:
  0.0 191.5 jit_solution(8987757507098515462)
XLA Ops:
  0.7 3.4 %prepare.1 = (f32[64,32,128]{2,1,0:T(8,128)}, s32[64,128]{1,0:T(8,128)}, f32[8,128]{1,0:T(8,128)}, f32[64,128]{1,0:T(8,128)}, f32[64,128]{1,0:T(8,128)}, /*index=5*/f32[64,128]{1,0:T(8,128)}, f32[64,128]{1,0:T(8,128)}) custom-call(s32[1]{0:T(128)} %bitcast.16.count, f32[2,4]{1,0:T(2,128)} %coupling.1, f32[32,64,128]{2,1,0:T(8,128)} %bitcast.21, ...), custom_call_target="tpu_custom_call" | custom-call | tf_op jit(solution)/shard_map/prepare/pallas_call | solution.py:157
  4.0 1.2 convert_reduce_fusion.starts
  5.2 6.7 %sort.33 = (s32[8192]{0:T(1024)S(1)}, f32[8192]{0:T(1024)S(1)}, f32[8192]{0:T(1024)S(1)}, f32[8192]{0:T(1024)S(1)}, f32[8192]{0:T(1024)S(1)}) sort(s32[8192]{0:T(1024)} %bitcast.23, f32[8192]{0:T(1024)} %bitcast.25, f32[8192]{0:T(1024)} %bitcast.26, f32[8192]{0:T(1024)} %bitcast.27, f32[8192]{0:T(1024)} %bitcast.28), dimensions={0}, to_apply=%region_1.0 | sort | flops 106496 | bytes 327680 | tf_op jit(solution)/shard_map/sort | solution.py:517
  12.2 5.7 %build.1.mat.refs_8_ = bf16[32,320,256]{2,1,0:T(8,128)(2,1)S(1)} custom-call(s32[65]{0:T(128)S(1)} %convert_reduce_fusion.starts, f32[5,8192]{1,0:T(8,128)S(1)} %stack.23.points), custom_call_target="tpu_custom_call" | custom-call | tf_op jit(solution)/shard_map/build/pallas_call | solution.py:225
  18.0 2.4 %first.1 = (f32[304,128]{1,0:T(8,128)S(1)}, f32[48,32,128]{2,1,0:T(8,128)S(1)}, f32[48,32,128]{2,1,0:T(8,128)S(1)}, f32[8,6,32,128]{3,2,1,0:T(8,128)S(1)}, f32[8,6,32,128]{3,2,1,0:T(8,128)S(1)}) custom-call(f32[64,32,128]{2,1,0:T(8,128)S(1)} %copy-done, bf16[32,320,256]{2,1,0:T(8,128)(2,1)S(1)} %build.1.mat.refs_8_, f32[8,128]{1,0:T(8,128)S(1)} %copy-done.2), custom_call_target="tpu_custom_call" | custom-call | tf_op jit(solution)/shard_map/first/pallas_call | solution.py:265
  20.3 4.9 %collective-permute-start = (f32[304,128]{1,0:T(8,128)S(1)}, f32[304,128]{1,0:T(8,128)S(1)}, u32[]{:S(2)}, u32[]{:S(2)}) collective-permute-start(f32[304,128]{1,0:T(8,128)S(1)} %get-tuple-element.67.mine), channel_id=1, source_target_pairs={{0,1},{1,0},{2,3},{3,2},{4,5},{5,4},{6,7},{7,6},{8,9},{9,8},{10,11... | collective-permute-start | bytes 466952 | tf_op jit(solution)/shard_map/ppermute | solution.py:504
  25.3 1.6 collective-permute-start.3
  26.9 2.6 %collective-permute-done.other.refs_1_ = f32[304,128]{1,0:T(8,128)S(1)} collective-permute-done((f32[304,128]{1,0:T(8,128)S(1)}, f32[304,128]{1,0:T(8,128)S(1)}, u32[]{:S(2)}, u32[]{:S(2)}) %collective-permute-start) | collective-permute-done | bytes 155680 | tf_op jit(solution)/shard_map/ppermute | solution.py:504
  29.8 3.3 %collective-permute-start.2 = (f32[48,32,128]{2,1,0:T(8,128)S(1)}, f32[48,32,128]{2,1,0:T(8,128)S(1)}, u32[]{:S(2)}, u32[]{:S(2)}) collective-permute-start(f32[48,32,128]{2,1,0:T(8,128)S(1)} %get-tuple-element.72), channel_id=1, source_target_pairs={{0,112},{16,0},{32,16},{48,32},{64,48},{80,64},{96,80},{112,96},{1... | collective-permute-start | bytes 2359304 | tf_op jit(solution)/shard_map/ppermute | solution.py:504
  33.2 11.3 %all_to_all.45.came = f32[8,48,128]{2,1,0:T(8,128)S(1)} all-to-all(f32[8,48,128]{2,1,0:T(8,128)S(1)} %spread.8), channel_id=1, replica_groups=mesh['gx'=8,'gy'=8,'gz'=2] {'gy'}, dimensions={0} | all-to-all | bytes 393216 | tf_op jit(solution)/shard_map/all_to_all | solution.py:533
  44.6 8.8 %all_to_all.46.refs_7_ = f32[8,48,128]{2,1,0:T(8,128)S(1)} all-to-all(f32[8,48,128]{2,1,0:T(8,128)S(1)} %spread.9), channel_id=1, replica_groups=mesh['gx'=8,'gy'=8,'gz'=2] {'gx'}, dimensions={0} | all-to-all | bytes 393216 | tf_op jit(solution)/shard_map/all_to_all | solution.py:534
  53.5 4.9 %step.4 = (f32[64,32,128]{2,1,0:T(8,128)S(1)}, f32[48,32,128]{2,1,0:T(8,128)S(1)}, f32[48,32,128]{2,1,0:T(8,128)S(1)}, f32[8,6,32,128]{3,2,1,0:T(8,128)S(1)}, f3...) custom-call(f32[64,32,128]{2,1,0:T(8,128)S(1)} %copy-done, ...), custom_call_target="tpu_custom_call" | custom-call | tf_op jit(solution)/shard_map/step/pallas_call | solution.py:433
  58.4 3.1 %collective-permute-start.5 = (f32[296,128]{1,0:T(8,128)S(1)}, f32[296,128]{1,0:T(8,128)S(1)}, u32[]{:S(2)}, u32[]{:S(2)}) collective-permute-start(f32[296,128]{1,0:T(8,128)S(1)} %get-tuple-element.76.mine), channel_id=1, source_target_pairs={{0,1},{1,0},{2,3},{3,2},{4,5},{5,4},{6,7},{7,6},{8,9},{9,8},{10,11... | collective-permute-start | bytes 454664 | tf_op jit(solution)/shard_map/ppermute | solution.py:504
  61.5 2.2 %collective-permute-start.8 = (f32[8,6,32,128]{3,2,1,0:T(8,128)S(1)}, f32[8,6,32,128]{3,2,1,0:T(8,128)S(1)}, u32[]{:S(2)}, u32[]{:S(2)}) collective-permute-start(f32[8,6,32,128]{3,2,1,0:T(8,128)S(1)} %get-tuple-element.82), channel_id=1, source_target_pairs={{0,2},{2,4},{4,6},{6,8},{8,10},{10,12},{12,14},{14,0},{1,3},{3,5},... | collective-permute-start | bytes 2359304 | tf_op jit(solution)/shard_map/ppermute | solution.py:504
  64.5 3.9 %collective-permute-start.7 = (f32[48,32,128]{2,1,0:T(8,128)S(1)}, f32[48,32,128]{2,1,0:T(8,128)S(1)}, u32[]{:S(2)}, u32[]{:S(2)}) collective-permute-start(f32[48,32,128]{2,1,0:T(8,128)S(1)} %get-tuple-element.81), channel_id=1, source_target_pairs={{0,112},{16,0},{32,16},{48,32},{64,48},{80,64},{96,80},{112,96},{1... | collective-permute-start | bytes 2359304 | tf_op jit(solution)/shard_map/ppermute | solution.py:504
  68.4 12.2 %all_to_all.47.came = f32[8,40,128]{2,1,0:T(8,128)S(1)} all-to-all(f32[8,40,128]{2,1,0:T(8,128)S(1)} %spread.10), channel_id=1, replica_groups=mesh['gx'=8,'gy'=8,'gz'=2] {'gy'}, dimensions={0} | all-to-all | bytes 327680 | tf_op jit(solution)/shard_map/all_to_all | solution.py:533
  80.6 9.1 %all_to_all.48.refs_7_ = f32[8,40,128]{2,1,0:T(8,128)S(1)} all-to-all(f32[8,40,128]{2,1,0:T(8,128)S(1)} %spread.11), channel_id=1, replica_groups=mesh['gx'=8,'gy'=8,'gz'=2] {'gx'}, dimensions={0} | all-to-all | bytes 327680 | tf_op jit(solution)/shard_map/all_to_all | solution.py:534
  89.7 5.0 %step.5 = (f32[64,32,128]{2,1,0:T(8,128)S(1)}, f32[48,32,128]{2,1,0:T(8,128)S(1)}, f32[48,32,128]{2,1,0:T(8,128)S(1)}, f32[8,6,32,128]{3,2,1,0:T(8,128)S(1)}, f3...) custom-call(f32[64,32,128]{2,1,0:T(8,128)S(1)} %get-tuple-element.75.refs_0_.refs_9_, ...), custom_call_target="tpu_custom_call" | custom-call | tf_op jit(solution)/shard_map/step/pallas_call | solution.py:433
  94.7 3.0 %collective-permute-start.10 = (f32[296,128]{1,0:T(8,128)S(1)}, f32[296,128]{1,0:T(8,128)S(1)}, u32[]{:S(2)}, u32[]{:S(2)}) collective-permute-start(f32[296,128]{1,0:T(8,128)S(1)} %get-tuple-element.86.mine), channel_id=1, source_target_pairs={{0,1},{1,0},{2,3},{3,2},{4,5},{5,4},{6,7},{7,6},{8,9},{9,8},{10,11... | collective-permute-start | bytes 454664 | tf_op jit(solution)/shard_map/ppermute | solution.py:504
  97.7 2.2 %collective-permute-start.13 = (f32[8,6,32,128]{3,2,1,0:T(8,128)S(1)}, f32[8,6,32,128]{3,2,1,0:T(8,128)S(1)}, u32[]{:S(2)}, u32[]{:S(2)}) collective-permute-start(f32[8,6,32,128]{3,2,1,0:T(8,128)S(1)} %get-tuple-element.92), channel_id=1, source_target_pairs={{0,2},{2,4},{4,6},{6,8},{8,10},{10,12},{12,14},{14,0},{1,3},{3,5},... | collective-permute-start | bytes 2359304 | tf_op jit(solution)/shard_map/ppermute | solution.py:504
  100.6 3.3 %collective-permute-start.12 = (f32[48,32,128]{2,1,0:T(8,128)S(1)}, f32[48,32,128]{2,1,0:T(8,128)S(1)}, u32[]{:S(2)}, u32[]{:S(2)}) collective-permute-start(f32[48,32,128]{2,1,0:T(8,128)S(1)} %get-tuple-element.91), channel_id=1, source_target_pairs={{0,112},{16,0},{32,16},{48,32},{64,48},{80,64},{96,80},{112,96},{1... | collective-permute-start | bytes 2359304 | tf_op jit(solution)/shard_map/ppermute | solution.py:504
  103.9 12.4 %all_to_all.49.came = f32[8,40,128]{2,1,0:T(8,128)S(1)} all-to-all(f32[8,40,128]{2,1,0:T(8,128)S(1)} %spread.12), channel_id=1, replica_groups=mesh['gx'=8,'gy'=8,'gz'=2] {'gy'}, dimensions={0} | all-to-all | bytes 327680 | tf_op jit(solution)/shard_map/all_to_all | solution.py:533
  116.3 8.6 %all_to_all.50.refs_7_ = f32[8,40,128]{2,1,0:T(8,128)S(1)} all-to-all(f32[8,40,128]{2,1,0:T(8,128)S(1)} %spread.13), channel_id=1, replica_groups=mesh['gx'=8,'gy'=8,'gz'=2] {'gx'}, dimensions={0} | all-to-all | bytes 327680 | tf_op jit(solution)/shard_map/all_to_all | solution.py:534
  125.0 5.0 %step.6 = (f32[64,32,128]{2,1,0:T(8,128)S(1)}, f32[48,32,128]{2,1,0:T(8,128)S(1)}, f32[48,32,128]{2,1,0:T(8,128)S(1)}, f32[8,6,32,128]{3,2,1,0:T(8,128)S(1)}, f3...) custom-call(f32[64,32,128]{2,1,0:T(8,128)S(1)} %get-tuple-element.85.refs_0_.refs_9_, ...), custom_call_target="tpu_custom_call" | custom-call | tf_op jit(solution)/shard_map/step/pallas_call | solution.py:433
  129.9 2.7 %collective-permute-start.15 = (f32[296,128]{1,0:T(8,128)S(1)}, f32[296,128]{1,0:T(8,128)S(1)}, u32[]{:S(2)}, u32[]{:S(2)}) collective-permute-start(f32[296,128]{1,0:T(8,128)S(1)} %get-tuple-element.95.mine), channel_id=1, source_target_pairs={{0,1},{1,0},{2,3},{3,2},{4,5},{5,4},{6,7},{7,6},{8,9},{9,8},{10,11... | collective-permute-start | bytes 454664 | tf_op jit(solution)/shard_map/ppermute | solution.py:504
  132.6 2.2 %collective-permute-start.18 = (f32[8,6,32,128]{3,2,1,0:T(8,128)S(1)}, f32[8,6,32,128]{3,2,1,0:T(8,128)S(1)}, u32[]{:S(2)}, u32[]{:S(2)}) collective-permute-start(f32[8,6,32,128]{3,2,1,0:T(8,128)S(1)} %get-tuple-element.101), channel_id=1, source_target_pairs={{0,2},{2,4},{4,6},{6,8},{8,10},{10,12},{12,14},{14,0},{1,3},{3,5},... | collective-permute-start | bytes 2359304 | tf_op jit(solution)/shard_map/ppermute | solution.py:504
  135.8 3.3 %collective-permute-start.17 = (f32[48,32,128]{2,1,0:T(8,128)S(1)}, f32[48,32,128]{2,1,0:T(8,128)S(1)}, u32[]{:S(2)}, u32[]{:S(2)}) collective-permute-start(f32[48,32,128]{2,1,0:T(8,128)S(1)} %get-tuple-element.100), channel_id=1, source_target_pairs={{0,112},{16,0},{32,16},{48,32},{64,48},{80,64},{96,80},{112,96},{1... | collective-permute-start | bytes 2359304 | tf_op jit(solution)/shard_map/ppermute | solution.py:504
  139.2 12.0 %all_to_all.51.came = f32[8,40,128]{2,1,0:T(8,128)S(1)} all-to-all(f32[8,40,128]{2,1,0:T(8,128)S(1)} %spread.14), channel_id=1, replica_groups=mesh['gx'=8,'gy'=8,'gz'=2] {'gy'}, dimensions={0} | all-to-all | bytes 327680 | tf_op jit(solution)/shard_map/all_to_all | solution.py:533
  151.3 8.6 %all_to_all.52.refs_7_ = f32[8,40,128]{2,1,0:T(8,128)S(1)} all-to-all(f32[8,40,128]{2,1,0:T(8,128)S(1)} %spread.15), channel_id=1, replica_groups=mesh['gx'=8,'gy'=8,'gz'=2] {'gx'}, dimensions={0} | all-to-all | bytes 327680 | tf_op jit(solution)/shard_map/all_to_all | solution.py:534
  159.9 4.3 %step.7 = (f32[64,32,128]{2,1,0:T(8,128)S(1)}, f32[8,128]{1,0:T(8,128)S(1)}) custom-call(f32[64,32,128]{2,1,0:T(8,128)S(1)} %get-tuple-element.94.refs_0_, f32[296,128]{1,0:T(8,128)S(1)} %collective-permute-done.15.other.refs_1_, f32[48,32,128]{2,1,0:T(8,128)S(1)} %collective-permute-done.16.refs_2_, f32[48,32,128]{2,1,0:T(8,128)S(1)} %collective-permute-done.17.refs_3_, ...), custom_call_target="tpu_custom_call" | custom-call | tf_op jit(solution)/shard_map/step/pallas_call | solution.py:433
  164.2 22.0 %all_to_all.53.grams = f32[128,8,128]{2,1,0:T(8,128)S(1)} all-to-all(f32[128,8,128]{2,1,0:T(8,128)S(1)} %broadcast_in_dim.2), channel_id=1, replica_groups=mesh['gx'=8,'gy'=8,'gz'=2] {'gx','gy','gz'}, dimensions={0} | all-to-all | bytes 1048576 | tf_op jit(solution)/shard_map/all_to_all | solution.py:548
  186.2 5.1 %finish.1 = f32[32,64,128]{2,1,0:T(8,128)} custom-call(f32[64,32,128]{2,1,0:T(8,128)S(1)} %get-tuple-element.103.field, f32[128,8,128]{2,1,0:T(8,128)S(1)} %all_to_all.53.grams), custom_call_target="tpu_custom_call" | custom-call | tf_op jit(solution)/shard_map/finish/pallas_call | solution.py:487
  (45 shorter events, 3.5 us)
Async XLA Ops:
  12.2 5.8 %copy-start = (f32[64,32,128]{2,1,0:T(8,128)S(1)}, f32[64,32,128]{2,1,0:T(8,128)}, u32[]{:S(2)}) copy-start(f32[64,32,128]{2,1,0:T(8,128)} %get-tuple-element.55.field.refs_0_.refs_9_) | copy-start | bytes 3145732
  12.2 5.8 %copy-start.2 = (f32[8,128]{1,0:T(8,128)S(1)}, f32[8,128]{1,0:T(8,128)}, u32[]{:S(2)}) copy-start(f32[8,128]{1,0:T(8,128)} %get-tuple-element.66.own) | copy-start | bytes 12292
  17.9 35.5 %copy-start.1 = (f32[8,8,128]{2,1,0:T(8,128)S(1)}, f32[8,8,128]{2,1,0:T(8,128)}, u32[]{:S(2)}) copy-start(f32[8,8,128]{2,1,0:T(8,128)} %param.8) | copy-start | bytes 98308
  20.3 9.2 %collective-permute-start = (f32[304,128]{1,0:T(8,128)S(1)}, f32[304,128]{1,0:T(8,128)S(1)}, u32[]{:S(2)}, u32[]{:S(2)}) collective-permute-start(f32[304,128]{1,0:T(8,128)S(1)} %get-tuple-element.67.mine), channel_id=1, source_target_pairs={{0,1},{1,0},{2,3},{3,2},{4,5},{5,4},{6,7},{7,6},{8,9},{9,8},{10,11... | collective-permute-start | bytes 466952 | tf_op jit(solution)/shard_map/ppermute | solution.py:504
  25.3 28.1 %collective-permute-start.3 = (f32[8,6,32,128]{3,2,1,0:T(8,128)S(1)}, f32[8,6,32,128]{3,2,1,0:T(8,128)S(1)}, u32[]{:S(2)}, u32[]{:S(2)}) collective-permute-start(f32[8,6,32,128]{3,2,1,0:T(8,128)S(1)} %get-tuple-element.73), channel_id=1, source_target_pairs={{0,2},{2,4},{4,6},{6,8},{8,10},{10,12},{12,14},{14,0},{1,3},{3,5},... | collective-permute-start | bytes 2359304 | tf_op jit(solution)/shard_map/ppermute | solution.py:504
  26.9 26.6 %collective-permute-start.4 = (f32[8,6,32,128]{3,2,1,0:T(8,128)S(1)}, f32[8,6,32,128]{3,2,1,0:T(8,128)S(1)}, u32[]{:S(2)}, u32[]{:S(2)}) collective-permute-start(f32[8,6,32,128]{3,2,1,0:T(8,128)S(1)} %get-tuple-element.74), channel_id=1, source_target_pairs={{0,14},{2,0},{4,2},{6,4},{8,6},{10,8},{12,10},{14,12},{1,15},{3,1}... | collective-permute-start | bytes 2359304 | tf_op jit(solution)/shard_map/ppermute | solution.py:504
  29.5 23.9 %collective-permute-start.1 = (f32[48,32,128]{2,1,0:T(8,128)S(1)}, f32[48,32,128]{2,1,0:T(8,128)S(1)}, u32[]{:S(2)}, u32[]{:S(2)}) collective-permute-start(f32[48,32,128]{2,1,0:T(8,128)S(1)} %get-tuple-element.71), channel_id=1, source_target_pairs={{0,16},{16,32},{32,48},{48,64},{64,80},{80,96},{96,112},{112,0},{1... | collective-permute-start | bytes 2359304 | tf_op jit(solution)/shard_map/ppermute | solution.py:504
  29.8 23.7 %collective-permute-start.2 = (f32[48,32,128]{2,1,0:T(8,128)S(1)}, f32[48,32,128]{2,1,0:T(8,128)S(1)}, u32[]{:S(2)}, u32[]{:S(2)}) collective-permute-start(f32[48,32,128]{2,1,0:T(8,128)S(1)} %get-tuple-element.72), channel_id=1, source_target_pairs={{0,112},{16,0},{32,16},{48,32},{64,48},{80,64},{96,80},{112,96},{1... | collective-permute-start | bytes 2359304 | tf_op jit(solution)/shard_map/ppermute | solution.py:504
  58.4 5.7 %collective-permute-start.5 = (f32[296,128]{1,0:T(8,128)S(1)}, f32[296,128]{1,0:T(8,128)S(1)}, u32[]{:S(2)}, u32[]{:S(2)}) collective-permute-start(f32[296,128]{1,0:T(8,128)S(1)} %get-tuple-element.76.mine), channel_id=1, source_target_pairs={{0,1},{1,0},{2,3},{3,2},{4,5},{5,4},{6,7},{7,6},{8,9},{9,8},{10,11... | collective-permute-start | bytes 454664 | tf_op jit(solution)/shard_map/ppermute | solution.py:504
  61.5 28.2 %collective-permute-start.8 = (f32[8,6,32,128]{3,2,1,0:T(8,128)S(1)}, f32[8,6,32,128]{3,2,1,0:T(8,128)S(1)}, u32[]{:S(2)}, u32[]{:S(2)}) collective-permute-start(f32[8,6,32,128]{3,2,1,0:T(8,128)S(1)} %get-tuple-element.82), channel_id=1, source_target_pairs={{0,2},{2,4},{4,6},{6,8},{8,10},{10,12},{12,14},{14,0},{1,3},{3,5},... | collective-permute-start | bytes 2359304 | tf_op jit(solution)/shard_map/ppermute | solution.py:504
  63.7 25.9 %collective-permute-start.9 = (f32[8,6,32,128]{3,2,1,0:T(8,128)S(1)}, f32[8,6,32,128]{3,2,1,0:T(8,128)S(1)}, u32[]{:S(2)}, u32[]{:S(2)}) collective-permute-start(f32[8,6,32,128]{3,2,1,0:T(8,128)S(1)} %get-tuple-element.83), channel_id=1, source_target_pairs={{0,14},{2,0},{4,2},{6,4},{8,6},{10,8},{12,10},{14,12},{1,15},{3,1}... | collective-permute-start | bytes 2359304 | tf_op jit(solution)/shard_map/ppermute | solution.py:504
  64.1 25.6 %collective-permute-start.6 = (f32[48,32,128]{2,1,0:T(8,128)S(1)}, f32[48,32,128]{2,1,0:T(8,128)S(1)}, u32[]{:S(2)}, u32[]{:S(2)}) collective-permute-start(f32[48,32,128]{2,1,0:T(8,128)S(1)} %get-tuple-element.80), channel_id=1, source_target_pairs={{0,16},{16,32},{32,48},{48,64},{64,80},{80,96},{96,112},{112,0},{1... | collective-permute-start | bytes 2359304 | tf_op jit(solution)/shard_map/ppermute | solution.py:504
  64.5 25.2 %collective-permute-start.7 = (f32[48,32,128]{2,1,0:T(8,128)S(1)}, f32[48,32,128]{2,1,0:T(8,128)S(1)}, u32[]{:S(2)}, u32[]{:S(2)}) collective-permute-start(f32[48,32,128]{2,1,0:T(8,128)S(1)} %get-tuple-element.81), channel_id=1, source_target_pairs={{0,112},{16,0},{32,16},{48,32},{64,48},{80,64},{96,80},{112,96},{1... | collective-permute-start | bytes 2359304 | tf_op jit(solution)/shard_map/ppermute | solution.py:504
  94.7 5.6 %collective-permute-start.10 = (f32[296,128]{1,0:T(8,128)S(1)}, f32[296,128]{1,0:T(8,128)S(1)}, u32[]{:S(2)}, u32[]{:S(2)}) collective-permute-start(f32[296,128]{1,0:T(8,128)S(1)} %get-tuple-element.86.mine), channel_id=1, source_target_pairs={{0,1},{1,0},{2,3},{3,2},{4,5},{5,4},{6,7},{7,6},{8,9},{9,8},{10,11... | collective-permute-start | bytes 454664 | tf_op jit(solution)/shard_map/ppermute | solution.py:504
  97.7 27.2 %collective-permute-start.13 = (f32[8,6,32,128]{3,2,1,0:T(8,128)S(1)}, f32[8,6,32,128]{3,2,1,0:T(8,128)S(1)}, u32[]{:S(2)}, u32[]{:S(2)}) collective-permute-start(f32[8,6,32,128]{3,2,1,0:T(8,128)S(1)} %get-tuple-element.92), channel_id=1, source_target_pairs={{0,2},{2,4},{4,6},{6,8},{8,10},{10,12},{12,14},{14,0},{1,3},{3,5},... | collective-permute-start | bytes 2359304 | tf_op jit(solution)/shard_map/ppermute | solution.py:504
  99.9 25.0 %collective-permute-start.14 = (f32[8,6,32,128]{3,2,1,0:T(8,128)S(1)}, f32[8,6,32,128]{3,2,1,0:T(8,128)S(1)}, u32[]{:S(2)}, u32[]{:S(2)}) collective-permute-start(f32[8,6,32,128]{3,2,1,0:T(8,128)S(1)} %get-tuple-element.93), channel_id=1, source_target_pairs={{0,14},{2,0},{4,2},{6,4},{8,6},{10,8},{12,10},{14,12},{1,15},{3,1}... | collective-permute-start | bytes 2359304 | tf_op jit(solution)/shard_map/ppermute | solution.py:504
  100.3 24.6 %collective-permute-start.11 = (f32[48,32,128]{2,1,0:T(8,128)S(1)}, f32[48,32,128]{2,1,0:T(8,128)S(1)}, u32[]{:S(2)}, u32[]{:S(2)}) collective-permute-start(f32[48,32,128]{2,1,0:T(8,128)S(1)} %get-tuple-element.90), channel_id=1, source_target_pairs={{0,16},{16,32},{32,48},{48,64},{64,80},{80,96},{96,112},{112,0},{1... | collective-permute-start | bytes 2359304 | tf_op jit(solution)/shard_map/ppermute | solution.py:504
  100.6 24.3 %collective-permute-start.12 = (f32[48,32,128]{2,1,0:T(8,128)S(1)}, f32[48,32,128]{2,1,0:T(8,128)S(1)}, u32[]{:S(2)}, u32[]{:S(2)}) collective-permute-start(f32[48,32,128]{2,1,0:T(8,128)S(1)} %get-tuple-element.91), channel_id=1, source_target_pairs={{0,112},{16,0},{32,16},{48,32},{64,48},{80,64},{96,80},{112,96},{1... | collective-permute-start | bytes 2359304 | tf_op jit(solution)/shard_map/ppermute | solution.py:504
  129.9 5.6 %collective-permute-start.15 = (f32[296,128]{1,0:T(8,128)S(1)}, f32[296,128]{1,0:T(8,128)S(1)}, u32[]{:S(2)}, u32[]{:S(2)}) collective-permute-start(f32[296,128]{1,0:T(8,128)S(1)} %get-tuple-element.95.mine), channel_id=1, source_target_pairs={{0,1},{1,0},{2,3},{3,2},{4,5},{5,4},{6,7},{7,6},{8,9},{9,8},{10,11... | collective-permute-start | bytes 454664 | tf_op jit(solution)/shard_map/ppermute | solution.py:504
  132.6 27.2 %collective-permute-start.18 = (f32[8,6,32,128]{3,2,1,0:T(8,128)S(1)}, f32[8,6,32,128]{3,2,1,0:T(8,128)S(1)}, u32[]{:S(2)}, u32[]{:S(2)}) collective-permute-start(f32[8,6,32,128]{3,2,1,0:T(8,128)S(1)} %get-tuple-element.101), channel_id=1, source_target_pairs={{0,2},{2,4},{4,6},{6,8},{8,10},{10,12},{12,14},{14,0},{1,3},{3,5},... | collective-permute-start | bytes 2359304 | tf_op jit(solution)/shard_map/ppermute | solution.py:504
  134.8 25.0 %collective-permute-start.19 = (f32[8,6,32,128]{3,2,1,0:T(8,128)S(1)}, f32[8,6,32,128]{3,2,1,0:T(8,128)S(1)}, u32[]{:S(2)}, u32[]{:S(2)}) collective-permute-start(f32[8,6,32,128]{3,2,1,0:T(8,128)S(1)} %get-tuple-element.102), channel_id=1, source_target_pairs={{0,14},{2,0},{4,2},{6,4},{8,6},{10,8},{12,10},{14,12},{1,15},{3,1}... | collective-permute-start | bytes 2359304 | tf_op jit(solution)/shard_map/ppermute | solution.py:504
  135.5 24.3 %collective-permute-start.16 = (f32[48,32,128]{2,1,0:T(8,128)S(1)}, f32[48,32,128]{2,1,0:T(8,128)S(1)}, u32[]{:S(2)}, u32[]{:S(2)}) collective-permute-start(f32[48,32,128]{2,1,0:T(8,128)S(1)} %get-tuple-element.99), channel_id=1, source_target_pairs={{0,16},{16,32},{32,48},{48,64},{64,80},{80,96},{96,112},{112,0},{1... | collective-permute-start | bytes 2359304 | tf_op jit(solution)/shard_map/ppermute | solution.py:504
  135.8 24.0 %collective-permute-start.17 = (f32[48,32,128]{2,1,0:T(8,128)S(1)}, f32[48,32,128]{2,1,0:T(8,128)S(1)}, u32[]{:S(2)}, u32[]{:S(2)}) collective-permute-start(f32[48,32,128]{2,1,0:T(8,128)S(1)} %get-tuple-element.100), channel_id=1, source_target_pairs={{0,112},{16,0},{32,16},{48,32},{64,48},{80,64},{96,80},{112,96},{1... | collective-permute-start | bytes 2359304 | tf_op jit(solution)/shard_map/ppermute | solution.py:504

commit v10 on v9

--- a/solution.py
+++ b/solution.py
@@ -33,9 +33,10 @@
 TGT = 40
 CH = NPJ * TGT
 GROUPS = ROWS // 4
-TOTAL = (2 * CH, 2 * NB)
+TOTAL = (NB, CH)
 BATCH = 16
 ZROWS = GROUPS * 16
+PACK = 24
 LANES = 128
 F32 = jnp.float32
 BF16 = jnp.bfloat16
@@ -238,11 +239,12 @@
 
 def partial_of(mat, values):
     hi, lo = split2(values)
-    return dot(mat, jnp.concatenate([hi, lo], axis=0), NT)
+    both = dot(jnp.concatenate([hi, lo], axis=0), mat[:CH], NT)
+    return both[:NB] + both[NB:] + dot(hi, mat[CH:], NT)
 
 
 def packed_partial(total):
-    joined = total[:CH, :NB] + total[:CH, NB:] + total[CH:, :NB]
+    joined = total.T
     return jnp.concatenate([joined[j * TGT : (j + 1) * TGT] for j in range(NPJ)], axis=1)
 
 
@@ -273,60 +275,106 @@
     )(field, mat, own)
 
 
-def spread(frame, axis, stride, along, out, at):
+def neighbours(axis):
     me = lax.axis_index(axis)
-    target = lax.broadcasted_iota(jnp.int32, frame.shape, along)
+    return [(d, (me + d + 8) % 8, (me - d + 8) % 8) for d in (-2, -1, 1, 2)]
+
+
+def packed(frame, stride, d):
+    found = []
+    for start in range(0, 36, 3 * stride):
+        rows = frame[start : start + 3 * stride]
+        gap = jnp.zeros((stride, LANES), F32)
+        if d == 1:
+            found.append(rows[stride:])
+        elif d == -1:
+            found.append(rows[: 2 * stride])
+        elif d == 2:
+            found += [rows[2 * stride :], gap]
+        else:
+            found += [gap, rows[:stride]]
+    return jnp.concatenate(found, axis=0)
+
+
+def shifted(frame, stride, d):
+    target = lax.broadcasted_iota(jnp.int32, frame.shape, 1)
     digit = (target // stride) % 3
-    for distance in range(-3, 5):
-        if abs(distance) > 2:
-            piece = jnp.zeros(frame.shape, F32)
+    valid = (digit + d >= 0) & (digit + d <= 2) & (target < 36)
+    return jnp.where(valid, pltpu.roll(frame, (-stride * d) % LANES, 1), 0.0)
+
+
+def send(axis, stride, frame, out):
+    me = lax.axis_index(axis)
+    for d in (-3, 0, 3, 4):
+        out[(me + d + 8) % 8] = jnp.zeros(out.shape[1:], F32)
+    for d, to, _ in neighbours(axis):
+        out[to, pl.ds(0, PACK), :] = packed(frame[:TGT], stride, d)
+        if frame.shape[0] > TGT:
+            out[to, pl.ds(PACK, 8), :] = shifted(frame[TGT:], stride, d)
+
+
+def received(axis, stride, frame, came):
+    below = above = couplings = 0.0
+    for d, _, source in neighbours(axis):
+        block = came[source]
+        if d > 0:
+            below = below + block[:PACK]
         else:
-            by = (-stride * distance) % frame.shape[along]
-            moved = frame if distance == 0 else pltpu.roll(frame, by, along)
-            valid = (digit + distance >= 0) & (digit + distance <= 2) & (target < 36)
-            piece = jnp.where(valid, moved, 0.0)
-        out[(me + distance + 8) % 8, at, :] = piece
-
-
-def parts_of(rows):
-    return ((0, TGT, 0),) if rows == TGT else ((0, TGT, 0), (TGT, 8, 1))
-
-
-def spread_zy_kernel(mine, other, out):
-    for start, size, along in parts_of(out.shape[1]):
-        at = pl.ds(ZROWS + start, size)
-        theirs = other[at, :]
-        target = lax.broadcasted_iota(jnp.int32, theirs.shape, along)
-        up = pltpu.roll(theirs, theirs.shape[along] - 2, along)
-        swapped = jnp.where(target & 2 == 0, up, pltpu.roll(theirs, 2, along))
-        spread(mine[at, :] + swapped, "gy", 4, along, out, pl.ds(start, size))
-
-
-def spread_x_kernel(came, out):
-    for start, size, along in parts_of(out.shape[1]):
-        at = pl.ds(start, size)
-        frame = came[0, at, :]
-        for slot in range(1, 8):
-            frame = frame + came[slot, at, :]
-        spread(frame, "gx", 12, along, out, at)
+            above = above + block[:PACK]
+        if frame.shape[0] > TGT:
+            couplings = couplings + block[PACK:]
+    gap = jnp.zeros((stride, LANES), F32)
+    first, last = [], []
+    for start in range(0, PACK, 2 * stride):
+        first += [below[start : start + 2 * stride], gap]
+        last += [gap, above[start : start + 2 * stride]]
+    rest = [jnp.zeros((TGT - 36, LANES), F32)]
+    added = jnp.concatenate(first + rest, axis=0) + jnp.concatenate(last + rest, axis=0)
+    if frame.shape[0] == TGT:
+        return frame + added
+    return frame + jnp.concatenate([added, couplings], axis=0)
+
+
+def swap_z(theirs, along):
+    target = lax.broadcasted_iota(jnp.int32, theirs.shape, along)
+    up = pltpu.roll(theirs, theirs.shape[along] - 2, along)
+    return jnp.where(target & 2 == 0, up, pltpu.roll(theirs, 2, along))
+
+
+def spread_zy_kernel(mine, other, out, kept):
+    frame = mine[pl.ds(ZROWS, TGT), :] + swap_z(other[pl.ds(ZROWS, TGT), :], 0)
+    if kept.shape[0] > TGT:
+        at = pl.ds(ZROWS + TGT, 8)
+        frame = jnp.concatenate([frame, mine[at, :] + swap_z(other[at, :], 1)], axis=0)
+    kept[...] = frame
+    send("gy", 4, frame, out)
+
+
+def spread_x_kernel(held, came, out, kept):
+    frame = received("gy", 4, held[...], came)
+    kept[...] = frame
+    send("gx", 12, frame, out)
 
 
 def spread_call(kernel, rows, *arrays):
     return pl.pallas_call(
         kernel,
-        out_shape=jax.ShapeDtypeStruct((8, rows, LANES), F32),
+        out_shape=[
+            jax.ShapeDtypeStruct((8, rows - TGT + PACK, LANES), F32),
+            jax.ShapeDtypeStruct((rows, LANES), F32),
+        ],
         in_specs=vmem_specs(len(arrays)),
-        out_specs=pl.BlockSpec(memory_space=pltpu.VMEM),
+        out_specs=vmem_specs(2),
         compiler_params=PARAMS,
         name="spread",
     )(*arrays)
 
 
 def step_kernel(first_step, last_step, *refs):
-    count = 9 if first_step else 11
-    field, faces, x_left, x_right, y_left, y_right, potential, came, mat = refs[:9]
+    count = 10 if first_step else 12
+    field, faces, x_left, x_right, y_left, y_right, potential, kept, came, mat = refs[:10]
     if not first_step:
-        previous, coupling = refs[9:11]
+        previous, coupling = refs[10:12]
     refs = refs[count:]
     if last_step:
         (new, gram), refs = refs[:2], refs[2:]
@@ -375,9 +423,7 @@
             new[4 * g + i] = result
 
     total[...] = jnp.zeros_like(total)
-    frame = came[0]
-    for slot in range(1, came.shape[0]):
-        frame = frame + came[slot]
+    frame = received("gx", 12, kept[...], came)
     if first_step:
         by_channel = jnp.concatenate([frame[TGT:], jnp.zeros((LANES - 8, LANES), F32)], axis=0).T
         columns = [jnp.broadcast_to(by_channel[:TGT, j : j + 1], (TGT, NB)) for j in range(NPJ)]
@@ -458,7 +504,7 @@
     work = jnp.concatenate([gram, eye], axis=1)
     below = lax.broadcasted_iota(jnp.int32, (NB, 2 * NB), 0)
     for k in range(NB):
-        root = 1.0 / jnp.sqrt(work[k : k + 1, k : k + 1])
+        root = lax.rsqrt(work[k : k + 1, k : k + 1])
         line = work[k : k + 1, :] * root
         inverse[pl.ds(k, 1), :] = line[:, NB:]
         if k < NB - 1:
@@ -530,9 +576,11 @@
         x_left = shift(x_high, "gx", 1)
         x_right = shift(x_low, "gx", -1)
         rows = message.shape[0] - ZROWS
-        came = lax.all_to_all(spread_call(spread_zy_kernel, rows, message, faces), "gy", 0, 0)
-        came = lax.all_to_all(spread_call(spread_x_kernel, rows, came), "gx", 0, 0)
-        outs = step(start, last, field, faces, x_left, x_right, y_left, y_right, pot, came, mat, *other)
+        sends, kept = spread_call(spread_zy_kernel, rows, message, faces)
+        came = lax.all_to_all(sends, "gy", 0, 0)
+        sends, kept = spread_call(spread_x_kernel, rows, kept, came)
+        came = lax.all_to_all(sends, "gx", 0, 0)
+        outs = step(start, last, field, faces, x_left, x_right, y_left, y_right, pot, kept, came, mat, *other)
         previous = field
         if last:
             field, gram = outs

time: 191 us -> 185 us (0.969)
  blocking collectives: 105 us -> 100 us
    all_to_all x8, blocking collectives: 82.9 us -> 79.7 us  [the longest x4 48.6 us: local(): came = lax.all_to_all(sends, 'gy', 0, 0)]
  transfers between devices with their start and end apart: 20 -> 20, of which waited for: 4 -> 2; matrix products, arithmetic and copies ran while one was open for 0% -> 0% of each run, Pallas kernels for 0% -> 0%
where the time goes in v10:
time: 185 us; the launch traced here: 184 us
  blocking collectives  100 us (54%)
  starting transfers between devices  37.2 us (20%)
  Pallas kernels  34.8 us (19%)
  other arithmetic  7.86 us (4%)
  waiting for transfers between devices  2.36 us (1%)
    all_to_all x4, blocking collectives, local(): came = lax.all_to_all(sends, 'gy', 0, 0)  48.6 us
    ppermute x20, starting transfers between devices, shift(): lax.ppermute(value, axis, [(i, (i + by) % count) for i in range(count)])  37.2 us
    all_to_all x4, blocking collectives, local(): came = lax.all_to_all(sends, 'gx', 0, 0)  31.1 us
    all_to_all x1, blocking collectives, local(): lax.all_to_all(jnp.broadcast_to(gram[None], (devices,) + gram.shape), axe...  20.6 us
    pallas_call x4, Pallas kernels, step(): pl.pallas_call(functools.partial(step_kernel, first_step, last_step), out...  18.4 us
    sort x1, other arithmetic, local(): lax.sort((key, *[w.reshape(SLOTS) for w in weights]), num_keys=1, is_stab...  6.69 us
    pallas_call x1, Pallas kernels, build(): pl.pallas_call(build_kernel, out_shape=MATRIX, in_specs=[pl.BlockSpec(mem...  5.72 us
    pallas_call x1, Pallas kernels, finish(): pl.pallas_call(functools.partial(finish_kernel, scale), out_shape=jax.Sha...  4.74 us
  transfers between devices with their start and end apart: 20, of which 2 were waited for; matrix products, arithmetic and copies ran while one was open for 0% of the time, Pallas kernels for 0%

profile of v10, /device:TPU:1, one launch (start us, length us, event | category | flops | bytes accessed | tf_op | source)
XLA Modules:
  0.0 183.9 jit_solution(8546236869249433607)
XLA Ops:
  0.7 3.4 %prepare.1 = (f32[64,32,128]{2,1,0:T(8,128)}, s32[64,128]{1,0:T(8,128)}, f32[8,128]{1,0:T(8,128)}, f32[64,128]{1,0:T(8,128)}, f32[64,128]{1,0:T(8,128)}, /*index=5*/f32[64,128]{1,0:T(8,128)}, f32[64,128]{1,0:T(8,128)}) custom-call(s32[1]{0:T(128)} %bitcast.16.count, f32[2,4]{1,0:T(2,128)} %coupling.1, f32[32,64,128]{2,1,0:T(8,128)} %bitcast.21, ...), custom_call_target="tpu_custom_call" | custom-call | tf_op jit(solution)/shard_map/prepare/pallas_call | solution.py:158
  5.2 6.7 %sort.33 = (s32[8192]{0:T(1024)S(1)}, f32[8192]{0:T(1024)S(1)}, f32[8192]{0:T(1024)S(1)}, f32[8192]{0:T(1024)S(1)}, f32[8192]{0:T(1024)S(1)}) sort(s32[8192]{0:T(1024)} %bitcast.23, f32[8192]{0:T(1024)} %bitcast.25, f32[8192]{0:T(1024)} %bitcast.26, f32[8192]{0:T(1024)} %bitcast.27, f32[8192]{0:T(1024)} %bitcast.28), dimensions={0}, to_apply=%region_1.0 | sort | flops 106496 | bytes 327680 | tf_op jit(solution)/shard_map/sort | solution.py:563
  12.2 5.7 %build.1.mat.refs_9_ = bf16[32,320,256]{2,1,0:T(8,128)(2,1)S(1)} custom-call(s32[65]{0:T(128)S(1)} %convert_reduce_fusion.starts, f32[5,8192]{1,0:T(8,128)S(1)} %stack.23.points), custom_call_target="tpu_custom_call" | custom-call | tf_op jit(solution)/shard_map/build/pallas_call | solution.py:226
  18.0 2.1 %first.1 = (f32[304,128]{1,0:T(8,128)S(1)}, f32[48,32,128]{2,1,0:T(8,128)S(1)}, f32[48,32,128]{2,1,0:T(8,128)S(1)}, f32[8,6,32,128]{3,2,1,0:T(8,128)S(1)}, f32[8,6,32,128]{3,2,1,0:T(8,128)S(1)}) custom-call(f32[64,32,128]{2,1,0:T(8,128)S(1)} %copy-done, bf16[32,320,256]{2,1,0:T(8,128)(2,1)S(1)} %build.1.mat.refs_9_, f32[8,128]{1,0:T(8,128)S(1)} %copy-done.2), custom_call_target="tpu_custom_call" | custom-call | tf_op jit(solution)/shard_map/first/pallas_call | solution.py:267
  20.1 4.5 %collective-permute-start = (f32[304,128]{1,0:T(8,128)S(1)}, f32[304,128]{1,0:T(8,128)S(1)}, u32[]{:S(2)}, u32[]{:S(2)}) collective-permute-start(f32[304,128]{1,0:T(8,128)S(1)} %get-tuple-element.83.mine), channel_id=1, source_target_pairs={{0,1},{1,0},{2,3},{3,2},{4,5},{5,4},{6,7},{7,6},{8,9},{9,8},{10,11... | collective-permute-start | bytes 466952 | tf_op jit(solution)/shard_map/ppermute | solution.py:550
  24.6 2.1 %collective-permute-start.3 = (f32[8,6,32,128]{3,2,1,0:T(8,128)S(1)}, f32[8,6,32,128]{3,2,1,0:T(8,128)S(1)}, u32[]{:S(2)}, u32[]{:S(2)}) collective-permute-start(f32[8,6,32,128]{3,2,1,0:T(8,128)S(1)} %get-tuple-element.89), channel_id=1, source_target_pairs={{0,2},{2,4},{4,6},{6,8},{8,10},{10,12},{12,14},{14,0},{1,3},{3,5},... | collective-permute-start | bytes 2359304 | tf_op jit(solution)/shard_map/ppermute | solution.py:550
  26.6 1.7 collective-permute-done.other.refs_1_
  28.3 1.2 collective-permute-start.1
  29.5 2.4 %collective-permute-start.2 = (f32[48,32,128]{2,1,0:T(8,128)S(1)}, f32[48,32,128]{2,1,0:T(8,128)S(1)}, u32[]{:S(2)}, u32[]{:S(2)}) collective-permute-start(f32[48,32,128]{2,1,0:T(8,128)S(1)} %get-tuple-element.88), channel_id=1, source_target_pairs={{0,112},{16,0},{32,16},{48,32},{64,48},{80,64},{96,80},{112,96},{1... | collective-permute-start | bytes 2359304 | tf_op jit(solution)/shard_map/ppermute | solution.py:550
  32.0 11.9 %all_to_all.45.came = f32[8,32,128]{2,1,0:T(8,128)S(1)} all-to-all(f32[8,32,128]{2,1,0:T(8,128)S(1)} %get-tuple-element.92), channel_id=1, replica_groups=mesh['gx'=8,'gy'=8,'gz'=2] {'gy'}, dimensions={0} | all-to-all | bytes 262144 | tf_op jit(solution)/shard_map/all_to_all | solution.py:580
  44.0 8.1 %all_to_all.46.refs_8_ = f32[8,32,128]{2,1,0:T(8,128)S(1)} all-to-all(f32[8,32,128]{2,1,0:T(8,128)S(1)} %get-tuple-element.94), channel_id=1, replica_groups=mesh['gx'=8,'gy'=8,'gz'=2] {'gx'}, dimensions={0} | all-to-all | bytes 262144 | tf_op jit(solution)/shard_map/all_to_all | solution.py:582
  52.1 4.7 %step.4 = (f32[64,32,128]{2,1,0:T(8,128)S(1)}, f32[48,32,128]{2,1,0:T(8,128)S(1)}, f32[48,32,128]{2,1,0:T(8,128)S(1)}, f32[8,6,32,128]{3,2,1,0:T(8,128)S(1)}, f3...) custom-call(f32[64,32,128]{2,1,0:T(8,128)S(1)} %copy-done, ...), custom_call_target="tpu_custom_call" | custom-call | tf_op jit(solution)/shard_map/step/pallas_call | solution.py:479
  56.8 3.0 %collective-permute-start.5 = (f32[296,128]{1,0:T(8,128)S(1)}, f32[296,128]{1,0:T(8,128)S(1)}, u32[]{:S(2)}, u32[]{:S(2)}) collective-permute-start(f32[296,128]{1,0:T(8,128)S(1)} %get-tuple-element.96.mine), channel_id=1, source_target_pairs={{0,1},{1,0},{2,3},{3,2},{4,5},{5,4},{6,7},{7,6},{8,9},{9,8},{10,11... | collective-permute-start | bytes 454664 | tf_op jit(solution)/shard_map/ppermute | solution.py:550
  59.8 2.6 %collective-permute-start.8 = (f32[8,6,32,128]{3,2,1,0:T(8,128)S(1)}, f32[8,6,32,128]{3,2,1,0:T(8,128)S(1)}, u32[]{:S(2)}, u32[]{:S(2)}) collective-permute-start(f32[8,6,32,128]{3,2,1,0:T(8,128)S(1)} %get-tuple-element.102), channel_id=1, source_target_pairs={{0,2},{2,4},{4,6},{6,8},{8,10},{10,12},{12,14},{14,0},{1,3},{3,5},... | collective-permute-start | bytes 2359304 | tf_op jit(solution)/shard_map/ppermute | solution.py:550
  63.1 3.0 %collective-permute-start.7 = (f32[48,32,128]{2,1,0:T(8,128)S(1)}, f32[48,32,128]{2,1,0:T(8,128)S(1)}, u32[]{:S(2)}, u32[]{:S(2)}) collective-permute-start(f32[48,32,128]{2,1,0:T(8,128)S(1)} %get-tuple-element.101), channel_id=1, source_target_pairs={{0,112},{16,0},{32,16},{48,32},{64,48},{80,64},{96,80},{112,96},{1... | collective-permute-start | bytes 2359304 | tf_op jit(solution)/shard_map/ppermute | solution.py:550
  66.1 12.2 %all_to_all.47.came = f32[8,24,128]{2,1,0:T(8,128)S(1)} all-to-all(f32[8,24,128]{2,1,0:T(8,128)S(1)} %get-tuple-element.105), channel_id=1, replica_groups=mesh['gx'=8,'gy'=8,'gz'=2] {'gy'}, dimensions={0} | all-to-all | bytes 196608 | tf_op jit(solution)/shard_map/all_to_all | solution.py:580
  78.3 7.7 %all_to_all.48.refs_8_ = f32[8,24,128]{2,1,0:T(8,128)S(1)} all-to-all(f32[8,24,128]{2,1,0:T(8,128)S(1)} %get-tuple-element.107), channel_id=1, replica_groups=mesh['gx'=8,'gy'=8,'gz'=2] {'gx'}, dimensions={0} | all-to-all | bytes 196608 | tf_op jit(solution)/shard_map/all_to_all | solution.py:582
  86.0 4.8 %step.5 = (f32[64,32,128]{2,1,0:T(8,128)S(1)}, f32[48,32,128]{2,1,0:T(8,128)S(1)}, f32[48,32,128]{2,1,0:T(8,128)S(1)}, f32[8,6,32,128]{3,2,1,0:T(8,128)S(1)}, f3...) custom-call(f32[64,32,128]{2,1,0:T(8,128)S(1)} %get-tuple-element.95.refs_0_.refs_10_, ...), custom_call_target="tpu_custom_call" | custom-call | tf_op jit(solution)/shard_map/step/pallas_call | solution.py:479
  90.8 3.0 %collective-permute-start.10 = (f32[296,128]{1,0:T(8,128)S(1)}, f32[296,128]{1,0:T(8,128)S(1)}, u32[]{:S(2)}, u32[]{:S(2)}) collective-permute-start(f32[296,128]{1,0:T(8,128)S(1)} %get-tuple-element.110.mine), channel_id=1, source_target_pairs={{0,1},{1,0},{2,3},{3,2},{4,5},{5,4},{6,7},{7,6},{8,9},{9,8},{10,11... | collective-permute-start | bytes 454664 | tf_op jit(solution)/shard_map/ppermute | solution.py:550
  93.8 2.4 %collective-permute-start.13 = (f32[8,6,32,128]{3,2,1,0:T(8,128)S(1)}, f32[8,6,32,128]{3,2,1,0:T(8,128)S(1)}, u32[]{:S(2)}, u32[]{:S(2)}) collective-permute-start(f32[8,6,32,128]{3,2,1,0:T(8,128)S(1)} %get-tuple-element.116), channel_id=1, source_target_pairs={{0,2},{2,4},{4,6},{6,8},{8,10},{10,12},{12,14},{14,0},{1,3},{3,5},... | collective-permute-start | bytes 2359304 | tf_op jit(solution)/shard_map/ppermute | solution.py:550
  97.7 2.5 %collective-permute-start.12 = (f32[48,32,128]{2,1,0:T(8,128)S(1)}, f32[48,32,128]{2,1,0:T(8,128)S(1)}, u32[]{:S(2)}, u32[]{:S(2)}) collective-permute-start(f32[48,32,128]{2,1,0:T(8,128)S(1)} %get-tuple-element.115), channel_id=1, source_target_pairs={{0,112},{16,0},{32,16},{48,32},{64,48},{80,64},{96,80},{112,96},{1... | collective-permute-start | bytes 2359304 | tf_op jit(solution)/shard_map/ppermute | solution.py:550
  100.2 12.3 %all_to_all.49.came = f32[8,24,128]{2,1,0:T(8,128)S(1)} all-to-all(f32[8,24,128]{2,1,0:T(8,128)S(1)} %get-tuple-element.119), channel_id=1, replica_groups=mesh['gx'=8,'gy'=8,'gz'=2] {'gy'}, dimensions={0} | all-to-all | bytes 196608 | tf_op jit(solution)/shard_map/all_to_all | solution.py:580
  112.5 7.7 %all_to_all.50.refs_8_ = f32[8,24,128]{2,1,0:T(8,128)S(1)} all-to-all(f32[8,24,128]{2,1,0:T(8,128)S(1)} %get-tuple-element.121), channel_id=1, replica_groups=mesh['gx'=8,'gy'=8,'gz'=2] {'gx'}, dimensions={0} | all-to-all | bytes 196608 | tf_op jit(solution)/shard_map/all_to_all | solution.py:582
  120.2 4.8 %step.6 = (f32[64,32,128]{2,1,0:T(8,128)S(1)}, f32[48,32,128]{2,1,0:T(8,128)S(1)}, f32[48,32,128]{2,1,0:T(8,128)S(1)}, f32[8,6,32,128]{3,2,1,0:T(8,128)S(1)}, f3...) custom-call(f32[64,32,128]{2,1,0:T(8,128)S(1)} %get-tuple-element.109.refs_0_.refs_10_, ...), custom_call_target="tpu_custom_call" | custom-call | tf_op jit(solution)/shard_map/step/pallas_call | solution.py:479
  125.0 2.9 %collective-permute-start.15 = (f32[296,128]{1,0:T(8,128)S(1)}, f32[296,128]{1,0:T(8,128)S(1)}, u32[]{:S(2)}, u32[]{:S(2)}) collective-permute-start(f32[296,128]{1,0:T(8,128)S(1)} %get-tuple-element.123.mine), channel_id=1, source_target_pairs={{0,1},{1,0},{2,3},{3,2},{4,5},{5,4},{6,7},{7,6},{8,9},{9,8},{10,11... | collective-permute-start | bytes 454664 | tf_op jit(solution)/shard_map/ppermute | solution.py:550
  127.8 2.1 %collective-permute-start.18 = (f32[8,6,32,128]{3,2,1,0:T(8,128)S(1)}, f32[8,6,32,128]{3,2,1,0:T(8,128)S(1)}, u32[]{:S(2)}, u32[]{:S(2)}) collective-permute-start(f32[8,6,32,128]{3,2,1,0:T(8,128)S(1)} %get-tuple-element.129), channel_id=1, source_target_pairs={{0,2},{2,4},{4,6},{6,8},{8,10},{10,12},{12,14},{14,0},{1,3},{3,5},... | collective-permute-start | bytes 2359304 | tf_op jit(solution)/shard_map/ppermute | solution.py:550
  131.1 3.0 %collective-permute-start.17 = (f32[48,32,128]{2,1,0:T(8,128)S(1)}, f32[48,32,128]{2,1,0:T(8,128)S(1)}, u32[]{:S(2)}, u32[]{:S(2)}) collective-permute-start(f32[48,32,128]{2,1,0:T(8,128)S(1)} %get-tuple-element.128), channel_id=1, source_target_pairs={{0,112},{16,0},{32,16},{48,32},{64,48},{80,64},{96,80},{112,96},{1... | collective-permute-start | bytes 2359304 | tf_op jit(solution)/shard_map/ppermute | solution.py:550
  134.2 12.3 %all_to_all.51.came = f32[8,24,128]{2,1,0:T(8,128)S(1)} all-to-all(f32[8,24,128]{2,1,0:T(8,128)S(1)} %get-tuple-element.132), channel_id=1, replica_groups=mesh['gx'=8,'gy'=8,'gz'=2] {'gy'}, dimensions={0} | all-to-all | bytes 196608 | tf_op jit(solution)/shard_map/all_to_all | solution.py:580
  146.5 7.7 %all_to_all.52.refs_8_ = f32[8,24,128]{2,1,0:T(8,128)S(1)} all-to-all(f32[8,24,128]{2,1,0:T(8,128)S(1)} %get-tuple-element.134), channel_id=1, replica_groups=mesh['gx'=8,'gy'=8,'gz'=2] {'gx'}, dimensions={0} | all-to-all | bytes 196608 | tf_op jit(solution)/shard_map/all_to_all | solution.py:582
  154.2 4.2 %step.7 = (f32[64,32,128]{2,1,0:T(8,128)S(1)}, f32[8,128]{1,0:T(8,128)S(1)}) custom-call(f32[64,32,128]{2,1,0:T(8,128)S(1)} %get-tuple-element.122.refs_0_, f32[296,128]{1,0:T(8,128)S(1)} %collective-permute-done.15.other.refs_1_, f32[48,32,128]{2,1,0:T(8,128)S(1)} %collective-permute-done.16.refs_2_, f32[48,32,128]{2,1,0:T(8,128)S(1)} %collective-permute-done.17.refs_3_, ...), custom_call_target="tpu_custom_call" | custom-call | tf_op jit(solution)/shard_map/step/pallas_call | solution.py:479
  158.4 20.6 %all_to_all.53.grams = f32[128,8,128]{2,1,0:T(8,128)S(1)} all-to-all(f32[128,8,128]{2,1,0:T(8,128)S(1)} %broadcast_in_dim.2), channel_id=1, replica_groups=mesh['gx'=8,'gy'=8,'gz'=2] {'gx','gy','gz'}, dimensions={0} | all-to-all | bytes 1048576 | tf_op jit(solution)/shard_map/all_to_all | solution.py:596
  179.0 4.7 %finish.1 = f32[32,64,128]{2,1,0:T(8,128)} custom-call(f32[64,32,128]{2,1,0:T(8,128)S(1)} %get-tuple-element.135.field, f32[128,8,128]{2,1,0:T(8,128)S(1)} %all_to_all.53.grams), custom_call_target="tpu_custom_call" | custom-call | tf_op jit(solution)/shard_map/finish/pallas_call | solution.py:533
  (45 shorter events, 5.2 us)
Async XLA Ops:
  12.2 5.8 %copy-start = (f32[64,32,128]{2,1,0:T(8,128)S(1)}, f32[64,32,128]{2,1,0:T(8,128)}, u32[]{:S(2)}) copy-start(f32[64,32,128]{2,1,0:T(8,128)} %get-tuple-element.71.field.refs_0_.refs_10_) | copy-start | bytes 3145732
  12.2 5.8 %copy-start.2 = (f32[8,128]{1,0:T(8,128)S(1)}, f32[8,128]{1,0:T(8,128)}, u32[]{:S(2)}) copy-start(f32[8,128]{1,0:T(8,128)} %get-tuple-element.82.own) | copy-start | bytes 12292
  17.9 34.2 %copy-start.1 = (f32[8,8,128]{2,1,0:T(8,128)S(1)}, f32[8,8,128]{2,1,0:T(8,128)}, u32[]{:S(2)}) copy-start(f32[8,8,128]{2,1,0:T(8,128)} %param.8) | copy-start | bytes 98308
  20.1 8.2 %collective-permute-start = (f32[304,128]{1,0:T(8,128)S(1)}, f32[304,128]{1,0:T(8,128)S(1)}, u32[]{:S(2)}, u32[]{:S(2)}) collective-permute-start(f32[304,128]{1,0:T(8,128)S(1)} %get-tuple-element.83.mine), channel_id=1, source_target_pairs={{0,1},{1,0},{2,3},{3,2},{4,5},{5,4},{6,7},{7,6},{8,9},{9,8},{10,11... | collective-permute-start | bytes 466952 | tf_op jit(solution)/shard_map/ppermute | solution.py:550
  24.6 27.5 %collective-permute-start.3 = (f32[8,6,32,128]{3,2,1,0:T(8,128)S(1)}, f32[8,6,32,128]{3,2,1,0:T(8,128)S(1)}, u32[]{:S(2)}, u32[]{:S(2)}) collective-permute-start(f32[8,6,32,128]{3,2,1,0:T(8,128)S(1)} %get-tuple-element.89), channel_id=1, source_target_pairs={{0,2},{2,4},{4,6},{6,8},{8,10},{10,12},{12,14},{14,0},{1,3},{3,5},... | collective-permute-start | bytes 2359304 | tf_op jit(solution)/shard_map/ppermute | solution.py:550
  26.6 25.5 %collective-permute-start.4 = (f32[8,6,32,128]{3,2,1,0:T(8,128)S(1)}, f32[8,6,32,128]{3,2,1,0:T(8,128)S(1)}, u32[]{:S(2)}, u32[]{:S(2)}) collective-permute-start(f32[8,6,32,128]{3,2,1,0:T(8,128)S(1)} %get-tuple-element.90), channel_id=1, source_target_pairs={{0,14},{2,0},{4,2},{6,4},{8,6},{10,8},{12,10},{14,12},{1,15},{3,1}... | collective-permute-start | bytes 2359304 | tf_op jit(solution)/shard_map/ppermute | solution.py:550
  28.3 23.8 %collective-permute-start.1 = (f32[48,32,128]{2,1,0:T(8,128)S(1)}, f32[48,32,128]{2,1,0:T(8,128)S(1)}, u32[]{:S(2)}, u32[]{:S(2)}) collective-permute-start(f32[48,32,128]{2,1,0:T(8,128)S(1)} %get-tuple-element.87), channel_id=1, source_target_pairs={{0,16},{16,32},{32,48},{48,64},{64,80},{80,96},{96,112},{112,0},{1... | collective-permute-start | bytes 2359304 | tf_op jit(solution)/shard_map/ppermute | solution.py:550
  29.5 22.6 %collective-permute-start.2 = (f32[48,32,128]{2,1,0:T(8,128)S(1)}, f32[48,32,128]{2,1,0:T(8,128)S(1)}, u32[]{:S(2)}, u32[]{:S(2)}) collective-permute-start(f32[48,32,128]{2,1,0:T(8,128)S(1)} %get-tuple-element.88), channel_id=1, source_target_pairs={{0,112},{16,0},{32,16},{48,32},{64,48},{80,64},{96,80},{112,96},{1... | collective-permute-start | bytes 2359304 | tf_op jit(solution)/shard_map/ppermute | solution.py:550
  56.8 5.6 %collective-permute-start.5 = (f32[296,128]{1,0:T(8,128)S(1)}, f32[296,128]{1,0:T(8,128)S(1)}, u32[]{:S(2)}, u32[]{:S(2)}) collective-permute-start(f32[296,128]{1,0:T(8,128)S(1)} %get-tuple-element.96.mine), channel_id=1, source_target_pairs={{0,1},{1,0},{2,3},{3,2},{4,5},{5,4},{6,7},{7,6},{8,9},{9,8},{10,11... | collective-permute-start | bytes 454664 | tf_op jit(solution)/shard_map/ppermute | solution.py:550
  59.8 26.2 %collective-permute-start.8 = (f32[8,6,32,128]{3,2,1,0:T(8,128)S(1)}, f32[8,6,32,128]{3,2,1,0:T(8,128)S(1)}, u32[]{:S(2)}, u32[]{:S(2)}) collective-permute-start(f32[8,6,32,128]{3,2,1,0:T(8,128)S(1)} %get-tuple-element.102), channel_id=1, source_target_pairs={{0,2},{2,4},{4,6},{6,8},{8,10},{10,12},{12,14},{14,0},{1,3},{3,5},... | collective-permute-start | bytes 2359304 | tf_op jit(solution)/shard_map/ppermute | solution.py:550
  62.4 23.6 %collective-permute-start.9 = (f32[8,6,32,128]{3,2,1,0:T(8,128)S(1)}, f32[8,6,32,128]{3,2,1,0:T(8,128)S(1)}, u32[]{:S(2)}, u32[]{:S(2)}) collective-permute-start(f32[8,6,32,128]{3,2,1,0:T(8,128)S(1)} %get-tuple-element.103), channel_id=1, source_target_pairs={{0,14},{2,0},{4,2},{6,4},{8,6},{10,8},{12,10},{14,12},{1,15},{3,1}... | collective-permute-start | bytes 2359304 | tf_op jit(solution)/shard_map/ppermute | solution.py:550
  62.5 23.6 %collective-permute-start.6 = (f32[48,32,128]{2,1,0:T(8,128)S(1)}, f32[48,32,128]{2,1,0:T(8,128)S(1)}, u32[]{:S(2)}, u32[]{:S(2)}) collective-permute-start(f32[48,32,128]{2,1,0:T(8,128)S(1)} %get-tuple-element.100), channel_id=1, source_target_pairs={{0,16},{16,32},{32,48},{48,64},{64,80},{80,96},{96,112},{112,0},{1... | collective-permute-start | bytes 2359304 | tf_op jit(solution)/shard_map/ppermute | solution.py:550
  63.1 22.9 %collective-permute-start.7 = (f32[48,32,128]{2,1,0:T(8,128)S(1)}, f32[48,32,128]{2,1,0:T(8,128)S(1)}, u32[]{:S(2)}, u32[]{:S(2)}) collective-permute-start(f32[48,32,128]{2,1,0:T(8,128)S(1)} %get-tuple-element.101), channel_id=1, source_target_pairs={{0,112},{16,0},{32,16},{48,32},{64,48},{80,64},{96,80},{112,96},{1... | collective-permute-start | bytes 2359304 | tf_op jit(solution)/shard_map/ppermute | solution.py:550
  90.8 5.7 %collective-permute-start.10 = (f32[296,128]{1,0:T(8,128)S(1)}, f32[296,128]{1,0:T(8,128)S(1)}, u32[]{:S(2)}, u32[]{:S(2)}) collective-permute-start(f32[296,128]{1,0:T(8,128)S(1)} %get-tuple-element.110.mine), channel_id=1, source_target_pairs={{0,1},{1,0},{2,3},{3,2},{4,5},{5,4},{6,7},{7,6},{8,9},{9,8},{10,11... | collective-permute-start | bytes 454664 | tf_op jit(solution)/shard_map/ppermute | solution.py:550
  93.8 26.4 %collective-permute-start.13 = (f32[8,6,32,128]{3,2,1,0:T(8,128)S(1)}, f32[8,6,32,128]{3,2,1,0:T(8,128)S(1)}, u32[]{:S(2)}, u32[]{:S(2)}) collective-permute-start(f32[8,6,32,128]{3,2,1,0:T(8,128)S(1)} %get-tuple-element.116), channel_id=1, source_target_pairs={{0,2},{2,4},{4,6},{6,8},{8,10},{10,12},{12,14},{14,0},{1,3},{3,5},... | collective-permute-start | bytes 2359304 | tf_op jit(solution)/shard_map/ppermute | solution.py:550
  96.2 24.0 %collective-permute-start.14 = (f32[8,6,32,128]{3,2,1,0:T(8,128)S(1)}, f32[8,6,32,128]{3,2,1,0:T(8,128)S(1)}, u32[]{:S(2)}, u32[]{:S(2)}) collective-permute-start(f32[8,6,32,128]{3,2,1,0:T(8,128)S(1)} %get-tuple-element.117), channel_id=1, source_target_pairs={{0,14},{2,0},{4,2},{6,4},{8,6},{10,8},{12,10},{14,12},{1,15},{3,1}... | collective-permute-start | bytes 2359304 | tf_op jit(solution)/shard_map/ppermute | solution.py:550
  96.6 23.6 %collective-permute-start.11 = (f32[48,32,128]{2,1,0:T(8,128)S(1)}, f32[48,32,128]{2,1,0:T(8,128)S(1)}, u32[]{:S(2)}, u32[]{:S(2)}) collective-permute-start(f32[48,32,128]{2,1,0:T(8,128)S(1)} %get-tuple-element.114), channel_id=1, source_target_pairs={{0,16},{16,32},{32,48},{48,64},{64,80},{80,96},{96,112},{112,0},{1... | collective-permute-start | bytes 2359304 | tf_op jit(solution)/shard_map/ppermute | solution.py:550
  97.7 22.5 %collective-permute-start.12 = (f32[48,32,128]{2,1,0:T(8,128)S(1)}, f32[48,32,128]{2,1,0:T(8,128)S(1)}, u32[]{:S(2)}, u32[]{:S(2)}) collective-permute-start(f32[48,32,128]{2,1,0:T(8,128)S(1)} %get-tuple-element.115), channel_id=1, source_target_pairs={{0,112},{16,0},{32,16},{48,32},{64,48},{80,64},{96,80},{112,96},{1... | collective-permute-start | bytes 2359304 | tf_op jit(solution)/shard_map/ppermute | solution.py:550
  125.0 5.6 %collective-permute-start.15 = (f32[296,128]{1,0:T(8,128)S(1)}, f32[296,128]{1,0:T(8,128)S(1)}, u32[]{:S(2)}, u32[]{:S(2)}) collective-permute-start(f32[296,128]{1,0:T(8,128)S(1)} %get-tuple-element.123.mine), channel_id=1, source_target_pairs={{0,1},{1,0},{2,3},{3,2},{4,5},{5,4},{6,7},{7,6},{8,9},{9,8},{10,11... | collective-permute-start | bytes 454664 | tf_op jit(solution)/shard_map/ppermute | solution.py:550
  127.8 26.3 %collective-permute-start.18 = (f32[8,6,32,128]{3,2,1,0:T(8,128)S(1)}, f32[8,6,32,128]{3,2,1,0:T(8,128)S(1)}, u32[]{:S(2)}, u32[]{:S(2)}) collective-permute-start(f32[8,6,32,128]{3,2,1,0:T(8,128)S(1)} %get-tuple-element.129), channel_id=1, source_target_pairs={{0,2},{2,4},{4,6},{6,8},{8,10},{10,12},{12,14},{14,0},{1,3},{3,5},... | collective-permute-start | bytes 2359304 | tf_op jit(solution)/shard_map/ppermute | solution.py:550
  129.9 24.2 %collective-permute-start.19 = (f32[8,6,32,128]{3,2,1,0:T(8,128)S(1)}, f32[8,6,32,128]{3,2,1,0:T(8,128)S(1)}, u32[]{:S(2)}, u32[]{:S(2)}) collective-permute-start(f32[8,6,32,128]{3,2,1,0:T(8,128)S(1)} %get-tuple-element.130), channel_id=1, source_target_pairs={{0,14},{2,0},{4,2},{6,4},{8,6},{10,8},{12,10},{14,12},{1,15},{3,1}... | collective-permute-start | bytes 2359304 | tf_op jit(solution)/shard_map/ppermute | solution.py:550
  130.6 23.6 %collective-permute-start.16 = (f32[48,32,128]{2,1,0:T(8,128)S(1)}, f32[48,32,128]{2,1,0:T(8,128)S(1)}, u32[]{:S(2)}, u32[]{:S(2)}) collective-permute-start(f32[48,32,128]{2,1,0:T(8,128)S(1)} %get-tuple-element.127), channel_id=1, source_target_pairs={{0,16},{16,32},{32,48},{48,64},{64,80},{80,96},{96,112},{112,0},{1... | collective-permute-start | bytes 2359304 | tf_op jit(solution)/shard_map/ppermute | solution.py:550
  131.1 23.0 %collective-permute-start.17 = (f32[48,32,128]{2,1,0:T(8,128)S(1)}, f32[48,32,128]{2,1,0:T(8,128)S(1)}, u32[]{:S(2)}, u32[]{:S(2)}) collective-permute-start(f32[48,32,128]{2,1,0:T(8,128)S(1)} %get-tuple-element.128), channel_id=1, source_target_pairs={{0,112},{16,0},{32,16},{48,32},{64,48},{80,64},{96,80},{112,96},{1... | collective-permute-start | bytes 2359304 | tf_op jit(solution)/shard_map/ppermute | solution.py:550

commit v11 on v10

--- a/solution.py
+++ b/solution.py
@@ -38,6 +38,7 @@
 ZROWS = GROUPS * 16
 PACK = 24
 LANES = 128
+LOWER = [(i, j) for i in range(4) for j in range(i + 1)]
 F32 = jnp.float32
 BF16 = jnp.bfloat16
 NN = (((1,), (0,)), ((), ()))
@@ -465,7 +466,10 @@
         t = total[...]
         summed = t[2 * NB :, :NB] + t[:NB, 2 * NB :] + t[NB : 2 * NB, NB : 2 * NB]
         summed = summed + (t[NB : 2 * NB, :NB] + t[:NB, NB : 2 * NB]) + t[:NB, :NB]
-        gram[...] = jnp.concatenate([summed[8 * q : 8 * q + 8] for q in range(4)], axis=1)
+        blocks = [summed[8 * i : 8 * i + 8, 8 * j : 8 * j + 8] for i, j in LOWER]
+        blocks = jnp.concatenate(blocks, axis=1)
+        for r in range(8):
+            gram[:, pl.ds(r * 8 * len(LOWER), 8 * len(LOWER))] = blocks[r : r + 1]
     else:
         message[pl.ds(ZROWS, TGT), :] = packed_partial(total[...])
 
@@ -473,7 +477,7 @@
 def step(first_step, last_step, *arrays):
     total = (3 * NB, 3 * NB) if last_step else TOTAL
     if last_step:
-        outs = [BLOCK, jax.ShapeDtypeStruct((8, LANES), F32)]
+        outs = [BLOCK, jax.ShapeDtypeStruct((1, 64 * len(LOWER)), F32)]
     else:
         outs = [BLOCK, X_FACE, X_FACE, Y_FACE, Y_FACE, MESSAGE] + ([FRAME] if first_step else [])
     return pl.pallas_call(
@@ -497,19 +501,26 @@
     for slot in range(1, grams.shape[0]):
         packed = packed + grams[slot]
     packed = packed * scale
-    gram = jnp.concatenate([packed[:, q * NB : (q + 1) * NB] for q in range(4)], axis=0)
+    width = 8 * len(LOWER)
+    blocks = jnp.concatenate([packed[:, r * width : (r + 1) * width] for r in range(8)], axis=0)
+    lower = []
+    for i in range(4):
+        found = [blocks[:, 8 * b : 8 * b + 8] for b, (k, _) in enumerate(LOWER) if k == i]
+        lower.append(jnp.concatenate(found + [jnp.zeros((8, NB - 8 * i - 8), F32)] * (i < 3), axis=1))
+    lower = jnp.concatenate(lower, axis=0)
     row = lax.broadcasted_iota(jnp.int32, (NB, NB), 0)
     column = lax.broadcasted_iota(jnp.int32, (NB, NB), 1)
+    gram = jnp.where(row // 8 >= column // 8, lower, lower.T)
     eye = jnp.where(row == column, 1.0, 0.0)
     work = jnp.concatenate([gram, eye], axis=1)
     below = lax.broadcasted_iota(jnp.int32, (NB, 2 * NB), 0)
     for k in range(NB):
-        root = lax.rsqrt(work[k : k + 1, k : k + 1])
-        line = work[k : k + 1, :] * root
+        column = jnp.broadcast_to(work[:, k : k + 1], work.shape)
+        root = lax.rsqrt(column[k : k + 1])
+        line = work[k : k + 1] * root
         inverse[pl.ds(k, 1), :] = line[:, NB:]
         if k < NB - 1:
-            factor = work[:, k : k + 1] * root
-            work = work - jnp.where(below > k, factor * line, 0.0)
+            work = work - jnp.where(below > k, column, 0.0) * (line * root)
     hi, mid, lo = split3(inverse[...])
     left = jnp.concatenate([lo, mid, hi, mid, hi, hi], axis=1)
 

time: 185 us -> 183 us (0.989)
    all_to_all x4, blocking collectives: 48.6 us -> 46.3 us  [local(): came = lax.all_to_all(sends, 'gy', 0, 0)]
where the time goes in v11:
time: 183 us
  blocking collectives  98.3 us (54%)
  starting transfers between devices  38.1 us (21%)
  Pallas kernels  35.1 us (19%)
  other arithmetic  7.88 us (4%)
  waiting for transfers between devices  2.19 us (1%)
    all_to_all x4, blocking collectives, local(): came = lax.all_to_all(sends, 'gy', 0, 0)  46.3 us
    ppermute x20, starting transfers between devices, shift(): lax.ppermute(value, axis, [(i, (i + by) % count) for i in range(count)])  38.1 us
    all_to_all x4, blocking collectives, local(): came = lax.all_to_all(sends, 'gx', 0, 0)  31 us
    all_to_all x1, blocking collectives, local(): lax.all_to_all(jnp.broadcast_to(gram[None], (devices,) + gram.shape), axe...  20.9 us
    pallas_call x4, Pallas kernels, step(): pl.pallas_call(functools.partial(step_kernel, first_step, last_step), out...  18.5 us
    sort x1, other arithmetic, local(): lax.sort((key, *[w.reshape(SLOTS) for w in weights]), num_keys=1, is_stab...  6.69 us
    pallas_call x1, Pallas kernels, build(): pl.pallas_call(build_kernel, out_shape=MATRIX, in_specs=[pl.BlockSpec(mem...  5.72 us
    pallas_call x1, Pallas kernels, finish(): pl.pallas_call(functools.partial(finish_kernel, scale), out_shape=jax.Sha...  4.99 us
  transfers between devices with their start and end apart: 20, of which 2 were waited for; matrix products, arithmetic and copies ran while one was open for 0% of the time, Pallas kernels for 0%

profile of v11, /device:TPU:1, one launch (start us, length us, event | category | flops | bytes accessed | tf_op | source)
XLA Modules:
  0.0 183.1 jit_solution(1974771338660256811)
XLA Ops:
  0.7 3.4 %prepare.1 = (f32[64,32,128]{2,1,0:T(8,128)}, s32[64,128]{1,0:T(8,128)}, f32[8,128]{1,0:T(8,128)}, f32[64,128]{1,0:T(8,128)}, f32[64,128]{1,0:T(8,128)}, /*index=5*/f32[64,128]{1,0:T(8,128)}, f32[64,128]{1,0:T(8,128)}) custom-call(s32[1]{0:T(128)} %bitcast.16.count, f32[2,4]{1,0:T(2,128)} %coupling.1, f32[32,64,128]{2,1,0:T(8,128)} %bitcast.21, ...), custom_call_target="tpu_custom_call" | custom-call | tf_op jit(solution)/shard_map/prepare/pallas_call | solution.py:159
  5.2 6.7 %sort.33 = (s32[8192]{0:T(1024)S(1)}, f32[8192]{0:T(1024)S(1)}, f32[8192]{0:T(1024)S(1)}, f32[8192]{0:T(1024)S(1)}, f32[8192]{0:T(1024)S(1)}) sort(s32[8192]{0:T(1024)} %bitcast.23, f32[8192]{0:T(1024)} %bitcast.25, f32[8192]{0:T(1024)} %bitcast.26, f32[8192]{0:T(1024)} %bitcast.27, f32[8192]{0:T(1024)} %bitcast.28), dimensions={0}, to_apply=%region_1.0 | sort | flops 106496 | bytes 327680 | tf_op jit(solution)/shard_map/sort | solution.py:574
  12.2 5.7 %build.1.mat.refs_9_ = bf16[32,320,256]{2,1,0:T(8,128)(2,1)S(1)} custom-call(s32[65]{0:T(128)S(1)} %convert_reduce_fusion.starts, f32[5,8192]{1,0:T(8,128)S(1)} %stack.23.points), custom_call_target="tpu_custom_call" | custom-call | tf_op jit(solution)/shard_map/build/pallas_call | solution.py:227
  17.9 2.1 %first.1 = (f32[304,128]{1,0:T(8,128)S(1)}, f32[48,32,128]{2,1,0:T(8,128)S(1)}, f32[48,32,128]{2,1,0:T(8,128)S(1)}, f32[8,6,32,128]{3,2,1,0:T(8,128)S(1)}, f32[8,6,32,128]{3,2,1,0:T(8,128)S(1)}) custom-call(f32[64,32,128]{2,1,0:T(8,128)S(1)} %copy-done, bf16[32,320,256]{2,1,0:T(8,128)(2,1)S(1)} %build.1.mat.refs_9_, f32[8,128]{1,0:T(8,128)S(1)} %copy-done.2), custom_call_target="tpu_custom_call" | custom-call | tf_op jit(solution)/shard_map/first/pallas_call | solution.py:268
  20.1 4.5 %collective-permute-start = (f32[304,128]{1,0:T(8,128)S(1)}, f32[304,128]{1,0:T(8,128)S(1)}, u32[]{:S(2)}, u32[]{:S(2)}) collective-permute-start(f32[304,128]{1,0:T(8,128)S(1)} %get-tuple-element.83.mine), channel_id=1, source_target_pairs={{0,1},{1,0},{2,3},{3,2},{4,5},{5,4},{6,7},{7,6},{8,9},{9,8},{10,11... | collective-permute-start | bytes 466952 | tf_op jit(solution)/shard_map/ppermute | solution.py:561
  24.6 2.1 %collective-permute-start.3 = (f32[8,6,32,128]{3,2,1,0:T(8,128)S(1)}, f32[8,6,32,128]{3,2,1,0:T(8,128)S(1)}, u32[]{:S(2)}, u32[]{:S(2)}) collective-permute-start(f32[8,6,32,128]{3,2,1,0:T(8,128)S(1)} %get-tuple-element.89), channel_id=1, source_target_pairs={{0,2},{2,4},{4,6},{6,8},{8,10},{10,12},{12,14},{14,0},{1,3},{3,5},... | collective-permute-start | bytes 2359304 | tf_op jit(solution)/shard_map/ppermute | solution.py:561
  26.6 1.7 collective-permute-done.other.refs_1_
  28.3 1.3 collective-permute-start.1
  29.6 2.3 %collective-permute-start.2 = (f32[48,32,128]{2,1,0:T(8,128)S(1)}, f32[48,32,128]{2,1,0:T(8,128)S(1)}, u32[]{:S(2)}, u32[]{:S(2)}) collective-permute-start(f32[48,32,128]{2,1,0:T(8,128)S(1)} %get-tuple-element.88), channel_id=1, source_target_pairs={{0,112},{16,0},{32,16},{48,32},{64,48},{80,64},{96,80},{112,96},{1... | collective-permute-start | bytes 2359304 | tf_op jit(solution)/shard_map/ppermute | solution.py:561
  32.1 11.4 %all_to_all.45.came = f32[8,32,128]{2,1,0:T(8,128)S(1)} all-to-all(f32[8,32,128]{2,1,0:T(8,128)S(1)} %get-tuple-element.92), channel_id=1, replica_groups=mesh['gx'=8,'gy'=8,'gz'=2] {'gy'}, dimensions={0} | all-to-all | bytes 262144 | tf_op jit(solution)/shard_map/all_to_all | solution.py:591
  43.6 7.8 %all_to_all.46.refs_8_ = f32[8,32,128]{2,1,0:T(8,128)S(1)} all-to-all(f32[8,32,128]{2,1,0:T(8,128)S(1)} %get-tuple-element.94), channel_id=1, replica_groups=mesh['gx'=8,'gy'=8,'gz'=2] {'gx'}, dimensions={0} | all-to-all | bytes 262144 | tf_op jit(solution)/shard_map/all_to_all | solution.py:593
  51.5 4.7 %step.4 = (f32[64,32,128]{2,1,0:T(8,128)S(1)}, f32[48,32,128]{2,1,0:T(8,128)S(1)}, f32[48,32,128]{2,1,0:T(8,128)S(1)}, f32[8,6,32,128]{3,2,1,0:T(8,128)S(1)}, f3...) custom-call(f32[64,32,128]{2,1,0:T(8,128)S(1)} %copy-done, ...), custom_call_target="tpu_custom_call" | custom-call | tf_op jit(solution)/shard_map/step/pallas_call | solution.py:483
  56.2 3.4 %collective-permute-start.5 = (f32[296,128]{1,0:T(8,128)S(1)}, f32[296,128]{1,0:T(8,128)S(1)}, u32[]{:S(2)}, u32[]{:S(2)}) collective-permute-start(f32[296,128]{1,0:T(8,128)S(1)} %get-tuple-element.96.mine), channel_id=1, source_target_pairs={{0,1},{1,0},{2,3},{3,2},{4,5},{5,4},{6,7},{7,6},{8,9},{9,8},{10,11... | collective-permute-start | bytes 454664 | tf_op jit(solution)/shard_map/ppermute | solution.py:561
  59.6 2.6 %collective-permute-start.8 = (f32[8,6,32,128]{3,2,1,0:T(8,128)S(1)}, f32[8,6,32,128]{3,2,1,0:T(8,128)S(1)}, u32[]{:S(2)}, u32[]{:S(2)}) collective-permute-start(f32[8,6,32,128]{3,2,1,0:T(8,128)S(1)} %get-tuple-element.102), channel_id=1, source_target_pairs={{0,2},{2,4},{4,6},{6,8},{8,10},{10,12},{12,14},{14,0},{1,3},{3,5},... | collective-permute-start | bytes 2359304 | tf_op jit(solution)/shard_map/ppermute | solution.py:561
  62.9 3.3 %collective-permute-start.7 = (f32[48,32,128]{2,1,0:T(8,128)S(1)}, f32[48,32,128]{2,1,0:T(8,128)S(1)}, u32[]{:S(2)}, u32[]{:S(2)}) collective-permute-start(f32[48,32,128]{2,1,0:T(8,128)S(1)} %get-tuple-element.101), channel_id=1, source_target_pairs={{0,112},{16,0},{32,16},{48,32},{64,48},{80,64},{96,80},{112,96},{1... | collective-permute-start | bytes 2359304 | tf_op jit(solution)/shard_map/ppermute | solution.py:561
  66.3 11.3 %all_to_all.47.came = f32[8,24,128]{2,1,0:T(8,128)S(1)} all-to-all(f32[8,24,128]{2,1,0:T(8,128)S(1)} %get-tuple-element.105), channel_id=1, replica_groups=mesh['gx'=8,'gy'=8,'gz'=2] {'gy'}, dimensions={0} | all-to-all | bytes 196608 | tf_op jit(solution)/shard_map/all_to_all | solution.py:591
  77.6 7.9 %all_to_all.48.refs_8_ = f32[8,24,128]{2,1,0:T(8,128)S(1)} all-to-all(f32[8,24,128]{2,1,0:T(8,128)S(1)} %get-tuple-element.107), channel_id=1, replica_groups=mesh['gx'=8,'gy'=8,'gz'=2] {'gx'}, dimensions={0} | all-to-all | bytes 196608 | tf_op jit(solution)/shard_map/all_to_all | solution.py:593
  85.5 4.8 %step.5 = (f32[64,32,128]{2,1,0:T(8,128)S(1)}, f32[48,32,128]{2,1,0:T(8,128)S(1)}, f32[48,32,128]{2,1,0:T(8,128)S(1)}, f32[8,6,32,128]{3,2,1,0:T(8,128)S(1)}, f3...) custom-call(f32[64,32,128]{2,1,0:T(8,128)S(1)} %get-tuple-element.95.refs_0_.refs_10_, ...), custom_call_target="tpu_custom_call" | custom-call | tf_op jit(solution)/shard_map/step/pallas_call | solution.py:483
  90.3 2.9 %collective-permute-start.10 = (f32[296,128]{1,0:T(8,128)S(1)}, f32[296,128]{1,0:T(8,128)S(1)}, u32[]{:S(2)}, u32[]{:S(2)}) collective-permute-start(f32[296,128]{1,0:T(8,128)S(1)} %get-tuple-element.110.mine), channel_id=1, source_target_pairs={{0,1},{1,0},{2,3},{3,2},{4,5},{5,4},{6,7},{7,6},{8,9},{9,8},{10,11... | collective-permute-start | bytes 454664 | tf_op jit(solution)/shard_map/ppermute | solution.py:561
  93.2 2.7 %collective-permute-start.13 = (f32[8,6,32,128]{3,2,1,0:T(8,128)S(1)}, f32[8,6,32,128]{3,2,1,0:T(8,128)S(1)}, u32[]{:S(2)}, u32[]{:S(2)}) collective-permute-start(f32[8,6,32,128]{3,2,1,0:T(8,128)S(1)} %get-tuple-element.116), channel_id=1, source_target_pairs={{0,2},{2,4},{4,6},{6,8},{8,10},{10,12},{12,14},{14,0},{1,3},{3,5},... | collective-permute-start | bytes 2359304 | tf_op jit(solution)/shard_map/ppermute | solution.py:561
  97.0 2.4 %collective-permute-start.12 = (f32[48,32,128]{2,1,0:T(8,128)S(1)}, f32[48,32,128]{2,1,0:T(8,128)S(1)}, u32[]{:S(2)}, u32[]{:S(2)}) collective-permute-start(f32[48,32,128]{2,1,0:T(8,128)S(1)} %get-tuple-element.115), channel_id=1, source_target_pairs={{0,112},{16,0},{32,16},{48,32},{64,48},{80,64},{96,80},{112,96},{1... | collective-permute-start | bytes 2359304 | tf_op jit(solution)/shard_map/ppermute | solution.py:561
  99.5 12.3 %all_to_all.49.came = f32[8,24,128]{2,1,0:T(8,128)S(1)} all-to-all(f32[8,24,128]{2,1,0:T(8,128)S(1)} %get-tuple-element.119), channel_id=1, replica_groups=mesh['gx'=8,'gy'=8,'gz'=2] {'gy'}, dimensions={0} | all-to-all | bytes 196608 | tf_op jit(solution)/shard_map/all_to_all | solution.py:591
  111.8 7.7 %all_to_all.50.refs_8_ = f32[8,24,128]{2,1,0:T(8,128)S(1)} all-to-all(f32[8,24,128]{2,1,0:T(8,128)S(1)} %get-tuple-element.121), channel_id=1, replica_groups=mesh['gx'=8,'gy'=8,'gz'=2] {'gx'}, dimensions={0} | all-to-all | bytes 196608 | tf_op jit(solution)/shard_map/all_to_all | solution.py:593
  119.5 4.8 %step.6 = (f32[64,32,128]{2,1,0:T(8,128)S(1)}, f32[48,32,128]{2,1,0:T(8,128)S(1)}, f32[48,32,128]{2,1,0:T(8,128)S(1)}, f32[8,6,32,128]{3,2,1,0:T(8,128)S(1)}, f3...) custom-call(f32[64,32,128]{2,1,0:T(8,128)S(1)} %get-tuple-element.109.refs_0_.refs_10_, ...), custom_call_target="tpu_custom_call" | custom-call | tf_op jit(solution)/shard_map/step/pallas_call | solution.py:483
  124.3 3.0 %collective-permute-start.15 = (f32[296,128]{1,0:T(8,128)S(1)}, f32[296,128]{1,0:T(8,128)S(1)}, u32[]{:S(2)}, u32[]{:S(2)}) collective-permute-start(f32[296,128]{1,0:T(8,128)S(1)} %get-tuple-element.123.mine), channel_id=1, source_target_pairs={{0,1},{1,0},{2,3},{3,2},{4,5},{5,4},{6,7},{7,6},{8,9},{9,8},{10,11... | collective-permute-start | bytes 454664 | tf_op jit(solution)/shard_map/ppermute | solution.py:561
  127.3 2.2 %collective-permute-start.18 = (f32[8,6,32,128]{3,2,1,0:T(8,128)S(1)}, f32[8,6,32,128]{3,2,1,0:T(8,128)S(1)}, u32[]{:S(2)}, u32[]{:S(2)}) collective-permute-start(f32[8,6,32,128]{3,2,1,0:T(8,128)S(1)} %get-tuple-element.129), channel_id=1, source_target_pairs={{0,2},{2,4},{4,6},{6,8},{8,10},{10,12},{12,14},{14,0},{1,3},{3,5},... | collective-permute-start | bytes 2359304 | tf_op jit(solution)/shard_map/ppermute | solution.py:561
  130.5 3.0 %collective-permute-start.17 = (f32[48,32,128]{2,1,0:T(8,128)S(1)}, f32[48,32,128]{2,1,0:T(8,128)S(1)}, u32[]{:S(2)}, u32[]{:S(2)}) collective-permute-start(f32[48,32,128]{2,1,0:T(8,128)S(1)} %get-tuple-element.128), channel_id=1, source_target_pairs={{0,112},{16,0},{32,16},{48,32},{64,48},{80,64},{96,80},{112,96},{1... | collective-permute-start | bytes 2359304 | tf_op jit(solution)/shard_map/ppermute | solution.py:561
  133.5 11.3 %all_to_all.51.came = f32[8,24,128]{2,1,0:T(8,128)S(1)} all-to-all(f32[8,24,128]{2,1,0:T(8,128)S(1)} %get-tuple-element.132), channel_id=1, replica_groups=mesh['gx'=8,'gy'=8,'gz'=2] {'gy'}, dimensions={0} | all-to-all | bytes 196608 | tf_op jit(solution)/shard_map/all_to_all | solution.py:591
  144.9 7.7 %all_to_all.52.refs_8_ = f32[8,24,128]{2,1,0:T(8,128)S(1)} all-to-all(f32[8,24,128]{2,1,0:T(8,128)S(1)} %get-tuple-element.134), channel_id=1, replica_groups=mesh['gx'=8,'gy'=8,'gz'=2] {'gx'}, dimensions={0} | all-to-all | bytes 196608 | tf_op jit(solution)/shard_map/all_to_all | solution.py:593
  152.6 4.2 %step.7 = (f32[64,32,128]{2,1,0:T(8,128)S(1)}, f32[1,640]{1,0:T(1,128)S(1)}) custom-call(f32[64,32,128]{2,1,0:T(8,128)S(1)} %get-tuple-element.122.refs_0_, f32[296,128]{1,0:T(8,128)S(1)} %collective-permute-done.15.other.refs_1_, f32[48,32,128]{2,1,0:T(8,128)S(1)} %collective-permute-done.16.refs_2_, f32[48,32,128]{2,1,0:T(8,128)S(1)} %collective-permute-done.17.refs_3_, ...), custom_call_target="tpu_custom_call" | custom-call | tf_op jit(solution)/shard_map/step/pallas_call | solution.py:483
  157.0 20.9 %all_to_all.53.grams = f32[128,1,640]{2,1,0:T(1,128)S(1)} all-to-all(f32[128,1,640]{2,1,0:T(1,128)S(1)} %broadcast_in_dim.10), channel_id=1, replica_groups=mesh['gx'=8,'gy'=8,'gz'=2] {'gx','gy','gz'}, dimensions={0} | all-to-all | bytes 655360 | tf_op jit(solution)/shard_map/all_to_all | solution.py:607
  177.9 5.0 %finish.1 = f32[32,64,128]{2,1,0:T(8,128)} custom-call(f32[64,32,128]{2,1,0:T(8,128)S(1)} %get-tuple-element.135.field, f32[128,1,640]{2,1,0:T(1,128)S(1)} %all_to_all.53.grams), custom_call_target="tpu_custom_call" | custom-call | tf_op jit(solution)/shard_map/finish/pallas_call | solution.py:544
  (46 shorter events, 4.9 us)
Async XLA Ops:
  12.2 5.8 %copy-start = (f32[64,32,128]{2,1,0:T(8,128)S(1)}, f32[64,32,128]{2,1,0:T(8,128)}, u32[]{:S(2)}) copy-start(f32[64,32,128]{2,1,0:T(8,128)} %get-tuple-element.71.field.refs_0_.refs_10_) | copy-start | bytes 3145732
  12.2 5.8 %copy-start.2 = (f32[8,128]{1,0:T(8,128)S(1)}, f32[8,128]{1,0:T(8,128)}, u32[]{:S(2)}) copy-start(f32[8,128]{1,0:T(8,128)} %get-tuple-element.82.own) | copy-start | bytes 12292
  17.9 33.5 %copy-start.1 = (f32[8,8,128]{2,1,0:T(8,128)S(1)}, f32[8,8,128]{2,1,0:T(8,128)}, u32[]{:S(2)}) copy-start(f32[8,8,128]{2,1,0:T(8,128)} %param.8) | copy-start | bytes 98308
  20.1 8.3 %collective-permute-start = (f32[304,128]{1,0:T(8,128)S(1)}, f32[304,128]{1,0:T(8,128)S(1)}, u32[]{:S(2)}, u32[]{:S(2)}) collective-permute-start(f32[304,128]{1,0:T(8,128)S(1)} %get-tuple-element.83.mine), channel_id=1, source_target_pairs={{0,1},{1,0},{2,3},{3,2},{4,5},{5,4},{6,7},{7,6},{8,9},{9,8},{10,11... | collective-permute-start | bytes 466952 | tf_op jit(solution)/shard_map/ppermute | solution.py:561
  24.6 26.8 %collective-permute-start.3 = (f32[8,6,32,128]{3,2,1,0:T(8,128)S(1)}, f32[8,6,32,128]{3,2,1,0:T(8,128)S(1)}, u32[]{:S(2)}, u32[]{:S(2)}) collective-permute-start(f32[8,6,32,128]{3,2,1,0:T(8,128)S(1)} %get-tuple-element.89), channel_id=1, source_target_pairs={{0,2},{2,4},{4,6},{6,8},{8,10},{10,12},{12,14},{14,0},{1,3},{3,5},... | collective-permute-start | bytes 2359304 | tf_op jit(solution)/shard_map/ppermute | solution.py:561
  26.6 24.8 %collective-permute-start.4 = (f32[8,6,32,128]{3,2,1,0:T(8,128)S(1)}, f32[8,6,32,128]{3,2,1,0:T(8,128)S(1)}, u32[]{:S(2)}, u32[]{:S(2)}) collective-permute-start(f32[8,6,32,128]{3,2,1,0:T(8,128)S(1)} %get-tuple-element.90), channel_id=1, source_target_pairs={{0,14},{2,0},{4,2},{6,4},{8,6},{10,8},{12,10},{14,12},{1,15},{3,1}... | collective-permute-start | bytes 2359304 | tf_op jit(solution)/shard_map/ppermute | solution.py:561
  28.3 23.1 %collective-permute-start.1 = (f32[48,32,128]{2,1,0:T(8,128)S(1)}, f32[48,32,128]{2,1,0:T(8,128)S(1)}, u32[]{:S(2)}, u32[]{:S(2)}) collective-permute-start(f32[48,32,128]{2,1,0:T(8,128)S(1)} %get-tuple-element.87), channel_id=1, source_target_pairs={{0,16},{16,32},{32,48},{48,64},{64,80},{80,96},{96,112},{112,0},{1... | collective-permute-start | bytes 2359304 | tf_op jit(solution)/shard_map/ppermute | solution.py:561
  29.6 21.8 %collective-permute-start.2 = (f32[48,32,128]{2,1,0:T(8,128)S(1)}, f32[48,32,128]{2,1,0:T(8,128)S(1)}, u32[]{:S(2)}, u32[]{:S(2)}) collective-permute-start(f32[48,32,128]{2,1,0:T(8,128)S(1)} %get-tuple-element.88), channel_id=1, source_target_pairs={{0,112},{16,0},{32,16},{48,32},{64,48},{80,64},{96,80},{112,96},{1... | collective-permute-start | bytes 2359304 | tf_op jit(solution)/shard_map/ppermute | solution.py:561
  56.2 6.0 %collective-permute-start.5 = (f32[296,128]{1,0:T(8,128)S(1)}, f32[296,128]{1,0:T(8,128)S(1)}, u32[]{:S(2)}, u32[]{:S(2)}) collective-permute-start(f32[296,128]{1,0:T(8,128)S(1)} %get-tuple-element.96.mine), channel_id=1, source_target_pairs={{0,1},{1,0},{2,3},{3,2},{4,5},{5,4},{6,7},{7,6},{8,9},{9,8},{10,11... | collective-permute-start | bytes 454664 | tf_op jit(solution)/shard_map/ppermute | solution.py:561
  59.6 25.9 %collective-permute-start.8 = (f32[8,6,32,128]{3,2,1,0:T(8,128)S(1)}, f32[8,6,32,128]{3,2,1,0:T(8,128)S(1)}, u32[]{:S(2)}, u32[]{:S(2)}) collective-permute-start(f32[8,6,32,128]{3,2,1,0:T(8,128)S(1)} %get-tuple-element.102), channel_id=1, source_target_pairs={{0,2},{2,4},{4,6},{6,8},{8,10},{10,12},{12,14},{14,0},{1,3},{3,5},... | collective-permute-start | bytes 2359304 | tf_op jit(solution)/shard_map/ppermute | solution.py:561
  62.2 23.3 %collective-permute-start.9 = (f32[8,6,32,128]{3,2,1,0:T(8,128)S(1)}, f32[8,6,32,128]{3,2,1,0:T(8,128)S(1)}, u32[]{:S(2)}, u32[]{:S(2)}) collective-permute-start(f32[8,6,32,128]{3,2,1,0:T(8,128)S(1)} %get-tuple-element.103), channel_id=1, source_target_pairs={{0,14},{2,0},{4,2},{6,4},{8,6},{10,8},{12,10},{14,12},{1,15},{3,1}... | collective-permute-start | bytes 2359304 | tf_op jit(solution)/shard_map/ppermute | solution.py:561
  62.2 23.3 %collective-permute-start.6 = (f32[48,32,128]{2,1,0:T(8,128)S(1)}, f32[48,32,128]{2,1,0:T(8,128)S(1)}, u32[]{:S(2)}, u32[]{:S(2)}) collective-permute-start(f32[48,32,128]{2,1,0:T(8,128)S(1)} %get-tuple-element.100), channel_id=1, source_target_pairs={{0,16},{16,32},{32,48},{48,64},{64,80},{80,96},{96,112},{112,0},{1... | collective-permute-start | bytes 2359304 | tf_op jit(solution)/shard_map/ppermute | solution.py:561
  62.9 22.6 %collective-permute-start.7 = (f32[48,32,128]{2,1,0:T(8,128)S(1)}, f32[48,32,128]{2,1,0:T(8,128)S(1)}, u32[]{:S(2)}, u32[]{:S(2)}) collective-permute-start(f32[48,32,128]{2,1,0:T(8,128)S(1)} %get-tuple-element.101), channel_id=1, source_target_pairs={{0,112},{16,0},{32,16},{48,32},{64,48},{80,64},{96,80},{112,96},{1... | collective-permute-start | bytes 2359304 | tf_op jit(solution)/shard_map/ppermute | solution.py:561
  90.3 5.6 %collective-permute-start.10 = (f32[296,128]{1,0:T(8,128)S(1)}, f32[296,128]{1,0:T(8,128)S(1)}, u32[]{:S(2)}, u32[]{:S(2)}) collective-permute-start(f32[296,128]{1,0:T(8,128)S(1)} %get-tuple-element.110.mine), channel_id=1, source_target_pairs={{0,1},{1,0},{2,3},{3,2},{4,5},{5,4},{6,7},{7,6},{8,9},{9,8},{10,11... | collective-permute-start | bytes 454664 | tf_op jit(solution)/shard_map/ppermute | solution.py:561
  93.2 26.3 %collective-permute-start.13 = (f32[8,6,32,128]{3,2,1,0:T(8,128)S(1)}, f32[8,6,32,128]{3,2,1,0:T(8,128)S(1)}, u32[]{:S(2)}, u32[]{:S(2)}) collective-permute-start(f32[8,6,32,128]{3,2,1,0:T(8,128)S(1)} %get-tuple-element.116), channel_id=1, source_target_pairs={{0,2},{2,4},{4,6},{6,8},{8,10},{10,12},{12,14},{14,0},{1,3},{3,5},... | collective-permute-start | bytes 2359304 | tf_op jit(solution)/shard_map/ppermute | solution.py:561
  95.9 23.6 %collective-permute-start.14 = (f32[8,6,32,128]{3,2,1,0:T(8,128)S(1)}, f32[8,6,32,128]{3,2,1,0:T(8,128)S(1)}, u32[]{:S(2)}, u32[]{:S(2)}) collective-permute-start(f32[8,6,32,128]{3,2,1,0:T(8,128)S(1)} %get-tuple-element.117), channel_id=1, source_target_pairs={{0,14},{2,0},{4,2},{6,4},{8,6},{10,8},{12,10},{14,12},{1,15},{3,1}... | collective-permute-start | bytes 2359304 | tf_op jit(solution)/shard_map/ppermute | solution.py:561
  95.9 23.6 %collective-permute-start.11 = (f32[48,32,128]{2,1,0:T(8,128)S(1)}, f32[48,32,128]{2,1,0:T(8,128)S(1)}, u32[]{:S(2)}, u32[]{:S(2)}) collective-permute-start(f32[48,32,128]{2,1,0:T(8,128)S(1)} %get-tuple-element.114), channel_id=1, source_target_pairs={{0,16},{16,32},{32,48},{48,64},{64,80},{80,96},{96,112},{112,0},{1... | collective-permute-start | bytes 2359304 | tf_op jit(solution)/shard_map/ppermute | solution.py:561
  97.0 22.5 %collective-permute-start.12 = (f32[48,32,128]{2,1,0:T(8,128)S(1)}, f32[48,32,128]{2,1,0:T(8,128)S(1)}, u32[]{:S(2)}, u32[]{:S(2)}) collective-permute-start(f32[48,32,128]{2,1,0:T(8,128)S(1)} %get-tuple-element.115), channel_id=1, source_target_pairs={{0,112},{16,0},{32,16},{48,32},{64,48},{80,64},{96,80},{112,96},{1... | collective-permute-start | bytes 2359304 | tf_op jit(solution)/shard_map/ppermute | solution.py:561
  124.3 5.6 %collective-permute-start.15 = (f32[296,128]{1,0:T(8,128)S(1)}, f32[296,128]{1,0:T(8,128)S(1)}, u32[]{:S(2)}, u32[]{:S(2)}) collective-permute-start(f32[296,128]{1,0:T(8,128)S(1)} %get-tuple-element.123.mine), channel_id=1, source_target_pairs={{0,1},{1,0},{2,3},{3,2},{4,5},{5,4},{6,7},{7,6},{8,9},{9,8},{10,11... | collective-permute-start | bytes 454664 | tf_op jit(solution)/shard_map/ppermute | solution.py:561
  127.3 25.3 %collective-permute-start.18 = (f32[8,6,32,128]{3,2,1,0:T(8,128)S(1)}, f32[8,6,32,128]{3,2,1,0:T(8,128)S(1)}, u32[]{:S(2)}, u32[]{:S(2)}) collective-permute-start(f32[8,6,32,128]{3,2,1,0:T(8,128)S(1)} %get-tuple-element.129), channel_id=1, source_target_pairs={{0,2},{2,4},{4,6},{6,8},{8,10},{10,12},{12,14},{14,0},{1,3},{3,5},... | collective-permute-start | bytes 2359304 | tf_op jit(solution)/shard_map/ppermute | solution.py:561
  129.5 23.0 %collective-permute-start.19 = (f32[8,6,32,128]{3,2,1,0:T(8,128)S(1)}, f32[8,6,32,128]{3,2,1,0:T(8,128)S(1)}, u32[]{:S(2)}, u32[]{:S(2)}) collective-permute-start(f32[8,6,32,128]{3,2,1,0:T(8,128)S(1)} %get-tuple-element.130), channel_id=1, source_target_pairs={{0,14},{2,0},{4,2},{6,4},{8,6},{10,8},{12,10},{14,12},{1,15},{3,1}... | collective-permute-start | bytes 2359304 | tf_op jit(solution)/shard_map/ppermute | solution.py:561
  129.9 22.6 %collective-permute-start.16 = (f32[48,32,128]{2,1,0:T(8,128)S(1)}, f32[48,32,128]{2,1,0:T(8,128)S(1)}, u32[]{:S(2)}, u32[]{:S(2)}) collective-permute-start(f32[48,32,128]{2,1,0:T(8,128)S(1)} %get-tuple-element.127), channel_id=1, source_target_pairs={{0,16},{16,32},{32,48},{48,64},{64,80},{80,96},{96,112},{112,0},{1... | collective-permute-start | bytes 2359304 | tf_op jit(solution)/shard_map/ppermute | solution.py:561
  130.5 22.1 %collective-permute-start.17 = (f32[48,32,128]{2,1,0:T(8,128)S(1)}, f32[48,32,128]{2,1,0:T(8,128)S(1)}, u32[]{:S(2)}, u32[]{:S(2)}) collective-permute-start(f32[48,32,128]{2,1,0:T(8,128)S(1)} %get-tuple-element.128), channel_id=1, source_target_pairs={{0,112},{16,0},{32,16},{48,32},{64,48},{80,64},{96,80},{112,96},{1... | collective-permute-start | bytes 2359304 | tf_op jit(solution)/shard_map/ppermute | solution.py:561

commit v12 on v11

--- a/solution.py
+++ b/solution.py
@@ -35,7 +35,8 @@
 GROUPS = ROWS // 4
 TOTAL = (NB, CH)
 BATCH = 16
-ZROWS = GROUPS * 16
+EDGE = 2 * REACH
+ZROWS = GROUPS * EDGE
 PACK = 24
 LANES = 128
 LOWER = [(i, j) for i in range(4) for j in range(i + 1)]
@@ -74,12 +75,14 @@
     source = lax.broadcasted_iota(jnp.int32, (SZ, SZ), 0)
     z = lax.broadcasted_iota(jnp.int32, (SZ, SZ), 1)
     inner_hi, inner_lo = split2(band(source - z))
-    e = lax.broadcasted_iota(jnp.int32, (16, SZ), 0)
-    z = lax.broadcasted_iota(jnp.int32, (16, SZ), 1)
-    face_hi, face_lo = split2(band(jnp.where(e < 8, SZ + e - z, z + 16 - e)))
+    e = lax.broadcasted_iota(jnp.int32, (EDGE, SZ), 0)
+    z = lax.broadcasted_iota(jnp.int32, (EDGE, SZ), 1)
+    face = band(jnp.where(e < REACH, SZ + e - z, z + EDGE - e))
+    face_hi = face.astype(BF16).astype(F32)
     first[...] = jnp.concatenate([inner_hi, inner_hi], axis=0)
-    unused = jnp.zeros((SZ - 48, SZ), BF16)
-    second[...] = jnp.concatenate([inner_lo, face_hi, face_hi, face_lo, unused], axis=0)
+    unused = jnp.zeros((SZ - 3 * EDGE, SZ), F32)
+    sides = jnp.concatenate([face_hi, face_hi, face - face_hi, unused], axis=0).astype(BF16)
+    second[...] = jnp.concatenate([inner_lo, sides], axis=0)
 
 
 def any_specs(count):
@@ -95,7 +98,7 @@
 
 def z_faces(rows):
     turned = jnp.concatenate(rows, axis=0).T
-    return jnp.concatenate([turned[:8], turned[SZ - 8 :]], axis=0)
+    return jnp.concatenate([turned[:REACH], turned[SZ - REACH :]], axis=0)
 
 
 BLOCK = jax.ShapeDtypeStruct((ROWS, NB, SZ), F32)
@@ -212,14 +215,15 @@
 
             @pl.when(windows > 1)
             def _():
+                at = (step * (BATCH // 2) + i // 2, slice(None), pl.ds((i % 2) * SZ, SZ))
+                both = out[at].astype(F32)
                 total = lax.fori_loop(
-                    0,
+                    1,
                     windows,
                     lambda k, acc: acc + window(row, bases[i] + 2 * k),
-                    jnp.zeros((CH, SZ), F32),
+                    both[:CH] + both[CH:],
                 )
                 hi, lo = split2(total)
-                at = (step * (BATCH // 2) + i // 2, slice(None), pl.ds((i % 2) * SZ, SZ))
                 out[at] = jnp.concatenate([hi, lo], axis=0)
 
 
@@ -251,7 +255,7 @@
 
 def first_kernel(field, mat, own, out, x_low, x_high, y_low, y_high, total):
     for g in range(GROUPS):
-        out[pl.ds(16 * g, 16), :] = z_faces([field[4 * g + i] for i in range(4)])
+        out[pl.ds(EDGE * g, EDGE), :] = z_faces([field[4 * g + i] for i in range(4)])
     for x in range(SX):
         rows = [field[x * SY + y] for y in range(SY)]
         write_x_faces(x, rows, x_low, x_high)
@@ -403,10 +407,10 @@
     for g in range(GROUPS):
         rows = [field[4 * g + i] for i in range(4)]
         hi, lo = split2(jnp.concatenate(rows, axis=0))
-        face = faces[pl.ds(g * 16, 16), :]
+        face = faces[pl.ds(g * EDGE, EDGE), :]
         face_hi = face.astype(BF16).astype(F32)
         side = jnp.concatenate(
-            [face_hi, face - face_hi, face_hi, jnp.zeros((LANES - 48, LANES), F32)], axis=0
+            [face_hi, face - face_hi, face_hi, jnp.zeros((LANES - 3 * EDGE, LANES), F32)], axis=0
         ).T.astype(BF16)
         along_z = dot(jnp.concatenate([hi, lo], axis=1), first_z[...]) + dot(
             jnp.concatenate([hi, side], axis=1), second_z[...]
@@ -460,7 +464,7 @@
         total[...] = acc
         if not last_step:
             for part in range(2):
-                message[pl.ds((2 * x + part) * 16, 16), :] = z_faces(rows[4 * part : 4 * part + 4])
+                message[pl.ds((2 * x + part) * EDGE, EDGE), :] = z_faces(rows[4 * part : 4 * part + 4])
 
     if last_step:
         t = total[...]
@@ -514,13 +518,20 @@
     eye = jnp.where(row == column, 1.0, 0.0)
     work = jnp.concatenate([gram, eye], axis=1)
     below = lax.broadcasted_iota(jnp.int32, (NB, 2 * NB), 0)
-    for k in range(NB):
-        column = jnp.broadcast_to(work[:, k : k + 1], work.shape)
-        root = lax.rsqrt(column[k : k + 1])
+    for k in range(0, NB, 2):
+        left = jnp.broadcast_to(work[:, k : k + 1], work.shape)
+        right = jnp.broadcast_to(work[:, k + 1 : k + 2], work.shape)
+        root = lax.rsqrt(left[k : k + 1])
+        beside = left[k + 1 : k + 2] * root
+        next_root = lax.rsqrt(right[k + 1 : k + 2] - beside * beside)
         line = work[k : k + 1] * root
+        next_line = (work[k + 1 : k + 2] - beside * line) * next_root
         inverse[pl.ds(k, 1), :] = line[:, NB:]
-        if k < NB - 1:
-            work = work - jnp.where(below > k, column, 0.0) * (line * root)
+        inverse[pl.ds(k + 1, 1), :] = next_line[:, NB:]
+        if k < NB - 2:
+            factor = left * root
+            next_factor = (right - factor * beside) * next_root
+            work = work - jnp.where(below > k + 1, factor * line + next_factor * next_line, 0.0)
     hi, mid, lo = split3(inverse[...])
     left = jnp.concatenate([lo, mid, hi, mid, hi, hi], axis=1)
 

time: 183 us -> 181 us (0.989)
  no operation moved by 1% of the time
where the time goes in v12:
time: 181 us; the launch traced here: 180 us
  blocking collectives  97.7 us (54%)
  starting transfers between devices  37.5 us (21%)
  Pallas kernels  33.8 us (19%)
  other arithmetic  7.88 us (4%)
    all_to_all x4, blocking collectives, local(): came = lax.all_to_all(sends, 'gy', 0, 0)  46.2 us
    ppermute x20, starting transfers between devices, shift(): lax.ppermute(value, axis, [(i, (i + by) % count) for i in range(count)])  37.5 us
    all_to_all x4, blocking collectives, local(): came = lax.all_to_all(sends, 'gx', 0, 0)  31.1 us
    all_to_all x1, blocking collectives, local(): lax.all_to_all(jnp.broadcast_to(gram[None], (devices,) + gram.shape), axe...  20.5 us
    pallas_call x4, Pallas kernels, step(): pl.pallas_call(functools.partial(step_kernel, first_step, last_step), out...  18.4 us
    sort x1, other arithmetic, local(): lax.sort((key, *[w.reshape(SLOTS) for w in weights]), num_keys=1, is_stab...  6.69 us
    pallas_call x1, Pallas kernels, build(): pl.pallas_call(build_kernel, out_shape=MATRIX, in_specs=[pl.BlockSpec(mem...  5.69 us
    pallas_call x1, Pallas kernels, finish(): pl.pallas_call(functools.partial(finish_kernel, scale), out_shape=jax.Sha...  3.84 us
  transfers between devices with their start and end apart: 20, of which 2 were waited for; matrix products, arithmetic and copies ran while one was open for 0% of the time, Pallas kernels for 0%

profile of v12, /device:TPU:1, one launch (start us, length us, event | category | flops | bytes accessed | tf_op | source)
XLA Modules:
  0.0 179.5 jit_solution(9579943895520403194)
XLA Ops:
  0.7 3.4 %prepare.1 = (f32[64,32,128]{2,1,0:T(8,128)}, s32[64,128]{1,0:T(8,128)}, f32[8,128]{1,0:T(8,128)}, f32[64,128]{1,0:T(8,128)}, f32[64,128]{1,0:T(8,128)}, /*index=5*/f32[64,128]{1,0:T(8,128)}, f32[64,128]{1,0:T(8,128)}) custom-call(s32[1]{0:T(128)} %bitcast.16.count, f32[2,4]{1,0:T(2,128)} %coupling.1, f32[32,64,128]{2,1,0:T(8,128)} %bitcast.21, ...), custom_call_target="tpu_custom_call" | custom-call | tf_op jit(solution)/shard_map/prepare/pallas_call | solution.py:162
  4.0 1.2 convert_reduce_fusion.starts
  5.2 6.7 %sort.33 = (s32[8192]{0:T(1024)S(1)}, f32[8192]{0:T(1024)S(1)}, f32[8192]{0:T(1024)S(1)}, f32[8192]{0:T(1024)S(1)}, f32[8192]{0:T(1024)S(1)}) sort(s32[8192]{0:T(1024)} %bitcast.23, f32[8192]{0:T(1024)} %bitcast.25, f32[8192]{0:T(1024)} %bitcast.26, f32[8192]{0:T(1024)} %bitcast.27, f32[8192]{0:T(1024)} %bitcast.28), dimensions={0}, to_apply=%region_1.0 | sort | flops 106496 | bytes 327680 | tf_op jit(solution)/shard_map/sort | solution.py:585
  12.2 5.7 %build.1.mat.refs_9_ = bf16[32,320,256]{2,1,0:T(8,128)(2,1)S(1)} custom-call(s32[65]{0:T(128)S(1)} %convert_reduce_fusion.starts, f32[5,8192]{1,0:T(8,128)S(1)} %stack.23.points), custom_call_target="tpu_custom_call" | custom-call | tf_op jit(solution)/shard_map/build/pallas_call | solution.py:231
  17.9 2.1 %first.1 = (f32[240,128]{1,0:T(8,128)S(1)}, f32[48,32,128]{2,1,0:T(8,128)S(1)}, f32[48,32,128]{2,1,0:T(8,128)S(1)}, f32[8,6,32,128]{3,2,1,0:T(8,128)S(1)}, f32[8,6,32,128]{3,2,1,0:T(8,128)S(1)}) custom-call(f32[64,32,128]{2,1,0:T(8,128)S(1)} %copy-done, bf16[32,320,256]{2,1,0:T(8,128)(2,1)S(1)} %build.1.mat.refs_9_, f32[8,128]{1,0:T(8,128)S(1)} %copy-done.2), custom_call_target="tpu_custom_call" | custom-call | tf_op jit(solution)/shard_map/first/pallas_call | solution.py:272
  20.0 4.5 %collective-permute-start = (f32[240,128]{1,0:T(8,128)S(1)}, f32[240,128]{1,0:T(8,128)S(1)}, u32[]{:S(2)}, u32[]{:S(2)}) collective-permute-start(f32[240,128]{1,0:T(8,128)S(1)} %get-tuple-element.83.mine), channel_id=1, source_target_pairs={{0,1},{1,0},{2,3},{3,2},{4,5},{5,4},{6,7},{7,6},{8,9},{9,8},{10,11... | collective-permute-start | bytes 368648 | tf_op jit(solution)/shard_map/ppermute | solution.py:572
  24.6 2.1 %collective-permute-start.3 = (f32[8,6,32,128]{3,2,1,0:T(8,128)S(1)}, f32[8,6,32,128]{3,2,1,0:T(8,128)S(1)}, u32[]{:S(2)}, u32[]{:S(2)}) collective-permute-start(f32[8,6,32,128]{3,2,1,0:T(8,128)S(1)} %get-tuple-element.89), channel_id=1, source_target_pairs={{0,2},{2,4},{4,6},{6,8},{8,10},{10,12},{12,14},{14,0},{1,3},{3,5},... | collective-permute-start | bytes 2359304 | tf_op jit(solution)/shard_map/ppermute | solution.py:572
  27.6 1.6 collective-permute-start.1
  29.2 1.9 %collective-permute-start.2 = (f32[48,32,128]{2,1,0:T(8,128)S(1)}, f32[48,32,128]{2,1,0:T(8,128)S(1)}, u32[]{:S(2)}, u32[]{:S(2)}) collective-permute-start(f32[48,32,128]{2,1,0:T(8,128)S(1)} %get-tuple-element.88), channel_id=1, source_target_pairs={{0,112},{16,0},{32,16},{48,32},{64,48},{80,64},{96,80},{112,96},{1... | collective-permute-start | bytes 2359304 | tf_op jit(solution)/shard_map/ppermute | solution.py:572
  31.3 11.4 %all_to_all.45.came = f32[8,32,128]{2,1,0:T(8,128)S(1)} all-to-all(f32[8,32,128]{2,1,0:T(8,128)S(1)} %get-tuple-element.92), channel_id=1, replica_groups=mesh['gx'=8,'gy'=8,'gz'=2] {'gy'}, dimensions={0} | all-to-all | bytes 262144 | tf_op jit(solution)/shard_map/all_to_all | solution.py:602
  42.9 7.9 %all_to_all.46.refs_8_ = f32[8,32,128]{2,1,0:T(8,128)S(1)} all-to-all(f32[8,32,128]{2,1,0:T(8,128)S(1)} %get-tuple-element.94), channel_id=1, replica_groups=mesh['gx'=8,'gy'=8,'gz'=2] {'gx'}, dimensions={0} | all-to-all | bytes 262144 | tf_op jit(solution)/shard_map/all_to_all | solution.py:604
  50.8 4.7 %step.4 = (f32[64,32,128]{2,1,0:T(8,128)S(1)}, f32[48,32,128]{2,1,0:T(8,128)S(1)}, f32[48,32,128]{2,1,0:T(8,128)S(1)}, f32[8,6,32,128]{3,2,1,0:T(8,128)S(1)}, f3...) custom-call(f32[64,32,128]{2,1,0:T(8,128)S(1)} %copy-done, ...), custom_call_target="tpu_custom_call" | custom-call | tf_op jit(solution)/shard_map/step/pallas_call | solution.py:487
  55.6 3.4 %collective-permute-start.5 = (f32[232,128]{1,0:T(8,128)S(1)}, f32[232,128]{1,0:T(8,128)S(1)}, u32[]{:S(2)}, u32[]{:S(2)}) collective-permute-start(f32[232,128]{1,0:T(8,128)S(1)} %get-tuple-element.96.mine), channel_id=1, source_target_pairs={{0,1},{1,0},{2,3},{3,2},{4,5},{5,4},{6,7},{7,6},{8,9},{9,8},{10,11... | collective-permute-start | bytes 356360 | tf_op jit(solution)/shard_map/ppermute | solution.py:572
  58.9 2.5 %collective-permute-start.8 = (f32[8,6,32,128]{3,2,1,0:T(8,128)S(1)}, f32[8,6,32,128]{3,2,1,0:T(8,128)S(1)}, u32[]{:S(2)}, u32[]{:S(2)}) collective-permute-start(f32[8,6,32,128]{3,2,1,0:T(8,128)S(1)} %get-tuple-element.102), channel_id=1, source_target_pairs={{0,2},{2,4},{4,6},{6,8},{8,10},{10,12},{12,14},{14,0},{1,3},{3,5},... | collective-permute-start | bytes 2359304 | tf_op jit(solution)/shard_map/ppermute | solution.py:572
  62.2 2.8 %collective-permute-start.7 = (f32[48,32,128]{2,1,0:T(8,128)S(1)}, f32[48,32,128]{2,1,0:T(8,128)S(1)}, u32[]{:S(2)}, u32[]{:S(2)}) collective-permute-start(f32[48,32,128]{2,1,0:T(8,128)S(1)} %get-tuple-element.101), channel_id=1, source_target_pairs={{0,112},{16,0},{32,16},{48,32},{64,48},{80,64},{96,80},{112,96},{1... | collective-permute-start | bytes 2359304 | tf_op jit(solution)/shard_map/ppermute | solution.py:572
  65.1 11.2 %all_to_all.47.came = f32[8,24,128]{2,1,0:T(8,128)S(1)} all-to-all(f32[8,24,128]{2,1,0:T(8,128)S(1)} %get-tuple-element.105), channel_id=1, replica_groups=mesh['gx'=8,'gy'=8,'gz'=2] {'gy'}, dimensions={0} | all-to-all | bytes 196608 | tf_op jit(solution)/shard_map/all_to_all | solution.py:602
  76.3 7.8 %all_to_all.48.refs_8_ = f32[8,24,128]{2,1,0:T(8,128)S(1)} all-to-all(f32[8,24,128]{2,1,0:T(8,128)S(1)} %get-tuple-element.107), channel_id=1, replica_groups=mesh['gx'=8,'gy'=8,'gz'=2] {'gx'}, dimensions={0} | all-to-all | bytes 196608 | tf_op jit(solution)/shard_map/all_to_all | solution.py:604
  84.1 4.7 %step.5 = (f32[64,32,128]{2,1,0:T(8,128)S(1)}, f32[48,32,128]{2,1,0:T(8,128)S(1)}, f32[48,32,128]{2,1,0:T(8,128)S(1)}, f32[8,6,32,128]{3,2,1,0:T(8,128)S(1)}, f3...) custom-call(f32[64,32,128]{2,1,0:T(8,128)S(1)} %get-tuple-element.95.refs_0_.refs_10_, ...), custom_call_target="tpu_custom_call" | custom-call | tf_op jit(solution)/shard_map/step/pallas_call | solution.py:487
  88.8 3.2 %collective-permute-start.10 = (f32[232,128]{1,0:T(8,128)S(1)}, f32[232,128]{1,0:T(8,128)S(1)}, u32[]{:S(2)}, u32[]{:S(2)}) collective-permute-start(f32[232,128]{1,0:T(8,128)S(1)} %get-tuple-element.110.mine), channel_id=1, source_target_pairs={{0,1},{1,0},{2,3},{3,2},{4,5},{5,4},{6,7},{7,6},{8,9},{9,8},{10,11... | collective-permute-start | bytes 356360 | tf_op jit(solution)/shard_map/ppermute | solution.py:572
  92.0 2.3 %collective-permute-start.13 = (f32[8,6,32,128]{3,2,1,0:T(8,128)S(1)}, f32[8,6,32,128]{3,2,1,0:T(8,128)S(1)}, u32[]{:S(2)}, u32[]{:S(2)}) collective-permute-start(f32[8,6,32,128]{3,2,1,0:T(8,128)S(1)} %get-tuple-element.116), channel_id=1, source_target_pairs={{0,2},{2,4},{4,6},{6,8},{8,10},{10,12},{12,14},{14,0},{1,3},{3,5},... | collective-permute-start | bytes 2359304 | tf_op jit(solution)/shard_map/ppermute | solution.py:572
  95.5 2.4 %collective-permute-start.12 = (f32[48,32,128]{2,1,0:T(8,128)S(1)}, f32[48,32,128]{2,1,0:T(8,128)S(1)}, u32[]{:S(2)}, u32[]{:S(2)}) collective-permute-start(f32[48,32,128]{2,1,0:T(8,128)S(1)} %get-tuple-element.115), channel_id=1, source_target_pairs={{0,112},{16,0},{32,16},{48,32},{64,48},{80,64},{96,80},{112,96},{1... | collective-permute-start | bytes 2359304 | tf_op jit(solution)/shard_map/ppermute | solution.py:572
  98.0 12.3 %all_to_all.49.came = f32[8,24,128]{2,1,0:T(8,128)S(1)} all-to-all(f32[8,24,128]{2,1,0:T(8,128)S(1)} %get-tuple-element.119), channel_id=1, replica_groups=mesh['gx'=8,'gy'=8,'gz'=2] {'gy'}, dimensions={0} | all-to-all | bytes 196608 | tf_op jit(solution)/shard_map/all_to_all | solution.py:602
  110.3 7.7 %all_to_all.50.refs_8_ = f32[8,24,128]{2,1,0:T(8,128)S(1)} all-to-all(f32[8,24,128]{2,1,0:T(8,128)S(1)} %get-tuple-element.121), channel_id=1, replica_groups=mesh['gx'=8,'gy'=8,'gz'=2] {'gx'}, dimensions={0} | all-to-all | bytes 196608 | tf_op jit(solution)/shard_map/all_to_all | solution.py:604
  118.0 4.7 %step.6 = (f32[64,32,128]{2,1,0:T(8,128)S(1)}, f32[48,32,128]{2,1,0:T(8,128)S(1)}, f32[48,32,128]{2,1,0:T(8,128)S(1)}, f32[8,6,32,128]{3,2,1,0:T(8,128)S(1)}, f3...) custom-call(f32[64,32,128]{2,1,0:T(8,128)S(1)} %get-tuple-element.109.refs_0_.refs_10_, ...), custom_call_target="tpu_custom_call" | custom-call | tf_op jit(solution)/shard_map/step/pallas_call | solution.py:487
  122.7 2.7 %collective-permute-start.15 = (f32[232,128]{1,0:T(8,128)S(1)}, f32[232,128]{1,0:T(8,128)S(1)}, u32[]{:S(2)}, u32[]{:S(2)}) collective-permute-start(f32[232,128]{1,0:T(8,128)S(1)} %get-tuple-element.123.mine), channel_id=1, source_target_pairs={{0,1},{1,0},{2,3},{3,2},{4,5},{5,4},{6,7},{7,6},{8,9},{9,8},{10,11... | collective-permute-start | bytes 356360 | tf_op jit(solution)/shard_map/ppermute | solution.py:572
  125.4 2.4 %collective-permute-start.18 = (f32[8,6,32,128]{3,2,1,0:T(8,128)S(1)}, f32[8,6,32,128]{3,2,1,0:T(8,128)S(1)}, u32[]{:S(2)}, u32[]{:S(2)}) collective-permute-start(f32[8,6,32,128]{3,2,1,0:T(8,128)S(1)} %get-tuple-element.129), channel_id=1, source_target_pairs={{0,2},{2,4},{4,6},{6,8},{8,10},{10,12},{12,14},{14,0},{1,3},{3,5},... | collective-permute-start | bytes 2359304 | tf_op jit(solution)/shard_map/ppermute | solution.py:572
  128.5 3.0 %collective-permute-start.17 = (f32[48,32,128]{2,1,0:T(8,128)S(1)}, f32[48,32,128]{2,1,0:T(8,128)S(1)}, u32[]{:S(2)}, u32[]{:S(2)}) collective-permute-start(f32[48,32,128]{2,1,0:T(8,128)S(1)} %get-tuple-element.128), channel_id=1, source_target_pairs={{0,112},{16,0},{32,16},{48,32},{64,48},{80,64},{96,80},{112,96},{1... | collective-permute-start | bytes 2359304 | tf_op jit(solution)/shard_map/ppermute | solution.py:572
  131.6 11.3 %all_to_all.51.came = f32[8,24,128]{2,1,0:T(8,128)S(1)} all-to-all(f32[8,24,128]{2,1,0:T(8,128)S(1)} %get-tuple-element.132), channel_id=1, replica_groups=mesh['gx'=8,'gy'=8,'gz'=2] {'gy'}, dimensions={0} | all-to-all | bytes 196608 | tf_op jit(solution)/shard_map/all_to_all | solution.py:602
  142.9 7.7 %all_to_all.52.refs_8_ = f32[8,24,128]{2,1,0:T(8,128)S(1)} all-to-all(f32[8,24,128]{2,1,0:T(8,128)S(1)} %get-tuple-element.134), channel_id=1, replica_groups=mesh['gx'=8,'gy'=8,'gz'=2] {'gx'}, dimensions={0} | all-to-all | bytes 196608 | tf_op jit(solution)/shard_map/all_to_all | solution.py:604
  150.6 4.2 %step.7 = (f32[64,32,128]{2,1,0:T(8,128)S(1)}, f32[1,640]{1,0:T(1,128)S(1)}) custom-call(f32[64,32,128]{2,1,0:T(8,128)S(1)} %get-tuple-element.122.refs_0_, f32[232,128]{1,0:T(8,128)S(1)} %collective-permute-done.15.other.refs_1_, f32[48,32,128]{2,1,0:T(8,128)S(1)} %collective-permute-done.16.refs_2_, f32[48,32,128]{2,1,0:T(8,128)S(1)} %collective-permute-done.17.refs_3_, ...), custom_call_target="tpu_custom_call" | custom-call | tf_op jit(solution)/shard_map/step/pallas_call | solution.py:487
  155.0 20.5 %all_to_all.53.grams = f32[128,1,640]{2,1,0:T(1,128)S(1)} all-to-all(f32[128,1,640]{2,1,0:T(1,128)S(1)} %broadcast_in_dim.10), channel_id=1, replica_groups=mesh['gx'=8,'gy'=8,'gz'=2] {'gx','gy','gz'}, dimensions={0} | all-to-all | bytes 655360 | tf_op jit(solution)/shard_map/all_to_all | solution.py:618
  175.5 3.8 %finish.1 = f32[32,64,128]{2,1,0:T(8,128)} custom-call(f32[64,32,128]{2,1,0:T(8,128)S(1)} %get-tuple-element.135.field, f32[128,1,640]{2,1,0:T(1,128)S(1)} %all_to_all.53.grams), custom_call_target="tpu_custom_call" | custom-call | tf_op jit(solution)/shard_map/finish/pallas_call | solution.py:555
  (46 shorter events, 4.4 us)
Async XLA Ops:
  12.2 5.7 %copy-start = (f32[64,32,128]{2,1,0:T(8,128)S(1)}, f32[64,32,128]{2,1,0:T(8,128)}, u32[]{:S(2)}) copy-start(f32[64,32,128]{2,1,0:T(8,128)} %get-tuple-element.71.field.refs_0_.refs_10_) | copy-start | bytes 3145732
  12.2 5.7 %copy-start.2 = (f32[8,128]{1,0:T(8,128)S(1)}, f32[8,128]{1,0:T(8,128)}, u32[]{:S(2)}) copy-start(f32[8,128]{1,0:T(8,128)} %get-tuple-element.82.own) | copy-start | bytes 12292
  17.9 32.9 %copy-start.1 = (f32[8,8,128]{2,1,0:T(8,128)S(1)}, f32[8,8,128]{2,1,0:T(8,128)}, u32[]{:S(2)}) copy-start(f32[8,8,128]{2,1,0:T(8,128)} %param.8) | copy-start | bytes 98308
  20.0 7.6 %collective-permute-start = (f32[240,128]{1,0:T(8,128)S(1)}, f32[240,128]{1,0:T(8,128)S(1)}, u32[]{:S(2)}, u32[]{:S(2)}) collective-permute-start(f32[240,128]{1,0:T(8,128)S(1)} %get-tuple-element.83.mine), channel_id=1, source_target_pairs={{0,1},{1,0},{2,3},{3,2},{4,5},{5,4},{6,7},{7,6},{8,9},{9,8},{10,11... | collective-permute-start | bytes 368648 | tf_op jit(solution)/shard_map/ppermute | solution.py:572
  24.6 26.2 %collective-permute-start.3 = (f32[8,6,32,128]{3,2,1,0:T(8,128)S(1)}, f32[8,6,32,128]{3,2,1,0:T(8,128)S(1)}, u32[]{:S(2)}, u32[]{:S(2)}) collective-permute-start(f32[8,6,32,128]{3,2,1,0:T(8,128)S(1)} %get-tuple-element.89), channel_id=1, source_target_pairs={{0,2},{2,4},{4,6},{6,8},{8,10},{10,12},{12,14},{14,0},{1,3},{3,5},... | collective-permute-start | bytes 2359304 | tf_op jit(solution)/shard_map/ppermute | solution.py:572
  26.6 24.2 %collective-permute-start.4 = (f32[8,6,32,128]{3,2,1,0:T(8,128)S(1)}, f32[8,6,32,128]{3,2,1,0:T(8,128)S(1)}, u32[]{:S(2)}, u32[]{:S(2)}) collective-permute-start(f32[8,6,32,128]{3,2,1,0:T(8,128)S(1)} %get-tuple-element.90), channel_id=1, source_target_pairs={{0,14},{2,0},{4,2},{6,4},{8,6},{10,8},{12,10},{14,12},{1,15},{3,1}... | collective-permute-start | bytes 2359304 | tf_op jit(solution)/shard_map/ppermute | solution.py:572
  27.6 23.2 %collective-permute-start.1 = (f32[48,32,128]{2,1,0:T(8,128)S(1)}, f32[48,32,128]{2,1,0:T(8,128)S(1)}, u32[]{:S(2)}, u32[]{:S(2)}) collective-permute-start(f32[48,32,128]{2,1,0:T(8,128)S(1)} %get-tuple-element.87), channel_id=1, source_target_pairs={{0,16},{16,32},{32,48},{48,64},{64,80},{80,96},{96,112},{112,0},{1... | collective-permute-start | bytes 2359304 | tf_op jit(solution)/shard_map/ppermute | solution.py:572
  29.2 21.6 %collective-permute-start.2 = (f32[48,32,128]{2,1,0:T(8,128)S(1)}, f32[48,32,128]{2,1,0:T(8,128)S(1)}, u32[]{:S(2)}, u32[]{:S(2)}) collective-permute-start(f32[48,32,128]{2,1,0:T(8,128)S(1)} %get-tuple-element.88), channel_id=1, source_target_pairs={{0,112},{16,0},{32,16},{48,32},{64,48},{80,64},{96,80},{112,96},{1... | collective-permute-start | bytes 2359304 | tf_op jit(solution)/shard_map/ppermute | solution.py:572
  55.6 5.9 %collective-permute-start.5 = (f32[232,128]{1,0:T(8,128)S(1)}, f32[232,128]{1,0:T(8,128)S(1)}, u32[]{:S(2)}, u32[]{:S(2)}) collective-permute-start(f32[232,128]{1,0:T(8,128)S(1)} %get-tuple-element.96.mine), channel_id=1, source_target_pairs={{0,1},{1,0},{2,3},{3,2},{4,5},{5,4},{6,7},{7,6},{8,9},{9,8},{10,11... | collective-permute-start | bytes 356360 | tf_op jit(solution)/shard_map/ppermute | solution.py:572
  58.9 25.1 %collective-permute-start.8 = (f32[8,6,32,128]{3,2,1,0:T(8,128)S(1)}, f32[8,6,32,128]{3,2,1,0:T(8,128)S(1)}, u32[]{:S(2)}, u32[]{:S(2)}) collective-permute-start(f32[8,6,32,128]{3,2,1,0:T(8,128)S(1)} %get-tuple-element.102), channel_id=1, source_target_pairs={{0,2},{2,4},{4,6},{6,8},{8,10},{10,12},{12,14},{14,0},{1,3},{3,5},... | collective-permute-start | bytes 2359304 | tf_op jit(solution)/shard_map/ppermute | solution.py:572
  61.5 22.6 %collective-permute-start.9 = (f32[8,6,32,128]{3,2,1,0:T(8,128)S(1)}, f32[8,6,32,128]{3,2,1,0:T(8,128)S(1)}, u32[]{:S(2)}, u32[]{:S(2)}) collective-permute-start(f32[8,6,32,128]{3,2,1,0:T(8,128)S(1)} %get-tuple-element.103), channel_id=1, source_target_pairs={{0,14},{2,0},{4,2},{6,4},{8,6},{10,8},{12,10},{14,12},{1,15},{3,1}... | collective-permute-start | bytes 2359304 | tf_op jit(solution)/shard_map/ppermute | solution.py:572
  61.5 22.6 %collective-permute-start.6 = (f32[48,32,128]{2,1,0:T(8,128)S(1)}, f32[48,32,128]{2,1,0:T(8,128)S(1)}, u32[]{:S(2)}, u32[]{:S(2)}) collective-permute-start(f32[48,32,128]{2,1,0:T(8,128)S(1)} %get-tuple-element.100), channel_id=1, source_target_pairs={{0,16},{16,32},{32,48},{48,64},{64,80},{80,96},{96,112},{112,0},{1... | collective-permute-start | bytes 2359304 | tf_op jit(solution)/shard_map/ppermute | solution.py:572
  62.2 21.9 %collective-permute-start.7 = (f32[48,32,128]{2,1,0:T(8,128)S(1)}, f32[48,32,128]{2,1,0:T(8,128)S(1)}, u32[]{:S(2)}, u32[]{:S(2)}) collective-permute-start(f32[48,32,128]{2,1,0:T(8,128)S(1)} %get-tuple-element.101), channel_id=1, source_target_pairs={{0,112},{16,0},{32,16},{48,32},{64,48},{80,64},{96,80},{112,96},{1... | collective-permute-start | bytes 2359304 | tf_op jit(solution)/shard_map/ppermute | solution.py:572
  88.8 5.5 %collective-permute-start.10 = (f32[232,128]{1,0:T(8,128)S(1)}, f32[232,128]{1,0:T(8,128)S(1)}, u32[]{:S(2)}, u32[]{:S(2)}) collective-permute-start(f32[232,128]{1,0:T(8,128)S(1)} %get-tuple-element.110.mine), channel_id=1, source_target_pairs={{0,1},{1,0},{2,3},{3,2},{4,5},{5,4},{6,7},{7,6},{8,9},{9,8},{10,11... | collective-permute-start | bytes 356360 | tf_op jit(solution)/shard_map/ppermute | solution.py:572
  92.0 25.9 %collective-permute-start.13 = (f32[8,6,32,128]{3,2,1,0:T(8,128)S(1)}, f32[8,6,32,128]{3,2,1,0:T(8,128)S(1)}, u32[]{:S(2)}, u32[]{:S(2)}) collective-permute-start(f32[8,6,32,128]{3,2,1,0:T(8,128)S(1)} %get-tuple-element.116), channel_id=1, source_target_pairs={{0,2},{2,4},{4,6},{6,8},{8,10},{10,12},{12,14},{14,0},{1,3},{3,5},... | collective-permute-start | bytes 2359304 | tf_op jit(solution)/shard_map/ppermute | solution.py:572
  94.4 23.6 %collective-permute-start.14 = (f32[8,6,32,128]{3,2,1,0:T(8,128)S(1)}, f32[8,6,32,128]{3,2,1,0:T(8,128)S(1)}, u32[]{:S(2)}, u32[]{:S(2)}) collective-permute-start(f32[8,6,32,128]{3,2,1,0:T(8,128)S(1)} %get-tuple-element.117), channel_id=1, source_target_pairs={{0,14},{2,0},{4,2},{6,4},{8,6},{10,8},{12,10},{14,12},{1,15},{3,1}... | collective-permute-start | bytes 2359304 | tf_op jit(solution)/shard_map/ppermute | solution.py:572
  94.4 23.6 %collective-permute-start.11 = (f32[48,32,128]{2,1,0:T(8,128)S(1)}, f32[48,32,128]{2,1,0:T(8,128)S(1)}, u32[]{:S(2)}, u32[]{:S(2)}) collective-permute-start(f32[48,32,128]{2,1,0:T(8,128)S(1)} %get-tuple-element.114), channel_id=1, source_target_pairs={{0,16},{16,32},{32,48},{48,64},{64,80},{80,96},{96,112},{112,0},{1... | collective-permute-start | bytes 2359304 | tf_op jit(solution)/shard_map/ppermute | solution.py:572
  95.5 22.5 %collective-permute-start.12 = (f32[48,32,128]{2,1,0:T(8,128)S(1)}, f32[48,32,128]{2,1,0:T(8,128)S(1)}, u32[]{:S(2)}, u32[]{:S(2)}) collective-permute-start(f32[48,32,128]{2,1,0:T(8,128)S(1)} %get-tuple-element.115), channel_id=1, source_target_pairs={{0,112},{16,0},{32,16},{48,32},{64,48},{80,64},{96,80},{112,96},{1... | collective-permute-start | bytes 2359304 | tf_op jit(solution)/shard_map/ppermute | solution.py:572
  122.7 5.3 %collective-permute-start.15 = (f32[232,128]{1,0:T(8,128)S(1)}, f32[232,128]{1,0:T(8,128)S(1)}, u32[]{:S(2)}, u32[]{:S(2)}) collective-permute-start(f32[232,128]{1,0:T(8,128)S(1)} %get-tuple-element.123.mine), channel_id=1, source_target_pairs={{0,1},{1,0},{2,3},{3,2},{4,5},{5,4},{6,7},{7,6},{8,9},{9,8},{10,11... | collective-permute-start | bytes 356360 | tf_op jit(solution)/shard_map/ppermute | solution.py:572
  125.4 25.2 %collective-permute-start.18 = (f32[8,6,32,128]{3,2,1,0:T(8,128)S(1)}, f32[8,6,32,128]{3,2,1,0:T(8,128)S(1)}, u32[]{:S(2)}, u32[]{:S(2)}) collective-permute-start(f32[8,6,32,128]{3,2,1,0:T(8,128)S(1)} %get-tuple-element.129), channel_id=1, source_target_pairs={{0,2},{2,4},{4,6},{6,8},{8,10},{10,12},{12,14},{14,0},{1,3},{3,5},... | collective-permute-start | bytes 2359304 | tf_op jit(solution)/shard_map/ppermute | solution.py:572
  127.8 22.8 %collective-permute-start.19 = (f32[8,6,32,128]{3,2,1,0:T(8,128)S(1)}, f32[8,6,32,128]{3,2,1,0:T(8,128)S(1)}, u32[]{:S(2)}, u32[]{:S(2)}) collective-permute-start(f32[8,6,32,128]{3,2,1,0:T(8,128)S(1)} %get-tuple-element.130), channel_id=1, source_target_pairs={{0,14},{2,0},{4,2},{6,4},{8,6},{10,8},{12,10},{14,12},{1,15},{3,1}... | collective-permute-start | bytes 2359304 | tf_op jit(solution)/shard_map/ppermute | solution.py:572
  128.0 22.6 %collective-permute-start.16 = (f32[48,32,128]{2,1,0:T(8,128)S(1)}, f32[48,32,128]{2,1,0:T(8,128)S(1)}, u32[]{:S(2)}, u32[]{:S(2)}) collective-permute-start(f32[48,32,128]{2,1,0:T(8,128)S(1)} %get-tuple-element.127), channel_id=1, source_target_pairs={{0,16},{16,32},{32,48},{48,64},{64,80},{80,96},{96,112},{112,0},{1... | collective-permute-start | bytes 2359304 | tf_op jit(solution)/shard_map/ppermute | solution.py:572
  128.5 22.1 %collective-permute-start.17 = (f32[48,32,128]{2,1,0:T(8,128)S(1)}, f32[48,32,128]{2,1,0:T(8,128)S(1)}, u32[]{:S(2)}, u32[]{:S(2)}) collective-permute-start(f32[48,32,128]{2,1,0:T(8,128)S(1)} %get-tuple-element.128), channel_id=1, source_target_pairs={{0,112},{16,0},{32,16},{48,32},{64,48},{80,64},{96,80},{112,96},{1... | collective-permute-start | bytes 2359304 | tf_op jit(solution)/shard_map/ppermute | solution.py:572

commit v13 on v12

--- a/solution.py
+++ b/solution.py
@@ -39,6 +39,7 @@
 ZROWS = GROUPS * EDGE
 PACK = 24
 LANES = 128
+STRIP = 8
 LOWER = [(i, j) for i in range(4) for j in range(i + 1)]
 F32 = jnp.float32
 BF16 = jnp.bfloat16
@@ -393,39 +394,45 @@
     diagonal = -1.5 * STENCIL[0] - FILTER_CENTRE
     write_z_matrices(first_z, second_z)
 
-    def at(x, y):
+    def at(x, y, b):
+        some = pl.ds(b, 8)
         if x < 0:
-            return x_left[(x + REACH) * SY + y]
+            return x_left[(x + REACH) * SY + y, some, :]
         if x >= SX:
-            return x_right[(x - SX) * SY + y]
+            return x_right[(x - SX) * SY + y, some, :]
         if y < 0:
-            return y_left[x, y + REACH]
+            return y_left[x, y + REACH, some, :]
         if y >= SY:
-            return y_right[x, y - SY]
-        return field[x * SY + y]
-
-    for g in range(GROUPS):
-        rows = [field[4 * g + i] for i in range(4)]
-        hi, lo = split2(jnp.concatenate(rows, axis=0))
-        face = faces[pl.ds(g * EDGE, EDGE), :]
-        face_hi = face.astype(BF16).astype(F32)
-        side = jnp.concatenate(
-            [face_hi, face - face_hi, face_hi, jnp.zeros((LANES - 3 * EDGE, LANES), F32)], axis=0
-        ).T.astype(BF16)
-        along_z = dot(jnp.concatenate([hi, lo], axis=1), first_z[...]) + dot(
-            jnp.concatenate([hi, side], axis=1), second_z[...]
-        )
-        for i in range(4):
-            x, y = divmod(4 * g + i, SY)
-            summed = along_z[i * NB : (i + 1) * NB]
-            for m in range(1, REACH + 1):
-                around = (at(x + m, y) + at(x - m, y)) + (at(x, y + m) + at(x, y - m))
-                summed = summed + half[m] * around
-            summed = summed + (potential[pl.ds(4 * g + i, 1), :] + diagonal) * rows[i]
-            result = alpha * summed
-            if not first_step:
-                result = result - previous[4 * g + i]
-            new[4 * g + i] = result
+            return y_right[x, y - SY, some, :]
+        return field[x * SY + y, some, :]
+
+    for x in range(SX):
+        along_z = []
+        for g in (2 * x, 2 * x + 1):
+            block = jnp.concatenate([field[4 * g + i] for i in range(4)], axis=0)
+            hi, lo = split2(block)
+            face = faces[pl.ds(g * EDGE, EDGE), :]
+            face_hi = face.astype(BF16).astype(F32)
+            side = jnp.concatenate(
+                [face_hi, face - face_hi, face_hi, jnp.zeros((LANES - 3 * EDGE, LANES), F32)], axis=0
+            ).T.astype(BF16)
+            along_z.append(
+                dot(jnp.concatenate([hi, lo], axis=1), first_z[...])
+                + dot(jnp.concatenate([hi, side], axis=1), second_z[...])
+            )
+        for b in range(0, NB, 8):
+            line = [at(x, y, b) for y in range(-REACH, SY + REACH)]
+            for y in range(SY):
+                part, i = divmod(y, 4)
+                summed = along_z[part][i * NB + b : i * NB + b + 8]
+                for m in range(1, REACH + 1):
+                    around = (at(x + m, y, b) + at(x - m, y, b)) + (line[y + REACH + m] + line[y + REACH - m])
+                    summed = summed + half[m] * around
+                summed = summed + (potential[pl.ds(x * SY + y, 1), :] + diagonal) * line[y + REACH]
+                result = alpha * summed
+                if not first_step:
+                    result = result - previous[x * SY + y, pl.ds(b, 8), :]
+                new[x * SY + y, pl.ds(b, 8), :] = result
 
     total[...] = jnp.zeros_like(total)
     frame = received("gx", 12, kept[...], came)
@@ -518,20 +525,23 @@
     eye = jnp.where(row == column, 1.0, 0.0)
     work = jnp.concatenate([gram, eye], axis=1)
     below = lax.broadcasted_iota(jnp.int32, (NB, 2 * NB), 0)
-    for k in range(0, NB, 2):
-        left = jnp.broadcast_to(work[:, k : k + 1], work.shape)
-        right = jnp.broadcast_to(work[:, k + 1 : k + 2], work.shape)
-        root = lax.rsqrt(left[k : k + 1])
-        beside = left[k + 1 : k + 2] * root
-        next_root = lax.rsqrt(right[k + 1 : k + 2] - beside * beside)
-        line = work[k : k + 1] * root
-        next_line = (work[k + 1 : k + 2] - beside * line) * next_root
-        inverse[pl.ds(k, 1), :] = line[:, NB:]
-        inverse[pl.ds(k + 1, 1), :] = next_line[:, NB:]
-        if k < NB - 2:
-            factor = left * root
-            next_factor = (right - factor * beside) * next_root
-            work = work - jnp.where(below > k + 1, factor * line + next_factor * next_line, 0.0)
+    for k in range(0, NB, STRIP):
+        columns = [jnp.broadcast_to(work[:, k + i : k + i + 1], work.shape) for i in range(STRIP)]
+        lines = [work[k + i : k + i + 1] for i in range(STRIP)]
+        for i in range(STRIP):
+            root = lax.rsqrt(columns[i][k + i : k + i + 1])
+            columns[i] = columns[i] * root
+            lines[i] = lines[i] * root
+            inverse[pl.ds(k + i, 1), :] = lines[i][:, NB:]
+            for j in range(i + 1, STRIP):
+                beside = columns[i][k + j : k + j + 1]
+                columns[j] = columns[j] - columns[i] * beside
+                lines[j] = lines[j] - lines[i] * beside
+        if k < NB - STRIP:
+            removed = columns[0] * lines[0]
+            for i in range(1, STRIP):
+                removed = removed + columns[i] * lines[i]
+            work = work - jnp.where(below >= k + STRIP, removed, 0.0)
     hi, mid, lo = split3(inverse[...])
     left = jnp.concatenate([lo, mid, hi, mid, hi, hi], axis=1)
 

time: 181 us -> 178 us (0.983)
  Pallas kernels: 33.8 us -> 31.8 us
where the time goes in v13:
time: 178 us; the launch traced here: 177 us
  blocking collectives  98.1 us (55%)
  starting transfers between devices  36.9 us (21%)
  Pallas kernels  31.8 us (18%)
  other arithmetic  7.88 us (4%)
    all_to_all x4, blocking collectives, local(): came = lax.all_to_all(sends, 'gy', 0, 0)  46.1 us
    ppermute x20, starting transfers between devices, shift(): lax.ppermute(value, axis, [(i, (i + by) % count) for i in range(count)])  36.9 us
    all_to_all x4, blocking collectives, local(): came = lax.all_to_all(sends, 'gx', 0, 0)  31.6 us
    all_to_all x1, blocking collectives, local(): lax.all_to_all(jnp.broadcast_to(gram[None], (devices,) + gram.shape), axe...  20.4 us
    pallas_call x4, Pallas kernels, step(): pl.pallas_call(functools.partial(step_kernel, first_step, last_step), out...  17.2 us
    sort x1, other arithmetic, local(): lax.sort((key, *[w.reshape(SLOTS) for w in weights]), num_keys=1, is_stab...  6.69 us
    pallas_call x1, Pallas kernels, build(): pl.pallas_call(build_kernel, out_shape=MATRIX, in_specs=[pl.BlockSpec(mem...  5.69 us
  transfers between devices with their start and end apart: 20, of which 2 were waited for; matrix products, arithmetic and copies ran while one was open for 0% of the time, Pallas kernels for 0%

profile of v13, /device:TPU:1, one launch (start us, length us, event | category | flops | bytes accessed | tf_op | source)
XLA Modules:
  0.0 177.3 jit_solution(12009130109045609693)
XLA Ops:
  0.7 3.4 %prepare.1 = (f32[64,32,128]{2,1,0:T(8,128)}, s32[64,128]{1,0:T(8,128)}, f32[8,128]{1,0:T(8,128)}, f32[64,128]{1,0:T(8,128)}, f32[64,128]{1,0:T(8,128)}, /*index=5*/f32[64,128]{1,0:T(8,128)}, f32[64,128]{1,0:T(8,128)}) custom-call(s32[1]{0:T(128)} %bitcast.16.count, f32[2,4]{1,0:T(2,128)} %coupling.1, f32[32,64,128]{2,1,0:T(8,128)} %bitcast.21, ...), custom_call_target="tpu_custom_call" | custom-call | tf_op jit(solution)/shard_map/prepare/pallas_call | solution.py:163
  4.0 1.2 convert_reduce_fusion.starts
  5.2 6.7 %sort.33 = (s32[8192]{0:T(1024)S(1)}, f32[8192]{0:T(1024)S(1)}, f32[8192]{0:T(1024)S(1)}, f32[8192]{0:T(1024)S(1)}, f32[8192]{0:T(1024)S(1)}) sort(s32[8192]{0:T(1024)} %bitcast.23, f32[8192]{0:T(1024)} %bitcast.25, f32[8192]{0:T(1024)} %bitcast.26, f32[8192]{0:T(1024)} %bitcast.27, f32[8192]{0:T(1024)} %bitcast.28), dimensions={0}, to_apply=%region_1.0 | sort | flops 106496 | bytes 327680 | tf_op jit(solution)/shard_map/sort | solution.py:595
  12.2 5.7 %build.1.mat.refs_9_ = bf16[32,320,256]{2,1,0:T(8,128)(2,1)S(1)} custom-call(s32[65]{0:T(128)S(1)} %convert_reduce_fusion.starts, f32[5,8192]{1,0:T(8,128)S(1)} %stack.23.points), custom_call_target="tpu_custom_call" | custom-call | tf_op jit(solution)/shard_map/build/pallas_call | solution.py:232
  17.9 2.1 %first.1 = (f32[240,128]{1,0:T(8,128)S(1)}, f32[48,32,128]{2,1,0:T(8,128)S(1)}, f32[48,32,128]{2,1,0:T(8,128)S(1)}, f32[8,6,32,128]{3,2,1,0:T(8,128)S(1)}, f32[8,6,32,128]{3,2,1,0:T(8,128)S(1)}) custom-call(f32[64,32,128]{2,1,0:T(8,128)S(1)} %copy-done, bf16[32,320,256]{2,1,0:T(8,128)(2,1)S(1)} %build.1.mat.refs_9_, f32[8,128]{1,0:T(8,128)S(1)} %copy-done.2), custom_call_target="tpu_custom_call" | custom-call | tf_op jit(solution)/shard_map/first/pallas_call | solution.py:273
  20.0 4.5 %collective-permute-start = (f32[240,128]{1,0:T(8,128)S(1)}, f32[240,128]{1,0:T(8,128)S(1)}, u32[]{:S(2)}, u32[]{:S(2)}) collective-permute-start(f32[240,128]{1,0:T(8,128)S(1)} %get-tuple-element.83.mine), channel_id=1, source_target_pairs={{0,1},{1,0},{2,3},{3,2},{4,5},{5,4},{6,7},{7,6},{8,9},{9,8},{10,11... | collective-permute-start | bytes 368648 | tf_op jit(solution)/shard_map/ppermute | solution.py:582
  24.6 2.1 %collective-permute-start.3 = (f32[8,6,32,128]{3,2,1,0:T(8,128)S(1)}, f32[8,6,32,128]{3,2,1,0:T(8,128)S(1)}, u32[]{:S(2)}, u32[]{:S(2)}) collective-permute-start(f32[8,6,32,128]{3,2,1,0:T(8,128)S(1)} %get-tuple-element.89), channel_id=1, source_target_pairs={{0,2},{2,4},{4,6},{6,8},{8,10},{10,12},{12,14},{14,0},{1,3},{3,5},... | collective-permute-start | bytes 2359304 | tf_op jit(solution)/shard_map/ppermute | solution.py:582
  27.6 1.3 collective-permute-start.1
  28.9 2.3 %collective-permute-start.2 = (f32[48,32,128]{2,1,0:T(8,128)S(1)}, f32[48,32,128]{2,1,0:T(8,128)S(1)}, u32[]{:S(2)}, u32[]{:S(2)}) collective-permute-start(f32[48,32,128]{2,1,0:T(8,128)S(1)} %get-tuple-element.88), channel_id=1, source_target_pairs={{0,112},{16,0},{32,16},{48,32},{64,48},{80,64},{96,80},{112,96},{1... | collective-permute-start | bytes 2359304 | tf_op jit(solution)/shard_map/ppermute | solution.py:582
  31.3 11.4 %all_to_all.45.came = f32[8,32,128]{2,1,0:T(8,128)S(1)} all-to-all(f32[8,32,128]{2,1,0:T(8,128)S(1)} %get-tuple-element.92), channel_id=1, replica_groups=mesh['gx'=8,'gy'=8,'gz'=2] {'gy'}, dimensions={0} | all-to-all | bytes 262144 | tf_op jit(solution)/shard_map/all_to_all | solution.py:612
  42.9 8.5 %all_to_all.46.refs_8_ = f32[8,32,128]{2,1,0:T(8,128)S(1)} all-to-all(f32[8,32,128]{2,1,0:T(8,128)S(1)} %get-tuple-element.94), channel_id=1, replica_groups=mesh['gx'=8,'gy'=8,'gz'=2] {'gx'}, dimensions={0} | all-to-all | bytes 262144 | tf_op jit(solution)/shard_map/all_to_all | solution.py:614
  51.4 4.4 %step.4 = (f32[64,32,128]{2,1,0:T(8,128)S(1)}, f32[48,32,128]{2,1,0:T(8,128)S(1)}, f32[48,32,128]{2,1,0:T(8,128)S(1)}, f32[8,6,32,128]{3,2,1,0:T(8,128)S(1)}, f3...) custom-call(f32[64,32,128]{2,1,0:T(8,128)S(1)} %copy-done, ...), custom_call_target="tpu_custom_call" | custom-call | tf_op jit(solution)/shard_map/step/pallas_call | solution.py:494
  55.8 2.8 %collective-permute-start.5 = (f32[232,128]{1,0:T(8,128)S(1)}, f32[232,128]{1,0:T(8,128)S(1)}, u32[]{:S(2)}, u32[]{:S(2)}) collective-permute-start(f32[232,128]{1,0:T(8,128)S(1)} %get-tuple-element.96.mine), channel_id=1, source_target_pairs={{0,1},{1,0},{2,3},{3,2},{4,5},{5,4},{6,7},{7,6},{8,9},{9,8},{10,11... | collective-permute-start | bytes 356360 | tf_op jit(solution)/shard_map/ppermute | solution.py:582
  58.6 2.5 %collective-permute-start.8 = (f32[8,6,32,128]{3,2,1,0:T(8,128)S(1)}, f32[8,6,32,128]{3,2,1,0:T(8,128)S(1)}, u32[]{:S(2)}, u32[]{:S(2)}) collective-permute-start(f32[8,6,32,128]{3,2,1,0:T(8,128)S(1)} %get-tuple-element.102), channel_id=1, source_target_pairs={{0,2},{2,4},{4,6},{6,8},{8,10},{10,12},{12,14},{14,0},{1,3},{3,5},... | collective-permute-start | bytes 2359304 | tf_op jit(solution)/shard_map/ppermute | solution.py:582
  61.9 2.8 %collective-permute-start.7 = (f32[48,32,128]{2,1,0:T(8,128)S(1)}, f32[48,32,128]{2,1,0:T(8,128)S(1)}, u32[]{:S(2)}, u32[]{:S(2)}) collective-permute-start(f32[48,32,128]{2,1,0:T(8,128)S(1)} %get-tuple-element.101), channel_id=1, source_target_pairs={{0,112},{16,0},{32,16},{48,32},{64,48},{80,64},{96,80},{112,96},{1... | collective-permute-start | bytes 2359304 | tf_op jit(solution)/shard_map/ppermute | solution.py:582
  64.8 11.5 %all_to_all.47.came = f32[8,24,128]{2,1,0:T(8,128)S(1)} all-to-all(f32[8,24,128]{2,1,0:T(8,128)S(1)} %get-tuple-element.105), channel_id=1, replica_groups=mesh['gx'=8,'gy'=8,'gz'=2] {'gy'}, dimensions={0} | all-to-all | bytes 196608 | tf_op jit(solution)/shard_map/all_to_all | solution.py:612
  76.3 7.7 %all_to_all.48.refs_8_ = f32[8,24,128]{2,1,0:T(8,128)S(1)} all-to-all(f32[8,24,128]{2,1,0:T(8,128)S(1)} %get-tuple-element.107), channel_id=1, replica_groups=mesh['gx'=8,'gy'=8,'gz'=2] {'gx'}, dimensions={0} | all-to-all | bytes 196608 | tf_op jit(solution)/shard_map/all_to_all | solution.py:614
  84.0 4.5 %step.5 = (f32[64,32,128]{2,1,0:T(8,128)S(1)}, f32[48,32,128]{2,1,0:T(8,128)S(1)}, f32[48,32,128]{2,1,0:T(8,128)S(1)}, f32[8,6,32,128]{3,2,1,0:T(8,128)S(1)}, f3...) custom-call(f32[64,32,128]{2,1,0:T(8,128)S(1)} %get-tuple-element.95.refs_0_.refs_10_, ...), custom_call_target="tpu_custom_call" | custom-call | tf_op jit(solution)/shard_map/step/pallas_call | solution.py:494
  88.5 3.0 %collective-permute-start.10 = (f32[232,128]{1,0:T(8,128)S(1)}, f32[232,128]{1,0:T(8,128)S(1)}, u32[]{:S(2)}, u32[]{:S(2)}) collective-permute-start(f32[232,128]{1,0:T(8,128)S(1)} %get-tuple-element.110.mine), channel_id=1, source_target_pairs={{0,1},{1,0},{2,3},{3,2},{4,5},{5,4},{6,7},{7,6},{8,9},{9,8},{10,11... | collective-permute-start | bytes 356360 | tf_op jit(solution)/shard_map/ppermute | solution.py:582
  91.5 2.6 %collective-permute-start.13 = (f32[8,6,32,128]{3,2,1,0:T(8,128)S(1)}, f32[8,6,32,128]{3,2,1,0:T(8,128)S(1)}, u32[]{:S(2)}, u32[]{:S(2)}) collective-permute-start(f32[8,6,32,128]{3,2,1,0:T(8,128)S(1)} %get-tuple-element.116), channel_id=1, source_target_pairs={{0,2},{2,4},{4,6},{6,8},{8,10},{10,12},{12,14},{14,0},{1,3},{3,5},... | collective-permute-start | bytes 2359304 | tf_op jit(solution)/shard_map/ppermute | solution.py:582
  95.3 2.4 %collective-permute-start.12 = (f32[48,32,128]{2,1,0:T(8,128)S(1)}, f32[48,32,128]{2,1,0:T(8,128)S(1)}, u32[]{:S(2)}, u32[]{:S(2)}) collective-permute-start(f32[48,32,128]{2,1,0:T(8,128)S(1)} %get-tuple-element.115), channel_id=1, source_target_pairs={{0,112},{16,0},{32,16},{48,32},{64,48},{80,64},{96,80},{112,96},{1... | collective-permute-start | bytes 2359304 | tf_op jit(solution)/shard_map/ppermute | solution.py:582
  97.7 11.8 %all_to_all.49.came = f32[8,24,128]{2,1,0:T(8,128)S(1)} all-to-all(f32[8,24,128]{2,1,0:T(8,128)S(1)} %get-tuple-element.119), channel_id=1, replica_groups=mesh['gx'=8,'gy'=8,'gz'=2] {'gy'}, dimensions={0} | all-to-all | bytes 196608 | tf_op jit(solution)/shard_map/all_to_all | solution.py:612
  109.5 7.7 %all_to_all.50.refs_8_ = f32[8,24,128]{2,1,0:T(8,128)S(1)} all-to-all(f32[8,24,128]{2,1,0:T(8,128)S(1)} %get-tuple-element.121), channel_id=1, replica_groups=mesh['gx'=8,'gy'=8,'gz'=2] {'gx'}, dimensions={0} | all-to-all | bytes 196608 | tf_op jit(solution)/shard_map/all_to_all | solution.py:614
  117.2 4.5 %step.6 = (f32[64,32,128]{2,1,0:T(8,128)S(1)}, f32[48,32,128]{2,1,0:T(8,128)S(1)}, f32[48,32,128]{2,1,0:T(8,128)S(1)}, f32[8,6,32,128]{3,2,1,0:T(8,128)S(1)}, f3...) custom-call(f32[64,32,128]{2,1,0:T(8,128)S(1)} %get-tuple-element.109.refs_0_.refs_10_, ...), custom_call_target="tpu_custom_call" | custom-call | tf_op jit(solution)/shard_map/step/pallas_call | solution.py:494
  121.8 2.9 %collective-permute-start.15 = (f32[232,128]{1,0:T(8,128)S(1)}, f32[232,128]{1,0:T(8,128)S(1)}, u32[]{:S(2)}, u32[]{:S(2)}) collective-permute-start(f32[232,128]{1,0:T(8,128)S(1)} %get-tuple-element.123.mine), channel_id=1, source_target_pairs={{0,1},{1,0},{2,3},{3,2},{4,5},{5,4},{6,7},{7,6},{8,9},{9,8},{10,11... | collective-permute-start | bytes 356360 | tf_op jit(solution)/shard_map/ppermute | solution.py:582
  124.7 2.2 %collective-permute-start.18 = (f32[8,6,32,128]{3,2,1,0:T(8,128)S(1)}, f32[8,6,32,128]{3,2,1,0:T(8,128)S(1)}, u32[]{:S(2)}, u32[]{:S(2)}) collective-permute-start(f32[8,6,32,128]{3,2,1,0:T(8,128)S(1)} %get-tuple-element.129), channel_id=1, source_target_pairs={{0,2},{2,4},{4,6},{6,8},{8,10},{10,12},{12,14},{14,0},{1,3},{3,5},... | collective-permute-start | bytes 2359304 | tf_op jit(solution)/shard_map/ppermute | solution.py:582
  127.6 3.0 %collective-permute-start.17 = (f32[48,32,128]{2,1,0:T(8,128)S(1)}, f32[48,32,128]{2,1,0:T(8,128)S(1)}, u32[]{:S(2)}, u32[]{:S(2)}) collective-permute-start(f32[48,32,128]{2,1,0:T(8,128)S(1)} %get-tuple-element.128), channel_id=1, source_target_pairs={{0,112},{16,0},{32,16},{48,32},{64,48},{80,64},{96,80},{112,96},{1... | collective-permute-start | bytes 2359304 | tf_op jit(solution)/shard_map/ppermute | solution.py:582
  130.7 11.4 %all_to_all.51.came = f32[8,24,128]{2,1,0:T(8,128)S(1)} all-to-all(f32[8,24,128]{2,1,0:T(8,128)S(1)} %get-tuple-element.132), channel_id=1, replica_groups=mesh['gx'=8,'gy'=8,'gz'=2] {'gy'}, dimensions={0} | all-to-all | bytes 196608 | tf_op jit(solution)/shard_map/all_to_all | solution.py:612
  142.1 7.7 %all_to_all.52.refs_8_ = f32[8,24,128]{2,1,0:T(8,128)S(1)} all-to-all(f32[8,24,128]{2,1,0:T(8,128)S(1)} %get-tuple-element.134), channel_id=1, replica_groups=mesh['gx'=8,'gy'=8,'gz'=2] {'gx'}, dimensions={0} | all-to-all | bytes 196608 | tf_op jit(solution)/shard_map/all_to_all | solution.py:614
  149.8 3.7 %step.7 = (f32[64,32,128]{2,1,0:T(8,128)S(1)}, f32[1,640]{1,0:T(1,128)S(1)}) custom-call(f32[64,32,128]{2,1,0:T(8,128)S(1)} %get-tuple-element.122.refs_0_, f32[232,128]{1,0:T(8,128)S(1)} %collective-permute-done.15.other.refs_1_, f32[48,32,128]{2,1,0:T(8,128)S(1)} %collective-permute-done.16.refs_2_, f32[48,32,128]{2,1,0:T(8,128)S(1)} %collective-permute-done.17.refs_3_, ...), custom_call_target="tpu_custom_call" | custom-call | tf_op jit(solution)/shard_map/step/pallas_call | solution.py:494
  153.7 20.4 %all_to_all.53.grams = f32[128,1,640]{2,1,0:T(1,128)S(1)} all-to-all(f32[128,1,640]{2,1,0:T(1,128)S(1)} %broadcast_in_dim.10), channel_id=1, replica_groups=mesh['gx'=8,'gy'=8,'gz'=2] {'gx','gy','gz'}, dimensions={0} | all-to-all | bytes 655360 | tf_op jit(solution)/shard_map/all_to_all | solution.py:628
  174.1 3.0 %finish.1 = f32[32,64,128]{2,1,0:T(8,128)} custom-call(f32[64,32,128]{2,1,0:T(8,128)S(1)} %get-tuple-element.135.field, f32[128,1,640]{2,1,0:T(1,128)S(1)} %all_to_all.53.grams), custom_call_target="tpu_custom_call" | custom-call | tf_op jit(solution)/shard_map/finish/pallas_call | solution.py:565
  (46 shorter events, 4.4 us)
Async XLA Ops:
  12.2 5.7 %copy-start = (f32[64,32,128]{2,1,0:T(8,128)S(1)}, f32[64,32,128]{2,1,0:T(8,128)}, u32[]{:S(2)}) copy-start(f32[64,32,128]{2,1,0:T(8,128)} %get-tuple-element.71.field.refs_0_.refs_10_) | copy-start | bytes 3145732
  12.2 5.7 %copy-start.2 = (f32[8,128]{1,0:T(8,128)S(1)}, f32[8,128]{1,0:T(8,128)}, u32[]{:S(2)}) copy-start(f32[8,128]{1,0:T(8,128)} %get-tuple-element.82.own) | copy-start | bytes 12292
  17.9 33.5 %copy-start.1 = (f32[8,8,128]{2,1,0:T(8,128)S(1)}, f32[8,8,128]{2,1,0:T(8,128)}, u32[]{:S(2)}) copy-start(f32[8,8,128]{2,1,0:T(8,128)} %param.8) | copy-start | bytes 98308
  20.0 7.6 %collective-permute-start = (f32[240,128]{1,0:T(8,128)S(1)}, f32[240,128]{1,0:T(8,128)S(1)}, u32[]{:S(2)}, u32[]{:S(2)}) collective-permute-start(f32[240,128]{1,0:T(8,128)S(1)} %get-tuple-element.83.mine), channel_id=1, source_target_pairs={{0,1},{1,0},{2,3},{3,2},{4,5},{5,4},{6,7},{7,6},{8,9},{9,8},{10,11... | collective-permute-start | bytes 368648 | tf_op jit(solution)/shard_map/ppermute | solution.py:582
  24.6 26.9 %collective-permute-start.3 = (f32[8,6,32,128]{3,2,1,0:T(8,128)S(1)}, f32[8,6,32,128]{3,2,1,0:T(8,128)S(1)}, u32[]{:S(2)}, u32[]{:S(2)}) collective-permute-start(f32[8,6,32,128]{3,2,1,0:T(8,128)S(1)} %get-tuple-element.89), channel_id=1, source_target_pairs={{0,2},{2,4},{4,6},{6,8},{8,10},{10,12},{12,14},{14,0},{1,3},{3,5},... | collective-permute-start | bytes 2359304 | tf_op jit(solution)/shard_map/ppermute | solution.py:582
  26.6 24.8 %collective-permute-start.4 = (f32[8,6,32,128]{3,2,1,0:T(8,128)S(1)}, f32[8,6,32,128]{3,2,1,0:T(8,128)S(1)}, u32[]{:S(2)}, u32[]{:S(2)}) collective-permute-start(f32[8,6,32,128]{3,2,1,0:T(8,128)S(1)} %get-tuple-element.90), channel_id=1, source_target_pairs={{0,14},{2,0},{4,2},{6,4},{8,6},{10,8},{12,10},{14,12},{1,15},{3,1}... | collective-permute-start | bytes 2359304 | tf_op jit(solution)/shard_map/ppermute | solution.py:582
  27.6 23.8 %collective-permute-start.1 = (f32[48,32,128]{2,1,0:T(8,128)S(1)}, f32[48,32,128]{2,1,0:T(8,128)S(1)}, u32[]{:S(2)}, u32[]{:S(2)}) collective-permute-start(f32[48,32,128]{2,1,0:T(8,128)S(1)} %get-tuple-element.87), channel_id=1, source_target_pairs={{0,16},{16,32},{32,48},{48,64},{64,80},{80,96},{96,112},{112,0},{1... | collective-permute-start | bytes 2359304 | tf_op jit(solution)/shard_map/ppermute | solution.py:582
  28.9 22.5 %collective-permute-start.2 = (f32[48,32,128]{2,1,0:T(8,128)S(1)}, f32[48,32,128]{2,1,0:T(8,128)S(1)}, u32[]{:S(2)}, u32[]{:S(2)}) collective-permute-start(f32[48,32,128]{2,1,0:T(8,128)S(1)} %get-tuple-element.88), channel_id=1, source_target_pairs={{0,112},{16,0},{32,16},{48,32},{64,48},{80,64},{96,80},{112,96},{1... | collective-permute-start | bytes 2359304 | tf_op jit(solution)/shard_map/ppermute | solution.py:582
  55.8 5.3 %collective-permute-start.5 = (f32[232,128]{1,0:T(8,128)S(1)}, f32[232,128]{1,0:T(8,128)S(1)}, u32[]{:S(2)}, u32[]{:S(2)}) collective-permute-start(f32[232,128]{1,0:T(8,128)S(1)} %get-tuple-element.96.mine), channel_id=1, source_target_pairs={{0,1},{1,0},{2,3},{3,2},{4,5},{5,4},{6,7},{7,6},{8,9},{9,8},{10,11... | collective-permute-start | bytes 356360 | tf_op jit(solution)/shard_map/ppermute | solution.py:582
  58.6 25.4 %collective-permute-start.8 = (f32[8,6,32,128]{3,2,1,0:T(8,128)S(1)}, f32[8,6,32,128]{3,2,1,0:T(8,128)S(1)}, u32[]{:S(2)}, u32[]{:S(2)}) collective-permute-start(f32[8,6,32,128]{3,2,1,0:T(8,128)S(1)} %get-tuple-element.102), channel_id=1, source_target_pairs={{0,2},{2,4},{4,6},{6,8},{8,10},{10,12},{12,14},{14,0},{1,3},{3,5},... | collective-permute-start | bytes 2359304 | tf_op jit(solution)/shard_map/ppermute | solution.py:582
  61.1 22.8 %collective-permute-start.9 = (f32[8,6,32,128]{3,2,1,0:T(8,128)S(1)}, f32[8,6,32,128]{3,2,1,0:T(8,128)S(1)}, u32[]{:S(2)}, u32[]{:S(2)}) collective-permute-start(f32[8,6,32,128]{3,2,1,0:T(8,128)S(1)} %get-tuple-element.103), channel_id=1, source_target_pairs={{0,14},{2,0},{4,2},{6,4},{8,6},{10,8},{12,10},{14,12},{1,15},{3,1}... | collective-permute-start | bytes 2359304 | tf_op jit(solution)/shard_map/ppermute | solution.py:582
  61.1 22.8 %collective-permute-start.6 = (f32[48,32,128]{2,1,0:T(8,128)S(1)}, f32[48,32,128]{2,1,0:T(8,128)S(1)}, u32[]{:S(2)}, u32[]{:S(2)}) collective-permute-start(f32[48,32,128]{2,1,0:T(8,128)S(1)} %get-tuple-element.100), channel_id=1, source_target_pairs={{0,16},{16,32},{32,48},{48,64},{64,80},{80,96},{96,112},{112,0},{1... | collective-permute-start | bytes 2359304 | tf_op jit(solution)/shard_map/ppermute | solution.py:582
  61.9 22.1 %collective-permute-start.7 = (f32[48,32,128]{2,1,0:T(8,128)S(1)}, f32[48,32,128]{2,1,0:T(8,128)S(1)}, u32[]{:S(2)}, u32[]{:S(2)}) collective-permute-start(f32[48,32,128]{2,1,0:T(8,128)S(1)} %get-tuple-element.101), channel_id=1, source_target_pairs={{0,112},{16,0},{32,16},{48,32},{64,48},{80,64},{96,80},{112,96},{1... | collective-permute-start | bytes 2359304 | tf_op jit(solution)/shard_map/ppermute | solution.py:582
  88.5 5.6 %collective-permute-start.10 = (f32[232,128]{1,0:T(8,128)S(1)}, f32[232,128]{1,0:T(8,128)S(1)}, u32[]{:S(2)}, u32[]{:S(2)}) collective-permute-start(f32[232,128]{1,0:T(8,128)S(1)} %get-tuple-element.110.mine), channel_id=1, source_target_pairs={{0,1},{1,0},{2,3},{3,2},{4,5},{5,4},{6,7},{7,6},{8,9},{9,8},{10,11... | collective-permute-start | bytes 356360 | tf_op jit(solution)/shard_map/ppermute | solution.py:582
  91.5 25.7 %collective-permute-start.13 = (f32[8,6,32,128]{3,2,1,0:T(8,128)S(1)}, f32[8,6,32,128]{3,2,1,0:T(8,128)S(1)}, u32[]{:S(2)}, u32[]{:S(2)}) collective-permute-start(f32[8,6,32,128]{3,2,1,0:T(8,128)S(1)} %get-tuple-element.116), channel_id=1, source_target_pairs={{0,2},{2,4},{4,6},{6,8},{8,10},{10,12},{12,14},{14,0},{1,3},{3,5},... | collective-permute-start | bytes 2359304 | tf_op jit(solution)/shard_map/ppermute | solution.py:582
  94.1 23.1 %collective-permute-start.14 = (f32[8,6,32,128]{3,2,1,0:T(8,128)S(1)}, f32[8,6,32,128]{3,2,1,0:T(8,128)S(1)}, u32[]{:S(2)}, u32[]{:S(2)}) collective-permute-start(f32[8,6,32,128]{3,2,1,0:T(8,128)S(1)} %get-tuple-element.117), channel_id=1, source_target_pairs={{0,14},{2,0},{4,2},{6,4},{8,6},{10,8},{12,10},{14,12},{1,15},{3,1}... | collective-permute-start | bytes 2359304 | tf_op jit(solution)/shard_map/ppermute | solution.py:582
  94.1 23.1 %collective-permute-start.11 = (f32[48,32,128]{2,1,0:T(8,128)S(1)}, f32[48,32,128]{2,1,0:T(8,128)S(1)}, u32[]{:S(2)}, u32[]{:S(2)}) collective-permute-start(f32[48,32,128]{2,1,0:T(8,128)S(1)} %get-tuple-element.114), channel_id=1, source_target_pairs={{0,16},{16,32},{32,48},{48,64},{64,80},{80,96},{96,112},{112,0},{1... | collective-permute-start | bytes 2359304 | tf_op jit(solution)/shard_map/ppermute | solution.py:582
  95.3 22.0 %collective-permute-start.12 = (f32[48,32,128]{2,1,0:T(8,128)S(1)}, f32[48,32,128]{2,1,0:T(8,128)S(1)}, u32[]{:S(2)}, u32[]{:S(2)}) collective-permute-start(f32[48,32,128]{2,1,0:T(8,128)S(1)} %get-tuple-element.115), channel_id=1, source_target_pairs={{0,112},{16,0},{32,16},{48,32},{64,48},{80,64},{96,80},{112,96},{1... | collective-permute-start | bytes 2359304 | tf_op jit(solution)/shard_map/ppermute | solution.py:582
  121.8 5.3 %collective-permute-start.15 = (f32[232,128]{1,0:T(8,128)S(1)}, f32[232,128]{1,0:T(8,128)S(1)}, u32[]{:S(2)}, u32[]{:S(2)}) collective-permute-start(f32[232,128]{1,0:T(8,128)S(1)} %get-tuple-element.123.mine), channel_id=1, source_target_pairs={{0,1},{1,0},{2,3},{3,2},{4,5},{5,4},{6,7},{7,6},{8,9},{9,8},{10,11... | collective-permute-start | bytes 356360 | tf_op jit(solution)/shard_map/ppermute | solution.py:582
  124.7 25.1 %collective-permute-start.18 = (f32[8,6,32,128]{3,2,1,0:T(8,128)S(1)}, f32[8,6,32,128]{3,2,1,0:T(8,128)S(1)}, u32[]{:S(2)}, u32[]{:S(2)}) collective-permute-start(f32[8,6,32,128]{3,2,1,0:T(8,128)S(1)} %get-tuple-element.129), channel_id=1, source_target_pairs={{0,2},{2,4},{4,6},{6,8},{8,10},{10,12},{12,14},{14,0},{1,3},{3,5},... | collective-permute-start | bytes 2359304 | tf_op jit(solution)/shard_map/ppermute | solution.py:582
  126.9 22.9 %collective-permute-start.19 = (f32[8,6,32,128]{3,2,1,0:T(8,128)S(1)}, f32[8,6,32,128]{3,2,1,0:T(8,128)S(1)}, u32[]{:S(2)}, u32[]{:S(2)}) collective-permute-start(f32[8,6,32,128]{3,2,1,0:T(8,128)S(1)} %get-tuple-element.130), channel_id=1, source_target_pairs={{0,14},{2,0},{4,2},{6,4},{8,6},{10,8},{12,10},{14,12},{1,15},{3,1}... | collective-permute-start | bytes 2359304 | tf_op jit(solution)/shard_map/ppermute | solution.py:582
  127.0 22.7 %collective-permute-start.16 = (f32[48,32,128]{2,1,0:T(8,128)S(1)}, f32[48,32,128]{2,1,0:T(8,128)S(1)}, u32[]{:S(2)}, u32[]{:S(2)}) collective-permute-start(f32[48,32,128]{2,1,0:T(8,128)S(1)} %get-tuple-element.127), channel_id=1, source_target_pairs={{0,16},{16,32},{32,48},{48,64},{64,80},{80,96},{96,112},{112,0},{1... | collective-permute-start | bytes 2359304 | tf_op jit(solution)/shard_map/ppermute | solution.py:582
  127.6 22.2 %collective-permute-start.17 = (f32[48,32,128]{2,1,0:T(8,128)S(1)}, f32[48,32,128]{2,1,0:T(8,128)S(1)}, u32[]{:S(2)}, u32[]{:S(2)}) collective-permute-start(f32[48,32,128]{2,1,0:T(8,128)S(1)} %get-tuple-element.128), channel_id=1, source_target_pairs={{0,112},{16,0},{32,16},{48,32},{64,48},{80,64},{96,80},{112,96},{1... | collective-permute-start | bytes 2359304 | tf_op jit(solution)/shard_map/ppermute | solution.py:582

commit v14 on v13

--- a/solution.py
+++ b/solution.py
@@ -589,10 +589,10 @@
     )
     pot = potential.reshape(ROWS, SZ)
     key = key.reshape(SLOTS)
+    ordered = lax.sort((key, *[w.reshape(SLOTS) for w in weights]), num_keys=1, is_stable=False)
     starts = jnp.sum(
-        (key[None, :] < (lax.iota(jnp.int32, ROWS + 1) * (SZ * 64))[:, None]).astype(jnp.int32), axis=1
+        (ordered[0][None, :] < (lax.iota(jnp.int32, ROWS + 1) * (SZ * 64))[:, None]).astype(jnp.int32), axis=1
     )
-    ordered = lax.sort((key, *[w.reshape(SLOTS) for w in weights]), num_keys=1, is_stable=False)
     points = jnp.stack([ordered[0].astype(F32), *ordered[1:]])
     mat = build(starts, points)
 

time: 178 us -> 177 us (level)
  transfers between devices with their start and end apart: 20 -> 20, of which waited for: 2 -> 3; matrix products, arithmetic and copies ran while one was open for 0% -> 0% of each run, Pallas kernels for 0% -> 0%
where the time goes in v14:
time: 177 us
  blocking collectives  98.2 us (55%)
  starting transfers between devices  36.9 us (21%)
  Pallas kernels  31.8 us (18%)
  other arithmetic  7.14 us (4%)
    all_to_all x4, blocking collectives, local(): came = lax.all_to_all(sends, 'gy', 0, 0)  46.5 us
    ppermute x20, starting transfers between devices, shift(): lax.ppermute(value, axis, [(i, (i + by) % count) for i in range(count)])  36.9 us
    all_to_all x4, blocking collectives, local(): came = lax.all_to_all(sends, 'gx', 0, 0)  31.3 us
    all_to_all x1, blocking collectives, local(): lax.all_to_all(jnp.broadcast_to(gram[None], (devices,) + gram.shape), axe...  20.4 us
    pallas_call x4, Pallas kernels, step(): pl.pallas_call(functools.partial(step_kernel, first_step, last_step), out...  17.2 us
    sort x1, other arithmetic, local(): lax.sort((key, *[w.reshape(SLOTS) for w in weights]), num_keys=1, is_stab...  6.68 us
    pallas_call x1, Pallas kernels, build(): pl.pallas_call(build_kernel, out_shape=MATRIX, in_specs=[pl.BlockSpec(mem...  5.69 us
  transfers between devices with their start and end apart: 20, of which 3 were waited for; matrix products, arithmetic and copies ran while one was open for 0% of the time, Pallas kernels for 0%

profile of v14, /device:TPU:1, one launch (start us, length us, event | category | flops | bytes accessed | tf_op | source)
XLA Modules:
  0.0 177.0 jit_solution(2462186040413018390)
XLA Ops:
  0.7 3.4 %prepare.1 = (f32[64,32,128]{2,1,0:T(8,128)}, s32[64,128]{1,0:T(8,128)}, f32[8,128]{1,0:T(8,128)}, f32[64,128]{1,0:T(8,128)}, f32[64,128]{1,0:T(8,128)}, /*index=5*/f32[64,128]{1,0:T(8,128)}, f32[64,128]{1,0:T(8,128)}) custom-call(s32[1]{0:T(128)} %bitcast.16.count, f32[2,4]{1,0:T(2,128)} %coupling.1, f32[32,64,128]{2,1,0:T(8,128)} %bitcast.21, ...), custom_call_target="tpu_custom_call" | custom-call | tf_op jit(solution)/shard_map/prepare/pallas_call | solution.py:163
  4.0 6.7 %sort.33 = (s32[8192]{0:T(1024)S(1)}, f32[8192]{0:T(1024)S(1)}, f32[8192]{0:T(1024)S(1)}, f32[8192]{0:T(1024)S(1)}, f32[8192]{0:T(1024)S(1)}) sort(s32[8192]{0:T(1024)} %bitcast.23, f32[8192]{0:T(1024)} %bitcast.24, f32[8192]{0:T(1024)} %bitcast.25, f32[8192]{0:T(1024)} %bitcast.26, f32[8192]{0:T(1024)} %bitcast.27), dimensions={0}, to_apply=%region_0.0 | sort | flops 106496 | bytes 327680 | tf_op jit(solution)/shard_map/sort | solution.py:592
  11.4 5.7 %build.1.mat.refs_9_ = bf16[32,320,256]{2,1,0:T(8,128)(2,1)S(1)} custom-call(s32[65]{0:T(128)S(1)} %convert_reduce_fusion.starts, f32[5,8192]{1,0:T(8,128)S(1)} %stack.23.points), custom_call_target="tpu_custom_call" | custom-call | tf_op jit(solution)/shard_map/build/pallas_call | solution.py:232
  17.2 2.1 %first.1 = (f32[240,128]{1,0:T(8,128)S(1)}, f32[48,32,128]{2,1,0:T(8,128)S(1)}, f32[48,32,128]{2,1,0:T(8,128)S(1)}, f32[8,6,32,128]{3,2,1,0:T(8,128)S(1)}, f32[8,6,32,128]{3,2,1,0:T(8,128)S(1)}) custom-call(f32[64,32,128]{2,1,0:T(8,128)S(1)} %copy-done, bf16[32,320,256]{2,1,0:T(8,128)(2,1)S(1)} %build.1.mat.refs_9_, f32[8,128]{1,0:T(8,128)S(1)} %copy-done.2), custom_call_target="tpu_custom_call" | custom-call | tf_op jit(solution)/shard_map/first/pallas_call | solution.py:273
  19.3 4.5 %collective-permute-start = (f32[240,128]{1,0:T(8,128)S(1)}, f32[240,128]{1,0:T(8,128)S(1)}, u32[]{:S(2)}, u32[]{:S(2)}) collective-permute-start(f32[240,128]{1,0:T(8,128)S(1)} %get-tuple-element.83.mine), channel_id=1, source_target_pairs={{0,1},{1,0},{2,3},{3,2},{4,5},{5,4},{6,7},{7,6},{8,9},{9,8},{10,11... | collective-permute-start | bytes 368648 | tf_op jit(solution)/shard_map/ppermute | solution.py:582
  23.8 2.1 %collective-permute-start.3 = (f32[8,6,32,128]{3,2,1,0:T(8,128)S(1)}, f32[8,6,32,128]{3,2,1,0:T(8,128)S(1)}, u32[]{:S(2)}, u32[]{:S(2)}) collective-permute-start(f32[8,6,32,128]{3,2,1,0:T(8,128)S(1)} %get-tuple-element.89), channel_id=1, source_target_pairs={{0,2},{2,4},{4,6},{6,8},{8,10},{10,12},{12,14},{14,0},{1,3},{3,5},... | collective-permute-start | bytes 2359304 | tf_op jit(solution)/shard_map/ppermute | solution.py:582
  26.9 2.3 %collective-permute-start.1 = (f32[48,32,128]{2,1,0:T(8,128)S(1)}, f32[48,32,128]{2,1,0:T(8,128)S(1)}, u32[]{:S(2)}, u32[]{:S(2)}) collective-permute-start(f32[48,32,128]{2,1,0:T(8,128)S(1)} %get-tuple-element.87), channel_id=1, source_target_pairs={{0,16},{16,32},{32,48},{48,64},{64,80},{80,96},{96,112},{112,0},{1... | collective-permute-start | bytes 2359304 | tf_op jit(solution)/shard_map/ppermute | solution.py:582
  29.1 1.3 collective-permute-start.2
  30.6 11.7 %all_to_all.45.came = f32[8,32,128]{2,1,0:T(8,128)S(1)} all-to-all(f32[8,32,128]{2,1,0:T(8,128)S(1)} %get-tuple-element.92), channel_id=1, replica_groups=mesh['gx'=8,'gy'=8,'gz'=2] {'gy'}, dimensions={0} | all-to-all | bytes 262144 | tf_op jit(solution)/shard_map/all_to_all | solution.py:612
  42.3 7.8 %all_to_all.46.refs_8_ = f32[8,32,128]{2,1,0:T(8,128)S(1)} all-to-all(f32[8,32,128]{2,1,0:T(8,128)S(1)} %get-tuple-element.94), channel_id=1, replica_groups=mesh['gx'=8,'gy'=8,'gz'=2] {'gx'}, dimensions={0} | all-to-all | bytes 262144 | tf_op jit(solution)/shard_map/all_to_all | solution.py:614
  50.2 4.4 %step.4 = (f32[64,32,128]{2,1,0:T(8,128)S(1)}, f32[48,32,128]{2,1,0:T(8,128)S(1)}, f32[48,32,128]{2,1,0:T(8,128)S(1)}, f32[8,6,32,128]{3,2,1,0:T(8,128)S(1)}, f3...) custom-call(f32[64,32,128]{2,1,0:T(8,128)S(1)} %copy-done, ...), custom_call_target="tpu_custom_call" | custom-call | tf_op jit(solution)/shard_map/step/pallas_call | solution.py:494
  54.6 3.5 %collective-permute-start.5 = (f32[232,128]{1,0:T(8,128)S(1)}, f32[232,128]{1,0:T(8,128)S(1)}, u32[]{:S(2)}, u32[]{:S(2)}) collective-permute-start(f32[232,128]{1,0:T(8,128)S(1)} %get-tuple-element.96.mine), channel_id=1, source_target_pairs={{0,1},{1,0},{2,3},{3,2},{4,5},{5,4},{6,7},{7,6},{8,9},{9,8},{10,11... | collective-permute-start | bytes 356360 | tf_op jit(solution)/shard_map/ppermute | solution.py:582
  58.1 2.4 %collective-permute-start.8 = (f32[8,6,32,128]{3,2,1,0:T(8,128)S(1)}, f32[8,6,32,128]{3,2,1,0:T(8,128)S(1)}, u32[]{:S(2)}, u32[]{:S(2)}) collective-permute-start(f32[8,6,32,128]{3,2,1,0:T(8,128)S(1)} %get-tuple-element.102), channel_id=1, source_target_pairs={{0,2},{2,4},{4,6},{6,8},{8,10},{10,12},{12,14},{14,0},{1,3},{3,5},... | collective-permute-start | bytes 2359304 | tf_op jit(solution)/shard_map/ppermute | solution.py:582
  61.1 3.0 %collective-permute-start.7 = (f32[48,32,128]{2,1,0:T(8,128)S(1)}, f32[48,32,128]{2,1,0:T(8,128)S(1)}, u32[]{:S(2)}, u32[]{:S(2)}) collective-permute-start(f32[48,32,128]{2,1,0:T(8,128)S(1)} %get-tuple-element.101), channel_id=1, source_target_pairs={{0,112},{16,0},{32,16},{48,32},{64,48},{80,64},{96,80},{112,96},{1... | collective-permute-start | bytes 2359304 | tf_op jit(solution)/shard_map/ppermute | solution.py:582
  64.1 11.4 %all_to_all.47.came = f32[8,24,128]{2,1,0:T(8,128)S(1)} all-to-all(f32[8,24,128]{2,1,0:T(8,128)S(1)} %get-tuple-element.105), channel_id=1, replica_groups=mesh['gx'=8,'gy'=8,'gz'=2] {'gy'}, dimensions={0} | all-to-all | bytes 196608 | tf_op jit(solution)/shard_map/all_to_all | solution.py:612
  75.5 8.1 %all_to_all.48.refs_8_ = f32[8,24,128]{2,1,0:T(8,128)S(1)} all-to-all(f32[8,24,128]{2,1,0:T(8,128)S(1)} %get-tuple-element.107), channel_id=1, replica_groups=mesh['gx'=8,'gy'=8,'gz'=2] {'gx'}, dimensions={0} | all-to-all | bytes 196608 | tf_op jit(solution)/shard_map/all_to_all | solution.py:614
  83.7 4.5 %step.5 = (f32[64,32,128]{2,1,0:T(8,128)S(1)}, f32[48,32,128]{2,1,0:T(8,128)S(1)}, f32[48,32,128]{2,1,0:T(8,128)S(1)}, f32[8,6,32,128]{3,2,1,0:T(8,128)S(1)}, f3...) custom-call(f32[64,32,128]{2,1,0:T(8,128)S(1)} %get-tuple-element.95.refs_0_.refs_10_, ...), custom_call_target="tpu_custom_call" | custom-call | tf_op jit(solution)/shard_map/step/pallas_call | solution.py:494
  88.2 2.7 %collective-permute-start.10 = (f32[232,128]{1,0:T(8,128)S(1)}, f32[232,128]{1,0:T(8,128)S(1)}, u32[]{:S(2)}, u32[]{:S(2)}) collective-permute-start(f32[232,128]{1,0:T(8,128)S(1)} %get-tuple-element.110.mine), channel_id=1, source_target_pairs={{0,1},{1,0},{2,3},{3,2},{4,5},{5,4},{6,7},{7,6},{8,9},{9,8},{10,11... | collective-permute-start | bytes 356360 | tf_op jit(solution)/shard_map/ppermute | solution.py:582
  90.9 2.5 %collective-permute-start.13 = (f32[8,6,32,128]{3,2,1,0:T(8,128)S(1)}, f32[8,6,32,128]{3,2,1,0:T(8,128)S(1)}, u32[]{:S(2)}, u32[]{:S(2)}) collective-permute-start(f32[8,6,32,128]{3,2,1,0:T(8,128)S(1)} %get-tuple-element.116), channel_id=1, source_target_pairs={{0,2},{2,4},{4,6},{6,8},{8,10},{10,12},{12,14},{14,0},{1,3},{3,5},... | collective-permute-start | bytes 2359304 | tf_op jit(solution)/shard_map/ppermute | solution.py:582
  93.5 1.1 collective-permute-start.11
  94.5 2.5 %collective-permute-start.12 = (f32[48,32,128]{2,1,0:T(8,128)S(1)}, f32[48,32,128]{2,1,0:T(8,128)S(1)}, u32[]{:S(2)}, u32[]{:S(2)}) collective-permute-start(f32[48,32,128]{2,1,0:T(8,128)S(1)} %get-tuple-element.115), channel_id=1, source_target_pairs={{0,112},{16,0},{32,16},{48,32},{64,48},{80,64},{96,80},{112,96},{1... | collective-permute-start | bytes 2359304 | tf_op jit(solution)/shard_map/ppermute | solution.py:582
  97.1 12.4 %all_to_all.49.came = f32[8,24,128]{2,1,0:T(8,128)S(1)} all-to-all(f32[8,24,128]{2,1,0:T(8,128)S(1)} %get-tuple-element.119), channel_id=1, replica_groups=mesh['gx'=8,'gy'=8,'gz'=2] {'gy'}, dimensions={0} | all-to-all | bytes 196608 | tf_op jit(solution)/shard_map/all_to_all | solution.py:612
  109.5 7.7 %all_to_all.50.refs_8_ = f32[8,24,128]{2,1,0:T(8,128)S(1)} all-to-all(f32[8,24,128]{2,1,0:T(8,128)S(1)} %get-tuple-element.121), channel_id=1, replica_groups=mesh['gx'=8,'gy'=8,'gz'=2] {'gx'}, dimensions={0} | all-to-all | bytes 196608 | tf_op jit(solution)/shard_map/all_to_all | solution.py:614
  117.2 4.5 %step.6 = (f32[64,32,128]{2,1,0:T(8,128)S(1)}, f32[48,32,128]{2,1,0:T(8,128)S(1)}, f32[48,32,128]{2,1,0:T(8,128)S(1)}, f32[8,6,32,128]{3,2,1,0:T(8,128)S(1)}, f3...) custom-call(f32[64,32,128]{2,1,0:T(8,128)S(1)} %get-tuple-element.109.refs_0_.refs_10_, ...), custom_call_target="tpu_custom_call" | custom-call | tf_op jit(solution)/shard_map/step/pallas_call | solution.py:494
  121.7 2.7 %collective-permute-start.15 = (f32[232,128]{1,0:T(8,128)S(1)}, f32[232,128]{1,0:T(8,128)S(1)}, u32[]{:S(2)}, u32[]{:S(2)}) collective-permute-start(f32[232,128]{1,0:T(8,128)S(1)} %get-tuple-element.123.mine), channel_id=1, source_target_pairs={{0,1},{1,0},{2,3},{3,2},{4,5},{5,4},{6,7},{7,6},{8,9},{9,8},{10,11... | collective-permute-start | bytes 356360 | tf_op jit(solution)/shard_map/ppermute | solution.py:582
  124.5 2.2 %collective-permute-start.18 = (f32[8,6,32,128]{3,2,1,0:T(8,128)S(1)}, f32[8,6,32,128]{3,2,1,0:T(8,128)S(1)}, u32[]{:S(2)}, u32[]{:S(2)}) collective-permute-start(f32[8,6,32,128]{3,2,1,0:T(8,128)S(1)} %get-tuple-element.129), channel_id=1, source_target_pairs={{0,2},{2,4},{4,6},{6,8},{8,10},{10,12},{12,14},{14,0},{1,3},{3,5},... | collective-permute-start | bytes 2359304 | tf_op jit(solution)/shard_map/ppermute | solution.py:582
  127.6 3.0 %collective-permute-start.17 = (f32[48,32,128]{2,1,0:T(8,128)S(1)}, f32[48,32,128]{2,1,0:T(8,128)S(1)}, u32[]{:S(2)}, u32[]{:S(2)}) collective-permute-start(f32[48,32,128]{2,1,0:T(8,128)S(1)} %get-tuple-element.128), channel_id=1, source_target_pairs={{0,112},{16,0},{32,16},{48,32},{64,48},{80,64},{96,80},{112,96},{1... | collective-permute-start | bytes 2359304 | tf_op jit(solution)/shard_map/ppermute | solution.py:582
  130.6 11.1 %all_to_all.51.came = f32[8,24,128]{2,1,0:T(8,128)S(1)} all-to-all(f32[8,24,128]{2,1,0:T(8,128)S(1)} %get-tuple-element.132), channel_id=1, replica_groups=mesh['gx'=8,'gy'=8,'gz'=2] {'gy'}, dimensions={0} | all-to-all | bytes 196608 | tf_op jit(solution)/shard_map/all_to_all | solution.py:612
  141.8 7.7 %all_to_all.52.refs_8_ = f32[8,24,128]{2,1,0:T(8,128)S(1)} all-to-all(f32[8,24,128]{2,1,0:T(8,128)S(1)} %get-tuple-element.134), channel_id=1, replica_groups=mesh['gx'=8,'gy'=8,'gz'=2] {'gx'}, dimensions={0} | all-to-all | bytes 196608 | tf_op jit(solution)/shard_map/all_to_all | solution.py:614
  149.5 3.7 %step.7 = (f32[64,32,128]{2,1,0:T(8,128)S(1)}, f32[1,640]{1,0:T(1,128)S(1)}) custom-call(f32[64,32,128]{2,1,0:T(8,128)S(1)} %get-tuple-element.122.refs_0_, f32[232,128]{1,0:T(8,128)S(1)} %collective-permute-done.15.other.refs_1_, f32[48,32,128]{2,1,0:T(8,128)S(1)} %collective-permute-done.16.refs_2_, f32[48,32,128]{2,1,0:T(8,128)S(1)} %collective-permute-done.17.refs_3_, ...), custom_call_target="tpu_custom_call" | custom-call | tf_op jit(solution)/shard_map/step/pallas_call | solution.py:494
  153.4 20.4 %all_to_all.53.grams = f32[128,1,640]{2,1,0:T(1,128)S(1)} all-to-all(f32[128,1,640]{2,1,0:T(1,128)S(1)} %broadcast_in_dim.5), channel_id=1, replica_groups=mesh['gx'=8,'gy'=8,'gz'=2] {'gx','gy','gz'}, dimensions={0} | all-to-all | bytes 655360 | tf_op jit(solution)/shard_map/all_to_all | solution.py:628
  173.8 3.0 %finish.1 = f32[32,64,128]{2,1,0:T(8,128)} custom-call(f32[64,32,128]{2,1,0:T(8,128)S(1)} %get-tuple-element.135.field, f32[128,1,640]{2,1,0:T(1,128)S(1)} %all_to_all.53.grams), custom_call_target="tpu_custom_call" | custom-call | tf_op jit(solution)/shard_map/finish/pallas_call | solution.py:565
  (46 shorter events, 3.9 us)
Async XLA Ops:
  11.4 5.7 %copy-start = (f32[64,32,128]{2,1,0:T(8,128)S(1)}, f32[64,32,128]{2,1,0:T(8,128)}, u32[]{:S(2)}) copy-start(f32[64,32,128]{2,1,0:T(8,128)} %get-tuple-element.71.field.refs_0_.refs_10_) | copy-start | bytes 3145732
  11.4 5.7 %copy-start.2 = (f32[8,128]{1,0:T(8,128)S(1)}, f32[8,128]{1,0:T(8,128)}, u32[]{:S(2)}) copy-start(f32[8,128]{1,0:T(8,128)} %get-tuple-element.82.own) | copy-start | bytes 12292
  17.2 33.0 %copy-start.1 = (f32[8,8,128]{2,1,0:T(8,128)S(1)}, f32[8,8,128]{2,1,0:T(8,128)}, u32[]{:S(2)}) copy-start(f32[8,8,128]{2,1,0:T(8,128)} %param.8) | copy-start | bytes 98308
  19.3 7.6 %collective-permute-start = (f32[240,128]{1,0:T(8,128)S(1)}, f32[240,128]{1,0:T(8,128)S(1)}, u32[]{:S(2)}, u32[]{:S(2)}) collective-permute-start(f32[240,128]{1,0:T(8,128)S(1)} %get-tuple-element.83.mine), channel_id=1, source_target_pairs={{0,1},{1,0},{2,3},{3,2},{4,5},{5,4},{6,7},{7,6},{8,9},{9,8},{10,11... | collective-permute-start | bytes 368648 | tf_op jit(solution)/shard_map/ppermute | solution.py:582
  23.8 26.3 %collective-permute-start.3 = (f32[8,6,32,128]{3,2,1,0:T(8,128)S(1)}, f32[8,6,32,128]{3,2,1,0:T(8,128)S(1)}, u32[]{:S(2)}, u32[]{:S(2)}) collective-permute-start(f32[8,6,32,128]{3,2,1,0:T(8,128)S(1)} %get-tuple-element.89), channel_id=1, source_target_pairs={{0,2},{2,4},{4,6},{6,8},{8,10},{10,12},{12,14},{14,0},{1,3},{3,5},... | collective-permute-start | bytes 2359304 | tf_op jit(solution)/shard_map/ppermute | solution.py:582
  25.9 24.3 %collective-permute-start.4 = (f32[8,6,32,128]{3,2,1,0:T(8,128)S(1)}, f32[8,6,32,128]{3,2,1,0:T(8,128)S(1)}, u32[]{:S(2)}, u32[]{:S(2)}) collective-permute-start(f32[8,6,32,128]{3,2,1,0:T(8,128)S(1)} %get-tuple-element.90), channel_id=1, source_target_pairs={{0,14},{2,0},{4,2},{6,4},{8,6},{10,8},{12,10},{14,12},{1,15},{3,1}... | collective-permute-start | bytes 2359304 | tf_op jit(solution)/shard_map/ppermute | solution.py:582
  26.9 23.3 %collective-permute-start.1 = (f32[48,32,128]{2,1,0:T(8,128)S(1)}, f32[48,32,128]{2,1,0:T(8,128)S(1)}, u32[]{:S(2)}, u32[]{:S(2)}) collective-permute-start(f32[48,32,128]{2,1,0:T(8,128)S(1)} %get-tuple-element.87), channel_id=1, source_target_pairs={{0,16},{16,32},{32,48},{48,64},{64,80},{80,96},{96,112},{112,0},{1... | collective-permute-start | bytes 2359304 | tf_op jit(solution)/shard_map/ppermute | solution.py:582
  29.1 21.0 %collective-permute-start.2 = (f32[48,32,128]{2,1,0:T(8,128)S(1)}, f32[48,32,128]{2,1,0:T(8,128)S(1)}, u32[]{:S(2)}, u32[]{:S(2)}) collective-permute-start(f32[48,32,128]{2,1,0:T(8,128)S(1)} %get-tuple-element.88), channel_id=1, source_target_pairs={{0,112},{16,0},{32,16},{48,32},{64,48},{80,64},{96,80},{112,96},{1... | collective-permute-start | bytes 2359304 | tf_op jit(solution)/shard_map/ppermute | solution.py:582
  54.6 5.9 %collective-permute-start.5 = (f32[232,128]{1,0:T(8,128)S(1)}, f32[232,128]{1,0:T(8,128)S(1)}, u32[]{:S(2)}, u32[]{:S(2)}) collective-permute-start(f32[232,128]{1,0:T(8,128)S(1)} %get-tuple-element.96.mine), channel_id=1, source_target_pairs={{0,1},{1,0},{2,3},{3,2},{4,5},{5,4},{6,7},{7,6},{8,9},{9,8},{10,11... | collective-permute-start | bytes 356360 | tf_op jit(solution)/shard_map/ppermute | solution.py:582
  58.1 25.6 %collective-permute-start.8 = (f32[8,6,32,128]{3,2,1,0:T(8,128)S(1)}, f32[8,6,32,128]{3,2,1,0:T(8,128)S(1)}, u32[]{:S(2)}, u32[]{:S(2)}) collective-permute-start(f32[8,6,32,128]{3,2,1,0:T(8,128)S(1)} %get-tuple-element.102), channel_id=1, source_target_pairs={{0,2},{2,4},{4,6},{6,8},{8,10},{10,12},{12,14},{14,0},{1,3},{3,5},... | collective-permute-start | bytes 2359304 | tf_op jit(solution)/shard_map/ppermute | solution.py:582
  60.5 23.1 %collective-permute-start.9 = (f32[8,6,32,128]{3,2,1,0:T(8,128)S(1)}, f32[8,6,32,128]{3,2,1,0:T(8,128)S(1)}, u32[]{:S(2)}, u32[]{:S(2)}) collective-permute-start(f32[8,6,32,128]{3,2,1,0:T(8,128)S(1)} %get-tuple-element.103), channel_id=1, source_target_pairs={{0,14},{2,0},{4,2},{6,4},{8,6},{10,8},{12,10},{14,12},{1,15},{3,1}... | collective-permute-start | bytes 2359304 | tf_op jit(solution)/shard_map/ppermute | solution.py:582
  60.5 23.1 %collective-permute-start.6 = (f32[48,32,128]{2,1,0:T(8,128)S(1)}, f32[48,32,128]{2,1,0:T(8,128)S(1)}, u32[]{:S(2)}, u32[]{:S(2)}) collective-permute-start(f32[48,32,128]{2,1,0:T(8,128)S(1)} %get-tuple-element.100), channel_id=1, source_target_pairs={{0,16},{16,32},{32,48},{48,64},{64,80},{80,96},{96,112},{112,0},{1... | collective-permute-start | bytes 2359304 | tf_op jit(solution)/shard_map/ppermute | solution.py:582
  61.1 22.5 %collective-permute-start.7 = (f32[48,32,128]{2,1,0:T(8,128)S(1)}, f32[48,32,128]{2,1,0:T(8,128)S(1)}, u32[]{:S(2)}, u32[]{:S(2)}) collective-permute-start(f32[48,32,128]{2,1,0:T(8,128)S(1)} %get-tuple-element.101), channel_id=1, source_target_pairs={{0,112},{16,0},{32,16},{48,32},{64,48},{80,64},{96,80},{112,96},{1... | collective-permute-start | bytes 2359304 | tf_op jit(solution)/shard_map/ppermute | solution.py:582
  88.2 5.3 %collective-permute-start.10 = (f32[232,128]{1,0:T(8,128)S(1)}, f32[232,128]{1,0:T(8,128)S(1)}, u32[]{:S(2)}, u32[]{:S(2)}) collective-permute-start(f32[232,128]{1,0:T(8,128)S(1)} %get-tuple-element.110.mine), channel_id=1, source_target_pairs={{0,1},{1,0},{2,3},{3,2},{4,5},{5,4},{6,7},{7,6},{8,9},{9,8},{10,11... | collective-permute-start | bytes 356360 | tf_op jit(solution)/shard_map/ppermute | solution.py:582
  90.9 26.2 %collective-permute-start.13 = (f32[8,6,32,128]{3,2,1,0:T(8,128)S(1)}, f32[8,6,32,128]{3,2,1,0:T(8,128)S(1)}, u32[]{:S(2)}, u32[]{:S(2)}) collective-permute-start(f32[8,6,32,128]{3,2,1,0:T(8,128)S(1)} %get-tuple-element.116), channel_id=1, source_target_pairs={{0,2},{2,4},{4,6},{6,8},{8,10},{10,12},{12,14},{14,0},{1,3},{3,5},... | collective-permute-start | bytes 2359304 | tf_op jit(solution)/shard_map/ppermute | solution.py:582
  93.4 23.8 %collective-permute-start.14 = (f32[8,6,32,128]{3,2,1,0:T(8,128)S(1)}, f32[8,6,32,128]{3,2,1,0:T(8,128)S(1)}, u32[]{:S(2)}, u32[]{:S(2)}) collective-permute-start(f32[8,6,32,128]{3,2,1,0:T(8,128)S(1)} %get-tuple-element.117), channel_id=1, source_target_pairs={{0,14},{2,0},{4,2},{6,4},{8,6},{10,8},{12,10},{14,12},{1,15},{3,1}... | collective-permute-start | bytes 2359304 | tf_op jit(solution)/shard_map/ppermute | solution.py:582
  93.5 23.7 %collective-permute-start.11 = (f32[48,32,128]{2,1,0:T(8,128)S(1)}, f32[48,32,128]{2,1,0:T(8,128)S(1)}, u32[]{:S(2)}, u32[]{:S(2)}) collective-permute-start(f32[48,32,128]{2,1,0:T(8,128)S(1)} %get-tuple-element.114), channel_id=1, source_target_pairs={{0,16},{16,32},{32,48},{48,64},{64,80},{80,96},{96,112},{112,0},{1... | collective-permute-start | bytes 2359304 | tf_op jit(solution)/shard_map/ppermute | solution.py:582
  94.5 22.6 %collective-permute-start.12 = (f32[48,32,128]{2,1,0:T(8,128)S(1)}, f32[48,32,128]{2,1,0:T(8,128)S(1)}, u32[]{:S(2)}, u32[]{:S(2)}) collective-permute-start(f32[48,32,128]{2,1,0:T(8,128)S(1)} %get-tuple-element.115), channel_id=1, source_target_pairs={{0,112},{16,0},{32,16},{48,32},{64,48},{80,64},{96,80},{112,96},{1... | collective-permute-start | bytes 2359304 | tf_op jit(solution)/shard_map/ppermute | solution.py:582
  121.7 5.3 %collective-permute-start.15 = (f32[232,128]{1,0:T(8,128)S(1)}, f32[232,128]{1,0:T(8,128)S(1)}, u32[]{:S(2)}, u32[]{:S(2)}) collective-permute-start(f32[232,128]{1,0:T(8,128)S(1)} %get-tuple-element.123.mine), channel_id=1, source_target_pairs={{0,1},{1,0},{2,3},{3,2},{4,5},{5,4},{6,7},{7,6},{8,9},{9,8},{10,11... | collective-permute-start | bytes 356360 | tf_op jit(solution)/shard_map/ppermute | solution.py:582
  124.5 25.0 %collective-permute-start.18 = (f32[8,6,32,128]{3,2,1,0:T(8,128)S(1)}, f32[8,6,32,128]{3,2,1,0:T(8,128)S(1)}, u32[]{:S(2)}, u32[]{:S(2)}) collective-permute-start(f32[8,6,32,128]{3,2,1,0:T(8,128)S(1)} %get-tuple-element.129), channel_id=1, source_target_pairs={{0,2},{2,4},{4,6},{6,8},{8,10},{10,12},{12,14},{14,0},{1,3},{3,5},... | collective-permute-start | bytes 2359304 | tf_op jit(solution)/shard_map/ppermute | solution.py:582
  126.7 22.8 %collective-permute-start.19 = (f32[8,6,32,128]{3,2,1,0:T(8,128)S(1)}, f32[8,6,32,128]{3,2,1,0:T(8,128)S(1)}, u32[]{:S(2)}, u32[]{:S(2)}) collective-permute-start(f32[8,6,32,128]{3,2,1,0:T(8,128)S(1)} %get-tuple-element.130), channel_id=1, source_target_pairs={{0,14},{2,0},{4,2},{6,4},{8,6},{10,8},{12,10},{14,12},{1,15},{3,1}... | collective-permute-start | bytes 2359304 | tf_op jit(solution)/shard_map/ppermute | solution.py:582
  127.0 22.4 %collective-permute-start.16 = (f32[48,32,128]{2,1,0:T(8,128)S(1)}, f32[48,32,128]{2,1,0:T(8,128)S(1)}, u32[]{:S(2)}, u32[]{:S(2)}) collective-permute-start(f32[48,32,128]{2,1,0:T(8,128)S(1)} %get-tuple-element.127), channel_id=1, source_target_pairs={{0,16},{16,32},{32,48},{48,64},{64,80},{80,96},{96,112},{112,0},{1... | collective-permute-start | bytes 2359304 | tf_op jit(solution)/shard_map/ppermute | solution.py:582
  127.6 21.9 %collective-permute-start.17 = (f32[48,32,128]{2,1,0:T(8,128)S(1)}, f32[48,32,128]{2,1,0:T(8,128)S(1)}, u32[]{:S(2)}, u32[]{:S(2)}) collective-permute-start(f32[48,32,128]{2,1,0:T(8,128)S(1)} %get-tuple-element.128), channel_id=1, source_target_pairs={{0,112},{16,0},{32,16},{48,32},{64,48},{80,64},{96,80},{112,96},{1... | collective-permute-start | bytes 2359304 | tf_op jit(solution)/shard_map/ppermute | solution.py:582
